TPU v7x, 32 devices: a whole 2x2x4 slice. The times are simulated.
32 devices in a mesh: seq: 8 (over y, x, core), fsdp: 4 (over z).
Axes of the slice: x: 2, y: 2, z: 4, core: 2. Of those that a mesh axis runs over, the one named last changes fastest.
Arguments:
- clean_states: bfloat16 [4, 2048, 4096], P('fsdp', 'seq'), may hold values from -6 to 6
- noise_mask: int32 [4, 2048], P('fsdp', 'seq'), may hold values from 0 to 1, as said below
- mask_embed: bfloat16 [4096], replicated, may hold values from -6 to 6
- queries: bfloat16 [4, 2048, 2048], P('fsdp', 'seq'), may hold values from -96 to 96
- w_key: bfloat16 [4096, 512], P('fsdp'), may hold values from -0.09375 to 0.09375
- w_value: bfloat16 [4096, 512], P('fsdp'), may hold values from -0.09375 to 0.09375
Outputs:
- noisy_attention: bfloat16 [4, 2048, 2048], P('fsdp', 'seq')
Inputs may be any that keep to these rules, and one draw needn't show every extreme that they name: `noise_mask`: each block of 256 positions has its own masking rate; 1 marks a masked position.
All inputs are finite; a program needn't handle non-finite values.
Results may differ from a plain program's by a relative error of at most 0.011.
Values may be sent and summed in bfloat16 or wider, within the bound.
No kernel may reach another device: no remote copies, remote signals or barrier semaphores. Data moves between devices by JAX's collectives and lax.ppermute only.
A program may use at most 64 MiB of HBM per device.

v0:
```python
import jax
import jax.numpy as jnp
from jax import lax
from jax.sharding import PartitionSpec as P

HEADS = 16
HEAD_DIM = 128
BLOCK = 256


ROPE_BASE = 500000.0


def rotate(key_rows, positions):
    half_dim = key_rows.shape[-1] // 2
    frequency = ROPE_BASE ** (-(jnp.arange(half_dim, dtype=jnp.float32) * 2.0 / key_rows.shape[-1]))
    angles = positions[:, None] * frequency[None, :]
    cosine = jnp.cos(angles)[:, None, :]
    sine_part = jnp.sin(angles)[:, None, :]
    first_half = key_rows[..., :half_dim]
    second_half = key_rows[..., half_dim:]
    return jnp.concatenate(
        [
            first_half * cosine - second_half * sine_part,
            second_half * cosine + first_half * sine_part,
        ],
        -1,
    )


def shards(clean_states, noise_mask, mask_embed, queries, w_key, w_value):
    states = clean_states[0]
    noise_marks = noise_mask[0]
    length_dev = states.shape[0]
    kv_width = w_key.shape[1]
    kv_count = kv_width // HEAD_DIM
    groups = HEADS // kv_count
    score_scale = HEAD_DIM ** (-0.5)
    query_rows = queries[0].reshape(length_dev, kv_count, groups, HEAD_DIM)
    source_rows = jnp.concatenate([states, mask_embed[None, :]], 0)
    pieces = (
        lax.all_gather(w_key, "fsdp", axis=0, tiled=True),
        lax.all_gather(w_value, "fsdp", axis=0, tiled=True),
    )
    key_all = jnp.dot(source_rows, pieces[0], preferred_element_type=jnp.float32)
    value_all = jnp.dot(source_rows, pieces[1], preferred_element_type=jnp.float32)
    masked_rows = noise_marks[:, None] == 1
    clean_key_sums = key_all[:length_dev]
    clean_value_sums = value_all[:length_dev]
    noisy_key_sums = jnp.where(masked_rows, key_all[length_dev:], clean_key_sums)
    noisy_value_sums = jnp.where(masked_rows, value_all[length_dev:], clean_value_sums)
    key_sums = jnp.concatenate([clean_key_sums, noisy_key_sums], 0)
    value_sums = jnp.concatenate([clean_value_sums, noisy_value_sums], 0)
    first_row = lax.axis_index("seq") * length_dev
    positions = first_row + jnp.arange(length_dev, dtype=jnp.int32)
    both_positions = jnp.concatenate([positions, positions]).astype(jnp.float32)
    key_rows = (
        rotate(key_sums.reshape(2 * length_dev, kv_count, HEAD_DIM), both_positions)
        .astype(jnp.bfloat16)
        .reshape(2 * length_dev, kv_width)
    )
    value_rows = value_sums.astype(jnp.bfloat16)
    clean_keys = key_rows[:length_dev]
    clean_values = value_rows[:length_dev]
    noisy_keys = key_rows[length_dev:]
    noisy_values = value_rows[length_dev:]
    query_block = positions // BLOCK

    def absorb(running, key_part, value_part, allowed):
        row_max, row_sum, mixture = running
        key_count = key_part.shape[0]
        scores = (
            jnp.einsum(
                "qkgd,tkd->qkgt",
                query_rows,
                key_part.reshape(key_count, kv_count, HEAD_DIM),
                preferred_element_type=jnp.float32,
            )
            * score_scale
        )
        mask_wide = allowed[:, None, None, :]
        scores = jnp.where(mask_wide, scores, -1e30)
        new_max = jnp.maximum(row_max, jnp.max(scores, -1))
        weights = jnp.where(mask_wide, jnp.exp(scores - new_max[..., None]), 0.0)
        rescale = jnp.exp(row_max - new_max)
        row_sum = row_sum * rescale + jnp.sum(weights, -1)
        mixture = mixture * rescale[..., None] + jnp.einsum(
            "qkgt,tkd->qkgd",
            weights.astype(jnp.bfloat16),
            value_part.reshape(key_count, kv_count, HEAD_DIM),
            preferred_element_type=jnp.float32,
        )
        return (new_max, row_sum, mixture)

    def sweep(running, key_stack, value_stack, start_row, same_copy):
        rounds = key_stack.shape[0] // BLOCK

        def sub_step(number, running):
            offset = number * BLOCK
            key_part = lax.dynamic_slice_in_dim(key_stack, offset, BLOCK, 0)
            value_part = lax.dynamic_slice_in_dim(value_stack, offset, BLOCK, 0)
            key_block = (start_row + offset) // BLOCK
            if same_copy:
                allowed = query_block[:, None] == key_block
            else:
                allowed = (query_block[:, None] > key_block) & (key_block >= 0)
            allowed = jnp.broadcast_to(allowed, (length_dev, BLOCK))
            return absorb(running, key_part, value_part, allowed)

        return lax.fori_loop(0, rounds, sub_step, running)

    running = (
        jnp.full((length_dev, kv_count, groups), -1e30, jnp.float32),
        jnp.zeros((length_dev, kv_count, groups), jnp.float32),
        jnp.zeros((length_dev, kv_count, groups, HEAD_DIM), jnp.float32),
    )
    running = sweep(running, noisy_keys, noisy_values, first_row, True)
    pieces = (
        lax.all_gather(clean_keys, "seq", axis=0, tiled=True),
        lax.all_gather(clean_values, "seq", axis=0, tiled=True),
    )
    running = sweep(running, pieces[0], pieces[1], jnp.int32(0), False)
    row_max, row_sum, mixture = running
    output = (
        (mixture / row_sum[..., None])
        .astype(jnp.bfloat16)
        .reshape(length_dev, kv_count * groups * HEAD_DIM)
    )
    return output[None]


def solution(mesh):
    placed = (
        P("fsdp", "seq", None),
        P("fsdp", "seq"),
        P(),
        P("fsdp", "seq", None),
        P("fsdp", None),
        P("fsdp", None),
    )
    return jax.shard_map(
        shards, mesh=mesh, in_specs=placed, out_specs=P("fsdp", "seq", None), check_vma=False
    )
```

profile of v0, /device:TPU:7, one launch (start us, length us, event | category | flops | bytes accessed | tf_op | source)
XLA Modules:
  0.0 293.3 jit_solution(13838438799487748107)
XLA Ops:
  9.5 81.5 %all-gather.7.cloned.1.call-done = bf16[4096,512]{1,0:T(8,128)(2,1)} async-done(((bf16[1024,512]{1,0:T(8,128)(2,1)}), bf16[4096,512]{1,0:T(8,128)(2,1)}) %all-gather.7.cloned.1.call-update) | async-done | bytes 4194320 | tf_op jit(solution)/shard_map/all_gather | solution.py:43
  90.9 4.2 %fusion.33 = f32[257,512]{1,0:T(8,128)S(1)} fusion(bf16[4096,512]{1,0:T(8,128)(2,1)} %all-gather.7.cloned.1.call-done, bf16[1,4096]{1,0:T(2,128)(2,1)S(1)} %broadcast_in_dim.141, bf16[256,4096]{1,0:T(8,128)(2,1)} %bitcast.118), kind=kOutput, calls=%fused_computation.45 | convolution fusion | flops 1082146816 | bytes 6825984 | tf_op jit(solution)/shard_map/dot_general | solution.py:46
  96.0 1.0 multiply_cosine_fusion
  97.0 74.8 %all-gather.5.cloned.1.call-done = bf16[4096,512]{1,0:T(8,128)(2,1)} async-done(((bf16[1024,512]{1,0:T(8,128)(2,1)}), bf16[4096,512]{1,0:T(8,128)(2,1)}) %all-gather.5.cloned.1.call-update) | async-done | bytes 4194320 | tf_op jit(solution)/shard_map/all_gather | solution.py:42
  171.8 3.5 %fusion.34 = f32[257,512]{1,0:T(8,128)S(1)} fusion(bf16[4096,512]{1,0:T(8,128)(2,1)} %all-gather.5.cloned.1.call-done, bf16[1,4096]{1,0:T(2,128)(2,1)S(1)} %broadcast_in_dim.141, bf16[256,4096]{1,0:T(8,128)(2,1)S(1)} %bitcast.119), kind=kOutput, calls=%fused_computation.46 | convolution fusion | flops 1082146816 | bytes 6825984 | tf_op jit(solution)/shard_map/dot_general | solution.py:45
  177.0 0.8 copy.22
  177.8 1.5 copy.18
  180.0 0.8 copy.33
  180.9 0.8 bitcast_reduce_fusion.1
  181.7 1.0 fusion.22
  182.8 2.4 bitcast_add_fusion.1
  185.3 14.4 %all-gather.11.cloned.1.call-done = bf16[2048,512]{1,0:T(8,128)(2,1)} async-done(((bf16[256,512]{1,0:T(8,128)(2,1)}), bf16[2048,512]{1,0:T(8,128)(2,1)}) %all-gather.11.cloned.1.call-update) | async-done | bytes 2097168 | tf_op jit(solution)/shard_map/all_gather | solution.py:120
  199.7 30.0 %all-gather.9.cloned.1.call-done = bf16[2048,512]{0,1:T(8,128)(2,1)} async-done(((bf16[256,512]{0,1:T(8,128)(2,1)}), bf16[2048,512]{0,1:T(8,128)(2,1)}) %all-gather.9.cloned.1.call-update) | async-done | bytes 2097168 | tf_op jit(solution)/shard_map/all_gather | solution.py:119
  229.6 53.9 %while.13 = (s32[]{:T(128)}, f32[256,4,4]{0,2,1:T(4,128)S(1)}, f32[256,4,4]{0,2,1:T(4,128)S(1)}, f32[256,4,4,128]{0,3,2,1:T(8,128)}, bf16[2048,512]{0,1:T(8,128)...) while((s32[]{:T(128)}, f32[256,4,4]{0,2,1:T(4,128)S(1)}, ...), condition=%wide.region_5.6_spmd.clone, body=%wide.region_2.5_spmd.clone.sunk | while | flops 551563776 | bytes 36963736 | solution.py:110
  229.6 1.0 constant_dynamic-slice_fusion.5
  230.7 1.0 constant_dynamic-slice_fusion.4
  231.7 0.8 bitcast_reduce_fusion.3
  232.6 1.0 fusion.66
  233.6 1.4 bitcast_add_fusion.3
  235.0 1.3 copy-done.1
  236.4 1.0 constant_dynamic-slice_fusion.5
  237.5 1.0 constant_dynamic-slice_fusion.4
  238.5 0.8 bitcast_reduce_fusion.3
  239.3 1.0 fusion.66
  240.4 1.4 bitcast_add_fusion.3
  241.8 1.3 copy-done.1
  243.1 1.0 constant_dynamic-slice_fusion.5
  244.2 1.0 constant_dynamic-slice_fusion.4
  245.2 0.8 bitcast_reduce_fusion.3
  246.0 1.0 fusion.66
  247.1 1.4 bitcast_add_fusion.3
  248.5 1.3 copy-done.1
  249.8 1.0 constant_dynamic-slice_fusion.5
  250.9 1.0 constant_dynamic-slice_fusion.4
  251.9 0.8 bitcast_reduce_fusion.3
  252.8 1.0 fusion.66
  253.8 1.4 bitcast_add_fusion.3
  255.3 1.3 copy-done.1
  256.6 1.0 constant_dynamic-slice_fusion.5
  257.7 1.0 constant_dynamic-slice_fusion.4
  258.7 0.8 bitcast_reduce_fusion.3
  259.5 1.0 fusion.66
  260.6 1.4 bitcast_add_fusion.3
  262.0 1.3 copy-done.1
  263.3 1.0 constant_dynamic-slice_fusion.5
  264.4 1.0 constant_dynamic-slice_fusion.4
  265.4 0.8 bitcast_reduce_fusion.3
  266.3 1.0 fusion.66
  267.3 1.4 bitcast_add_fusion.3
  268.7 1.3 copy-done.1
  270.0 1.0 constant_dynamic-slice_fusion.5
  271.2 1.0 constant_dynamic-slice_fusion.4
  272.1 0.8 bitcast_reduce_fusion.3
  273.0 1.0 fusion.66
  274.0 1.4 bitcast_add_fusion.3
  275.5 1.3 copy-done.1
  276.8 1.0 constant_dynamic-slice_fusion.5
  277.9 1.0 constant_dynamic-slice_fusion.4
  278.9 0.8 bitcast_reduce_fusion.3
  279.7 1.0 fusion.66
  280.8 1.4 bitcast_add_fusion.3
  282.2 1.3 copy-done.1
  283.5 1.8 divide_convert_fusion
  285.3 1.4 copy.34
  (94 shorter events, 7.4 us)
Async XLA Ops:
  6.5 84.4 %all-gather.7.cloned.1.call-start = ((), (), s32[]{:S(2)}) async-start(), calls=%async_computation.1 | async-start | bytes 5242880 | tf_op jit(solution)/shard_map/all_gather | solution.py:43
  7.3 164.6 %all-gather.5.cloned.1.call-start = ((), (), s32[]{:S(2)}) async-start(), calls=%async_computation | async-start | bytes 5242880 | tf_op jit(solution)/shard_map/all_gather | solution.py:42
  8.0 191.7 %all-gather.11.cloned.1.call-start = ((), (), s32[]{:S(2)}) async-start(), calls=%async_computation.3 | async-start | bytes 2359296 | tf_op jit(solution)/shard_map/all_gather | solution.py:120
  90.9 80.9 %copy-start.3 = (bf16[1,256,4096]{2,1,0:T(8,128)(2,1)S(1)}, bf16[1,256,4096]{2,1,0:T(8,128)(2,1)}, u32[]{:S(2)}) copy-start(bf16[1,256,4096]{2,1,0:T(8,128)(2,1)} %param.8) | copy-start | bytes 6291460
  95.9 133.7 %all-gather.9.cloned.1.call-start = ((), (), s32[]{:S(2)}) async-start(), calls=%async_computation.2 | async-start | bytes 2359296 | tf_op jit(solution)/shard_map/all_gather | solution.py:119
  180.9 1.9 copy-start.2
  231.7 1.9 copy-start
  235.0 1.3 copy-start.1
  238.4 1.9 copy-start
  241.8 1.3 copy-start.1
  245.2 1.9 copy-start
  248.5 1.3 copy-start.1
  251.9 1.9 copy-start
  255.2 1.3 copy-start.1
  258.7 1.9 copy-start
  262.0 1.3 copy-start.1
  265.4 1.9 copy-start
  268.7 1.3 copy-start.1
  272.1 1.9 copy-start
  275.4 1.3 copy-start.1
  278.9 1.9 copy-start
  282.2 1.3 copy-start.1
Sparse Core Ops, SparseCore 0:
  8.9 81.9 all-gather.6
  92.5 79.2 all-gather.4
  173.7 25.9 all-gather.10
  201.4 28.1 all-gather.8
where the time goes:
time: 296 us; the launch traced here: 293 us
  waiting for transfers between devices  202 us (68%)
  local copies, waits for them, and re-layouts  34 us (11%)
  matrix products  28.8 us (10%)
  other arithmetic  14.4 us (5%)
  between operations  13.3 us (4%)
    all_gather x1, waiting for transfers between devices, shards(): lax.all_gather(w_value, 'fsdp', axis=0, tiled=True)  81.5 us
    all_gather x1, waiting for transfers between devices, shards(): lax.all_gather(w_key, 'fsdp', axis=0, tiled=True)  74.8 us
    all_gather x1, waiting for transfers between devices, shards(): lax.all_gather(clean_keys, 'seq', axis=0, tiled=True)  30 us
    all_gather x1, waiting for transfers between devices, shards(): lax.all_gather(clean_values, 'seq', axis=0, tiled=True)  14.4 us
    dot_general x9, matrix products, absorb(): jnp.einsum('qkgt,tkd->qkgd', weights.astype(jnp.bfloat16), value_part.res...  13.5 us
    while x40, local copies, waits for them, and re-layouts  10.5 us
    reduce_sum x9, other arithmetic, absorb(): row_sum = row_sum * rescale + jnp.sum(weights, -1)  9.23 us
    dynamic_slice x16, local copies, waits for them, and re-layouts, sub_step(): value_part = lax.dynamic_slice_in_dim(value_stack, offset, BLOCK, 0)  8.85 us
  transfers between devices with their start and end apart: 4, of which 4 were waited for; matrix products, arithmetic and copies ran while one was open for 7% of the time, Pallas kernels for 0%

commit v1 on v0

v1 whole, which is shorter than its diff:
```python
import functools
import math

import jax
import jax.numpy as jnp
from jax import lax
from jax.experimental import pallas as pl
from jax.experimental.pallas import tpu as pltpu
from jax.sharding import PartitionSpec as P

HEADS = 16
HEAD_DIM = 128
BLOCK = 256
ROPE_BASE = 500000.0
MASK_ROWS = 16
LOG2E = math.log2(math.e)
VMEM_LIMIT = 48 * 1024 * 1024


def rotation(positions):
    half_dim = HEAD_DIM // 2
    frequency = ROPE_BASE ** (-(jnp.arange(half_dim, dtype=jnp.float32) * 2.0 / HEAD_DIM))
    angles = positions.astype(jnp.float32)[:, None] * frequency[None, :]
    cosine = jnp.cos(angles)
    sine = jnp.sin(angles)
    return jnp.concatenate([cosine, cosine], -1), jnp.concatenate([-sine, sine], -1)


def partial_kernel(count, has_total, starts, rows_ref, *refs):
    total_in = refs[0] if has_total else None
    pieces = refs[int(has_total) : int(has_total) + count]
    total_out = refs[-1]
    total_out[...] = gather_sum(starts, rows_ref, total_in, pieces)


def gather_sum(starts, rows_ref, total_in, pieces):
    total = None if total_in is None else total_in[...]
    for number, piece in enumerate(pieces):
        depth = piece.shape[0]
        first = pl.multiple_of(starts[number], 128)
        term = jnp.dot(rows_ref[:, pl.ds(first, depth)], piece[...], preferred_element_type=jnp.float32)
        total = term if total is None else total + term
    return total


def finish_kernel(count, has_total, starts, rows_ref, *refs):
    total_in = refs[0] if has_total else None
    refs = refs[int(has_total) :]
    pieces = refs[:count]
    cos_ref, sin_ref, marks_ref, clean_ref, noisy_ref = refs[count:]
    sums = gather_sum(starts, rows_ref, total_in, pieces)
    tokens = clean_ref.shape[0]
    width = clean_ref.shape[1]
    clean_sums = sums[:tokens]
    noisy_sums = jnp.where(marks_ref[...] == 1, sums[tokens : tokens + 1], clean_sums)
    cosine, sine = cos_ref[...], sin_ref[...]
    for part, out_ref in ((clean_sums, clean_ref), (noisy_sums, noisy_ref)):
        for lane in range(0, width // 2, HEAD_DIM):
            key = part[:, lane : lane + HEAD_DIM]
            rotated = key * cosine + pltpu.roll(key, HEAD_DIM // 2, 1) * sine
            out_ref[:, lane : lane + HEAD_DIM] = rotated.astype(jnp.bfloat16)
        out_ref[:, width // 2 :] = part[:, width // 2 :].astype(jnp.bfloat16)


def whole(array):
    zeros = (0,) * array.ndim
    return pl.BlockSpec(array.shape, lambda i, *_: zeros)


def project_partial(rows, total, pieces, starts):
    extra = [] if total is None else [total]
    width = pieces[0].shape[1]
    operands = [rows, *extra, *pieces]
    return pl.pallas_call(
        functools.partial(partial_kernel, len(pieces), total is not None),
        out_shape=jax.ShapeDtypeStruct((rows.shape[0], width), jnp.float32),
        grid_spec=pltpu.PrefetchScalarGridSpec(
            num_scalar_prefetch=1,
            grid=(1,),
            in_specs=[whole(a) for a in operands],
            out_specs=pl.BlockSpec((rows.shape[0], width), lambda i, *_: (0, 0)),
        ),
        compiler_params=pltpu.CompilerParams(vmem_limit_bytes=VMEM_LIMIT),
        name="project_partial",
    )(starts, *operands)


def project_finish(rows, total, pieces, starts, cosine, sine, marks):
    extra = [] if total is None else [total]
    width = pieces[0].shape[1]
    tokens = marks.shape[0]
    operands = [rows, *extra, *pieces, cosine, sine, marks]
    shape = jax.ShapeDtypeStruct((tokens, width), jnp.bfloat16)
    return pl.pallas_call(
        functools.partial(finish_kernel, len(pieces), total is not None),
        out_shape=(shape, shape),
        grid_spec=pltpu.PrefetchScalarGridSpec(
            num_scalar_prefetch=1,
            grid=(1,),
            in_specs=[whole(a) for a in operands],
            out_specs=[pl.BlockSpec((tokens, width), lambda i, *_: (0, 0))] * 2,
        ),
        compiler_params=pltpu.CompilerParams(vmem_limit_bytes=VMEM_LIMIT),
        name="project_finish",
    )(starts, *operands)


def scores_of(query, key):
    scores = lax.dot_general(query, key, (((1,), (1,)), ((), ())), preferred_element_type=jnp.float32)
    return scores * (HEAD_DIM**-0.5 * LOG2E)


def own_kernel(groups, flags, q_ref, ck_ref, cv_ref, nk_ref, nv_ref, acc_ref, stat_ref):
    core = flags[0]
    lanes = lax.broadcasted_iota(jnp.int32, (BLOCK, HEAD_DIM), 1)
    for head in range(groups):
        for side in range(2):
            mine = pl.ds(side * BLOCK, BLOCK)
            other = pl.ds((1 - side) * BLOCK, BLOCK)
            query = q_ref[mine, head * HEAD_DIM : (head + 1) * HEAD_DIM]
            near = scores_of(query, nk_ref[mine, :])
            far = scores_of(query, ck_ref[other, :])
            far = jnp.where(core == 1 - side, far, -1e30)
            top = jnp.maximum(jnp.max(near, -1, keepdims=True), jnp.max(far, -1, keepdims=True))
            near = jnp.exp2(near - top)
            far = jnp.where(core == 1 - side, jnp.exp2(far - top), 0.0)
            total = jnp.sum(near, -1, keepdims=True) + jnp.sum(far, -1, keepdims=True)
            mixed = jnp.dot(near.astype(jnp.bfloat16), nv_ref[mine, :], preferred_element_type=jnp.float32)
            mixed += jnp.dot(far.astype(jnp.bfloat16), cv_ref[other, :], preferred_element_type=jnp.float32)
            acc_ref[head, mine, :] = mixed
            stat_ref[head, mine, :] = jnp.where(lanes < HEAD_DIM // 2, top, total)


def later_kernel(groups, count, last, flags, q_ref, acc_in, stat_in, *refs):
    keys, values = refs[:count], refs[count : 2 * count]
    if last:
        own_out, other_out, acc_ref, stat_ref = refs[2 * count :]
    else:
        acc_ref, stat_ref = refs[2 * count :]
    acc_ref[...] = acc_in[...]
    stat_ref[...] = stat_in[...]
    lanes = lax.broadcasted_iota(jnp.int32, (BLOCK, HEAD_DIM), 1)

    for number in range(count):

        @pl.when(flags[number] == 1)
        def _(key_ref=keys[number], value_ref=values[number]):
            for head in range(groups):
                for side in range(2):
                    mine = pl.ds(side * BLOCK, BLOCK)
                    query = q_ref[mine, head * HEAD_DIM : (head + 1) * HEAD_DIM]
                    stat = stat_ref[head, mine, :]
                    top, total = stat[:, :1], stat[:, HEAD_DIM // 2 : HEAD_DIM // 2 + 1]
                    scores = scores_of(query, key_ref[...])
                    new_top = jnp.maximum(top, jnp.max(scores, -1, keepdims=True))
                    weights = jnp.exp2(scores - new_top)
                    rescale = jnp.exp2(top - new_top)
                    total = total * rescale + jnp.sum(weights, -1, keepdims=True)
                    mixed = jnp.dot(
                        weights.astype(jnp.bfloat16), value_ref[...], preferred_element_type=jnp.float32
                    )
                    acc_ref[head, mine, :] = acc_ref[head, mine, :] * rescale + mixed
                    stat_ref[head, mine, :] = jnp.where(lanes < HEAD_DIM // 2, new_top, total)

    if last:
        for head in range(groups):
            for side, out_ref in ((0, own_out), (1, other_out)):
                mine = pl.ds(side * BLOCK, BLOCK)
                total = stat_ref[head, mine, :][:, HEAD_DIM // 2 : HEAD_DIM // 2 + 1]
                out_ref[:, head * HEAD_DIM : (head + 1) * HEAD_DIM] = (
                    acc_ref[head, mine, :] / total
                ).astype(jnp.bfloat16)


def attention_shapes(query_rows, kv_heads):
    tokens, columns = query_rows.shape
    heads = columns // HEAD_DIM
    groups = heads // kv_heads
    q_spec = pl.BlockSpec((tokens, groups * HEAD_DIM), lambda g, *_: (0, g))
    state_spec = pl.BlockSpec((groups, tokens, HEAD_DIM), lambda g, *_: (g, 0, 0))
    state = jax.ShapeDtypeStruct((heads, tokens, HEAD_DIM), jnp.float32)
    return tokens, groups, q_spec, state_spec, state


def kv_specs(part, kv_heads):
    rows = part.shape[0]
    key_spec = pl.BlockSpec((rows, HEAD_DIM), lambda g, *_: (0, g))
    value_spec = pl.BlockSpec((rows, HEAD_DIM), lambda g, *_: (0, g + kv_heads))
    return key_spec, value_spec


def attend_own(flags, query_rows, clean, noisy, kv_heads):
    tokens, groups, q_spec, state_spec, state = attention_shapes(query_rows, kv_heads)
    key_spec, value_spec = kv_specs(clean, kv_heads)
    return pl.pallas_call(
        functools.partial(own_kernel, groups),
        out_shape=(state, state),
        grid_spec=pltpu.PrefetchScalarGridSpec(
            num_scalar_prefetch=1,
            grid=(kv_heads,),
            in_specs=[q_spec, key_spec, value_spec, key_spec, value_spec],
            out_specs=[state_spec, state_spec],
        ),
        compiler_params=pltpu.CompilerParams(vmem_limit_bytes=VMEM_LIMIT),
        name="attend_own",
    )(flags, query_rows, clean, clean, noisy, noisy)


def attend_later(flags, query_rows, running, parts, kv_heads, last):
    tokens, groups, q_spec, state_spec, state = attention_shapes(query_rows, kv_heads)
    specs = [kv_specs(part, kv_heads) for part in parts]
    if last:
        half = jax.ShapeDtypeStruct((tokens // 2, query_rows.shape[1]), jnp.bfloat16)
        half_spec = pl.BlockSpec((tokens // 2, groups * HEAD_DIM), lambda g, *_: (0, g))
        out_shape, out_specs = (half, half), [half_spec, half_spec]
        scratch = [pltpu.VMEM((groups, tokens, HEAD_DIM), jnp.float32)] * 2
    else:
        out_shape, out_specs, scratch = (state, state), [state_spec, state_spec], []
    return pl.pallas_call(
        functools.partial(later_kernel, groups, len(parts), last),
        out_shape=out_shape,
        grid_spec=pltpu.PrefetchScalarGridSpec(
            num_scalar_prefetch=1,
            grid=(kv_heads,),
            in_specs=[q_spec, state_spec, state_spec, *(s[0] for s in specs), *(s[1] for s in specs)],
            out_specs=out_specs,
            scratch_shapes=scratch,
        ),
        compiler_params=pltpu.CompilerParams(vmem_limit_bytes=VMEM_LIMIT),
        name="attend_last" if last else "attend_later",
    )(flags, query_rows, *running, *parts, *parts)


def shards(seq_size, fsdp_size, clean_states, noise_mask, mask_embed, queries, w_key, w_value):
    chips = seq_size // 2
    place = lax.axis_index("seq")
    core = lax.rem(place, 2)
    chip = place // 2
    shard = lax.axis_index("fsdp")
    states = clean_states[0]
    marks = noise_mask[0]
    query_own = queries[0]
    tokens = states.shape[0]
    depth, kv_width = w_key.shape
    half_width = kv_width // 2
    kv_heads = half_width // HEAD_DIM
    query_half = query_own.shape[1] // 2

    def swap_cores(array):
        return lax.ppermute(array, "seq", [(s, s ^ 1) for s in range(seq_size)])

    def to_chip(array, flip, sources=None):
        sources = range(chips) if sources is None else sources
        pairs = [(2 * s + c, 2 * (s ^ flip) + c) for s in sources for c in range(2)]
        return lax.ppermute(array, "seq", pairs)

    def to_shard(array, flip):
        return lax.ppermute(array, "fsdp", [(s, s ^ flip) for s in range(fsdp_size)])

    def weight_rows(first, count):
        return jnp.concatenate(
            [lax.dynamic_slice(w, (first, core * half_width), (count, half_width)) for w in (w_key, w_value)], 1
        )

    rounds = []
    if chips == 4:
        quarter = depth // chips
        mine = weight_rows(chip * quarter, quarter)
        arrived = [(shard ^ flip, to_shard(mine, flip)) for flip in range(1, fsdp_size)]
        for source, piece in arrived:
            along_x = to_chip(piece, 1)
            along_y = to_chip(piece, 2)
            corner_a = to_chip(along_x[: quarter // 2], 2)
            corner_b = to_chip(along_y[quarter // 2 :], 1)
            base = source * depth
            rounds.append(
                (
                    [piece, along_x, along_y, corner_a, corner_b],
                    [
                        base + chip * quarter,
                        base + (chip ^ 1) * quarter,
                        base + (chip ^ 2) * quarter,
                        base + (chip ^ 3) * quarter,
                        base + (chip ^ 3) * quarter + quarter // 2,
                    ],
                )
            )
        early = ([weight_rows(0, depth)], [shard * depth])
        for pieces, starts in rounds[:-1]:
            early = (early[0] + pieces, early[1] + starts)
        final = rounds[-1]
    else:
        early = None
        gathered = lax.all_gather(weight_rows(0, depth), "fsdp", axis=0, tiled=True)
        final = ([gathered], [jnp.int32(0)])

    def as_scalars(values):
        return jnp.stack([jnp.asarray(v, jnp.int32) for v in values])

    mask_rows = jnp.broadcast_to(mask_embed[None, :], (MASK_ROWS, mask_embed.shape[0]))
    rows = jnp.concatenate([states, swap_cores(states), mask_rows], 0)
    all_marks = jnp.concatenate([marks, swap_cores(marks)])[:, None]
    query_kept = lax.dynamic_slice(query_own, (0, core * query_half), (tokens, query_half))
    query_sent = lax.dynamic_slice(query_own, (0, (1 - core) * query_half), (tokens, query_half))
    query_rows = jnp.concatenate([query_kept, swap_cores(query_sent)], 0)
    steps = jnp.arange(tokens, dtype=jnp.int32)
    cosine, sine = rotation(jnp.concatenate([place * tokens + steps, (place ^ 1) * tokens + steps]))

    total = None if early is None else project_partial(rows, None, early[0], as_scalars(early[1]))
    clean, noisy = project_finish(rows, total, final[0], as_scalars(final[1]), cosine, sine, all_marks)

    if chips == 4:
        along_x = to_chip(clean, 1, (0, 1, 2))
        along_y = to_chip(clean, 2, (0, 1))
        half = clean.shape[0] // 2
        corner_a = to_chip(along_x[:half], 2, (0, 1))
        corner_b = to_chip(along_y[half:], 1, (2, 3))
        stages = [([along_x, along_y], [1, 2]), ([corner_a, corner_b], [3, 3])]
    else:
        stages = []
        for flip in range(1, chips):
            stages.append(([to_chip(clean, flip, [s for s in range(chips) if s < s ^ flip])], [flip]))
    running = attend_own(as_scalars([core]), query_rows, clean, noisy, kv_heads)
    for number, (parts, flips) in enumerate(stages):
        flags = as_scalars([(chip ^ flip) < chip for flip in flips])
        running = attend_later(flags, query_rows, running, parts, kv_heads, number == len(stages) - 1)
    own_out, other_out = running
    received = swap_cores(other_out)
    output = jnp.where(
        core == 0,
        jnp.concatenate([own_out, received], 1),
        jnp.concatenate([received, own_out], 1),
    )
    return output[None]


def solution(mesh):
    placed = (
        P("fsdp", "seq", None),
        P("fsdp", "seq"),
        P(),
        P("fsdp", "seq", None),
        P("fsdp", None),
        P("fsdp", None),
    )
    return jax.shard_map(
        functools.partial(shards, mesh.shape["seq"], mesh.shape["fsdp"]),
        mesh=mesh,
        in_specs=placed,
        out_specs=P("fsdp", "seq", None),
        check_vma=False,
    )
```

time: 296 us -> 132 us (0.45)
  the two profiles are of different devices: /device:TPU:7 before, /device:TPU:23 now
where the time goes in v1:
time: 132 us; the launch traced here: 131 us
  Pallas kernels  51.4 us (39%)
  waiting for transfers between devices  33.3 us (25%)
  starting transfers between devices  28.8 us (22%)
  local copies, waits for them, and re-layouts  8.91 us (7%)
  other arithmetic  8.64 us (7%)
    pallas_call x2, Pallas kernels, attend_later(): pl.pallas_call(functools.partial(later_kernel, groups, len(parts), last),...  36 us
    ppermute x3, waiting for transfers between devices, to_shard(): lax.ppermute(array, 'fsdp', [(s, s ^ flip) for s in range(fsdp_size)])  19.1 us
    ppermute x4, starting transfers between devices, swap_cores(): return lax.ppermute(array, 'seq', [(s, s ^ 1) for s in range(seq_size)])  14.7 us
    ppermute x16, waiting for transfers between devices, to_chip(): return lax.ppermute(array, 'seq', pairs)  12.7 us
    ppermute x16, starting transfers between devices, to_chip(): return lax.ppermute(array, 'seq', pairs)  11.4 us
    pallas_call x1, Pallas kernels, attend_own(): pl.pallas_call(functools.partial(own_kernel, groups), out_shape=(state, s...  6.48 us
    pallas_call x1, Pallas kernels, project_partial(): pl.pallas_call(functools.partial(partial_kernel, len(pieces), total is no...  4.92 us
    pallas_call x1, Pallas kernels, project_finish(): pl.pallas_call(functools.partial(finish_kernel, len(pieces), total is not...  3.95 us
  transfers between devices with their start and end apart: 23, of which 9 were waited for; matrix products, arithmetic and copies ran while one was open for 11% of the time, Pallas kernels for 22%

profile of v1, /device:TPU:23, one launch (start us, length us, event | category | flops | bytes accessed | tf_op | source)
XLA Modules:
  0.0 131.3 jit_solution(13161962835477156026)
XLA Ops:
  0.0 0.7 collective-permute-start.1
  0.7 0.9 dynamic_slice.29
  1.6 0.9 dynamic_slice.28
  2.5 1.4 %collective-permute-start.2 = (bf16[256,512]{1,0:T(8,128)(2,1)S(1)}, bf16[256,512]{1,0:T(8,128)(2,1)S(1)}, u32[]{:S(2)}, u32[]{:S(2)}) collective-permute-start(bf16[256,512]{1,0:T(8,128)(2,1)S(1)} %pad_maximum_fusion.3), channel_id=1, source_target_pairs={{0,1},{1,0},{2,3},{3,2},{4,5},{5,4},{6,7},{7,6},{8,9},{9,8},{10,11... | collective-permute-start | bytes 786440 | tf_op jit(solution)/shard_map/ppermute | solution.py:258
  3.9 0.1 collective-permute-start.7
  4.0 1.3 collective-permute-start.12
  5.3 0.9 collective-permute-start.17
  6.2 1.0 fusion
  7.2 6.7 %collective-permute-done.2.refs_1_ = bf16[256,512]{1,0:T(8,128)(2,1)S(1)} collective-permute-done((bf16[256,512]{1,0:T(8,128)(2,1)S(1)}, bf16[256,512]{1,0:T(8,128)(2,1)S(1)}, u32[]{:S(2)}, u32[]{:S(2)}) %collective-permute-start.2) | collective-permute-done | bytes 262176 | tf_op jit(solution)/shard_map/ppermute | solution.py:258
  14.0 0.3 collective-permute-start.3
  14.2 0.0 collective-permute-done.17
  14.2 0.2 collective-permute-start.4
  14.4 1.7 %collective-permute-done.7.refs_6_ = bf16[256,512]{1,0:T(8,128)(2,1)} collective-permute-done((bf16[256,512]{1,0:T(8,128)(2,1)S(1)}, bf16[256,512]{1,0:T(8,128)(2,1)}, u32[]{:S(2)}, u32[]{:S(2)}) %collective-permute-start.7) | collective-permute-done | bytes 262176 | tf_op jit(solution)/shard_map/ppermute | solution.py:258
  16.1 0.3 collective-permute-start.8
  16.4 1.1 constant_dynamic-slice_fusion
  17.5 0.0 copy-start.4
  17.5 0.1 pad_maximum_fusion.2.refs_0_
  17.6 10.7 %collective-permute-done.12.refs_1_ = bf16[256,512]{1,0:T(8,128)(2,1)} collective-permute-done((bf16[256,512]{1,0:T(8,128)(2,1)S(1)}, bf16[256,512]{1,0:T(8,128)(2,1)}, u32[]{:S(2)}, u32[]{:S(2)}) %collective-permute-start.12) | collective-permute-done | bytes 262176 | tf_op jit(solution)/shard_map/ppermute | solution.py:258
  28.3 0.2 collective-permute-start.9
  28.6 0.3 collective-permute-start.13
  28.8 0.0 collective-permute-done.4.refs_3_
  28.8 1.2 collective-permute-start.14
  30.1 0.1 pad_maximum_fusion.4.refs_6_
  30.2 0.7 slice.32
  30.9 0.0 collective-permute-done.8.refs_7_
  30.9 0.2 collective-permute-start.5
  31.1 0.1 pad_maximum_fusion.5.refs_7_
  31.3 0.1 stack.93.starts
  31.4 0.1 stack.105.starts
  31.4 0.7 pad_add_fusion
  32.1 0.1 copy.7.refs_8_
  32.3 2.8 %collective-permute-done.9.refs_8_ = bf16[256,512]{1,0:T(8,128)(2,1)S(1)} collective-permute-done((bf16[256,512]{1,0:T(8,128)(2,1)}, bf16[256,512]{1,0:T(8,128)(2,1)S(1)}, u32[]{:S(2)}, u32[]{:S(2)}) %collective-permute-start.9) | collective-permute-done | bytes 262176 | tf_op jit(solution)/shard_map/ppermute | solution.py:255
  35.2 0.3 collective-permute-start.6
  35.4 0.9 collective-permute-start.10
  36.4 4.4 %collective-permute-done.14.refs_3_ = bf16[256,512]{1,0:T(8,128)(2,1)S(1)} collective-permute-done((bf16[256,512]{1,0:T(8,128)(2,1)}, bf16[256,512]{1,0:T(8,128)(2,1)S(1)}, u32[]{:S(2)}, u32[]{:S(2)}) %collective-permute-start.14) | collective-permute-done | bytes 262176 | tf_op jit(solution)/shard_map/ppermute | solution.py:255
  40.8 0.3 collective-permute-start.11
  41.0 2.5 %collective-permute-done.5.refs_4_ = bf16[128,512]{1,0:T(8,128)(2,1)S(1)} collective-permute-done((bf16[128,512]{1,0:T(8,128)(2,1)}, bf16[128,512]{1,0:T(8,128)(2,1)S(1)}, u32[]{:S(2)}, u32[]{:S(2)}) %collective-permute-start.5) | collective-permute-done | bytes 131104 | tf_op jit(solution)/shard_map/ppermute | solution.py:255
  43.6 0.2 collective-permute-start.15
  43.8 0.3 collective-permute-start.16
  44.1 0.7 broadcast_in_dim.4
  44.8 0.0 copy-start.2
  44.8 3.9 %pad_maximum_fusion.rows_ref = bf16[528,4096]{1,0:T(8,128)(2,1)} fusion(bf16[16,4096]{1,0:T(8,128)(2,1)S(1)} %broadcast_in_dim.4, bf16[256,4096]{1,0:T(8,128)(2,1)} %collective-permute-done.1, bf16[256,4096]{1,0:T(8,128)(2,1)} %bitcast.31), kind=kLoop, calls=%fused_computation | loop fusion | flops 12976128 | bytes 8650752 | tf_op jit(solution)/shard_map/concatenate | solution.py:301
  48.7 0.0 collective-permute-done.6.refs_5_
  48.8 4.9 %project_partial.1.refs_0_ = f32[528,512]{1,0:T(8,128)S(1)} custom-call(s32[11]{0:T(128)S(1)} %stack.105.starts, bf16[528,4096]{1,0:T(8,128)(2,1)} %pad_maximum_fusion.rows_ref, bf16[1024,512]{1,0:T(8,128)(2,1)S(1)} %pad_maximum_fusion.2.refs_0_, bf16[256,512]{1,0:T(8,128)(2,1)S(1)} %copy-done.2, bf16[256,512]{1,0:T(8,128)(2,1)S(1)} %collective-permute-done.3.refs_2_, ...), custom_call_target="tpu_custom_call" | custom-call | tf_op jit(solution)/shard_map/project_partial/pallas_call | solution.py:74
  53.7 4.0 %project_finish.1 = (bf16[512,512]{1,0:T(8,128)(2,1)S(1)}, bf16[512,512]{1,0:T(8,128)(2,1)S(1)}) custom-call(s32[5]{0:T(128)S(1)} %stack.93.starts, bf16[528,4096]{1,0:T(8,128)(2,1)} %pad_maximum_fusion.rows_ref, f32[528,512]{1,0:T(8,128)S(1)} %project_partial.1.refs_0_, bf16[256,512]{1,0:T(8,128)(2,1)} %collective-permute-done.12.refs_1_, ...), custom_call_target="tpu_custom_call" | custom-call | tf_op jit(solution)/shard_map/project_finish/pallas_call | solution.py:94
  57.7 1.3 collective-permute-start.18
  59.0 1.3 collective-permute-start.19
  60.3 2.1 %dynamic-slice_bitcast_fusion.1 = (bf16[256,1024]{1,0:T(8,128)(2,1)S(1)}, bf16[256,1024]{1,0:T(8,128)(2,1)}) fusion(bf16[1,256,2048]{2,1,0:T(8,128)(2,1)} %param.9, s32[]{:T(128)S(6)} %select_n.38, s32[]{:T(128)S(6)} %select_n.39), kind=kLoop, calls=%fused_computation.5 | loop fusion | bytes 2097160 | tf_op jit(solution)/shard_map/dynamic_slice | solution.py:303
  62.4 4.4 %collective-permute-start = (bf16[256,1024]{1,0:T(8,128)(2,1)}, bf16[256,1024]{1,0:T(8,128)(2,1)}, u32[]{:S(2)}, u32[]{:S(2)}) collective-permute-start(bf16[256,1024]{1,0:T(8,128)(2,1)} %get-tuple-element.22), channel_id=1, source_target_pairs={{0,4},{4,0},{8,12},{12,8},{16,20},{20,16},{24,28},{28,24},{1,5},{5... | collective-permute-start | bytes 1572872 | tf_op jit(solution)/shard_map/ppermute | solution.py:250
  66.7 1.9 %collective-permute-done.18.refs_0_.refs_2_ = bf16[512,512]{1,0:T(8,128)(2,1)S(1)} collective-permute-done((bf16[512,512]{1,0:T(8,128)(2,1)S(1)}, bf16[512,512]{1,0:T(8,128)(2,1)S(1)}, u32[]{:S(2)}, u32[]{:S(2)}) %collective-permute-start.18) | collective-permute-done | bytes 524320 | tf_op jit(solution)/shard_map/ppermute | solution.py:255
  68.6 1.3 collective-permute-start.20
  69.9 1.0 collective-permute-done.19.refs_1_.refs_3_
  70.9 0.7 slice.39
  71.6 2.9 %collective-permute-start.21 = (bf16[256,512]{1,0:T(8,128)(2,1)}, bf16[256,512]{1,0:T(8,128)(2,1)S(1)}, u32[]{:S(2)}, u32[]{:S(2)}) collective-permute-start(bf16[256,512]{1,0:T(8,128)(2,1)} %slice.39), channel_id=1, source_target_pairs={{16,24},{20,28},{24,16},{28,20},{17,25},{21,29},{25,17},{29,21},{1... | collective-permute-start | bytes 786440 | tf_op jit(solution)/shard_map/ppermute | solution.py:255
  74.5 0.1 add_convert_fusion.1.flags
  74.6 0.1 add_convert_fusion.2.flags
  74.7 1.1 pad_maximum_fusion.1.q_ref
  75.8 6.5 %attend_own.1 = (f32[8,512,128]{2,1,0:T(8,128)S(1)}, f32[8,512,128]{2,1,0:T(8,128)}) custom-call(s32[1]{0:T(128)} %bitcast.5.flags, bf16[512,1024]{1,0:T(8,128)(2,1)S(1)} %pad_maximum_fusion.1.q_ref, bf16[512,512]{1,0:T(8,128)(2,1)S(1)} %get-tuple-element.13.ck_ref.cv_ref, bf16[512,512]{1,0:T(8,128)(2,1)S(1)} %get-tuple-element.13.ck_ref.cv_ref, ...), custom_call_target="tpu_custom_call" | custom-call | tf_op jit(solution)/shard_map/attend_own/pallas_call | solution.py:195
  82.3 1.4 %copy-done = f32[8,512,128]{2,1,0:T(8,128)} copy-done((f32[8,512,128]{2,1,0:T(8,128)}, f32[8,512,128]{2,1,0:T(8,128)S(1)}, u32[]{:S(2)}) %copy-start) | copy-done | bytes 2097176
  83.7 16.9 %attend_later.1 = (f32[8,512,128]{2,1,0:T(8,128)S(1)}, f32[8,512,128]{2,1,0:T(8,128)}) custom-call(s32[2]{0:T(128)S(1)} %add_convert_fusion.2.flags, bf16[512,1024]{1,0:T(8,128)(2,1)S(1)} %pad_maximum_fusion.1.q_ref, f32[8,512,128]{2,1,0:T(8,128)} %copy-done, f32[8,512,128]{2,1,0:T(8,128)} %get-tuple-element.16.stat_in, ...), custom_call_target="tpu_custom_call" | custom-call | tf_op jit(solution)/shard_map/attend_later/pallas_call | solution.py:219
  100.6 19.1 %attend_last.1 = (bf16[256,1024]{1,0:T(8,128)(2,1)S(1)}, bf16[256,1024]{1,0:T(8,128)(2,1)S(1)}) custom-call(s32[2]{0:T(128)S(1)} %add_convert_fusion.1.flags, bf16[512,1024]{1,0:T(8,128)(2,1)S(1)} %pad_maximum_fusion.1.q_ref, f32[8,512,128]{2,1,0:T(8,128)S(1)} %get-tuple-element.17.acc_in, f32[8,512,128]{2,1,0:T(8,128)} %get-tuple-element.18.stat_in, ...), custom_call_target="tpu_custom_call" | custom-call | tf_op jit(solution)/shard_map/attend_last/pallas_call | solution.py:219
  119.7 8.7 %collective-permute-start.22 = (bf16[256,1024]{1,0:T(8,128)(2,1)S(1)}, bf16[256,1024]{1,0:T(8,128)(2,1)S(1)}, u32[]{:S(2)}, u32[]{:S(2)}) collective-permute-start(bf16[256,1024]{1,0:T(8,128)(2,1)S(1)} %get-tuple-element.20), channel_id=1, source_target_pairs={{0,4},{4,0},{8,12},{12,8},{16,20},{20,16},{24,28},{28,24},{1,5},{5... | collective-permute-start | bytes 1572872 | tf_op jit(solution)/shard_map/ppermute | solution.py:250
  128.4 1.5 %collective-permute-done.22 = bf16[256,1024]{1,0:T(8,128)(2,1)S(1)} collective-permute-done((bf16[256,1024]{1,0:T(8,128)(2,1)S(1)}, bf16[256,1024]{1,0:T(8,128)(2,1)S(1)}, u32[]{:S(2)}, u32[]{:S(2)}) %collective-permute-start.22) | collective-permute-done | bytes 524320 | tf_op jit(solution)/shard_map/ppermute | solution.py:250
  130.0 1.4 %maximum_select_fusion = bf16[1,256,2048]{2,1,0:T(8,128)(2,1)} fusion(bf16[1,256,1024]{2,1,0:T(8,128)(2,1)S(1)} %bitcast.32, bf16[1,256,1024]{2,1,0:T(8,128)(2,1)S(1)} %bitcast.29, pred[]{:T(512)S(6)} %eq.3), kind=kLoop, calls=%fused_computation.3 | loop fusion | flops 4718592 | bytes 2097153 | tf_op jit(solution)/shard_map/jit(_where)/select_n | solution.py:329
  (29 shorter events, 0.2 us)
Async XLA Ops:
  0.0 16.4 %copy-start.3 = (bf16[1024,512]{1,0:T(8,128)(2,1)S(1)}, bf16[1024,512]{1,0:T(8,128)(2,1)}, u32[]{:S(2)}) copy-start(bf16[1024,512]{1,0:T(8,128)(2,1)} %param.11) | copy-start | bytes 3145732
  0.0 43.8 %collective-permute-start.1 = (bf16[256,4096]{1,0:T(8,128)(2,1)}, bf16[256,4096]{1,0:T(8,128)(2,1)}, u32[]{:S(2)}, u32[]{:S(2)}) collective-permute-start(bf16[256,4096]{1,0:T(8,128)(2,1)} %bitcast.30), channel_id=1, source_target_pairs={{0,4},{4,0},{8,12},{12,8},{16,20},{20,16},{24,28},{28,24},{1,5},{5... | collective-permute-start | bytes 6291464 | tf_op jit(solution)/shard_map/ppermute | solution.py:250
  2.5 11.4 %collective-permute-start.2 = (bf16[256,512]{1,0:T(8,128)(2,1)S(1)}, bf16[256,512]{1,0:T(8,128)(2,1)S(1)}, u32[]{:S(2)}, u32[]{:S(2)}) collective-permute-start(bf16[256,512]{1,0:T(8,128)(2,1)S(1)} %pad_maximum_fusion.3), channel_id=1, source_target_pairs={{0,1},{1,0},{2,3},{3,2},{4,5},{5,4},{6,7},{7,6},{8,9},{9,8},{10,11... | collective-permute-start | bytes 786440 | tf_op jit(solution)/shard_map/ppermute | solution.py:258
  3.9 12.2 %collective-permute-start.7 = (bf16[256,512]{1,0:T(8,128)(2,1)S(1)}, bf16[256,512]{1,0:T(8,128)(2,1)}, u32[]{:S(2)}, u32[]{:S(2)}) collective-permute-start(bf16[256,512]{1,0:T(8,128)(2,1)S(1)} %pad_maximum_fusion.3), channel_id=1, source_target_pairs={{0,2},{1,3},{2,0},{3,1},{4,6},{5,7},{6,4},{7,5},{8,10},{9,11},{10,... | collective-permute-start | bytes 786440 | tf_op jit(solution)/shard_map/ppermute | solution.py:258
  4.0 24.4 %collective-permute-start.12 = (bf16[256,512]{1,0:T(8,128)(2,1)S(1)}, bf16[256,512]{1,0:T(8,128)(2,1)}, u32[]{:S(2)}, u32[]{:S(2)}) collective-permute-start(bf16[256,512]{1,0:T(8,128)(2,1)S(1)} %pad_maximum_fusion.3), channel_id=1, source_target_pairs={{0,3},{1,2},{2,1},{3,0},{4,7},{5,6},{6,5},{7,4},{8,11},{9,10},{10,... | collective-permute-start | bytes 786440 | tf_op jit(solution)/shard_map/ppermute | solution.py:258
  5.3 8.9 %collective-permute-start.17 = (s32[256]{0:T(256)}, s32[256]{0:T(256)S(1)}, u32[]{:S(2)}, u32[]{:S(2)}) collective-permute-start(s32[256]{0:T(256)} %bitcast.34), channel_id=1, source_target_pairs={{0,4},{4,0},{8,12},{12,8},{16,20},{20,16},{24,28},{28,24},{1,5},{5... | collective-permute-start | bytes 3080 | tf_op jit(solution)/shard_map/ppermute | solution.py:250
  13.9 3.7 %copy-start.1 = (bf16[256,512]{1,0:T(8,128)(2,1)}, bf16[256,512]{1,0:T(8,128)(2,1)S(1)}, u32[]{:S(2)}) copy-start(bf16[256,512]{1,0:T(8,128)(2,1)S(1)} %collective-permute-done.2.refs_1_) | copy-start | bytes 786436
  14.0 14.6 %collective-permute-start.3 = (bf16[256,512]{1,0:T(8,128)(2,1)S(1)}, bf16[256,512]{1,0:T(8,128)(2,1)S(1)}, u32[]{:S(2)}, u32[]{:S(2)}) collective-permute-start(bf16[256,512]{1,0:T(8,128)(2,1)S(1)} %collective-permute-done.2.refs_1_), channel_id=1, source_target_pairs={{0,8},{4,12},{8,0},{12,4},{16,24},{20,28},{24,16},{28,20},{1,9},{5... | collective-permute-start | bytes 786440 | tf_op jit(solution)/shard_map/ppermute | solution.py:255
  14.2 15.9 %copy-start.5 = (s32[256]{0:T(256)}, s32[256]{0:T(256)S(1)}, u32[]{:S(2)}) copy-start(s32[256]{0:T(256)S(1)} %collective-permute-done.17) | copy-start | bytes 3076
  14.2 14.6 %collective-permute-start.4 = (bf16[256,512]{1,0:T(8,128)(2,1)S(1)}, bf16[256,512]{1,0:T(8,128)(2,1)S(1)}, u32[]{:S(2)}, u32[]{:S(2)}) collective-permute-start(bf16[256,512]{1,0:T(8,128)(2,1)S(1)} %collective-permute-done.2.refs_1_), channel_id=1, source_target_pairs={{0,16},{4,20},{8,24},{12,28},{16,0},{20,4},{24,8},{28,12},{1,17},{... | collective-permute-start | bytes 786440 | tf_op jit(solution)/shard_map/ppermute | solution.py:255
  16.1 14.7 %collective-permute-start.8 = (bf16[256,512]{1,0:T(8,128)(2,1)}, bf16[256,512]{1,0:T(8,128)(2,1)S(1)}, u32[]{:S(2)}, u32[]{:S(2)}) collective-permute-start(bf16[256,512]{1,0:T(8,128)(2,1)} %collective-permute-done.7.refs_6_), channel_id=1, source_target_pairs={{0,8},{4,12},{8,0},{12,4},{16,24},{20,28},{24,16},{28,20},{1,9},{5... | collective-permute-start | bytes 786440 | tf_op jit(solution)/shard_map/ppermute | solution.py:255
  17.5 13.9 %copy-start.4 = (s32[1,256]{1,0:T(1,128)S(1)}, s32[1,256]{1,0:T(1,128)}, u32[]{:S(2)}) copy-start(s32[1,256]{1,0:T(1,128)} %param.7) | copy-start | bytes 3076
  28.3 6.8 %collective-permute-start.9 = (bf16[256,512]{1,0:T(8,128)(2,1)}, bf16[256,512]{1,0:T(8,128)(2,1)S(1)}, u32[]{:S(2)}, u32[]{:S(2)}) collective-permute-start(bf16[256,512]{1,0:T(8,128)(2,1)} %collective-permute-done.7.refs_6_), channel_id=1, source_target_pairs={{0,16},{4,20},{8,24},{12,28},{16,0},{20,4},{24,8},{28,12},{1,17},{... | collective-permute-start | bytes 786440 | tf_op jit(solution)/shard_map/ppermute | solution.py:255
  28.6 6.9 %collective-permute-start.13 = (bf16[256,512]{1,0:T(8,128)(2,1)}, bf16[256,512]{1,0:T(8,128)(2,1)S(1)}, u32[]{:S(2)}, u32[]{:S(2)}) collective-permute-start(bf16[256,512]{1,0:T(8,128)(2,1)} %collective-permute-done.12.refs_1_), channel_id=1, source_target_pairs={{0,8},{4,12},{8,0},{12,4},{16,24},{20,28},{24,16},{28,20},{1,9},{5... | collective-permute-start | bytes 786440 | tf_op jit(solution)/shard_map/ppermute | solution.py:255
  28.8 11.9 %collective-permute-start.14 = (bf16[256,512]{1,0:T(8,128)(2,1)}, bf16[256,512]{1,0:T(8,128)(2,1)S(1)}, u32[]{:S(2)}, u32[]{:S(2)}) collective-permute-start(bf16[256,512]{1,0:T(8,128)(2,1)} %collective-permute-done.12.refs_1_), channel_id=1, source_target_pairs={{0,16},{4,20},{8,24},{12,28},{16,0},{20,4},{24,8},{28,12},{1,17},{... | collective-permute-start | bytes 786440 | tf_op jit(solution)/shard_map/ppermute | solution.py:255
  30.9 12.7 %collective-permute-start.5 = (bf16[128,512]{1,0:T(8,128)(2,1)}, bf16[128,512]{1,0:T(8,128)(2,1)S(1)}, u32[]{:S(2)}, u32[]{:S(2)}) collective-permute-start(bf16[128,512]{1,0:T(8,128)(2,1)} %slice.32), channel_id=1, source_target_pairs={{0,16},{4,20},{8,24},{12,28},{16,0},{20,4},{24,8},{28,12},{1,17},{... | collective-permute-start | bytes 393224 | tf_op jit(solution)/shard_map/ppermute | solution.py:255
  35.2 13.6 %collective-permute-start.6 = (bf16[128,512]{1,0:T(8,128)(2,1)S(1)}, bf16[128,512]{1,0:T(8,128)(2,1)S(1)}, u32[]{:S(2)}, u32[]{:S(2)}) collective-permute-start(bf16[128,512]{1,0:T(8,128)(2,1)S(1)} %slice.33), channel_id=1, source_target_pairs={{0,8},{4,12},{8,0},{12,4},{16,24},{20,28},{24,16},{28,20},{1,9},{5... | collective-permute-start | bytes 393224 | tf_op jit(solution)/shard_map/ppermute | solution.py:255
  35.4 13.3 %collective-permute-start.10 = (bf16[128,512]{1,0:T(8,128)(2,1)S(1)}, bf16[128,512]{1,0:T(8,128)(2,1)S(1)}, u32[]{:S(2)}, u32[]{:S(2)}) collective-permute-start(bf16[128,512]{1,0:T(8,128)(2,1)S(1)} %slice.34), channel_id=1, source_target_pairs={{0,16},{4,20},{8,24},{12,28},{16,0},{20,4},{24,8},{28,12},{1,17},{... | collective-permute-start | bytes 393224 | tf_op jit(solution)/shard_map/ppermute | solution.py:255
  40.8 8.0 %collective-permute-start.11 = (bf16[128,512]{1,0:T(8,128)(2,1)S(1)}, bf16[128,512]{1,0:T(8,128)(2,1)S(1)}, u32[]{:S(2)}, u32[]{:S(2)}) collective-permute-start(bf16[128,512]{1,0:T(8,128)(2,1)S(1)} %slice.35), channel_id=1, source_target_pairs={{0,8},{4,12},{8,0},{12,4},{16,24},{20,28},{24,16},{28,20},{1,9},{5... | collective-permute-start | bytes 393224 | tf_op jit(solution)/shard_map/ppermute | solution.py:255
  43.6 10.1 %collective-permute-start.15 = (bf16[128,512]{1,0:T(8,128)(2,1)S(1)}, bf16[128,512]{1,0:T(8,128)(2,1)S(1)}, u32[]{:S(2)}, u32[]{:S(2)}) collective-permute-start(bf16[128,512]{1,0:T(8,128)(2,1)S(1)} %slice.36), channel_id=1, source_target_pairs={{0,16},{4,20},{8,24},{12,28},{16,0},{20,4},{24,8},{28,12},{1,17},{... | collective-permute-start | bytes 393224 | tf_op jit(solution)/shard_map/ppermute | solution.py:255
  43.8 9.9 %collective-permute-start.16 = (bf16[128,512]{1,0:T(8,128)(2,1)S(1)}, bf16[128,512]{1,0:T(8,128)(2,1)S(1)}, u32[]{:S(2)}, u32[]{:S(2)}) collective-permute-start(bf16[128,512]{1,0:T(8,128)(2,1)S(1)} %slice.37), channel_id=1, source_target_pairs={{0,8},{4,12},{8,0},{12,4},{16,24},{20,28},{24,16},{28,20},{1,9},{5... | collective-permute-start | bytes 393224 | tf_op jit(solution)/shard_map/ppermute | solution.py:255
  44.8 4.0 %copy-start.2 = (bf16[256,512]{1,0:T(8,128)(2,1)S(1)}, bf16[256,512]{1,0:T(8,128)(2,1)}, u32[]{:S(2)}) copy-start(bf16[256,512]{1,0:T(8,128)(2,1)} %copy-done.1) | copy-start | bytes 786436
  57.7 10.9 %collective-permute-start.18 = (bf16[512,512]{1,0:T(8,128)(2,1)S(1)}, bf16[512,512]{1,0:T(8,128)(2,1)S(1)}, u32[]{:S(2)}, u32[]{:S(2)}) collective-permute-start(bf16[512,512]{1,0:T(8,128)(2,1)S(1)} %get-tuple-element.13.ck_ref.cv_ref), channel_id=1, source_target_pairs={{0,8},{4,12},{8,0},{12,4},{16,24},{20,28},{1,9},{5,13},{9,1},{13,5... | collective-permute-start | bytes 1572872 | tf_op jit(solution)/shard_map/ppermute | solution.py:255
  59.0 11.9 %collective-permute-start.19 = (bf16[512,512]{1,0:T(8,128)(2,1)S(1)}, bf16[512,512]{1,0:T(8,128)(2,1)S(1)}, u32[]{:S(2)}, u32[]{:S(2)}) collective-permute-start(bf16[512,512]{1,0:T(8,128)(2,1)S(1)} %get-tuple-element.13.ck_ref.cv_ref), channel_id=1, source_target_pairs={{0,16},{4,20},{8,24},{12,28},{1,17},{5,21},{9,25},{13,29},{2,18},{... | collective-permute-start | bytes 1572872 | tf_op jit(solution)/shard_map/ppermute | solution.py:255
  62.4 12.3 %collective-permute-start = (bf16[256,1024]{1,0:T(8,128)(2,1)}, bf16[256,1024]{1,0:T(8,128)(2,1)}, u32[]{:S(2)}, u32[]{:S(2)}) collective-permute-start(bf16[256,1024]{1,0:T(8,128)(2,1)} %get-tuple-element.22), channel_id=1, source_target_pairs={{0,4},{4,0},{8,12},{12,8},{16,20},{20,16},{24,28},{28,24},{1,5},{5... | collective-permute-start | bytes 1572872 | tf_op jit(solution)/shard_map/ppermute | solution.py:250
  68.6 32.0 %collective-permute-start.20 = (bf16[256,512]{1,0:T(8,128)(2,1)S(1)}, bf16[256,512]{1,0:T(8,128)(2,1)S(1)}, u32[]{:S(2)}, u32[]{:S(2)}) collective-permute-start(bf16[256,512]{1,0:T(8,128)(2,1)S(1)} %slice.38), channel_id=1, source_target_pairs={{0,16},{4,20},{8,24},{12,28},{1,17},{5,21},{9,25},{13,29},{2,18},{... | collective-permute-start | bytes 786440 | tf_op jit(solution)/shard_map/ppermute | solution.py:255
  71.6 29.0 %collective-permute-start.21 = (bf16[256,512]{1,0:T(8,128)(2,1)}, bf16[256,512]{1,0:T(8,128)(2,1)S(1)}, u32[]{:S(2)}, u32[]{:S(2)}) collective-permute-start(bf16[256,512]{1,0:T(8,128)(2,1)} %slice.39), channel_id=1, source_target_pairs={{16,24},{20,28},{24,16},{28,20},{17,25},{21,29},{25,17},{29,21},{1... | collective-permute-start | bytes 786440 | tf_op jit(solution)/shard_map/ppermute | solution.py:255
  82.3 1.4 %copy-start = (f32[8,512,128]{2,1,0:T(8,128)}, f32[8,512,128]{2,1,0:T(8,128)S(1)}, u32[]{:S(2)}) copy-start(f32[8,512,128]{2,1,0:T(8,128)S(1)} %get-tuple-element.15.acc_in) | copy-start | bytes 6291460
  119.7 10.3 %collective-permute-start.22 = (bf16[256,1024]{1,0:T(8,128)(2,1)S(1)}, bf16[256,1024]{1,0:T(8,128)(2,1)S(1)}, u32[]{:S(2)}, u32[]{:S(2)}) collective-permute-start(bf16[256,1024]{1,0:T(8,128)(2,1)S(1)} %get-tuple-element.20), channel_id=1, source_target_pairs={{0,4},{4,0},{8,12},{12,8},{16,20},{20,16},{24,28},{28,24},{1,5},{5... | collective-permute-start | bytes 1572872 | tf_op jit(solution)/shard_map/ppermute | solution.py:250

commit v2 on v0

v2 whole, which is shorter than its diff:
```python
import functools
import math

import jax
import jax.numpy as jnp
from jax import lax
from jax.experimental import pallas as pl
from jax.experimental.pallas import tpu as pltpu
from jax.sharding import PartitionSpec as P

HEADS = 16
HEAD_DIM = 128
BLOCK = 256
ROPE_BASE = 500000.0
MASK_ROWS = 16
SCORE_SCALE = HEAD_DIM**-0.5 * math.log2(math.e)
VMEM_LIMIT = 16 * 1024 * 1024

IN_VMEM = pl.BlockSpec(memory_space=pltpu.VMEM)
IN_SMEM = pl.BlockSpec(memory_space=pltpu.SMEM)
IN_PLACE = pl.BlockSpec(memory_space=pl.ANY)


def kernel_call(body, name, out_shape, in_specs, out_specs, scratch=(), aliases=None, flops=0):
    return pl.pallas_call(
        body,
        out_shape=out_shape,
        in_specs=in_specs,
        out_specs=out_specs,
        scratch_shapes=scratch,
        input_output_aliases=aliases or {},
        compiler_params=pltpu.CompilerParams(vmem_limit_bytes=VMEM_LIMIT),
        cost_estimate=pl.CostEstimate(flops=flops, bytes_accessed=0, transcendentals=0),
        name=name,
    )


def bf16(*shape):
    return jax.ShapeDtypeStruct(shape, jnp.bfloat16)


def f32(*shape):
    return jax.ShapeDtypeStruct(shape, jnp.float32)


def rotation(positions):
    half_dim = HEAD_DIM // 2
    frequency = ROPE_BASE ** (-(jnp.arange(half_dim, dtype=jnp.float32) * 2.0 / HEAD_DIM))
    angles = positions.astype(jnp.float32)[:, None] * frequency[None, :]
    cosine = jnp.cos(angles)
    sine = jnp.sin(angles)
    return jnp.concatenate([cosine, cosine], -1), jnp.concatenate([-sine, sine], -1)


def cut_kernel(where, key_ref, value_ref, *refs):
    outs, sem = refs[:-1], refs[-1]
    half = key_ref.shape[1] // 2
    first_column = pl.multiple_of(where[0] * half, HEAD_DIM)
    copies = []
    for number, out in enumerate(outs):
        count = out.shape[0]
        rows = pl.ds(pl.multiple_of(where[1 + number] * count, 16), count)
        for side, weight in enumerate((key_ref, value_ref)):
            copies.append(
                pltpu.make_async_copy(
                    weight.at[rows, pl.ds(first_column, half)],
                    out.at[:, side * half : (side + 1) * half],
                    sem.at[2 * number + side],
                )
            )
    for copy in copies:
        copy.start()
    for copy in copies:
        copy.wait()


def cut_weights(core, starts, counts, w_key, w_value):
    where = jnp.stack([jnp.asarray(v, jnp.int32) for v in (core, *starts)])
    return kernel_call(
        cut_kernel,
        "cut_weights",
        [bf16(count, w_key.shape[1]) for count in counts],
        [IN_SMEM, IN_PLACE, IN_PLACE],
        [IN_VMEM] * len(counts),
        [pltpu.SemaphoreType.DMA((2 * len(counts),))],
    )(where, w_key, w_value)


def stage_kernel(where, states_ref, embed_ref, query_ref, rows_ref, kept_ref, sent_ref, sem):
    core = where[0]
    tokens = states_ref.shape[0]
    half = query_ref.shape[1] // 2
    kept = pl.ds(pl.multiple_of(core * half, HEAD_DIM), half)
    sent = pl.ds(pl.multiple_of((1 - core) * half, HEAD_DIM), half)
    copies = [
        pltpu.make_async_copy(query_ref.at[:, sent], sent_ref, sem.at[0]),
        pltpu.make_async_copy(query_ref.at[:, kept], kept_ref, sem.at[1]),
        pltpu.make_async_copy(states_ref, rows_ref.at[pl.ds(0, tokens), :], sem.at[2]),
    ]
    for copy in copies:
        copy.start()
    rows_ref[pl.ds(tokens, MASK_ROWS), :] = jnp.broadcast_to(embed_ref[...], (MASK_ROWS, embed_ref.shape[1]))
    for copy in copies:
        copy.wait()


def stage(core, states, mask_embed, queries):
    tokens, width = states.shape
    half = queries.shape[1] // 2
    return kernel_call(
        stage_kernel,
        "stage",
        [bf16(tokens + MASK_ROWS, width), bf16(tokens, half), bf16(tokens, half)],
        [IN_SMEM, IN_PLACE, IN_VMEM, IN_PLACE],
        [IN_VMEM] * 3,
        [pltpu.SemaphoreType.DMA((3,))],
    )(jnp.asarray(core, jnp.int32)[None], states, mask_embed[None, :], queries)


def gather_sum(starts, rows_ref, total_in, pieces):
    total = None if total_in is None else total_in[...]
    for number, piece in enumerate(pieces):
        depth = piece.shape[0]
        first = pl.multiple_of(starts[number], HEAD_DIM)
        term = jnp.dot(rows_ref[:, pl.ds(first, depth)], piece[...], preferred_element_type=jnp.float32)
        total = term if total is None else total + term
    return total


def partial_kernel(count, starts, rows_a, rows_b, *refs):
    pieces, (total_a, total_b) = refs[:count], refs[count:]
    total_a[...] = gather_sum(starts, rows_a, None, pieces)
    total_b[...] = gather_sum(starts, rows_b, None, pieces)


def project_partial(rows, pieces, starts):
    width = pieces[0].shape[1]
    depth = sum(p.shape[0] for p in pieces)
    return kernel_call(
        functools.partial(partial_kernel, len(pieces)),
        "project_partial",
        [f32(r.shape[0], width) for r in rows],
        [IN_SMEM] + [IN_VMEM] * (2 + len(pieces)),
        [IN_VMEM] * 2,
        flops=2 * width * depth * sum(r.shape[0] for r in rows),
    )(starts, *rows, *pieces)


def finish_kernel(count, has_total, starts, rows_a, rows_b, *refs):
    total_a = total_b = None
    if has_total:
        total_a, total_b = refs[:2]
        refs = refs[2:]
    pieces = refs[:count]
    cos_ref, sin_ref, marks_a, marks_b, clean_ref, noisy_ref = refs[count:]
    tokens = rows_b.shape[0]
    width = clean_ref.shape[1]
    sums_a = gather_sum(starts, rows_a, total_a, pieces)
    sums_b = gather_sum(starts, rows_b, total_b, pieces)
    mask_sums = sums_a[tokens : tokens + 1]
    for side, sums, marks in ((0, sums_a[:tokens], marks_a), (1, sums_b, marks_b)):
        mine = pl.ds(side * tokens, tokens)
        cosine, sine = cos_ref[mine, :], sin_ref[mine, :]
        masked = marks[...] == 1
        for lane in range(0, width, HEAD_DIM):
            clean = sums[:, lane : lane + HEAD_DIM]
            noisy = jnp.where(masked, mask_sums[:, lane : lane + HEAD_DIM], clean)
            for part, out_ref in ((clean, clean_ref), (noisy, noisy_ref)):
                if lane < width // 2:
                    part = part * cosine + pltpu.roll(part, HEAD_DIM // 2, 1) * sine
                out_ref[mine, lane : lane + HEAD_DIM] = part.astype(jnp.bfloat16)


def project_finish(rows, totals, pieces, starts, cosine, sine, marks):
    width = pieces[0].shape[1]
    tokens = rows[1].shape[0]
    depth = sum(p.shape[0] for p in pieces)
    operands = [*rows, *totals, *pieces, cosine, sine, *marks]
    return kernel_call(
        functools.partial(finish_kernel, len(pieces), bool(totals)),
        "project_finish",
        [bf16(2 * tokens, width)] * 2,
        [IN_SMEM] + [IN_VMEM] * len(operands),
        [IN_VMEM] * 2,
        flops=2 * width * depth * sum(r.shape[0] for r in rows),
    )(starts, *operands)


def scores_of(query, key):
    return lax.dot_general(query, key, (((1,), (1,)), ((), ())), preferred_element_type=jnp.float32)


def lane_tiles(array):
    return [array[:, lane : lane + HEAD_DIM] for lane in range(0, array.shape[1], HEAD_DIM)]


def absorb(scores, values, before):
    tiles = [lane_tiles(s) for s in scores]
    peak = functools.reduce(jnp.maximum, [t for part in tiles for t in part])
    top = jnp.broadcast_to(jnp.max(peak, -1, keepdims=True), peak.shape) * SCORE_SCALE
    if before is not None:
        top = jnp.maximum(top, before[0])
    total = mixture = None
    for part, value in zip(tiles, values):
        weights = [jnp.exp2(t * SCORE_SCALE - top) for t in part]
        for weight in weights:
            total = weight if total is None else total + weight
        mixed = jnp.dot(
            jnp.concatenate([w.astype(jnp.bfloat16) for w in weights], 1), value, preferred_element_type=jnp.float32
        )
        mixture = mixed if mixture is None else mixture + mixed
    if before is not None:
        rescale = jnp.exp2(before[0] - top)
        total = before[1] * rescale + total
        mixture = before[2] * rescale + mixture
    return top, total, mixture


def pipelined(tasks, score, use):
    waiting = None
    for task in tasks:
        scores = score(task)
        if waiting is not None:
            use(*waiting)
        waiting = (task, scores)
    use(*waiting)


def own_kernel(kv_heads, where, q_a, q_b, clean_ref, noisy_ref, top_ref, sum_ref, mix_ref):
    core = where[0]
    tokens = q_a.shape[0]
    heads = q_a.shape[1] // HEAD_DIM
    groups = heads // kv_heads
    tasks = [(head, side) for head in range(heads) for side in range(2)]

    def lanes(head, value):
        first = (head // groups + (kv_heads if value else 0)) * HEAD_DIM
        return slice(first, first + HEAD_DIM)

    def score(task):
        head, side = task
        query = (q_a, q_b)[side][:, head * HEAD_DIM : (head + 1) * HEAD_DIM]
        near = scores_of(query, noisy_ref[side * tokens : (side + 1) * tokens, lanes(head, False)])
        far = scores_of(query, clean_ref[(1 - side) * tokens : (2 - side) * tokens, lanes(head, False)])
        return [near, jnp.where(core == 1 - side, far, -1e30)]

    def use(task, scores):
        head, side = task
        values = [
            noisy_ref[side * tokens : (side + 1) * tokens, lanes(head, True)],
            clean_ref[(1 - side) * tokens : (2 - side) * tokens, lanes(head, True)],
        ]
        top, total, mixture = absorb(scores, values, None)
        mine = pl.ds(side * tokens, tokens)
        top_ref[head, mine, :] = top
        sum_ref[head, mine, :] = total
        mix_ref[head, mine, :] = mixture

    pipelined(tasks, score, use)


def attend_own(core, queries, clean, noisy, kv_heads):
    tokens = queries[0].shape[0]
    heads = queries[0].shape[1] // HEAD_DIM
    return kernel_call(
        functools.partial(own_kernel, kv_heads),
        "attend_own",
        [f32(heads, 2 * tokens, HEAD_DIM)] * 3,
        [IN_SMEM] + [IN_VMEM] * 4,
        [IN_VMEM] * 3,
        flops=8 * heads * tokens * tokens * HEAD_DIM,
    )(jnp.asarray(core, jnp.int32)[None], *queries, clean, noisy)


def later_tasks(kv_heads, groups, heads, q_a, q_b, keys, state, store):
    tokens = q_a.shape[0]

    def lanes(head, value):
        first = (head // groups + (kv_heads if value else 0)) * HEAD_DIM
        return slice(first, first + HEAD_DIM)

    def score(task):
        head, side = task
        query = (q_a, q_b)[side][:, head * HEAD_DIM : (head + 1) * HEAD_DIM]
        return [scores_of(query, key[:, lanes(head, False)]) for key in keys]

    def use(task, scores):
        head, side = task
        mine = pl.ds(side * tokens, tokens)
        values = [key[:, lanes(head, True)] for key in keys]
        store(head, side, absorb(scores, values, state(head, mine)))

    pipelined([(head, side) for head in heads for side in range(2)], score, use)


def later_kernel(kv_heads, count, flags, q_a, q_b, *refs):
    parts, refs = refs[:count], refs[count:]
    outs = refs[3:]
    heads = q_a.shape[1] // HEAD_DIM
    tokens = q_a.shape[0]

    def state(head, mine):
        return tuple(out[head, mine, :] for out in outs)

    def store(head, side, values):
        for out, value in zip(outs, values):
            out[head, pl.ds(side * tokens, tokens), :] = value

    for number in range(count):

        @pl.when(flags[number] == 1)
        def _(part=parts[number]):
            later_tasks(kv_heads, heads // kv_heads, range(heads), q_a, q_b, [part], state, store)


def attend_later(flags, queries, parts, running, kv_heads):
    tokens = queries[0].shape[0]
    heads = queries[0].shape[1] // HEAD_DIM
    count = len(parts)
    return kernel_call(
        functools.partial(later_kernel, kv_heads, count),
        "attend_later",
        [f32(heads, 2 * tokens, HEAD_DIM)] * 3,
        [IN_SMEM] + [IN_VMEM] * (5 + count),
        [IN_VMEM] * 3,
        aliases={3 + count + i: i for i in range(3)},
        flops=8 * heads * tokens * sum(p.shape[0] for p in parts) * HEAD_DIM,
    )(flags, *queries, *parts, *running)


def last_kernel(kv_heads, heads, count, flags, q_a, q_b, *refs):
    parts, state_refs, outs = refs[:count], refs[count : count + 3], refs[count + 3 :]
    groups = q_a.shape[1] // HEAD_DIM // kv_heads

    def state(head, mine):
        return tuple(ref[head, mine, :] for ref in state_refs)

    def store(head, side, values):
        _, total, mixture = values
        total = jnp.sum(total, -1, keepdims=True)
        place = (head - heads[0]) * HEAD_DIM
        outs[side][:, place : place + HEAD_DIM] = (mixture / total).astype(jnp.bfloat16)

    @pl.when(flags[0] == 1)
    def _():
        later_tasks(kv_heads, groups, heads, q_a, q_b, parts, state, store)

    @pl.when(flags[0] != 1)
    def _():
        for head in heads:
            for side in range(2):
                store(head, side, state(head, pl.ds(side * q_a.shape[0], q_a.shape[0])))


def attend_last(flags, queries, parts, running, kv_heads, heads):
    tokens = queries[0].shape[0]
    count = len(parts)
    return kernel_call(
        functools.partial(last_kernel, kv_heads, heads, count),
        "attend_last",
        [bf16(tokens, len(heads) * HEAD_DIM)] * 2,
        [IN_SMEM] + [IN_VMEM] * (5 + count),
        [IN_VMEM] * 2,
        flops=8 * len(heads) * tokens * sum(p.shape[0] for p in parts) * HEAD_DIM,
    )(flags, *queries, *parts, *running)


def place_kernel(count, where, *refs):
    parts, out, sem = refs[: 2 * count], refs[2 * count], refs[2 * count + 1]
    core = where[0]
    half = out.shape[1] // 2
    width = half // count
    copies = []
    for number, part in enumerate(parts):
        side = core if number < count else 1 - core
        first = pl.multiple_of(side * half + (number % count) * width, HEAD_DIM)
        copies.append(pltpu.make_async_copy(part, out.at[:, pl.ds(first, width)], sem.at[number]))
    for copy in copies:
        copy.start()
    for copy in copies:
        copy.wait()


def place_heads(core, mine, received):
    count = len(mine)
    tokens, width = mine[0].shape
    return kernel_call(
        functools.partial(place_kernel, count),
        "place_heads",
        bf16(tokens, 2 * count * width),
        [IN_SMEM] + [IN_VMEM] * (2 * count),
        IN_PLACE,
        [pltpu.SemaphoreType.DMA((2 * count,))],
    )(jnp.asarray(core, jnp.int32)[None], *mine, *received)


def as_scalars(values):
    return jnp.stack([jnp.asarray(v, jnp.int32) for v in values])


def shards(seq_size, fsdp_size, clean_states, noise_mask, mask_embed, queries, w_key, w_value):
    chips = seq_size // 2
    place = lax.axis_index("seq")
    core = lax.rem(place, 2)
    chip = place // 2
    shard = lax.axis_index("fsdp")
    states = clean_states[0]
    marks = noise_mask[0]
    tokens = states.shape[0]
    depth, kv_width = w_key.shape
    kv_heads = kv_width // 2 // HEAD_DIM
    square = chips == 4 and fsdp_size == 4

    def swap_cores(array):
        return lax.ppermute(array, "seq", [(s, s ^ 1) for s in range(seq_size)])

    def to_chip(array, flip, sources=None):
        sources = range(chips) if sources is None else sources
        pairs = [(2 * s + c, 2 * (s ^ flip) + c) for s in sources for c in range(2)]
        return lax.ppermute(array, "seq", pairs)

    def to_shard(array, flip):
        return lax.ppermute(array, "fsdp", [(s, s ^ flip) for s in range(fsdp_size)])

    if square:
        quarter = depth // chips
        mine, corner = cut_weights(core, (chip, chip ^ 3), (quarter, quarter), w_key, w_value)
        far, near, middle = to_shard(mine, 3), to_shard(mine, 1), to_shard(mine, 2)
        near_corner = to_shard(corner, 1)

    rows_a, query_a, query_sent = stage(core, states, mask_embed, queries[0])
    rows = (rows_a, swap_cores(states))
    query_rows = (query_a, swap_cores(query_sent))
    all_marks = [jnp.broadcast_to(m[:, None], (tokens, HEAD_DIM)) for m in (marks, swap_cores(marks))]
    steps = jnp.arange(tokens, dtype=jnp.int32)
    cosine, sine = rotation(jnp.concatenate([place * tokens + steps, (place ^ 1) * tokens + steps]))
    (own_half,) = cut_weights(core, (0,), (depth,), w_key, w_value)

    if square:
        far, own_half, cosine, sine, rows_a = lax.optimization_barrier((far, own_half, cosine, sine, rows_a))
        rows = (rows_a, rows[1])

        def plane(piece, source, diagonal):
            others = [to_chip(piece, 1), to_chip(piece, 2), to_chip(piece, 3) if diagonal is None else diagonal]
            return [piece, *others], [source * depth + (chip ^ flip) * quarter for flip in range(4)]

        first = plane(far, shard ^ 3, None)
        second = plane(near, shard ^ 1, near_corner)
        final = plane(middle, shard ^ 2, None)
        totals = project_partial(
            rows, [own_half] + first[0] + second[0], as_scalars([shard * depth] + first[1] + second[1])
        )
    else:
        totals = ()
        final = ([lax.all_gather(own_half, "fsdp", axis=0, tiled=True)], [jnp.int32(0)])
    clean, noisy = project_finish(rows, totals, final[0], as_scalars(final[1]), cosine, sine, all_marks)

    if square:
        along_x = to_chip(clean, 1, (0, 1, 2))
        along_y = to_chip(clean, 2, (0, 1))
        running = attend_own(core, query_rows, clean, noisy, kv_heads)
        along_x, along_y, running = lax.optimization_barrier((along_x, along_y, running))
        last_parts = [to_chip(along_x[:tokens], 2, (0, 1)), to_chip(along_y[tokens:], 1, (2, 3))]
        flags = as_scalars([(chip ^ flip) < chip for flip in (1, 2)])
        running = attend_later(flags, query_rows, [along_x, along_y], running, kv_heads)
        last_flip = 3
    else:
        running = attend_own(core, query_rows, clean, noisy, kv_heads)
        for flip in range(1, chips):
            part = to_chip(clean, flip, [s for s in range(chips) if s < s ^ flip])
            if flip < chips - 1:
                running = attend_later(as_scalars([(chip ^ flip) < chip]), query_rows, [part], running, kv_heads)
        last_parts, last_flip = [part], chips - 1
    flags = as_scalars([(chip ^ last_flip) < chip])
    kept, received = [], []
    heads = query_a.shape[1] // HEAD_DIM
    for first_head in range(0, heads, heads // kv_heads):
        own, other = attend_last(
            flags, query_rows, last_parts, running, kv_heads, range(first_head, first_head + heads // kv_heads)
        )
        kept.append(own)
        received.append(swap_cores(other))
    return place_heads(core, kept, received)[None]


def solution(mesh):
    placed = (
        P("fsdp", "seq", None),
        P("fsdp", "seq"),
        P(),
        P("fsdp", "seq", None),
        P("fsdp", None),
        P("fsdp", None),
    )
    return jax.shard_map(
        functools.partial(shards, mesh.shape["seq"], mesh.shape["fsdp"]),
        mesh=mesh,
        in_specs=placed,
        out_specs=P("fsdp", "seq", None),
        check_vma=False,
    )
```

time: 296 us -> 101 us (0.34)
  the two profiles are of different devices: /device:TPU:7 before, /device:TPU:23 now
where the time goes in v2:
time: 101 us
  waiting for transfers between devices  40.2 us (40%)
  Pallas kernels  25.9 us (26%)
  starting transfers between devices  20.8 us (21%)
  local copies, waits for them, and re-layouts  11.1 us (11%)
  other arithmetic  2.3 us (2%)
    ppermute x12, waiting for transfers between devices, to_chip(): return lax.ppermute(array, 'seq', pairs)  21.6 us
    ppermute x4, waiting for transfers between devices, to_shard(): lax.ppermute(array, 'fsdp', [(s, s ^ flip) for s in range(fsdp_size)])  17.1 us
    unnamed x40, local copies, waits for them, and re-layouts  10.8 us
    ppermute x12, starting transfers between devices, to_chip(): return lax.ppermute(array, 'seq', pairs)  10.6 us
    pallas_call x1, Pallas kernels, attend_later(): kernel_call(functools.partial(later_kernel, kv_heads, count), 'attend_lat...  7.42 us
    ppermute x5, starting transfers between devices, swap_cores(): return lax.ppermute(array, 'seq', [(s, s ^ 1) for s in range(seq_size)])  5.27 us
    ppermute x4, starting transfers between devices, to_shard(): lax.ppermute(array, 'fsdp', [(s, s ^ flip) for s in range(fsdp_size)])  4.91 us
    pallas_call x2, Pallas kernels, attend_last(): kernel_call(functools.partial(last_kernel, kv_heads, heads, count), 'atte...  3.99 us
  transfers between devices with their start and end apart: 21, of which 9 were waited for; matrix products, arithmetic and copies ran while one was open for 3% of the time, Pallas kernels for 23%

profile of v2, /device:TPU:23, one launch (start us, length us, event | category | flops | bytes accessed | tf_op | source)
XLA Modules:
  0.0 100.8 jit_solution(11995977800839277470)
XLA Ops:
  0.0 0.7 collective-permute-start.2
  0.7 0.1 pad_add_fusion.1.where
  0.8 1.2 %copy-done = bf16[1024,512]{1,0:T(8,128)(2,1)S(1)} copy-done((bf16[1024,512]{1,0:T(8,128)(2,1)S(1)}, bf16[1024,512]{1,0:T(8,128)(2,1)}, u32[]{:S(2)}) %copy-start) | copy-done | bytes 1048600
  2.0 1.2 %copy-done.2 = bf16[1024,512]{1,0:T(8,128)(2,1)S(1)} copy-done((bf16[1024,512]{1,0:T(8,128)(2,1)S(1)}, bf16[1024,512]{1,0:T(8,128)(2,1)}, u32[]{:S(2)}) %copy-start.2) | copy-done | bytes 1048600
  3.2 1.4 %cut_weights.2 = (bf16[256,512]{1,0:T(8,128)(2,1)}, bf16[256,512]{1,0:T(8,128)(2,1)}) custom-call(s32[3]{0:T(128)S(1)} %pad_add_fusion.1.where, bf16[1024,512]{1,0:T(8,128)(2,1)S(1)} %copy-done, bf16[1024,512]{1,0:T(8,128)(2,1)S(1)} %copy-done.2), custom_call_target="tpu_custom_call" | custom-call | tf_op jit(solution)/shard_map/cut_weights/pallas_call | solution.py:79
  4.7 0.1 collective-permute-start.10
  4.8 1.3 %collective-permute-start.6 = (bf16[256,512]{1,0:T(8,128)(2,1)}, bf16[256,512]{1,0:T(8,128)(2,1)S(1)}, u32[]{:S(2)}, u32[]{:S(2)}) collective-permute-start(bf16[256,512]{1,0:T(8,128)(2,1)} %get-tuple-element.36), channel_id=1, source_target_pairs={{0,1},{1,0},{2,3},{3,2},{4,5},{5,4},{6,7},{7,6},{8,9},{9,8},{10,11... | collective-permute-start | bytes 786440 | tf_op jit(solution)/shard_map/ppermute | solution.py:423
  6.1 1.3 %collective-permute-start.1 = (bf16[256,512]{1,0:T(8,128)(2,1)}, bf16[256,512]{1,0:T(8,128)(2,1)S(1)}, u32[]{:S(2)}, u32[]{:S(2)}) collective-permute-start(bf16[256,512]{1,0:T(8,128)(2,1)} %get-tuple-element.36), channel_id=1, source_target_pairs={{0,3},{1,2},{2,1},{3,0},{4,7},{5,6},{6,5},{7,4},{8,11},{9,10},{10,... | collective-permute-start | bytes 786440 | tf_op jit(solution)/shard_map/ppermute | solution.py:423
  7.4 2.2 %collective-permute-start.9 = (bf16[256,512]{1,0:T(8,128)(2,1)}, bf16[256,512]{1,0:T(8,128)(2,1)}, u32[]{:S(2)}, u32[]{:S(2)}) collective-permute-start(bf16[256,512]{1,0:T(8,128)(2,1)} %get-tuple-element.41), channel_id=1, source_target_pairs={{0,1},{1,0},{2,3},{3,2},{4,5},{5,4},{6,7},{7,6},{8,9},{9,8},{10,11... | collective-permute-start | bytes 786440 | tf_op jit(solution)/shard_map/ppermute | solution.py:423
  9.6 0.0 copy-start.6
  9.6 0.0 copy-start.8
  9.6 1.0 fusion
  10.6 0.8 pad_maximum_fusion.refs_6_
  11.5 7.0 %collective-permute-done.6.refs_5_ = bf16[256,512]{1,0:T(8,128)(2,1)S(1)} collective-permute-done((bf16[256,512]{1,0:T(8,128)(2,1)}, bf16[256,512]{1,0:T(8,128)(2,1)S(1)}, u32[]{:S(2)}, u32[]{:S(2)}) %collective-permute-start.6) | collective-permute-done | bytes 262176 | tf_op jit(solution)/shard_map/ppermute | solution.py:423
  18.4 0.2 collective-permute-start.8
  18.6 0.1 pad_add_fusion.2.where
  18.8 0.6 cut_weights.3.refs_0_
  19.4 0.0 copy-start.4
  19.4 1.0 copy-done.4
  20.4 0.3 stage.1
  20.7 0.1 pad_maximum_fusion.1.refs_7_
  20.8 10.2 %collective-permute-done.1.refs_1_ = bf16[256,512]{1,0:T(8,128)(2,1)S(1)} collective-permute-done((bf16[256,512]{1,0:T(8,128)(2,1)}, bf16[256,512]{1,0:T(8,128)(2,1)S(1)}, u32[]{:S(2)}, u32[]{:S(2)}) %collective-permute-start.1) | collective-permute-done | bytes 262176 | tf_op jit(solution)/shard_map/ppermute | solution.py:423
  31.0 0.3 collective-permute-start.7
  31.3 1.2 %collective-permute-start.5 = (bf16[256,512]{1,0:T(8,128)(2,1)S(1)}, bf16[256,512]{1,0:T(8,128)(2,1)}, u32[]{:S(2)}, u32[]{:S(2)}) collective-permute-start(bf16[256,512]{1,0:T(8,128)(2,1)S(1)} %collective-permute-done.1.refs_1_), channel_id=1, source_target_pairs={{0,24},{4,28},{8,16},{12,20},{16,8},{20,12},{24,0},{28,4},{1,25},{... | collective-permute-start | bytes 786440 | tf_op jit(solution)/shard_map/ppermute | solution.py:420
  32.4 1.2 %collective-permute-start.4 = (bf16[256,512]{1,0:T(8,128)(2,1)S(1)}, bf16[256,512]{1,0:T(8,128)(2,1)}, u32[]{:S(2)}, u32[]{:S(2)}) collective-permute-start(bf16[256,512]{1,0:T(8,128)(2,1)S(1)} %collective-permute-done.1.refs_1_), channel_id=1, source_target_pairs={{0,16},{4,20},{8,24},{12,28},{16,0},{20,4},{24,8},{28,12},{1,17},{... | collective-permute-start | bytes 786440 | tf_op jit(solution)/shard_map/ppermute | solution.py:420
  33.7 0.7 copy-done.15
  34.4 0.3 collective-permute-start.3
  34.7 0.7 copy-done.13
  35.4 0.1 stack.97.starts
  35.5 3.1 %collective-permute-done.7.refs_6_ = bf16[256,512]{1,0:T(8,128)(2,1)} collective-permute-done((bf16[256,512]{1,0:T(8,128)(2,1)S(1)}, bf16[256,512]{1,0:T(8,128)(2,1)}, u32[]{:S(2)}, u32[]{:S(2)}) %collective-permute-start.7) | collective-permute-done | bytes 262176 | tf_op jit(solution)/shard_map/ppermute | solution.py:420
  38.6 0.2 collective-permute-start.13
  38.8 5.4 %collective-permute-done.5.refs_4_ = bf16[256,512]{1,0:T(8,128)(2,1)} collective-permute-done((bf16[256,512]{1,0:T(8,128)(2,1)S(1)}, bf16[256,512]{1,0:T(8,128)(2,1)}, u32[]{:S(2)}, u32[]{:S(2)}) %collective-permute-start.5) | collective-permute-done | bytes 262176 | tf_op jit(solution)/shard_map/ppermute | solution.py:420
  44.2 1.2 %collective-permute-start.12 = (bf16[256,512]{1,0:T(8,128)(2,1)}, bf16[256,512]{1,0:T(8,128)(2,1)S(1)}, u32[]{:S(2)}, u32[]{:S(2)}) collective-permute-start(bf16[256,512]{1,0:T(8,128)(2,1)} %collective-permute-done.10.refs_2_), channel_id=1, source_target_pairs={{0,16},{4,20},{8,24},{12,28},{16,0},{20,4},{24,8},{28,12},{1,17},{... | collective-permute-start | bytes 786440 | tf_op jit(solution)/shard_map/ppermute | solution.py:420
  45.4 0.3 collective-permute-start.11
  45.7 0.1 pad_add_fusion.starts
  45.8 4.1 %collective-permute-done.3.refs_2_ = bf16[256,512]{1,0:T(8,128)(2,1)} collective-permute-done((bf16[256,512]{1,0:T(8,128)(2,1)S(1)}, bf16[256,512]{1,0:T(8,128)(2,1)}, u32[]{:S(2)}, u32[]{:S(2)}) %collective-permute-start.3) | collective-permute-done | bytes 262176 | tf_op jit(solution)/shard_map/ppermute | solution.py:420
  49.9 2.2 %collective-permute-start.14 = (s32[256]{0:T(256)S(1)}, s32[256]{0:T(256)S(1)}, u32[]{:S(2)}, u32[]{:S(2)}) collective-permute-start(s32[256]{0:T(256)S(1)} %bitcast.26), channel_id=1, source_target_pairs={{0,4},{4,0},{8,12},{12,8},{16,20},{20,16},{24,28},{28,24},{1,5},{5... | collective-permute-start | bytes 3080 | tf_op jit(solution)/shard_map/ppermute | solution.py:415
  52.0 0.1 collective-permute-start
  52.1 1.2 %copy-done.5 = bf16[1024,512]{1,0:T(8,128)(2,1)S(1)} copy-done((bf16[1024,512]{1,0:T(8,128)(2,1)S(1)}, bf16[1024,512]{1,0:T(8,128)(2,1)}, u32[]{:S(2)}) %copy-start.5) | copy-done | bytes 1048600
  53.3 0.9 copy-done.12
  54.3 0.9 copy-done.14
  55.2 0.9 copy-done.16
  56.2 3.8 %project_partial.1 = (f32[272,512]{1,0:T(8,128)S(1)}, f32[256,512]{1,0:T(8,128)S(1)}) custom-call(s32[9]{0:T(128)S(1)} %stack.97.starts, bf16[272,4096]{1,0:T(8,128)(2,1)S(1)} %get-tuple-element.38.rows_a, bf16[256,4096]{1,0:T(8,128)(2,1)} %collective-permute-done.2.rows_b, bf16[1024,512]{1,0:T(8,128)(2,1)S(1)} %copy-done.5, ...), custom_call_target="tpu_custom_call" | custom-call | flops 1660944384 | tf_op jit(solution)/shard_map/project_partial/pallas_call | solution.py:139
  60.0 1.0 %collective-permute-done.11.refs_3_ = bf16[256,512]{1,0:T(8,128)(2,1)S(1)} collective-permute-done((bf16[256,512]{1,0:T(8,128)(2,1)}, bf16[256,512]{1,0:T(8,128)(2,1)S(1)}, u32[]{:S(2)}, u32[]{:S(2)}) %collective-permute-start.11) | collective-permute-done | bytes 262176 | tf_op jit(solution)/shard_map/ppermute | solution.py:420
  61.0 0.1 broadcast_in_dim.30.refs_9_
  61.1 0.1 broadcast_in_dim.29.refs_8_
  61.2 3.3 %project_finish.1 = (bf16[512,512]{1,0:T(8,128)(2,1)}, bf16[512,512]{1,0:T(8,128)(2,1)S(1)}) custom-call(s32[4]{0:T(128)S(1)} %pad_add_fusion.starts, bf16[272,4096]{1,0:T(8,128)(2,1)S(1)} %get-tuple-element.38.rows_a, bf16[256,4096]{1,0:T(8,128)(2,1)} %collective-permute-done.2.rows_b, f32[272,512]{1,0:T(8,128)S(1)} %get-tuple-element.42.refs_0_, ...), custom_call_target="tpu_custom_call" | custom-call | flops 553648128 | tf_op jit(solution)/shard_map/project_finish/pallas_call | solution.py:179
  64.6 0.8 copy-done.9
  65.4 1.3 %collective-permute-start.16 = (bf16[512,512]{1,0:T(8,128)(2,1)}, bf16[512,512]{1,0:T(8,128)(2,1)S(1)}, u32[]{:S(2)}, u32[]{:S(2)}) collective-permute-start(bf16[512,512]{1,0:T(8,128)(2,1)} %get-tuple-element.46.clean_ref), channel_id=1, source_target_pairs={{0,16},{4,20},{8,24},{12,28},{1,17},{5,21},{9,25},{13,29},{2,18},{... | collective-permute-start | bytes 1572872 | tf_op jit(solution)/shard_map/ppermute | solution.py:420
  66.7 1.3 %collective-permute-start.15 = (bf16[512,512]{1,0:T(8,128)(2,1)}, bf16[512,512]{1,0:T(8,128)(2,1)S(1)}, u32[]{:S(2)}, u32[]{:S(2)}) collective-permute-start(bf16[512,512]{1,0:T(8,128)(2,1)} %get-tuple-element.46.clean_ref), channel_id=1, source_target_pairs={{0,8},{4,12},{8,0},{12,4},{16,24},{20,28},{1,9},{5,13},{9,1},{13,5... | collective-permute-start | bytes 1572872 | tf_op jit(solution)/shard_map/ppermute | solution.py:420
  68.0 1.0 %copy-done.10 = bf16[512,512]{1,0:T(8,128)(2,1)S(1)} copy-done((bf16[512,512]{1,0:T(8,128)(2,1)S(1)}, bf16[512,512]{1,0:T(8,128)(2,1)}, u32[]{:S(2)}) %copy-start.10) | copy-done | bytes 524312
  69.0 3.9 %attend_own.1 = (f32[8,512,128]{2,1,0:T(8,128)S(1)}, f32[8,512,128]{2,1,0:T(8,128)S(1)}, f32[8,512,128]{2,1,0:T(8,128)S(1)}) custom-call(s32[1]{0:T(128)} %bitcast.where, bf16[256,1024]{1,0:T(8,128)(2,1)S(1)} %get-tuple-element.34.q_a, bf16[256,1024]{1,0:T(8,128)(2,1)S(1)} %collective-permute-done.q_b, bf16[512,512]{1,0:T(8,128)(2,1)} %get-tuple-element.46.clean_ref, ...), custom_call_target="tpu_custom_call" | custom-call | flops 536870912 | tf_op jit(solution)/shard_map/attend_own/pallas_call | solution.py:265
  73.0 6.6 %collective-permute-done.16.refs_1_ = bf16[512,512]{1,0:T(8,128)(2,1)S(1)} collective-permute-done((bf16[512,512]{1,0:T(8,128)(2,1)}, bf16[512,512]{1,0:T(8,128)(2,1)S(1)}, u32[]{:S(2)}, u32[]{:S(2)}) %collective-permute-start.16) | collective-permute-done | bytes 524320 | tf_op jit(solution)/shard_map/ppermute | solution.py:420
  79.6 1.3 %collective-permute-done.15.refs_0_ = bf16[512,512]{1,0:T(8,128)(2,1)S(1)} collective-permute-done((bf16[512,512]{1,0:T(8,128)(2,1)}, bf16[512,512]{1,0:T(8,128)(2,1)S(1)}, u32[]{:S(2)}, u32[]{:S(2)}) %collective-permute-start.15) | collective-permute-done | bytes 524320 | tf_op jit(solution)/shard_map/ppermute | solution.py:420
  81.0 1.3 %collective-permute-start.17 = (bf16[256,512]{1,0:T(8,128)(2,1)S(1)}, bf16[256,512]{1,0:T(8,128)(2,1)S(1)}, u32[]{:S(2)}, u32[]{:S(2)}) collective-permute-start(bf16[256,512]{1,0:T(8,128)(2,1)S(1)} %slice.6), channel_id=1, source_target_pairs={{0,16},{4,20},{8,24},{12,28},{1,17},{5,21},{9,25},{13,29},{2,18},{... | collective-permute-start | bytes 786440 | tf_op jit(solution)/shard_map/ppermute | solution.py:420
  82.3 1.9 %collective-permute-start.18 = (bf16[256,512]{1,0:T(8,128)(2,1)S(1)}, bf16[256,512]{1,0:T(8,128)(2,1)S(1)}, u32[]{:S(2)}, u32[]{:S(2)}) collective-permute-start(bf16[256,512]{1,0:T(8,128)(2,1)S(1)} %slice.7), channel_id=1, source_target_pairs={{16,24},{20,28},{24,16},{28,20},{17,25},{21,29},{25,17},{29,21},{1... | collective-permute-start | bytes 786440 | tf_op jit(solution)/shard_map/ppermute | solution.py:420
  84.2 0.1 add_convert_fusion.1.flags
  84.3 7.4 %attend_later.1 = (f32[8,512,128]{2,1,0:T(8,128)S(1)}, f32[8,512,128]{2,1,0:T(8,128)S(1)}, f32[8,512,128]{2,1,0:T(8,128)S(1)}) custom-call(s32[2]{0:T(128)S(1)} %add_convert_fusion.1.flags, bf16[256,1024]{1,0:T(8,128)(2,1)S(1)} %get-tuple-element.34.q_a, ...), custom_call_target="tpu_custom_call", output_to_operand_aliasing={{0}: (5, {}), {1}: (6, {}), {2}: (7, {})} | custom-call | flops 2147483648 | tf_op jit(solution)/shard_map/attend_later/pallas_call | solution.py:320
  91.7 2.0 %attend_last.3 = (bf16[256,512]{1,0:T(8,128)(2,1)S(1)}, bf16[256,512]{1,0:T(8,128)(2,1)S(1)}) custom-call(s32[1]{0:T(128)} %bitcast.1.flags, bf16[256,1024]{1,0:T(8,128)(2,1)S(1)} %get-tuple-element.34.q_a, bf16[256,1024]{1,0:T(8,128)(2,1)S(1)} %collective-permute-done.q_b, bf16[256,512]{1,0:T(8,128)(2,1)S(1)} %collective-permute-done.17.refs_0_, ...), custom_call_target="tpu_custom_call" | custom-call | flops 536870912 | tf_op jit(solution)/shard_map/attend_last/pallas_call | solution.py:358
  93.7 2.3 %collective-permute-start.20 = (bf16[256,512]{1,0:T(8,128)(2,1)S(1)}, bf16[256,512]{1,0:T(8,128)(2,1)S(1)}, u32[]{:S(2)}, u32[]{:S(2)}) collective-permute-start(bf16[256,512]{1,0:T(8,128)(2,1)S(1)} %get-tuple-element.62), channel_id=1, source_target_pairs={{0,4},{4,0},{8,12},{12,8},{16,20},{20,16},{24,28},{28,24},{1,5},{5... | collective-permute-start | bytes 786440 | tf_op jit(solution)/shard_map/ppermute | solution.py:415
  96.0 2.0 %attend_last.2 = (bf16[256,512]{1,0:T(8,128)(2,1)S(1)}, bf16[256,512]{1,0:T(8,128)(2,1)S(1)}) custom-call(s32[1]{0:T(128)} %bitcast.1.flags, bf16[256,1024]{1,0:T(8,128)(2,1)S(1)} %get-tuple-element.34.q_a, bf16[256,1024]{1,0:T(8,128)(2,1)S(1)} %collective-permute-done.q_b, bf16[256,512]{1,0:T(8,128)(2,1)S(1)} %collective-permute-done.17.refs_0_, ...), custom_call_target="tpu_custom_call" | custom-call | flops 536870912 | tf_op jit(solution)/shard_map/attend_last/pallas_call | solution.py:358
  98.0 0.1 collective-permute-start.19
  98.1 1.5 %collective-permute-done.19.refs_2_ = bf16[256,512]{1,0:T(8,128)(2,1)S(1)} collective-permute-done((bf16[256,512]{1,0:T(8,128)(2,1)S(1)}, bf16[256,512]{1,0:T(8,128)(2,1)S(1)}, u32[]{:S(2)}, u32[]{:S(2)}) %collective-permute-start.19) | collective-permute-done | bytes 262176 | tf_op jit(solution)/shard_map/ppermute | solution.py:415
  99.6 1.0 place_heads.1
  (44 shorter events, 0.2 us)
Async XLA Ops:
  0.0 18.7 %copy-start.18 = (bf16[4096]{0:T(1024)(128)(2,1)S(1)}, bf16[4096]{0:T(1024)(128)(2,1)}, u32[]{:S(2)}) copy-start(bf16[4096]{0:T(1024)(128)(2,1)} %param.8) | copy-start | bytes 24580
  0.0 52.0 %collective-permute-start.2 = (bf16[256,4096]{1,0:T(8,128)(2,1)}, bf16[256,4096]{1,0:T(8,128)(2,1)}, u32[]{:S(2)}, u32[]{:S(2)}) collective-permute-start(bf16[256,4096]{1,0:T(8,128)(2,1)} %bitcast.23), channel_id=1, source_target_pairs={{0,4},{4,0},{8,12},{12,8},{16,20},{20,16},{24,28},{28,24},{1,5},{5... | collective-permute-start | bytes 6291464 | tf_op jit(solution)/shard_map/ppermute | solution.py:415
  0.8 1.2 %copy-start = (bf16[1024,512]{1,0:T(8,128)(2,1)S(1)}, bf16[1024,512]{1,0:T(8,128)(2,1)}, u32[]{:S(2)}) copy-start(bf16[1024,512]{1,0:T(8,128)(2,1)} %key_ref.3) | copy-start | bytes 3145732
  2.0 1.2 %copy-start.2 = (bf16[1024,512]{1,0:T(8,128)(2,1)S(1)}, bf16[1024,512]{1,0:T(8,128)(2,1)}, u32[]{:S(2)}) copy-start(bf16[1024,512]{1,0:T(8,128)(2,1)} %value_ref.3) | copy-start | bytes 3145732
  3.2 15.5 %copy-start.1 = (bf16[1024,512]{1,0:T(8,128)(2,1)S(1)}, bf16[1024,512]{1,0:T(8,128)(2,1)}, u32[]{:S(2)}) copy-start(bf16[1024,512]{1,0:T(8,128)(2,1)} %key_ref.3) | copy-start | bytes 3145732
  3.2 15.5 %copy-start.3 = (bf16[1024,512]{1,0:T(8,128)(2,1)S(1)}, bf16[1024,512]{1,0:T(8,128)(2,1)}, u32[]{:S(2)}) copy-start(bf16[1024,512]{1,0:T(8,128)(2,1)} %value_ref.3) | copy-start | bytes 3145732
  4.7 27.8 %collective-permute-start.10 = (bf16[256,512]{1,0:T(8,128)(2,1)}, bf16[256,512]{1,0:T(8,128)(2,1)}, u32[]{:S(2)}, u32[]{:S(2)}) collective-permute-start(bf16[256,512]{1,0:T(8,128)(2,1)} %get-tuple-element.36), channel_id=1, source_target_pairs={{0,2},{1,3},{2,0},{3,1},{4,6},{5,7},{6,4},{7,5},{8,10},{9,11},{10,... | collective-permute-start | bytes 786440 | tf_op jit(solution)/shard_map/ppermute | solution.py:423
  4.8 13.6 %collective-permute-start.6 = (bf16[256,512]{1,0:T(8,128)(2,1)}, bf16[256,512]{1,0:T(8,128)(2,1)S(1)}, u32[]{:S(2)}, u32[]{:S(2)}) collective-permute-start(bf16[256,512]{1,0:T(8,128)(2,1)} %get-tuple-element.36), channel_id=1, source_target_pairs={{0,1},{1,0},{2,3},{3,2},{4,5},{5,4},{6,7},{7,6},{8,9},{9,8},{10,11... | collective-permute-start | bytes 786440 | tf_op jit(solution)/shard_map/ppermute | solution.py:423
  6.1 24.9 %collective-permute-start.1 = (bf16[256,512]{1,0:T(8,128)(2,1)}, bf16[256,512]{1,0:T(8,128)(2,1)S(1)}, u32[]{:S(2)}, u32[]{:S(2)}) collective-permute-start(bf16[256,512]{1,0:T(8,128)(2,1)} %get-tuple-element.36), channel_id=1, source_target_pairs={{0,3},{1,2},{2,1},{3,0},{4,7},{5,6},{6,5},{7,4},{8,11},{9,10},{10,... | collective-permute-start | bytes 786440 | tf_op jit(solution)/shard_map/ppermute | solution.py:423
  7.4 23.9 %collective-permute-start.9 = (bf16[256,512]{1,0:T(8,128)(2,1)}, bf16[256,512]{1,0:T(8,128)(2,1)}, u32[]{:S(2)}, u32[]{:S(2)}) collective-permute-start(bf16[256,512]{1,0:T(8,128)(2,1)} %get-tuple-element.41), channel_id=1, source_target_pairs={{0,1},{1,0},{2,3},{3,2},{4,5},{5,4},{6,7},{7,6},{8,9},{9,8},{10,11... | collective-permute-start | bytes 786440 | tf_op jit(solution)/shard_map/ppermute | solution.py:423
  9.6 10.8 %copy-start.6 = (bf16[1,256,4096]{2,1,0:T(8,128)(2,1)S(1)}, bf16[1,256,4096]{2,1,0:T(8,128)(2,1)}, u32[]{:S(2)}) copy-start(bf16[1,256,4096]{2,1,0:T(8,128)(2,1)} %param.6) | copy-start | bytes 6291460
  9.6 10.8 %copy-start.8 = (bf16[1,256,2048]{2,1,0:T(8,128)(2,1)S(1)}, bf16[1,256,2048]{2,1,0:T(8,128)(2,1)}, u32[]{:S(2)}) copy-start(bf16[1,256,2048]{2,1,0:T(8,128)(2,1)} %param.9) | copy-start | bytes 3145732
  18.4 12.6 %copy-start.11 = (bf16[256,512]{1,0:T(8,128)(2,1)}, bf16[256,512]{1,0:T(8,128)(2,1)S(1)}, u32[]{:S(2)}) copy-start(bf16[256,512]{1,0:T(8,128)(2,1)S(1)} %collective-permute-done.6.refs_5_) | copy-start | bytes 786436
  18.4 15.3 %collective-permute-start.8 = (bf16[256,512]{1,0:T(8,128)(2,1)S(1)}, bf16[256,512]{1,0:T(8,128)(2,1)S(1)}, u32[]{:S(2)}, u32[]{:S(2)}) collective-permute-start(bf16[256,512]{1,0:T(8,128)(2,1)S(1)} %collective-permute-done.6.refs_5_), channel_id=1, source_target_pairs={{0,16},{4,20},{8,24},{12,28},{16,0},{20,4},{24,8},{28,12},{1,17},{... | collective-permute-start | bytes 786440 | tf_op jit(solution)/shard_map/ppermute | solution.py:420
  19.4 1.0 copy-start.4
  20.4 29.5 %copy-start.19 = (s32[1,256]{1,0:T(1,128)S(1)}, s32[1,256]{1,0:T(1,128)}, u32[]{:S(2)}) copy-start(s32[1,256]{1,0:T(1,128)} %param.7) | copy-start | bytes 3076
  20.7 13.0 %copy-start.17 = (bf16[256,1024]{1,0:T(8,128)(2,1)}, bf16[256,1024]{1,0:T(8,128)(2,1)S(1)}, u32[]{:S(2)}) copy-start(bf16[256,1024]{1,0:T(8,128)(2,1)S(1)} %get-tuple-element.35) | copy-start | bytes 1572868
  31.0 7.5 %collective-permute-start.7 = (bf16[256,512]{1,0:T(8,128)(2,1)S(1)}, bf16[256,512]{1,0:T(8,128)(2,1)}, u32[]{:S(2)}, u32[]{:S(2)}) collective-permute-start(bf16[256,512]{1,0:T(8,128)(2,1)S(1)} %collective-permute-done.6.refs_5_), channel_id=1, source_target_pairs={{0,8},{4,12},{8,0},{12,4},{16,24},{20,28},{24,16},{28,20},{1,9},{5... | collective-permute-start | bytes 786440 | tf_op jit(solution)/shard_map/ppermute | solution.py:420
  31.3 12.9 %collective-permute-start.5 = (bf16[256,512]{1,0:T(8,128)(2,1)S(1)}, bf16[256,512]{1,0:T(8,128)(2,1)}, u32[]{:S(2)}, u32[]{:S(2)}) collective-permute-start(bf16[256,512]{1,0:T(8,128)(2,1)S(1)} %collective-permute-done.1.refs_1_), channel_id=1, source_target_pairs={{0,24},{4,28},{8,16},{12,20},{16,8},{20,12},{24,0},{28,4},{1,25},{... | collective-permute-start | bytes 786440 | tf_op jit(solution)/shard_map/ppermute | solution.py:420
  32.4 13.0 %collective-permute-start.4 = (bf16[256,512]{1,0:T(8,128)(2,1)S(1)}, bf16[256,512]{1,0:T(8,128)(2,1)}, u32[]{:S(2)}, u32[]{:S(2)}) collective-permute-start(bf16[256,512]{1,0:T(8,128)(2,1)S(1)} %collective-permute-done.1.refs_1_), channel_id=1, source_target_pairs={{0,16},{4,20},{8,24},{12,28},{16,0},{20,4},{24,8},{28,12},{1,17},{... | collective-permute-start | bytes 786440 | tf_op jit(solution)/shard_map/ppermute | solution.py:420
  33.7 0.7 copy-start.15
  34.4 15.4 %collective-permute-start.3 = (bf16[256,512]{1,0:T(8,128)(2,1)S(1)}, bf16[256,512]{1,0:T(8,128)(2,1)}, u32[]{:S(2)}, u32[]{:S(2)}) collective-permute-start(bf16[256,512]{1,0:T(8,128)(2,1)S(1)} %collective-permute-done.1.refs_1_), channel_id=1, source_target_pairs={{0,8},{4,12},{8,0},{12,4},{16,24},{20,28},{24,16},{28,20},{1,9},{5... | collective-permute-start | bytes 786440 | tf_op jit(solution)/shard_map/ppermute | solution.py:420
  34.7 0.7 copy-start.13
  38.6 21.4 %collective-permute-start.13 = (bf16[256,512]{1,0:T(8,128)(2,1)}, bf16[256,512]{1,0:T(8,128)(2,1)S(1)}, u32[]{:S(2)}, u32[]{:S(2)}) collective-permute-start(bf16[256,512]{1,0:T(8,128)(2,1)} %collective-permute-done.10.refs_2_), channel_id=1, source_target_pairs={{0,24},{4,28},{8,16},{12,20},{16,8},{20,12},{24,0},{28,4},{1,25},{... | collective-permute-start | bytes 786440 | tf_op jit(solution)/shard_map/ppermute | solution.py:420
  44.2 15.8 %collective-permute-start.12 = (bf16[256,512]{1,0:T(8,128)(2,1)}, bf16[256,512]{1,0:T(8,128)(2,1)S(1)}, u32[]{:S(2)}, u32[]{:S(2)}) collective-permute-start(bf16[256,512]{1,0:T(8,128)(2,1)} %collective-permute-done.10.refs_2_), channel_id=1, source_target_pairs={{0,16},{4,20},{8,24},{12,28},{16,0},{20,4},{24,8},{28,12},{1,17},{... | collective-permute-start | bytes 786440 | tf_op jit(solution)/shard_map/ppermute | solution.py:420
  45.4 15.6 %collective-permute-start.11 = (bf16[256,512]{1,0:T(8,128)(2,1)}, bf16[256,512]{1,0:T(8,128)(2,1)S(1)}, u32[]{:S(2)}, u32[]{:S(2)}) collective-permute-start(bf16[256,512]{1,0:T(8,128)(2,1)} %collective-permute-done.10.refs_2_), channel_id=1, source_target_pairs={{0,8},{4,12},{8,0},{12,4},{16,24},{20,28},{24,16},{28,20},{1,9},{5... | collective-permute-start | bytes 786440 | tf_op jit(solution)/shard_map/ppermute | solution.py:420
  49.9 10.1 %collective-permute-start.14 = (s32[256]{0:T(256)S(1)}, s32[256]{0:T(256)S(1)}, u32[]{:S(2)}, u32[]{:S(2)}) collective-permute-start(s32[256]{0:T(256)S(1)} %bitcast.26), channel_id=1, source_target_pairs={{0,4},{4,0},{8,12},{12,8},{16,20},{20,16},{24,28},{28,24},{1,5},{5... | collective-permute-start | bytes 3080 | tf_op jit(solution)/shard_map/ppermute | solution.py:415
  52.0 16.0 %collective-permute-start = (bf16[256,1024]{1,0:T(8,128)(2,1)}, bf16[256,1024]{1,0:T(8,128)(2,1)S(1)}, u32[]{:S(2)}, u32[]{:S(2)}) collective-permute-start(bf16[256,1024]{1,0:T(8,128)(2,1)} %copy-done.17), channel_id=1, source_target_pairs={{0,4},{4,0},{8,12},{12,8},{16,20},{20,16},{24,28},{28,24},{1,5},{5... | collective-permute-start | bytes 1572872 | tf_op jit(solution)/shard_map/ppermute | solution.py:415
  52.1 1.2 %copy-start.5 = (bf16[1024,512]{1,0:T(8,128)(2,1)S(1)}, bf16[1024,512]{1,0:T(8,128)(2,1)}, u32[]{:S(2)}) copy-start(bf16[1024,512]{1,0:T(8,128)(2,1)} %copy-done.4) | copy-start | bytes 3145732
  53.3 0.9 copy-start.12
  54.3 0.9 copy-start.14
  55.2 0.9 copy-start.16
  56.2 5.1 %copy-start.7 = (f32[512,128]{1,0:T(8,128)S(1)}, f32[512,128]{1,0:T(8,128)}, u32[]{:S(2)}) copy-start(f32[512,128]{1,0:T(8,128)} %pad_maximum_fusion.refs_6_) | copy-start | bytes 786436
  64.6 0.8 copy-start.9
  65.4 14.2 %collective-permute-start.16 = (bf16[512,512]{1,0:T(8,128)(2,1)}, bf16[512,512]{1,0:T(8,128)(2,1)S(1)}, u32[]{:S(2)}, u32[]{:S(2)}) collective-permute-start(bf16[512,512]{1,0:T(8,128)(2,1)} %get-tuple-element.46.clean_ref), channel_id=1, source_target_pairs={{0,16},{4,20},{8,24},{12,28},{1,17},{5,21},{9,25},{13,29},{2,18},{... | collective-permute-start | bytes 1572872 | tf_op jit(solution)/shard_map/ppermute | solution.py:420
  66.7 14.2 %collective-permute-start.15 = (bf16[512,512]{1,0:T(8,128)(2,1)}, bf16[512,512]{1,0:T(8,128)(2,1)S(1)}, u32[]{:S(2)}, u32[]{:S(2)}) collective-permute-start(bf16[512,512]{1,0:T(8,128)(2,1)} %get-tuple-element.46.clean_ref), channel_id=1, source_target_pairs={{0,8},{4,12},{8,0},{12,4},{16,24},{20,28},{1,9},{5,13},{9,1},{13,5... | collective-permute-start | bytes 1572872 | tf_op jit(solution)/shard_map/ppermute | solution.py:420
  68.0 1.0 %copy-start.10 = (bf16[512,512]{1,0:T(8,128)(2,1)S(1)}, bf16[512,512]{1,0:T(8,128)(2,1)}, u32[]{:S(2)}) copy-start(bf16[512,512]{1,0:T(8,128)(2,1)} %copy-done.9) | copy-start | bytes 1572868
  81.0 10.7 %collective-permute-start.17 = (bf16[256,512]{1,0:T(8,128)(2,1)S(1)}, bf16[256,512]{1,0:T(8,128)(2,1)S(1)}, u32[]{:S(2)}, u32[]{:S(2)}) collective-permute-start(bf16[256,512]{1,0:T(8,128)(2,1)S(1)} %slice.6), channel_id=1, source_target_pairs={{0,16},{4,20},{8,24},{12,28},{1,17},{5,21},{9,25},{13,29},{2,18},{... | collective-permute-start | bytes 786440 | tf_op jit(solution)/shard_map/ppermute | solution.py:420
  82.3 9.5 %collective-permute-start.18 = (bf16[256,512]{1,0:T(8,128)(2,1)S(1)}, bf16[256,512]{1,0:T(8,128)(2,1)S(1)}, u32[]{:S(2)}, u32[]{:S(2)}) collective-permute-start(bf16[256,512]{1,0:T(8,128)(2,1)S(1)} %slice.7), channel_id=1, source_target_pairs={{16,24},{20,28},{24,16},{28,20},{17,25},{21,29},{25,17},{29,21},{1... | collective-permute-start | bytes 786440 | tf_op jit(solution)/shard_map/ppermute | solution.py:420
  93.7 4.4 %collective-permute-start.20 = (bf16[256,512]{1,0:T(8,128)(2,1)S(1)}, bf16[256,512]{1,0:T(8,128)(2,1)S(1)}, u32[]{:S(2)}, u32[]{:S(2)}) collective-permute-start(bf16[256,512]{1,0:T(8,128)(2,1)S(1)} %get-tuple-element.62), channel_id=1, source_target_pairs={{0,4},{4,0},{8,12},{12,8},{16,20},{20,16},{24,28},{28,24},{1,5},{5... | collective-permute-start | bytes 786440 | tf_op jit(solution)/shard_map/ppermute | solution.py:415
  98.0 1.6 %collective-permute-start.19 = (bf16[256,512]{1,0:T(8,128)(2,1)S(1)}, bf16[256,512]{1,0:T(8,128)(2,1)S(1)}, u32[]{:S(2)}, u32[]{:S(2)}) collective-permute-start(bf16[256,512]{1,0:T(8,128)(2,1)S(1)} %get-tuple-element.61), channel_id=1, source_target_pairs={{0,4},{4,0},{8,12},{12,8},{16,20},{20,16},{24,28},{28,24},{1,5},{5... | collective-permute-start | bytes 786440 | tf_op jit(solution)/shard_map/ppermute | solution.py:415

commit v3 on v2

v3 whole, which is shorter than its diff:
```python
import functools
import math

import jax
import jax.numpy as jnp
from jax import lax
from jax.experimental import pallas as pl
from jax.experimental.pallas import tpu as pltpu
from jax.sharding import PartitionSpec as P

HEADS = 16
HEAD_DIM = 128
BLOCK = 256
ROPE_BASE = 500000.0
MASK_ROWS = 16
CHIPS = 4
SCORE_SCALE = HEAD_DIM**-0.5 * math.log2(math.e)
VMEM_LIMIT = 12 * 1024 * 1024
WIDE_LIMIT = 56 * 1024 * 1024

IN_VMEM = pl.BlockSpec(memory_space=pltpu.VMEM)
IN_SMEM = pl.BlockSpec(memory_space=pltpu.SMEM)
IN_PLACE = pl.BlockSpec(memory_space=pl.ANY)


def kernel_call(body, name, out_shape, in_specs, out_specs, scratch=(), aliases=None, flops=0, limit=VMEM_LIMIT):
    return pl.pallas_call(
        body,
        out_shape=out_shape,
        in_specs=in_specs,
        out_specs=out_specs,
        scratch_shapes=scratch,
        input_output_aliases=aliases or {},
        compiler_params=pltpu.CompilerParams(vmem_limit_bytes=limit),
        cost_estimate=pl.CostEstimate(flops=flops, bytes_accessed=0, transcendentals=0),
        name=name,
    )


def bf16(*shape):
    return jax.ShapeDtypeStruct(shape, jnp.bfloat16)


def f32(*shape):
    return jax.ShapeDtypeStruct(shape, jnp.float32)


def rotation(positions):
    half_dim = HEAD_DIM // 2
    frequency = ROPE_BASE ** (-(jnp.arange(half_dim, dtype=jnp.float32) * 2.0 / HEAD_DIM))
    angles = positions.astype(jnp.float32)[:, None] * frequency[None, :]
    cosine = jnp.cos(angles)
    sine = jnp.sin(angles)
    return jnp.concatenate([cosine, cosine], -1), jnp.concatenate([-sine, sine], -1)


def run_copies(copies):
    for copy in copies:
        copy.start()
    for copy in copies:
        copy.wait()


def core_columns(where, weight):
    half = weight.shape[1] // 2
    return pl.ds(pl.multiple_of(where[0] * half, HEAD_DIM), half)


def cut_kernel(flips, where, key_ref, value_ref, *refs):
    outs, sem = refs[:-1], refs[-1]
    columns = core_columns(where, key_ref)
    copies = []
    for out, flip in zip(outs, flips):
        size, width = out.shape
        first = 0 if flip is None else pl.multiple_of((where[1] ^ flip) * size, 16)
        for side, weight in enumerate((key_ref, value_ref)):
            target = out.at[:, side * (width // 2) : (side + 1) * (width // 2)]
            copies.append(pltpu.make_async_copy(weight.at[pl.ds(first, size), columns], target, sem.at[len(copies)]))
    run_copies(copies)


def cut_weights(where, flips, size, w_key, w_value):
    return kernel_call(
        functools.partial(cut_kernel, flips),
        "cut_weights",
        [bf16(size, w_key.shape[1])] * len(flips),
        [IN_SMEM, IN_PLACE, IN_PLACE],
        [IN_VMEM] * len(flips),
        [pltpu.SemaphoreType.DMA((2 * len(flips),))],
        limit=WIDE_LIMIT,
    )(where, w_key, w_value)


def fetch(segments, where, rows, refs, rows_held, held, sem):
    refs = list(refs)
    place = number = 0
    waits = []
    for pieces in segments:
        copies = []
        start_at = place
        for shard_flip, chip_flip, depth, size, as_given in pieces:
            first = 0 if shard_flip is None else (where[2] ^ shard_flip) * depth
            if chip_flip is not None:
                first = first + (where[1] ^ chip_flip) * size
            columns = pl.ds(first if isinstance(first, int) else pl.multiple_of(first, HEAD_DIM), size)
            into = slice(place, place + size)
            low = 0
            for part in rows:
                copies.append((part.at[:, columns], rows_held.at[low : low + part.shape[0], into]))
                low += part.shape[0]
            if as_given:
                for side in range(2):
                    weight = refs.pop(0)
                    half = weight.shape[1] // 2
                    target = held.at[into, side * half : (side + 1) * half]
                    copies.append((weight.at[:, core_columns(where, weight)], target))
            else:
                copies.append((refs.pop(0), held.at[into, :]))
            place += size
        copies = [pltpu.make_async_copy(a, b, sem.at[number + i]) for i, (a, b) in enumerate(copies)]
        number += len(copies)
        for copy in copies:
            copy.start()
        waits.append((copies, slice(start_at, place)))
    return waits


def products(waits, rows_held, held, total):
    for copies, into in waits:
        for copy in copies:
            copy.wait()
        term = jnp.dot(rows_held[:, into], held[into, :], preferred_element_type=jnp.float32)
        total = term if total is None else total + term
    return total


def partial_kernel(segments, count, where, states, other, masks, *refs):
    total_ref, rows_held, held, sem = refs[count:]
    waits = fetch(segments, where, (states, other, masks), refs[:count], rows_held, held, sem)
    total_ref[...] = products(waits, rows_held, held, None)


def finish_kernel(segments, count, has_total, where, states, other, masks, *refs):
    pieces, refs = refs[:count], refs[count:]
    total_ref = refs[0] if has_total else None
    cos_ref, sin_ref, marks_a, marks_b, *outs = refs[int(has_total) :]
    *outs, rows_held, held, kept, sem, out_sem = outs
    waits = fetch(segments, where, (states, other, masks), pieces, rows_held, held, sem)
    tokens = other.shape[0]
    masked = [jnp.broadcast_to(m[...].astype(jnp.float32), (HEAD_DIM, tokens)).T > 0.5 for m in (marks_a, marks_b)]
    sums = products(waits, rows_held, held, None if total_ref is None else total_ref[...])
    kv_heads = len(outs) // 2
    mask_sums = sums[2 * tokens : 2 * tokens + 1]
    writes = []
    for head in range(kv_heads):
        for side in range(2):
            mine = slice(side * tokens, (side + 1) * tokens)
            for is_value in range(2):
                first = (is_value * kv_heads + head) * HEAD_DIM
                clean = sums[mine, first : first + HEAD_DIM]
                noisy = jnp.where(masked[side], mask_sums[:, first : first + HEAD_DIM], clean)
                for copy, part in enumerate((clean, noisy)):
                    if not is_value:
                        part = part * cos_ref[mine, :] + pltpu.roll(part, HEAD_DIM // 2, 1) * sin_ref[mine, :]
                    into = slice(is_value * HEAD_DIM, (is_value + 1) * HEAD_DIM)
                    kept[copy, head, mine, into] = part.astype(jnp.bfloat16)
        for copy in range(2):
            number = copy * kv_heads + head
            writes.append(pltpu.make_async_copy(kept.at[copy, head], outs[number], out_sem.at[number]))
            writes[-1].start()
    for write in writes:
        write.wait()


def project(rows, segments, where, total=None, ending=None):
    kinds, pieces = [], []
    copies = 0
    for segment in segments:
        kinds.append([])
        for piece, shard_flip, chip_flip, depth in segment:
            as_given = isinstance(piece, tuple)
            pieces.extend(piece if as_given else (piece,))
            kinds[-1].append((shard_flip, chip_flip, depth, pieces[-1].shape[0], as_given))
            copies += 5 if as_given else 4
    width = pieces[0].shape[1]
    height = sum(r.shape[0] for r in rows)
    tokens = rows[0].shape[0]
    inner = sum(kind[3] for segment in kinds for kind in segment)
    held = [
        pltpu.VMEM((height, inner), jnp.bfloat16),
        pltpu.VMEM((inner, width), jnp.bfloat16),
    ]
    sems = pltpu.SemaphoreType.DMA((copies,))
    flops = 2 * width * inner * height
    specs = [IN_SMEM] + [IN_PLACE] * (3 + len(pieces))
    if ending is None:
        return kernel_call(
            functools.partial(partial_kernel, kinds, len(pieces)),
            "project_partial",
            f32(height, width),
            specs,
            IN_VMEM,
            [*held, sems],
            flops=flops,
        )(where, *rows, *pieces)
    kv_heads = width // 2 // HEAD_DIM
    extra = [*(() if total is None else (total,)), *ending]
    outs = kernel_call(
        functools.partial(finish_kernel, kinds, len(pieces), total is not None),
        "project_finish",
        [bf16(2 * tokens, 2 * HEAD_DIM)] * (2 * kv_heads),
        specs + [IN_VMEM] * len(extra),
        [IN_PLACE] * (2 * kv_heads),
        [
            *held,
            pltpu.VMEM((2, kv_heads, 2 * tokens, 2 * HEAD_DIM), jnp.bfloat16),
            sems,
            pltpu.SemaphoreType.DMA((2 * kv_heads,)),
        ],
        flops=flops,
    )(where, *rows, *pieces, *extra)
    return outs[:kv_heads], outs[kv_heads:]


def scores_of(query, key):
    return lax.dot_general(query, key, (((1,), (1,)), ((), ())), preferred_element_type=jnp.float32)


def lane_tiles(array):
    return [array[:, lane : lane + HEAD_DIM] for lane in range(0, array.shape[1], HEAD_DIM)]


def absorb(scores, values, before):
    tiles = [lane_tiles(s) for s in scores]
    peak = functools.reduce(jnp.maximum, [t for part in tiles for t in part])
    top = jnp.broadcast_to(jnp.max(peak, -1, keepdims=True), peak.shape) * SCORE_SCALE
    if before is not None:
        top = jnp.maximum(top, before[0])
    total = mixture = None
    for part, value in zip(tiles, values):
        weights = [jnp.exp2(t * SCORE_SCALE - top) for t in part]
        for weight in weights:
            total = weight if total is None else total + weight
        mixed = jnp.dot(
            jnp.concatenate([w.astype(jnp.bfloat16) for w in weights], 1), value, preferred_element_type=jnp.float32
        )
        mixture = mixed if mixture is None else mixture + mixed
    if before is not None:
        rescale = jnp.exp2(before[0] - top)
        total = before[1] * rescale + total
        mixture = before[2] * rescale + mixture
    return top, total, mixture


def pipelined(tasks, score, use):
    waiting = None
    for task in tasks:
        scores = score(task)
        if waiting is not None:
            use(*waiting)
        waiting = (task, scores)
    use(*waiting)


def query_of(query_ref, core, head):
    first = core * (query_ref.shape[1] // 2) + head * HEAD_DIM
    return query_ref[:, pl.ds(pl.multiple_of(first, HEAD_DIM), HEAD_DIM)]


def own_kernel(head_first, groups, where, q_a, q_b, clean_in, noisy_in, *refs):
    *state, clean_ref, noisy_ref, sem = refs
    core = where[0]
    tokens = q_a.shape[0]
    run_copies(
        [
            pltpu.make_async_copy(noisy_in, noisy_ref, sem.at[0]),
            pltpu.make_async_copy(clean_in, clean_ref, sem.at[1]),
        ]
    )

    def score(task):
        head, side = task
        query = query_of((q_a, q_b)[side], core, head_first + head)
        near = scores_of(query, noisy_ref[side * tokens : (side + 1) * tokens, :HEAD_DIM])
        far = scores_of(query, clean_ref[(1 - side) * tokens : (2 - side) * tokens, :HEAD_DIM])
        return [near, jnp.where(core == 1 - side, far, -1e30)]

    def use(task, scores):
        head, side = task
        values = [
            noisy_ref[side * tokens : (side + 1) * tokens, HEAD_DIM:],
            clean_ref[(1 - side) * tokens : (2 - side) * tokens, HEAD_DIM:],
        ]
        mine = pl.ds(side * tokens, tokens)
        for ref, value in zip(state, absorb(scores, values, None)):
            ref[head, mine, :] = value

    pipelined([(head, side) for head in range(groups) for side in range(2)], score, use)


def attend_own(where, queries, clean, noisy, head_first, groups):
    tokens = queries[0].shape[0]
    return kernel_call(
        functools.partial(own_kernel, head_first, groups),
        "attend_own",
        [f32(groups, 2 * tokens, HEAD_DIM)] * 3,
        [IN_SMEM] + [IN_VMEM] * 2 + [IN_PLACE] * 2,
        [IN_VMEM] * 3,
        [pltpu.VMEM(clean.shape, jnp.bfloat16)] * 2 + [pltpu.SemaphoreType.DMA((2,))],
        flops=16 * groups * tokens * tokens * HEAD_DIM,
    )(where, *queries, clean, noisy)


def later_tasks(core, head_first, groups, q_a, q_b, parts, state, store):
    tokens = q_a.shape[0]

    def score(task):
        head, side = task
        query = query_of((q_a, q_b)[side], core, head_first + head)
        return [scores_of(query, part[:, :HEAD_DIM]) for part in parts]

    def use(task, scores):
        head, side = task
        before = state(head, pl.ds(side * tokens, tokens))
        store(head, side, absorb(scores, [part[:, HEAD_DIM:] for part in parts], before))

    pipelined([(head, side) for head in range(groups) for side in range(2)], score, use)


def is_earlier(where, flip):
    return (where[1] ^ flip) < where[1]


def later_kernel(head_first, groups, flips, where, q_a, q_b, *refs):
    count = len(flips)
    parts, outs = refs[:count], refs[count + 3 :]
    tokens = q_a.shape[0]

    def state(head, mine):
        return tuple(out[head, mine, :] for out in outs)

    def store(head, side, values):
        for out, value in zip(outs, values):
            out[head, pl.ds(side * tokens, tokens), :] = value

    for chosen in range(1, 1 << count):
        wanted = [bool(chosen >> number & 1) for number in range(count)]
        hits = [is_earlier(where, flip) if want else ~is_earlier(where, flip) for flip, want in zip(flips, wanted)]

        @pl.when(functools.reduce(jnp.logical_and, hits))
        def _(used=[part for part, want in zip(parts, wanted) if want]):
            later_tasks(where[0], head_first, groups, q_a, q_b, used, state, store)


def attend_later(where, queries, parts, flips, running, head_first, groups):
    tokens = queries[0].shape[0]
    count = len(parts)
    return kernel_call(
        functools.partial(later_kernel, head_first, groups, flips),
        "attend_later",
        [f32(groups, 2 * tokens, HEAD_DIM)] * 3,
        [IN_SMEM] + [IN_VMEM] * (5 + count),
        [IN_VMEM] * 3,
        aliases={3 + count + i: i for i in range(3)},
        flops=8 * groups * tokens * sum(p.shape[0] for p in parts) * HEAD_DIM,
    )(where, *queries, *parts, *running)


def last_kernel(head_first, groups, count, flip, where, q_a, q_b, *refs):
    parts, state_refs, outs = refs[:count], refs[count : count + 3], refs[count + 3 :]
    tokens = q_a.shape[0]

    def state(head, mine):
        return tuple(ref[head, mine, :] for ref in state_refs)

    def store(head, side, values):
        _, total, mixture = values
        total = jnp.sum(total, -1, keepdims=True)
        outs[side][:, head * HEAD_DIM : (head + 1) * HEAD_DIM] = (mixture / total).astype(jnp.bfloat16)

    @pl.when(is_earlier(where, flip))
    def _():
        later_tasks(where[0], head_first, groups, q_a, q_b, parts, state, store)

    @pl.when(~is_earlier(where, flip))
    def _():
        for head in range(groups):
            for side in range(2):
                store(head, side, state(head, pl.ds(side * tokens, tokens)))


def attend_last(where, queries, parts, flip, running, head_first, groups):
    tokens = queries[0].shape[0]
    count = len(parts)
    return kernel_call(
        functools.partial(last_kernel, head_first, groups, count, flip),
        "attend_last",
        [bf16(tokens, groups * HEAD_DIM)] * 2,
        [IN_SMEM] + [IN_VMEM] * (5 + count),
        [IN_VMEM] * 2,
        flops=8 * groups * tokens * sum(p.shape[0] for p in parts) * HEAD_DIM,
    )(where, *queries, *parts, *running)


def place_kernel(count, where, *refs):
    parts, out, sem = refs[: 2 * count], refs[2 * count], refs[2 * count + 1]
    core = where[0]
    half = out.shape[1] // 2
    width = half // count
    copies = []
    for number, part in enumerate(parts):
        side = core if number < count else 1 - core
        first = pl.multiple_of(side * half + (number % count) * width, HEAD_DIM)
        copies.append(pltpu.make_async_copy(part, out.at[:, pl.ds(first, width)], sem.at[number]))
    for copy in copies:
        copy.start()
    for copy in copies:
        copy.wait()


def place_heads(where, mine, received):
    count = len(mine)
    tokens, width = mine[0].shape
    return kernel_call(
        functools.partial(place_kernel, count),
        "place_heads",
        bf16(tokens, 2 * count * width),
        [IN_SMEM] + [IN_VMEM] * (2 * count),
        IN_PLACE,
        [pltpu.SemaphoreType.DMA((2 * count,))],
    )(where, *mine, *received)


def as_scalars(values):
    return jnp.stack([jnp.asarray(v, jnp.int32) for v in values])


def shards(seq_size, fsdp_size, clean_states, noise_mask, mask_embed, queries, w_key, w_value):
    chips = seq_size // 2
    place = lax.axis_index("seq")
    core = lax.rem(place, 2)
    chip = place // 2
    shard = lax.axis_index("fsdp")
    states = clean_states[0]
    marks = noise_mask
    tokens = states.shape[0]
    depth, kv_width = w_key.shape
    kv_heads = kv_width // 2 // HEAD_DIM

    def swap_cores(array):
        return lax.ppermute(array, "seq", [(s, s ^ 1) for s in range(seq_size)])

    def to_chip(array, flip, sources=None):
        sources = range(chips) if sources is None else sources
        pairs = [(2 * s + c, 2 * (s ^ flip) + c) for s in sources for c in range(2)]
        return lax.ppermute(array, "seq", pairs)

    def to_shard(array, flip):
        return lax.ppermute(array, "fsdp", [(s, s ^ flip) for s in range(fsdp_size)])

    square = chips == CHIPS and fsdp_size == 4
    barrier = lax.optimization_barrier
    where = as_scalars([core, chip, shard])
    query_own = queries[0]
    if square:
        quarter = depth // chips
        (mine,) = cut_weights(where, (0,), quarter, w_key, w_value)
        far, near = to_shard(mine, 3), to_shard(mine, 1)

    mask_rows = jnp.broadcast_to(mask_embed[None, :], (MASK_ROWS, mask_embed.shape[0]))
    rows = (states, swap_cores(states), mask_rows)
    query_rows = (query_own, swap_cores(query_own))
    both_marks = (marks, swap_cores(marks))
    steps = jnp.arange(tokens, dtype=jnp.int32)
    cosine, sine = rotation(jnp.concatenate([place * tokens + steps, (place ^ 1) * tokens + steps]))

    if square:
        (corner,) = cut_weights(where, (3,), quarter, w_key, w_value)
        far, near, mine, corner, rows, query_rows, both_marks, cosine, sine = barrier(
            (far, near, mine, corner, rows, query_rows, both_marks, cosine, sine)
        )
        middle = to_shard(mine, 2)
        near_x, far_x = to_chip(near, 1), to_chip(far, 1)
        near_y, far_y = to_chip(near, 2), to_chip(far, 2)
        middle, corner, near_x, near_y, far_x, far_y = barrier((middle, corner, near_x, near_y, far_x, far_y))
        last = [to_chip(middle, flip) for flip in (3, 1, 2)]
        far_corner, near_corner = to_shard(corner, 3), to_shard(corner, 1)
        segments = [
            [((w_key, w_value), 0, None, depth)],
            [
                (far, 3, 0, depth),
                (far_x, 3, 1, depth),
                (far_y, 3, 2, depth),
            ],
            [(near, 1, 0, depth), (near_x, 1, 1, depth), (near_y, 1, 2, depth)],
        ]
        final = [
            [
                (middle, 2, 0, depth),
                (last[0], 2, 3, depth),
                (last[1], 2, 1, depth),
                (last[2], 2, 2, depth),
                (near_corner, 1, 3, depth),
                (far_corner, 3, 3, depth),
            ]
        ]
        total = project(rows, segments, where)
    else:
        (half_weights,) = cut_weights(where, (None,), depth, w_key, w_value)
        gathered = lax.all_gather(half_weights, "fsdp", axis=0, tiled=True)
        final, total = [[(gathered, None, None, depth)]], None
    clean, noisy = project(rows, final, where, total, (cosine, sine, *both_marks))

    groups = query_own.shape[1] // 2 // HEAD_DIM // kv_heads

    def corner_chip(along_x, along_y):
        return [to_chip(along_x[:tokens], 2, (0, 1)), to_chip(along_y[tokens:], 1, (2, 3))]

    heads = range(kv_heads)
    clean, noisy = list(clean), list(noisy)
    running, last_parts = [None] * kv_heads, [None] * kv_heads
    if square:
        along_x = [to_chip(part, 1, (0, 1, 2)) for part in clean]
        along_y = [to_chip(part, 2, (0, 1)) for part in clean]
        along = list(zip(along_x, along_y))
        for head in heads:
            running[head] = attend_own(where, query_rows, clean[head], noisy[head], head * groups, groups)
            along[head], running[head], noisy = barrier((along[head], running[head], noisy))
            last_parts[head] = corner_chip(*along[head])
        for head in heads:
            running[head] = attend_later(where, query_rows, along[head], (1, 2), running[head], head * groups, groups)
    else:
        for head in heads:
            running[head] = attend_own(where, query_rows, clean[head], noisy[head], head * groups, groups)
            for flip in range(1, chips):
                part = to_chip(clean[head], flip, [s for s in range(chips) if s < s ^ flip])
                if flip < chips - 1:
                    running[head] = attend_later(
                        where, query_rows, [part], (flip,), running[head], head * groups, groups
                    )
            last_parts[head] = [part]
    kept, received = [], []
    for head in heads:
        own, other = attend_last(
            where, query_rows, last_parts[head], chips - 1, running[head], head * groups, groups
        )
        kept.append(own)
        received.append(swap_cores(other))
    return place_heads(where, kept, received)[None]


def solution(mesh):
    placed = (
        P("fsdp", "seq", None),
        P("fsdp", "seq"),
        P(),
        P("fsdp", "seq", None),
        P("fsdp", None),
        P("fsdp", None),
    )
    return jax.shard_map(
        functools.partial(shards, mesh.shape["seq"], mesh.shape["fsdp"]),
        mesh=mesh,
        in_specs=placed,
        out_specs=P("fsdp", "seq", None),
        check_vma=False,
    )
```

time: 101 us -> 95.9 us (0.950)
  the two profiles are of different devices: /device:TPU:23 before, /device:TPU:7 now
where the time goes in v3:
time: 95.9 us; the launch traced here: 95.6 us
  starting transfers between devices  33.6 us (35%)
  Pallas kernels  30.6 us (32%)
  waiting for transfers between devices  28.9 us (30%)
  other arithmetic  1.89 us (2%)
    ppermute x5, waiting for transfers between devices, to_shard(): lax.ppermute(array, 'fsdp', [(s, s ^ flip) for s in range(fsdp_size)])  19.6 us
    ppermute x15, starting transfers between devices, to_chip(): return lax.ppermute(array, 'seq', pairs)  19.5 us
    ppermute x5, starting transfers between devices, swap_cores(): return lax.ppermute(array, 'seq', [(s, s ^ 1) for s in range(seq_size)])  8.68 us
    pallas_call x2, Pallas kernels, attend_later(): kernel_call(functools.partial(later_kernel, head_first, groups, flips), '...  7.91 us
    ppermute x15, waiting for transfers between devices, to_chip(): return lax.ppermute(array, 'seq', pairs)  7.82 us
    ppermute x5, starting transfers between devices, to_shard(): lax.ppermute(array, 'fsdp', [(s, s ^ flip) for s in range(fsdp_size)])  5.38 us
    pallas_call x2, Pallas kernels, attend_last(): kernel_call(functools.partial(last_kernel, head_first, groups, count, fli...  5.34 us
    pallas_call x2, Pallas kernels, cut_weights(): kernel_call(functools.partial(cut_kernel, flips), 'cut_weights', [bf16(si...  4.84 us
  transfers between devices with their start and end apart: 25, of which 7 were waited for; matrix products, arithmetic and copies ran while one was open for 2% of the time, Pallas kernels for 27%

profile of v3, /device:TPU:7, one launch (start us, length us, event | category | flops | bytes accessed | tf_op | source)
XLA Modules:
  0.0 95.6 jit_solution(9647206914625034698)
XLA Ops:
  0.0 0.7 collective-permute-start.2
  0.7 0.1 collective-permute-start.3
  0.7 0.6 pad_add_fusion.where
  1.3 2.4 %cut_weights.2 = bf16[256,512]{1,0:T(8,128)(2,1)} custom-call(s32[3]{0:T(128)} %pad_add_fusion.where, bf16[1024,512]{1,0:T(8,128)(2,1)} %refs_0_.1, bf16[1024,512]{1,0:T(8,128)(2,1)} %refs_1_.1), custom_call_target="tpu_custom_call" | custom-call | tf_op jit(solution)/shard_map/cut_weights/pallas_call | solution.py:83
  3.7 3.4 %collective-permute-start = (bf16[256,512]{1,0:T(8,128)(2,1)}, bf16[256,512]{1,0:T(8,128)(2,1)}, u32[]{:S(2)}, u32[]{:S(2)}) collective-permute-start(bf16[256,512]{1,0:T(8,128)(2,1)} %cut_weights.2), channel_id=1, source_target_pairs={{0,3},{1,2},{2,1},{3,0},{4,7},{5,6},{6,5},{7,4},{8,11},{9,10},{10,... | collective-permute-start | bytes 786440 | tf_op jit(solution)/shard_map/ppermute | solution.py:459
  7.1 0.0 collective-permute-start.1
  7.1 0.7 collective-permute-start.4
  7.9 0.0 copy-start.7
  7.9 0.0 copy-start.3
  7.9 1.0 %fusion = (f32[512,64]{1,0:T(8,128)S(1)}, f32[512,64]{1,0:T(8,128)S(1)}, f32[512,64]{1,0:T(8,128)S(1)}) fusion(f32[64]{0:T(128)S(1)} %negate_power_fusion, f32[512]{0:T(512)S(1)} %add_convert_fusion), kind=kLoop, calls=%fused_computation.4 | loop fusion | flops 65536 | bytes 395520 | tf_op jit(solution)/shard_map/neg | solution.py:54
  8.9 0.0 copy-start.6
  8.9 0.0 copy-start.1
  8.9 0.0 copy-start.2
  8.9 0.1 pad_maximum_fusion.refs_7_
  9.1 0.1 pad_maximum_fusion.1.refs_8_
  9.2 2.5 %cut_weights.3 = bf16[256,512]{1,0:T(8,128)(2,1)} custom-call(s32[3]{0:T(128)} %pad_add_fusion.where, bf16[1024,512]{1,0:T(8,128)(2,1)} %refs_0_.1, bf16[1024,512]{1,0:T(8,128)(2,1)} %refs_1_.1), custom_call_target="tpu_custom_call" | custom-call | tf_op jit(solution)/shard_map/cut_weights/pallas_call | solution.py:83
  11.7 0.0 collective-permute-done.4.refs_10_
  11.7 1.8 %collective-permute-done.refs_2_ = bf16[256,512]{1,0:T(8,128)(2,1)} collective-permute-done((bf16[256,512]{1,0:T(8,128)(2,1)}, bf16[256,512]{1,0:T(8,128)(2,1)}, u32[]{:S(2)}, u32[]{:S(2)}) %collective-permute-start) | collective-permute-done | bytes 262176 | tf_op jit(solution)/shard_map/ppermute | solution.py:459
  13.5 6.4 %collective-permute-done.1.refs_5_ = bf16[256,512]{1,0:T(8,128)(2,1)} collective-permute-done((bf16[256,512]{1,0:T(8,128)(2,1)}, bf16[256,512]{1,0:T(8,128)(2,1)}, u32[]{:S(2)}, u32[]{:S(2)}) %collective-permute-start.1) | collective-permute-done | bytes 262176 | tf_op jit(solution)/shard_map/ppermute | solution.py:459
  19.9 0.0 collective-permute-done.3.q_b
  19.9 0.0 collective-permute-done.2.other
  19.9 0.1 collective-permute-start.5
  20.0 0.3 collective-permute-start.6
  20.3 0.2 collective-permute-start.7
  20.6 1.2 %collective-permute-start.8 = (bf16[256,512]{1,0:T(8,128)(2,1)}, bf16[256,512]{1,0:T(8,128)(2,1)S(1)}, u32[]{:S(2)}, u32[]{:S(2)}) collective-permute-start(bf16[256,512]{1,0:T(8,128)(2,1)} %collective-permute-done.refs_2_), channel_id=1, source_target_pairs={{0,8},{4,12},{8,0},{12,4},{16,24},{20,28},{24,16},{28,20},{1,9},{5... | collective-permute-start | bytes 786440 | tf_op jit(solution)/shard_map/ppermute | solution.py:456
  21.8 1.2 %collective-permute-start.9 = (bf16[256,512]{1,0:T(8,128)(2,1)}, bf16[256,512]{1,0:T(8,128)(2,1)S(1)}, u32[]{:S(2)}, u32[]{:S(2)}) collective-permute-start(bf16[256,512]{1,0:T(8,128)(2,1)} %collective-permute-done.refs_2_), channel_id=1, source_target_pairs={{0,16},{4,20},{8,24},{12,28},{16,0},{20,4},{24,8},{28,12},{1,17},{... | collective-permute-start | bytes 786440 | tf_op jit(solution)/shard_map/ppermute | solution.py:456
  23.0 11.4 %collective-permute-done.5.refs_0_ = bf16[256,512]{1,0:T(8,128)(2,1)S(1)} collective-permute-done((bf16[256,512]{1,0:T(8,128)(2,1)S(1)}, bf16[256,512]{1,0:T(8,128)(2,1)S(1)}, u32[]{:S(2)}, u32[]{:S(2)}) %collective-permute-start.5) | collective-permute-done | bytes 262176 | tf_op jit(solution)/shard_map/ppermute | solution.py:459
  34.4 0.0 collective-permute-done.6.refs_6_
  34.4 0.0 collective-permute-done.7.refs_7_
  34.4 0.0 collective-permute-done.8.refs_3_
  34.5 0.0 collective-permute-done.9.refs_4_
  34.5 0.3 collective-permute-start.10
  34.7 1.2 %collective-permute-start.11 = (bf16[256,512]{1,0:T(8,128)(2,1)S(1)}, bf16[256,512]{1,0:T(8,128)(2,1)S(1)}, u32[]{:S(2)}, u32[]{:S(2)}) collective-permute-start(bf16[256,512]{1,0:T(8,128)(2,1)S(1)} %collective-permute-done.5.refs_0_), channel_id=1, source_target_pairs={{0,8},{4,12},{8,0},{12,4},{16,24},{20,28},{24,16},{28,20},{1,9},{5... | collective-permute-start | bytes 786440 | tf_op jit(solution)/shard_map/ppermute | solution.py:456
  35.9 1.2 %collective-permute-start.12 = (bf16[256,512]{1,0:T(8,128)(2,1)S(1)}, bf16[256,512]{1,0:T(8,128)(2,1)S(1)}, u32[]{:S(2)}, u32[]{:S(2)}) collective-permute-start(bf16[256,512]{1,0:T(8,128)(2,1)S(1)} %collective-permute-done.5.refs_0_), channel_id=1, source_target_pairs={{0,16},{4,20},{8,24},{12,28},{16,0},{20,4},{24,8},{28,12},{1,17},{... | collective-permute-start | bytes 786440 | tf_op jit(solution)/shard_map/ppermute | solution.py:456
  37.2 0.0 collective-permute-start.13
  37.2 1.9 %collective-permute-start.14 = (bf16[256,512]{1,0:T(8,128)(2,1)}, bf16[256,512]{1,0:T(8,128)(2,1)S(1)}, u32[]{:S(2)}, u32[]{:S(2)}) collective-permute-start(bf16[256,512]{1,0:T(8,128)(2,1)} %cut_weights.3), channel_id=1, source_target_pairs={{0,3},{1,2},{2,1},{3,0},{4,7},{5,6},{6,5},{7,4},{8,11},{9,10},{10,... | collective-permute-start | bytes 786440 | tf_op jit(solution)/shard_map/ppermute | solution.py:459
  39.1 3.6 %project_partial.1.refs_6_ = f32[528,512]{1,0:T(8,128)S(1)} custom-call(s32[3]{0:T(128)S(1)} %copy-done.4, bf16[256,4096]{1,0:T(8,128)(2,1)S(1)} %bitcast.14, bf16[256,4096]{1,0:T(8,128)(2,1)S(1)} %collective-permute-done.2.other, bf16[16,4096]{1,0:T(8,128)(2,1)S(1)} %broadcast_in_dim.4.masks, bf16[1024,512]{1,0:T(8,128)(2,1)S(1)} %copy-done.1, ...), custom_call_target="tpu_custom_call" | custom-call | flops 1384120320 | tf_op jit(solution)/shard_map/project_partial/pallas_call | solution.py:197
  42.7 0.0 copy-start
  42.8 4.4 %collective-permute-done.11.refs_2_ = bf16[256,512]{1,0:T(8,128)(2,1)S(1)} collective-permute-done((bf16[256,512]{1,0:T(8,128)(2,1)S(1)}, bf16[256,512]{1,0:T(8,128)(2,1)S(1)}, u32[]{:S(2)}, u32[]{:S(2)}) %collective-permute-start.11) | collective-permute-done | bytes 262176 | tf_op jit(solution)/shard_map/ppermute | solution.py:456
  47.2 2.1 %collective-permute-done.12.refs_3_ = bf16[256,512]{1,0:T(8,128)(2,1)S(1)} collective-permute-done((bf16[256,512]{1,0:T(8,128)(2,1)S(1)}, bf16[256,512]{1,0:T(8,128)(2,1)S(1)}, u32[]{:S(2)}, u32[]{:S(2)}) %collective-permute-start.12) | collective-permute-done | bytes 262176 | tf_op jit(solution)/shard_map/ppermute | solution.py:456
  49.3 0.0 collective-permute-done.13.refs_4_
  49.3 0.0 collective-permute-done.14.refs_5_
  49.3 2.9 %project_finish.1 = (bf16[512,256]{1,0:T(8,128)(2,1)S(1)}, bf16[512,256]{1,0:T(8,128)(2,1)S(1)}, bf16[512,256]{1,0:T(8,128)(2,1)S(1)}, bf16[512,256]{1,0:T(8,128)(2,1)S(1)}) custom-call(s32[3]{0:T(128)S(1)} %copy-done.4, bf16[256,4096]{1,0:T(8,128)(2,1)S(1)} %bitcast.15, bf16[256,4096]{1,0:T(8,128)(2,1)S(1)} %collective-permute-done.2.other, ...), custom_call_target="tpu_custom_call" | custom-call | flops 830472192 | tf_op jit(solution)/shard_map/project_finish/pallas_call | solution.py:208
  52.2 1.3 %collective-permute-start.15 = (bf16[512,256]{1,0:T(8,128)(2,1)S(1)}, bf16[512,256]{1,0:T(8,128)(2,1)S(1)}, u32[]{:S(2)}, u32[]{:S(2)}) collective-permute-start(bf16[512,256]{1,0:T(8,128)(2,1)S(1)} %get-tuple-element.74.clean_in), channel_id=1, source_target_pairs={{0,8},{4,12},{8,0},{12,4},{16,24},{20,28},{1,9},{5,13},{9,1},{13,5... | collective-permute-start | bytes 786440 | tf_op jit(solution)/shard_map/ppermute | solution.py:456
  53.5 1.3 %collective-permute-start.16 = (bf16[512,256]{1,0:T(8,128)(2,1)S(1)}, bf16[512,256]{1,0:T(8,128)(2,1)S(1)}, u32[]{:S(2)}, u32[]{:S(2)}) collective-permute-start(bf16[512,256]{1,0:T(8,128)(2,1)S(1)} %get-tuple-element.74.clean_in), channel_id=1, source_target_pairs={{0,16},{4,20},{8,24},{12,28},{1,17},{5,21},{9,25},{13,29},{2,18},{... | collective-permute-start | bytes 786440 | tf_op jit(solution)/shard_map/ppermute | solution.py:456
  54.8 1.3 %collective-permute-start.19 = (bf16[512,256]{1,0:T(8,128)(2,1)S(1)}, bf16[512,256]{1,0:T(8,128)(2,1)S(1)}, u32[]{:S(2)}, u32[]{:S(2)}) collective-permute-start(bf16[512,256]{1,0:T(8,128)(2,1)S(1)} %get-tuple-element.89.clean_in), channel_id=1, source_target_pairs={{0,8},{4,12},{8,0},{12,4},{16,24},{20,28},{1,9},{5,13},{9,1},{13,5... | collective-permute-start | bytes 786440 | tf_op jit(solution)/shard_map/ppermute | solution.py:456
  56.1 1.3 %collective-permute-start.20 = (bf16[512,256]{1,0:T(8,128)(2,1)S(1)}, bf16[512,256]{1,0:T(8,128)(2,1)S(1)}, u32[]{:S(2)}, u32[]{:S(2)}) collective-permute-start(bf16[512,256]{1,0:T(8,128)(2,1)S(1)} %get-tuple-element.89.clean_in), channel_id=1, source_target_pairs={{0,16},{4,20},{8,24},{12,28},{1,17},{5,21},{9,25},{13,29},{2,18},{... | collective-permute-start | bytes 786440 | tf_op jit(solution)/shard_map/ppermute | solution.py:456
  57.4 2.2 %attend_own.2 = (f32[4,512,128]{2,1,0:T(8,128)S(1)}, f32[4,512,128]{2,1,0:T(8,128)S(1)}, f32[4,512,128]{2,1,0:T(8,128)S(1)}) custom-call(s32[3]{0:T(128)S(1)} %copy-done.4, bf16[256,2048]{1,0:T(8,128)(2,1)S(1)} %bitcast.7, bf16[256,2048]{1,0:T(8,128)(2,1)S(1)} %collective-permute-done.3.q_b, bf16[512,256]{1,0:T(8,128)(2,1)S(1)} %get-tuple-element.74.clean_in, ...), custom_call_target="tpu_custom_call" | custom-call | flops 536870912 | tf_op jit(solution)/shard_map/attend_own/pallas_call | solution.py:303
  59.6 0.0 collective-permute-done.15.refs_0_
  59.6 1.3 %collective-permute-done.16.refs_1_ = bf16[512,256]{1,0:T(8,128)(2,1)S(1)} collective-permute-done((bf16[512,256]{1,0:T(8,128)(2,1)S(1)}, bf16[512,256]{1,0:T(8,128)(2,1)S(1)}, u32[]{:S(2)}, u32[]{:S(2)}) %collective-permute-start.16) | collective-permute-done | bytes 262176 | tf_op jit(solution)/shard_map/ppermute | solution.py:456
  60.9 1.3 %collective-permute-start.17 = (bf16[256,256]{1,0:T(8,128)(2,1)S(1)}, bf16[256,256]{1,0:T(8,128)(2,1)S(1)}, u32[]{:S(2)}, u32[]{:S(2)}) collective-permute-start(bf16[256,256]{1,0:T(8,128)(2,1)S(1)} %slice.12), channel_id=1, source_target_pairs={{0,16},{4,20},{8,24},{12,28},{1,17},{5,21},{9,25},{13,29},{2,18},{... | collective-permute-start | bytes 393224 | tf_op jit(solution)/shard_map/ppermute | solution.py:456
  62.2 3.7 %collective-permute-start.18 = (bf16[256,256]{1,0:T(8,128)(2,1)S(1)}, bf16[256,256]{1,0:T(8,128)(2,1)S(1)}, u32[]{:S(2)}, u32[]{:S(2)}) collective-permute-start(bf16[256,256]{1,0:T(8,128)(2,1)S(1)} %slice.13), channel_id=1, source_target_pairs={{16,24},{20,28},{24,16},{28,20},{17,25},{21,29},{25,17},{29,21},{1... | collective-permute-start | bytes 393224 | tf_op jit(solution)/shard_map/ppermute | solution.py:456
  66.0 2.2 %attend_own.3 = (f32[4,512,128]{2,1,0:T(8,128)S(1)}, f32[4,512,128]{2,1,0:T(8,128)S(1)}, f32[4,512,128]{2,1,0:T(8,128)S(1)}) custom-call(s32[3]{0:T(128)S(1)} %copy-done.4, bf16[256,2048]{1,0:T(8,128)(2,1)S(1)} %bitcast.8, bf16[256,2048]{1,0:T(8,128)(2,1)S(1)} %collective-permute-done.3.q_b, bf16[512,256]{1,0:T(8,128)(2,1)S(1)} %get-tuple-element.89.clean_in, ...), custom_call_target="tpu_custom_call" | custom-call | flops 536870912 | tf_op jit(solution)/shard_map/attend_own/pallas_call | solution.py:303
  68.2 0.0 collective-permute-done.20.refs_1_
  68.2 1.3 %collective-permute-start.21 = (bf16[256,256]{1,0:T(8,128)(2,1)S(1)}, bf16[256,256]{1,0:T(8,128)(2,1)S(1)}, u32[]{:S(2)}, u32[]{:S(2)}) collective-permute-start(bf16[256,256]{1,0:T(8,128)(2,1)S(1)} %slice.14), channel_id=1, source_target_pairs={{0,16},{4,20},{8,24},{12,28},{1,17},{5,21},{9,25},{13,29},{2,18},{... | collective-permute-start | bytes 393224 | tf_op jit(solution)/shard_map/ppermute | solution.py:456
  69.5 2.3 %collective-permute-start.22 = (bf16[256,256]{1,0:T(8,128)(2,1)S(1)}, bf16[256,256]{1,0:T(8,128)(2,1)S(1)}, u32[]{:S(2)}, u32[]{:S(2)}) collective-permute-start(bf16[256,256]{1,0:T(8,128)(2,1)S(1)} %slice.15), channel_id=1, source_target_pairs={{16,24},{20,28},{24,16},{28,20},{17,25},{21,29},{25,17},{29,21},{1... | collective-permute-start | bytes 393224 | tf_op jit(solution)/shard_map/ppermute | solution.py:456
  71.9 4.1 %attend_later.2 = (f32[4,512,128]{2,1,0:T(8,128)S(1)}, f32[4,512,128]{2,1,0:T(8,128)S(1)}, f32[4,512,128]{2,1,0:T(8,128)S(1)}) custom-call(s32[3]{0:T(128)S(1)} %copy-done.4, bf16[256,2048]{1,0:T(8,128)(2,1)S(1)} %bitcast.9, bf16[256,2048]{1,0:T(8,128)(2,1)S(1)} %collective-permute-done.3.q_b, ...), custom_call_target="tpu_custom_call", output_to_operand_aliasing={{0}: (5, {}), {1}: (6, {}), {2}: (7, {})} | custom-call | flops 1073741824 | tf_op jit(solution)/shard_map/attend_later/pallas_call | solution.py:358
  75.9 3.9 %attend_later.3 = (f32[4,512,128]{2,1,0:T(8,128)S(1)}, f32[4,512,128]{2,1,0:T(8,128)S(1)}, f32[4,512,128]{2,1,0:T(8,128)S(1)}) custom-call(s32[3]{0:T(128)S(1)} %copy-done.4, bf16[256,2048]{1,0:T(8,128)(2,1)S(1)} %bitcast.10, bf16[256,2048]{1,0:T(8,128)(2,1)S(1)} %collective-permute-done.3.q_b, ...), custom_call_target="tpu_custom_call", output_to_operand_aliasing={{0}: (5, {}), {1}: (6, {}), {2}: (7, {})} | custom-call | flops 1073741824 | tf_op jit(solution)/shard_map/attend_later/pallas_call | solution.py:358
  79.8 2.8 %attend_last.2 = (bf16[256,512]{1,0:T(8,128)(2,1)S(1)}, bf16[256,512]{1,0:T(8,128)(2,1)S(1)}) custom-call(s32[3]{0:T(128)S(1)} %copy-done.4, bf16[256,2048]{1,0:T(8,128)(2,1)S(1)} %bitcast.11, bf16[256,2048]{1,0:T(8,128)(2,1)S(1)} %collective-permute-done.3.q_b, bf16[256,256]{1,0:T(8,128)(2,1)S(1)} %collective-permute-done.17.refs_0_, ...), custom_call_target="tpu_custom_call" | custom-call | flops 536870912 | tf_op jit(solution)/shard_map/attend_last/pallas_call | solution.py:395
  82.6 7.1 %collective-permute-start.23 = (bf16[256,512]{1,0:T(8,128)(2,1)S(1)}, bf16[256,512]{1,0:T(8,128)(2,1)S(1)}, u32[]{:S(2)}, u32[]{:S(2)}) collective-permute-start(bf16[256,512]{1,0:T(8,128)(2,1)S(1)} %get-tuple-element.103), channel_id=1, source_target_pairs={{0,4},{4,0},{8,12},{12,8},{16,20},{20,16},{24,28},{28,24},{1,5},{5... | collective-permute-start | bytes 786440 | tf_op jit(solution)/shard_map/ppermute | solution.py:451
  89.7 2.6 %attend_last.3 = (bf16[256,512]{1,0:T(8,128)(2,1)S(1)}, bf16[256,512]{1,0:T(8,128)(2,1)S(1)}) custom-call(s32[3]{0:T(128)S(1)} %copy-done.4, bf16[256,2048]{1,0:T(8,128)(2,1)S(1)} %bitcast.12, bf16[256,2048]{1,0:T(8,128)(2,1)S(1)} %collective-permute-done.3.q_b, bf16[256,256]{1,0:T(8,128)(2,1)S(1)} %collective-permute-done.21.refs_0_, ...), custom_call_target="tpu_custom_call" | custom-call | flops 536870912 | tf_op jit(solution)/shard_map/attend_last/pallas_call | solution.py:395
  92.3 0.1 collective-permute-start.24
  92.4 1.5 %collective-permute-done.24.refs_3_ = bf16[256,512]{1,0:T(8,128)(2,1)S(1)} collective-permute-done((bf16[256,512]{1,0:T(8,128)(2,1)S(1)}, bf16[256,512]{1,0:T(8,128)(2,1)S(1)}, u32[]{:S(2)}, u32[]{:S(2)}) %collective-permute-start.24) | collective-permute-done | bytes 262176 | tf_op jit(solution)/shard_map/ppermute | solution.py:451
  93.9 1.5 %place_heads.1 = bf16[256,2048]{1,0:T(8,128)(2,1)} custom-call(s32[3]{0:T(128)S(1)} %copy-done.4, bf16[256,512]{1,0:T(8,128)(2,1)S(1)} %get-tuple-element.88.refs_0_, bf16[256,512]{1,0:T(8,128)(2,1)S(1)} %get-tuple-element.102.refs_1_, bf16[256,512]{1,0:T(8,128)(2,1)S(1)} %collective-permute-done.23.refs_2_, bf16[256,512]{1,0:T(8,128)(2,1)S(1)} %collective-permute-done.24.refs_3_), custom_call_target="tpu_custom_call" | custom-call | tf_op jit(solution)/shard_map/place_heads/pallas_call | solution.py:424
  (25 shorter events, 0.1 us)
Async XLA Ops:
  0.0 7.1 %copy-start.5 = (s32[1,256]{1,0:T(1,128)S(1)}, s32[1,256]{1,0:T(1,128)}, u32[]{:S(2)}) copy-start(s32[1,256]{1,0:T(1,128)} %refs_9_) | copy-start | bytes 3076
  0.0 19.9 %collective-permute-start.2 = (bf16[256,4096]{1,0:T(8,128)(2,1)}, bf16[256,4096]{1,0:T(8,128)(2,1)S(1)}, u32[]{:S(2)}, u32[]{:S(2)}) collective-permute-start(bf16[256,4096]{1,0:T(8,128)(2,1)} %bitcast.13), channel_id=1, source_target_pairs={{0,4},{4,0},{8,12},{12,8},{16,20},{20,16},{24,28},{28,24},{1,5},{5... | collective-permute-start | bytes 6291464 | tf_op jit(solution)/shard_map/ppermute | solution.py:451
  0.7 19.2 %collective-permute-start.3 = (bf16[256,2048]{1,0:T(8,128)(2,1)}, bf16[256,2048]{1,0:T(8,128)(2,1)S(1)}, u32[]{:S(2)}, u32[]{:S(2)}) collective-permute-start(bf16[256,2048]{1,0:T(8,128)(2,1)} %bitcast.6), channel_id=1, source_target_pairs={{0,4},{4,0},{8,12},{12,8},{16,20},{20,16},{24,28},{28,24},{1,5},{5... | collective-permute-start | bytes 3145736 | tf_op jit(solution)/shard_map/ppermute | solution.py:451
  3.7 9.8 %collective-permute-start = (bf16[256,512]{1,0:T(8,128)(2,1)}, bf16[256,512]{1,0:T(8,128)(2,1)}, u32[]{:S(2)}, u32[]{:S(2)}) collective-permute-start(bf16[256,512]{1,0:T(8,128)(2,1)} %cut_weights.2), channel_id=1, source_target_pairs={{0,3},{1,2},{2,1},{3,0},{4,7},{5,6},{6,5},{7,4},{8,11},{9,10},{10,... | collective-permute-start | bytes 786440 | tf_op jit(solution)/shard_map/ppermute | solution.py:459
  7.1 12.8 %collective-permute-start.1 = (bf16[256,512]{1,0:T(8,128)(2,1)}, bf16[256,512]{1,0:T(8,128)(2,1)}, u32[]{:S(2)}, u32[]{:S(2)}) collective-permute-start(bf16[256,512]{1,0:T(8,128)(2,1)} %cut_weights.2), channel_id=1, source_target_pairs={{0,1},{1,0},{2,3},{3,2},{4,5},{5,4},{6,7},{7,6},{8,9},{9,8},{10,11... | collective-permute-start | bytes 786440 | tf_op jit(solution)/shard_map/ppermute | solution.py:459
  7.1 4.6 %collective-permute-start.4 = (s32[1,256]{1,0:T(1,128)S(1)}, s32[1,256]{1,0:T(1,128)S(1)}, u32[]{:S(2)}, u32[]{:S(2)}) collective-permute-start(s32[1,256]{1,0:T(1,128)S(1)} %copy-done.5), channel_id=1, source_target_pairs={{0,4},{4,0},{8,12},{12,8},{16,20},{20,16},{24,28},{28,24},{1,5},{5... | collective-permute-start | bytes 3080 | tf_op jit(solution)/shard_map/ppermute | solution.py:451
  7.9 12.1 %copy-start.7 = (bf16[4096]{0:T(1024)(128)(2,1)S(1)}, bf16[4096]{0:T(1024)(128)(2,1)}, u32[]{:S(2)}) copy-start(bf16[4096]{0:T(1024)(128)(2,1)} %param.8) | copy-start | bytes 24580
  7.9 31.2 %copy-start.3 = (bf16[1,256,4096]{2,1,0:T(8,128)(2,1)S(1)}, bf16[1,256,4096]{2,1,0:T(8,128)(2,1)}, u32[]{:S(2)}) copy-start(bf16[1,256,4096]{2,1,0:T(8,128)(2,1)} %param.6) | copy-start | bytes 6291460
  8.9 11.1 %copy-start.6 = (bf16[256,512]{1,0:T(8,128)(2,1)S(1)}, bf16[256,512]{1,0:T(8,128)(2,1)}, u32[]{:S(2)}) copy-start(bf16[256,512]{1,0:T(8,128)(2,1)} %cut_weights.2) | copy-start | bytes 786436
  8.9 30.2 %copy-start.1 = (bf16[1024,512]{1,0:T(8,128)(2,1)S(1)}, bf16[1024,512]{1,0:T(8,128)(2,1)}, u32[]{:S(2)}) copy-start(bf16[1024,512]{1,0:T(8,128)(2,1)} %refs_0_.1) | copy-start | bytes 3145732
  8.9 30.2 %copy-start.2 = (bf16[1024,512]{1,0:T(8,128)(2,1)S(1)}, bf16[1024,512]{1,0:T(8,128)(2,1)}, u32[]{:S(2)}) copy-start(bf16[1024,512]{1,0:T(8,128)(2,1)} %refs_1_.1) | copy-start | bytes 3145732
  8.9 30.2 %copy-start.4 = (s32[3]{0:T(128)S(1)}, s32[3]{0:T(128)}, u32[]{:S(2)}) copy-start(s32[3]{0:T(128)} %pad_add_fusion.where) | copy-start | bytes 40
  19.9 14.5 %collective-permute-start.5 = (bf16[256,512]{1,0:T(8,128)(2,1)S(1)}, bf16[256,512]{1,0:T(8,128)(2,1)S(1)}, u32[]{:S(2)}, u32[]{:S(2)}) collective-permute-start(bf16[256,512]{1,0:T(8,128)(2,1)S(1)} %copy-done.6), channel_id=1, source_target_pairs={{0,2},{1,3},{2,0},{3,1},{4,6},{5,7},{6,4},{7,5},{8,10},{9,11},{10,... | collective-permute-start | bytes 786440 | tf_op jit(solution)/shard_map/ppermute | solution.py:459
  20.0 14.4 %collective-permute-start.6 = (bf16[256,512]{1,0:T(8,128)(2,1)}, bf16[256,512]{1,0:T(8,128)(2,1)S(1)}, u32[]{:S(2)}, u32[]{:S(2)}) collective-permute-start(bf16[256,512]{1,0:T(8,128)(2,1)} %collective-permute-done.1.refs_5_), channel_id=1, source_target_pairs={{0,8},{4,12},{8,0},{12,4},{16,24},{20,28},{24,16},{28,20},{1,9},{5... | collective-permute-start | bytes 786440 | tf_op jit(solution)/shard_map/ppermute | solution.py:456
  20.3 14.1 %collective-permute-start.7 = (bf16[256,512]{1,0:T(8,128)(2,1)}, bf16[256,512]{1,0:T(8,128)(2,1)S(1)}, u32[]{:S(2)}, u32[]{:S(2)}) collective-permute-start(bf16[256,512]{1,0:T(8,128)(2,1)} %collective-permute-done.1.refs_5_), channel_id=1, source_target_pairs={{0,16},{4,20},{8,24},{12,28},{16,0},{20,4},{24,8},{28,12},{1,17},{... | collective-permute-start | bytes 786440 | tf_op jit(solution)/shard_map/ppermute | solution.py:456
  20.6 13.9 %collective-permute-start.8 = (bf16[256,512]{1,0:T(8,128)(2,1)}, bf16[256,512]{1,0:T(8,128)(2,1)S(1)}, u32[]{:S(2)}, u32[]{:S(2)}) collective-permute-start(bf16[256,512]{1,0:T(8,128)(2,1)} %collective-permute-done.refs_2_), channel_id=1, source_target_pairs={{0,8},{4,12},{8,0},{12,4},{16,24},{20,28},{24,16},{28,20},{1,9},{5... | collective-permute-start | bytes 786440 | tf_op jit(solution)/shard_map/ppermute | solution.py:456
  21.8 12.7 %collective-permute-start.9 = (bf16[256,512]{1,0:T(8,128)(2,1)}, bf16[256,512]{1,0:T(8,128)(2,1)S(1)}, u32[]{:S(2)}, u32[]{:S(2)}) collective-permute-start(bf16[256,512]{1,0:T(8,128)(2,1)} %collective-permute-done.refs_2_), channel_id=1, source_target_pairs={{0,16},{4,20},{8,24},{12,28},{16,0},{20,4},{24,8},{28,12},{1,17},{... | collective-permute-start | bytes 786440 | tf_op jit(solution)/shard_map/ppermute | solution.py:456
  34.5 8.3 %collective-permute-start.10 = (bf16[256,512]{1,0:T(8,128)(2,1)S(1)}, bf16[256,512]{1,0:T(8,128)(2,1)S(1)}, u32[]{:S(2)}, u32[]{:S(2)}) collective-permute-start(bf16[256,512]{1,0:T(8,128)(2,1)S(1)} %collective-permute-done.5.refs_0_), channel_id=1, source_target_pairs={{0,24},{4,28},{8,16},{12,20},{16,8},{20,12},{24,0},{28,4},{1,25},{... | collective-permute-start | bytes 786440 | tf_op jit(solution)/shard_map/ppermute | solution.py:456
  34.7 12.4 %collective-permute-start.11 = (bf16[256,512]{1,0:T(8,128)(2,1)S(1)}, bf16[256,512]{1,0:T(8,128)(2,1)S(1)}, u32[]{:S(2)}, u32[]{:S(2)}) collective-permute-start(bf16[256,512]{1,0:T(8,128)(2,1)S(1)} %collective-permute-done.5.refs_0_), channel_id=1, source_target_pairs={{0,8},{4,12},{8,0},{12,4},{16,24},{20,28},{24,16},{28,20},{1,9},{5... | collective-permute-start | bytes 786440 | tf_op jit(solution)/shard_map/ppermute | solution.py:456
  35.9 13.3 %collective-permute-start.12 = (bf16[256,512]{1,0:T(8,128)(2,1)S(1)}, bf16[256,512]{1,0:T(8,128)(2,1)S(1)}, u32[]{:S(2)}, u32[]{:S(2)}) collective-permute-start(bf16[256,512]{1,0:T(8,128)(2,1)S(1)} %collective-permute-done.5.refs_0_), channel_id=1, source_target_pairs={{0,16},{4,20},{8,24},{12,28},{16,0},{20,4},{24,8},{28,12},{1,17},{... | collective-permute-start | bytes 786440 | tf_op jit(solution)/shard_map/ppermute | solution.py:456
  37.2 12.1 %collective-permute-start.13 = (bf16[256,512]{1,0:T(8,128)(2,1)}, bf16[256,512]{1,0:T(8,128)(2,1)S(1)}, u32[]{:S(2)}, u32[]{:S(2)}) collective-permute-start(bf16[256,512]{1,0:T(8,128)(2,1)} %cut_weights.3), channel_id=1, source_target_pairs={{0,1},{1,0},{2,3},{3,2},{4,5},{5,4},{6,7},{7,6},{8,9},{9,8},{10,11... | collective-permute-start | bytes 786440 | tf_op jit(solution)/shard_map/ppermute | solution.py:459
  37.2 12.1 %collective-permute-start.14 = (bf16[256,512]{1,0:T(8,128)(2,1)}, bf16[256,512]{1,0:T(8,128)(2,1)S(1)}, u32[]{:S(2)}, u32[]{:S(2)}) collective-permute-start(bf16[256,512]{1,0:T(8,128)(2,1)} %cut_weights.3), channel_id=1, source_target_pairs={{0,3},{1,2},{2,1},{3,0},{4,7},{5,6},{6,5},{7,4},{8,11},{9,10},{10,... | collective-permute-start | bytes 786440 | tf_op jit(solution)/shard_map/ppermute | solution.py:459
  42.7 14.7 %copy-start = (bf16[1,256,2048]{2,1,0:T(8,128)(2,1)S(1)}, bf16[1,256,2048]{2,1,0:T(8,128)(2,1)}, u32[]{:S(2)}) copy-start(bf16[1,256,2048]{2,1,0:T(8,128)(2,1)} %param.9) | copy-start | bytes 3145732
  52.2 7.4 %collective-permute-start.15 = (bf16[512,256]{1,0:T(8,128)(2,1)S(1)}, bf16[512,256]{1,0:T(8,128)(2,1)S(1)}, u32[]{:S(2)}, u32[]{:S(2)}) collective-permute-start(bf16[512,256]{1,0:T(8,128)(2,1)S(1)} %get-tuple-element.74.clean_in), channel_id=1, source_target_pairs={{0,8},{4,12},{8,0},{12,4},{16,24},{20,28},{1,9},{5,13},{9,1},{13,5... | collective-permute-start | bytes 786440 | tf_op jit(solution)/shard_map/ppermute | solution.py:456
  53.5 7.4 %collective-permute-start.16 = (bf16[512,256]{1,0:T(8,128)(2,1)S(1)}, bf16[512,256]{1,0:T(8,128)(2,1)S(1)}, u32[]{:S(2)}, u32[]{:S(2)}) collective-permute-start(bf16[512,256]{1,0:T(8,128)(2,1)S(1)} %get-tuple-element.74.clean_in), channel_id=1, source_target_pairs={{0,16},{4,20},{8,24},{12,28},{1,17},{5,21},{9,25},{13,29},{2,18},{... | collective-permute-start | bytes 786440 | tf_op jit(solution)/shard_map/ppermute | solution.py:456
  54.8 13.4 %collective-permute-start.19 = (bf16[512,256]{1,0:T(8,128)(2,1)S(1)}, bf16[512,256]{1,0:T(8,128)(2,1)S(1)}, u32[]{:S(2)}, u32[]{:S(2)}) collective-permute-start(bf16[512,256]{1,0:T(8,128)(2,1)S(1)} %get-tuple-element.89.clean_in), channel_id=1, source_target_pairs={{0,8},{4,12},{8,0},{12,4},{16,24},{20,28},{1,9},{5,13},{9,1},{13,5... | collective-permute-start | bytes 786440 | tf_op jit(solution)/shard_map/ppermute | solution.py:456
  56.1 12.1 %collective-permute-start.20 = (bf16[512,256]{1,0:T(8,128)(2,1)S(1)}, bf16[512,256]{1,0:T(8,128)(2,1)S(1)}, u32[]{:S(2)}, u32[]{:S(2)}) collective-permute-start(bf16[512,256]{1,0:T(8,128)(2,1)S(1)} %get-tuple-element.89.clean_in), channel_id=1, source_target_pairs={{0,16},{4,20},{8,24},{12,28},{1,17},{5,21},{9,25},{13,29},{2,18},{... | collective-permute-start | bytes 786440 | tf_op jit(solution)/shard_map/ppermute | solution.py:456
  60.9 18.9 %collective-permute-start.17 = (bf16[256,256]{1,0:T(8,128)(2,1)S(1)}, bf16[256,256]{1,0:T(8,128)(2,1)S(1)}, u32[]{:S(2)}, u32[]{:S(2)}) collective-permute-start(bf16[256,256]{1,0:T(8,128)(2,1)S(1)} %slice.12), channel_id=1, source_target_pairs={{0,16},{4,20},{8,24},{12,28},{1,17},{5,21},{9,25},{13,29},{2,18},{... | collective-permute-start | bytes 393224 | tf_op jit(solution)/shard_map/ppermute | solution.py:456
  62.2 17.6 %collective-permute-start.18 = (bf16[256,256]{1,0:T(8,128)(2,1)S(1)}, bf16[256,256]{1,0:T(8,128)(2,1)S(1)}, u32[]{:S(2)}, u32[]{:S(2)}) collective-permute-start(bf16[256,256]{1,0:T(8,128)(2,1)S(1)} %slice.13), channel_id=1, source_target_pairs={{16,24},{20,28},{24,16},{28,20},{17,25},{21,29},{25,17},{29,21},{1... | collective-permute-start | bytes 393224 | tf_op jit(solution)/shard_map/ppermute | solution.py:456
  68.2 21.5 %collective-permute-start.21 = (bf16[256,256]{1,0:T(8,128)(2,1)S(1)}, bf16[256,256]{1,0:T(8,128)(2,1)S(1)}, u32[]{:S(2)}, u32[]{:S(2)}) collective-permute-start(bf16[256,256]{1,0:T(8,128)(2,1)S(1)} %slice.14), channel_id=1, source_target_pairs={{0,16},{4,20},{8,24},{12,28},{1,17},{5,21},{9,25},{13,29},{2,18},{... | collective-permute-start | bytes 393224 | tf_op jit(solution)/shard_map/ppermute | solution.py:456
  69.5 20.2 %collective-permute-start.22 = (bf16[256,256]{1,0:T(8,128)(2,1)S(1)}, bf16[256,256]{1,0:T(8,128)(2,1)S(1)}, u32[]{:S(2)}, u32[]{:S(2)}) collective-permute-start(bf16[256,256]{1,0:T(8,128)(2,1)S(1)} %slice.15), channel_id=1, source_target_pairs={{16,24},{20,28},{24,16},{28,20},{17,25},{21,29},{25,17},{29,21},{1... | collective-permute-start | bytes 393224 | tf_op jit(solution)/shard_map/ppermute | solution.py:456
  82.6 9.8 %collective-permute-start.23 = (bf16[256,512]{1,0:T(8,128)(2,1)S(1)}, bf16[256,512]{1,0:T(8,128)(2,1)S(1)}, u32[]{:S(2)}, u32[]{:S(2)}) collective-permute-start(bf16[256,512]{1,0:T(8,128)(2,1)S(1)} %get-tuple-element.103), channel_id=1, source_target_pairs={{0,4},{4,0},{8,12},{12,8},{16,20},{20,16},{24,28},{28,24},{1,5},{5... | collective-permute-start | bytes 786440 | tf_op jit(solution)/shard_map/ppermute | solution.py:451
  92.3 1.6 %collective-permute-start.24 = (bf16[256,512]{1,0:T(8,128)(2,1)S(1)}, bf16[256,512]{1,0:T(8,128)(2,1)S(1)}, u32[]{:S(2)}, u32[]{:S(2)}) collective-permute-start(bf16[256,512]{1,0:T(8,128)(2,1)S(1)} %get-tuple-element.104), channel_id=1, source_target_pairs={{0,4},{4,0},{8,12},{12,8},{16,20},{20,16},{24,28},{28,24},{1,5},{5... | collective-permute-start | bytes 786440 | tf_op jit(solution)/shard_map/ppermute | solution.py:451

commit v4 on v3

--- a/solution.py
+++ b/solution.py
@@ -149,9 +149,8 @@
     tokens = other.shape[0]
     masked = [jnp.broadcast_to(m[...].astype(jnp.float32), (HEAD_DIM, tokens)).T > 0.5 for m in (marks_a, marks_b)]
     sums = products(waits, rows_held, held, None if total_ref is None else total_ref[...])
-    kv_heads = len(outs) // 2
+    kv_heads = sums.shape[1] // 2 // HEAD_DIM
     mask_sums = sums[2 * tokens : 2 * tokens + 1]
-    writes = []
     for head in range(kv_heads):
         for side in range(2):
             mine = slice(side * tokens, (side + 1) * tokens)
@@ -162,14 +161,9 @@
                 for copy, part in enumerate((clean, noisy)):
                     if not is_value:
                         part = part * cos_ref[mine, :] + pltpu.roll(part, HEAD_DIM // 2, 1) * sin_ref[mine, :]
-                    into = slice(is_value * HEAD_DIM, (is_value + 1) * HEAD_DIM)
-                    kept[copy, head, mine, into] = part.astype(jnp.bfloat16)
-        for copy in range(2):
-            number = copy * kv_heads + head
-            writes.append(pltpu.make_async_copy(kept.at[copy, head], outs[number], out_sem.at[number]))
-            writes[-1].start()
-    for write in writes:
-        write.wait()
+                    place = 2 * head + is_value
+                    kept[copy, mine, place * HEAD_DIM : (place + 1) * HEAD_DIM] = part.astype(jnp.bfloat16)
+    run_copies([pltpu.make_async_copy(kept.at[copy], outs[copy], out_sem.at[copy]) for copy in range(2)])
 
 
 def project(rows, segments, where, total=None, ending=None):
@@ -203,23 +197,16 @@
             [*held, sems],
             flops=flops,
         )(where, *rows, *pieces)
-    kv_heads = width // 2 // HEAD_DIM
     extra = [*(() if total is None else (total,)), *ending]
-    outs = kernel_call(
+    return kernel_call(
         functools.partial(finish_kernel, kinds, len(pieces), total is not None),
         "project_finish",
-        [bf16(2 * tokens, 2 * HEAD_DIM)] * (2 * kv_heads),
+        [bf16(2 * tokens, width)] * 2,
         specs + [IN_VMEM] * len(extra),
-        [IN_PLACE] * (2 * kv_heads),
-        [
-            *held,
-            pltpu.VMEM((2, kv_heads, 2 * tokens, 2 * HEAD_DIM), jnp.bfloat16),
-            sems,
-            pltpu.SemaphoreType.DMA((2 * kv_heads,)),
-        ],
+        [IN_PLACE] * 2,
+        [*held, pltpu.VMEM((2, 2 * tokens, width), jnp.bfloat16), sems, pltpu.SemaphoreType.DMA((2,))],
         flops=flops,
     )(where, *rows, *pieces, *extra)
-    return outs[:kv_heads], outs[kv_heads:]
 
 
 def scores_of(query, key):
@@ -267,10 +254,16 @@
     return query_ref[:, pl.ds(pl.multiple_of(first, HEAD_DIM), HEAD_DIM)]
 
 
-def own_kernel(head_first, groups, where, q_a, q_b, clean_in, noisy_in, *refs):
+def kv_lanes(groups, head, is_value):
+    first = (2 * (head // groups) + is_value) * HEAD_DIM
+    return slice(first, first + HEAD_DIM)
+
+
+def own_kernel(groups, where, q_a, q_b, clean_in, noisy_in, *refs):
     *state, clean_ref, noisy_ref, sem = refs
     core = where[0]
     tokens = q_a.shape[0]
+    heads = state[0].shape[0]
     run_copies(
         [
             pltpu.make_async_copy(noisy_in, noisy_ref, sem.at[0]),
@@ -278,60 +271,60 @@
         ]
     )
 
+    def rows_of(side, ref, head, is_value):
+        return ref[side * tokens : (side + 1) * tokens, kv_lanes(groups, head, is_value)]
+
     def score(task):
         head, side = task
-        query = query_of((q_a, q_b)[side], core, head_first + head)
-        near = scores_of(query, noisy_ref[side * tokens : (side + 1) * tokens, :HEAD_DIM])
-        far = scores_of(query, clean_ref[(1 - side) * tokens : (2 - side) * tokens, :HEAD_DIM])
+        query = query_of((q_a, q_b)[side], core, head)
+        near = scores_of(query, rows_of(side, noisy_ref, head, 0))
+        far = scores_of(query, rows_of(1 - side, clean_ref, head, 0))
         return [near, jnp.where(core == 1 - side, far, -1e30)]
 
     def use(task, scores):
         head, side = task
-        values = [
-            noisy_ref[side * tokens : (side + 1) * tokens, HEAD_DIM:],
-            clean_ref[(1 - side) * tokens : (2 - side) * tokens, HEAD_DIM:],
-        ]
+        values = [rows_of(side, noisy_ref, head, 1), rows_of(1 - side, clean_ref, head, 1)]
         mine = pl.ds(side * tokens, tokens)
         for ref, value in zip(state, absorb(scores, values, None)):
             ref[head, mine, :] = value
 
-    pipelined([(head, side) for head in range(groups) for side in range(2)], score, use)
-
-
-def attend_own(where, queries, clean, noisy, head_first, groups):
+    pipelined([(head, side) for head in range(heads) for side in range(2)], score, use)
+
+
+def attend_own(where, queries, clean, noisy, heads, groups):
     tokens = queries[0].shape[0]
     return kernel_call(
-        functools.partial(own_kernel, head_first, groups),
+        functools.partial(own_kernel, groups),
         "attend_own",
-        [f32(groups, 2 * tokens, HEAD_DIM)] * 3,
+        [f32(heads, 2 * tokens, HEAD_DIM)] * 3,
         [IN_SMEM] + [IN_VMEM] * 2 + [IN_PLACE] * 2,
         [IN_VMEM] * 3,
         [pltpu.VMEM(clean.shape, jnp.bfloat16)] * 2 + [pltpu.SemaphoreType.DMA((2,))],
-        flops=16 * groups * tokens * tokens * HEAD_DIM,
+        flops=16 * heads * tokens * tokens * HEAD_DIM,
     )(where, *queries, clean, noisy)
 
 
-def later_tasks(core, head_first, groups, q_a, q_b, parts, state, store):
+def later_tasks(core, heads, groups, q_a, q_b, parts, state, store):
     tokens = q_a.shape[0]
 
     def score(task):
         head, side = task
-        query = query_of((q_a, q_b)[side], core, head_first + head)
-        return [scores_of(query, part[:, :HEAD_DIM]) for part in parts]
+        query = query_of((q_a, q_b)[side], core, head)
+        return [scores_of(query, part[:, kv_lanes(groups, head, 0)]) for part in parts]
 
     def use(task, scores):
         head, side = task
         before = state(head, pl.ds(side * tokens, tokens))
-        store(head, side, absorb(scores, [part[:, HEAD_DIM:] for part in parts], before))
-
-    pipelined([(head, side) for head in range(groups) for side in range(2)], score, use)
+        store(head, side, absorb(scores, [part[:, kv_lanes(groups, head, 1)] for part in parts], before))
+
+    pipelined([(head, side) for head in heads for side in range(2)], score, use)
 
 
 def is_earlier(where, flip):
     return (where[1] ^ flip) < where[1]
 
 
-def later_kernel(head_first, groups, flips, where, q_a, q_b, *refs):
+def later_kernel(groups, flips, where, q_a, q_b, *refs):
     count = len(flips)
     parts, outs = refs[:count], refs[count + 3 :]
     tokens = q_a.shape[0]
@@ -349,56 +342,58 @@
 
         @pl.when(functools.reduce(jnp.logical_and, hits))
         def _(used=[part for part, want in zip(parts, wanted) if want]):
-            later_tasks(where[0], head_first, groups, q_a, q_b, used, state, store)
-
-
-def attend_later(where, queries, parts, flips, running, head_first, groups):
+            later_tasks(where[0], range(outs[0].shape[0]), groups, q_a, q_b, used, state, store)
+
+
+def attend_later(where, queries, parts, flips, running, groups):
+    tokens = queries[0].shape[0]
+    heads = running[0].shape[0]
+    count = len(parts)
+    return kernel_call(
+        functools.partial(later_kernel, groups, flips),
+        "attend_later",
+        [f32(heads, 2 * tokens, HEAD_DIM)] * 3,
+        [IN_SMEM] + [IN_VMEM] * (5 + count),
+        [IN_VMEM] * 3,
+        aliases={3 + count + i: i for i in range(3)},
+        flops=8 * heads * tokens * sum(p.shape[0] for p in parts) * HEAD_DIM,
+    )(where, *queries, *parts, *running)
+
+
+def last_kernel(heads, groups, count, flip, where, q_a, q_b, *refs):
+    parts, state_refs, outs = refs[:count], refs[count : count + 3], refs[count + 3 :]
+    tokens = q_a.shape[0]
+
+    def state(head, mine):
+        return tuple(ref[head, mine, :] for ref in state_refs)
+
+    def store(head, side, values):
+        _, total, mixture = values
+        total = jnp.sum(total, -1, keepdims=True)
+        place = (head - heads[0]) * HEAD_DIM
+        outs[side][:, place : place + HEAD_DIM] = (mixture / total).astype(jnp.bfloat16)
+
+    @pl.when(is_earlier(where, flip))
+    def _():
+        later_tasks(where[0], heads, groups, q_a, q_b, parts, state, store)
+
+    @pl.when(~is_earlier(where, flip))
+    def _():
+        for head in heads:
+            for side in range(2):
+                store(head, side, state(head, pl.ds(side * tokens, tokens)))
+
+
+def attend_last(where, queries, parts, flip, running, heads, groups):
     tokens = queries[0].shape[0]
     count = len(parts)
     return kernel_call(
-        functools.partial(later_kernel, head_first, groups, flips),
-        "attend_later",
-        [f32(groups, 2 * tokens, HEAD_DIM)] * 3,
-        [IN_SMEM] + [IN_VMEM] * (5 + count),
-        [IN_VMEM] * 3,
-        aliases={3 + count + i: i for i in range(3)},
-        flops=8 * groups * tokens * sum(p.shape[0] for p in parts) * HEAD_DIM,
-    )(where, *queries, *parts, *running)
-
-
-def last_kernel(head_first, groups, count, flip, where, q_a, q_b, *refs):
-    parts, state_refs, outs = refs[:count], refs[count : count + 3], refs[count + 3 :]
-    tokens = q_a.shape[0]
-
-    def state(head, mine):
-        return tuple(ref[head, mine, :] for ref in state_refs)
-
-    def store(head, side, values):
-        _, total, mixture = values
-        total = jnp.sum(total, -1, keepdims=True)
-        outs[side][:, head * HEAD_DIM : (head + 1) * HEAD_DIM] = (mixture / total).astype(jnp.bfloat16)
-
-    @pl.when(is_earlier(where, flip))
-    def _():
-        later_tasks(where[0], head_first, groups, q_a, q_b, parts, state, store)
-
-    @pl.when(~is_earlier(where, flip))
-    def _():
-        for head in range(groups):
-            for side in range(2):
-                store(head, side, state(head, pl.ds(side * tokens, tokens)))
-
-
-def attend_last(where, queries, parts, flip, running, head_first, groups):
-    tokens = queries[0].shape[0]
-    count = len(parts)
-    return kernel_call(
-        functools.partial(last_kernel, head_first, groups, count, flip),
+        functools.partial(last_kernel, heads, groups, count, flip),
         "attend_last",
-        [bf16(tokens, groups * HEAD_DIM)] * 2,
+        [bf16(tokens, len(heads) * HEAD_DIM)] * 2,
         [IN_SMEM] + [IN_VMEM] * (5 + count),
         [IN_VMEM] * 2,
-        flops=8 * groups * tokens * sum(p.shape[0] for p in parts) * HEAD_DIM,
+        flops=8 * len(heads) * tokens * sum(p.shape[0] for p in parts) * HEAD_DIM,
     )(where, *queries, *parts, *running)
 
 
@@ -511,38 +506,26 @@
         final, total = [[(gathered, None, None, depth)]], None
     clean, noisy = project(rows, final, where, total, (cosine, sine, *both_marks))
 
-    groups = query_own.shape[1] // 2 // HEAD_DIM // kv_heads
-
-    def corner_chip(along_x, along_y):
-        return [to_chip(along_x[:tokens], 2, (0, 1)), to_chip(along_y[tokens:], 1, (2, 3))]
-
-    heads = range(kv_heads)
-    clean, noisy = list(clean), list(noisy)
-    running, last_parts = [None] * kv_heads, [None] * kv_heads
+    heads = query_own.shape[1] // 2 // HEAD_DIM
+    groups = heads // kv_heads
     if square:
-        along_x = [to_chip(part, 1, (0, 1, 2)) for part in clean]
-        along_y = [to_chip(part, 2, (0, 1)) for part in clean]
-        along = list(zip(along_x, along_y))
-        for head in heads:
-            running[head] = attend_own(where, query_rows, clean[head], noisy[head], head * groups, groups)
-            along[head], running[head], noisy = barrier((along[head], running[head], noisy))
-            last_parts[head] = corner_chip(*along[head])
-        for head in heads:
-            running[head] = attend_later(where, query_rows, along[head], (1, 2), running[head], head * groups, groups)
+        along_x = to_chip(clean, 1, (0, 1, 2))
+        along_y = to_chip(clean, 2, (0, 1))
+        running = attend_own(where, query_rows, clean, noisy, heads, groups)
+        along_x, along_y, running = barrier((along_x, along_y, running))
+        last_parts = [to_chip(along_x[:tokens], 2, (0, 1)), to_chip(along_y[tokens:], 1, (2, 3))]
+        running = attend_later(where, query_rows, [along_x, along_y], (1, 2), running, groups)
     else:
-        for head in heads:
-            running[head] = attend_own(where, query_rows, clean[head], noisy[head], head * groups, groups)
-            for flip in range(1, chips):
-                part = to_chip(clean[head], flip, [s for s in range(chips) if s < s ^ flip])
-                if flip < chips - 1:
-                    running[head] = attend_later(
-                        where, query_rows, [part], (flip,), running[head], head * groups, groups
-                    )
-            last_parts[head] = [part]
+        running = attend_own(where, query_rows, clean, noisy, heads, groups)
+        for flip in range(1, chips):
+            part = to_chip(clean, flip, [s for s in range(chips) if s < s ^ flip])
+            if flip < chips - 1:
+                running = attend_later(where, query_rows, [part], (flip,), running, groups)
+        last_parts = [part]
     kept, received = [], []
-    for head in heads:
+    for first in range(0, heads, groups):
         own, other = attend_last(
-            where, query_rows, last_parts[head], chips - 1, running[head], head * groups, groups
+            where, query_rows, last_parts, chips - 1, running, range(first, first + groups), groups
         )
         kept.append(own)
         received.append(swap_cores(other))

time: 95.9 us -> 86.8 us (0.905)
  starting transfers between devices: 33.6 us -> 22.5 us
  waiting for transfers between devices: 28.9 us -> 33.5 us
  Pallas kernels: 30.6 us -> 28.1 us
    ppermute x15 -> x11, starting transfers between devices: 19.5 us -> 11.4 us  [to_chip(): return lax.ppermute(array, 'seq', pairs)]
    ppermute x5, starting transfers between devices: 8.68 us -> 4.79 us  [swap_cores(): return lax.ppermute(array, 'seq', [(s, s ^ 1) for s in range(seq_size)])]
    ppermute x5, waiting for transfers between devices: 19.6 us -> 23.4 us  [to_shard(): lax.ppermute(array, 'fsdp', [(s, s ^ flip) for s in range(fsdp_size)])]
    pallas_call x6 -> x4, Pallas kernels: 17.7 us -> 15.3 us  [the longest x1 6.92 us: attend_later(): kernel_call(functools.partial(later_kernel, groups, flips), 'attend_later...]
    ppermute x5, starting transfers between devices: 5.38 us -> 6.34 us  [to_shard(): lax.ppermute(array, 'fsdp', [(s, s ^ flip) for s in range(fsdp_size)])]
    ppermute x15 -> x11, waiting for transfers between devices: 7.82 us -> 8.53 us  [to_chip(): return lax.ppermute(array, 'seq', pairs)]
  transfers between devices with their start and end apart: 25 -> 21, of which waited for: 7 -> 6; matrix products, arithmetic and copies ran while one was open for 2% -> 2% of each run, Pallas kernels for 27% -> 25%
where the time goes in v4:
time: 86.8 us; the launch traced here: 86.5 us
  waiting for transfers between devices  33.5 us (39%)
  Pallas kernels  28.1 us (32%)
  starting transfers between devices  22.5 us (26%)
  other arithmetic  1.9 us (2%)
    ppermute x5, waiting for transfers between devices, to_shard(): lax.ppermute(array, 'fsdp', [(s, s ^ flip) for s in range(fsdp_size)])  23.4 us
    ppermute x11, starting transfers between devices, to_chip(): return lax.ppermute(array, 'seq', pairs)  11.4 us
    ppermute x11, waiting for transfers between devices, to_chip(): return lax.ppermute(array, 'seq', pairs)  8.53 us
    pallas_call x1, Pallas kernels, attend_later(): kernel_call(functools.partial(later_kernel, groups, flips), 'attend_later...  6.92 us
    ppermute x5, starting transfers between devices, to_shard(): lax.ppermute(array, 'fsdp', [(s, s ^ flip) for s in range(fsdp_size)])  6.34 us
    pallas_call x2, Pallas kernels, attend_last(): kernel_call(functools.partial(last_kernel, heads, groups, count, flip), '...  4.93 us
    pallas_call x2, Pallas kernels, cut_weights(): kernel_call(functools.partial(cut_kernel, flips), 'cut_weights', [bf16(si...  4.83 us
    ppermute x5, starting transfers between devices, swap_cores(): return lax.ppermute(array, 'seq', [(s, s ^ 1) for s in range(seq_size)])  4.79 us
  transfers between devices with their start and end apart: 21, of which 6 were waited for; matrix products, arithmetic and copies ran while one was open for 2% of the time, Pallas kernels for 25%

profile of v4, /device:TPU:7, one launch (start us, length us, event | category | flops | bytes accessed | tf_op | source)
XLA Modules:
  0.0 86.5 jit_solution(7406775115335533581)
XLA Ops:
  0.0 0.7 collective-permute-start.2
  0.7 0.1 collective-permute-start.3
  0.7 0.6 pad_add_fusion.where
  1.4 2.4 %cut_weights.2 = bf16[256,512]{1,0:T(8,128)(2,1)} custom-call(s32[3]{0:T(128)} %pad_add_fusion.where, bf16[1024,512]{1,0:T(8,128)(2,1)} %refs_0_.1, bf16[1024,512]{1,0:T(8,128)(2,1)} %refs_1_.1), custom_call_target="tpu_custom_call" | custom-call | tf_op jit(solution)/shard_map/cut_weights/pallas_call | solution.py:83
  3.7 1.4 %collective-permute-start.1 = (bf16[256,512]{1,0:T(8,128)(2,1)}, bf16[256,512]{1,0:T(8,128)(2,1)}, u32[]{:S(2)}, u32[]{:S(2)}) collective-permute-start(bf16[256,512]{1,0:T(8,128)(2,1)} %cut_weights.2), channel_id=1, source_target_pairs={{0,1},{1,0},{2,3},{3,2},{4,5},{5,4},{6,7},{7,6},{8,9},{9,8},{10,11... | collective-permute-start | bytes 786440 | tf_op jit(solution)/shard_map/ppermute | solution.py:454
  5.1 2.2 %collective-permute-start = (bf16[256,512]{1,0:T(8,128)(2,1)}, bf16[256,512]{1,0:T(8,128)(2,1)}, u32[]{:S(2)}, u32[]{:S(2)}) collective-permute-start(bf16[256,512]{1,0:T(8,128)(2,1)} %cut_weights.2), channel_id=1, source_target_pairs={{0,3},{1,2},{2,1},{3,0},{4,7},{5,6},{6,5},{7,4},{8,11},{9,10},{10,... | collective-permute-start | bytes 786440 | tf_op jit(solution)/shard_map/ppermute | solution.py:454
  7.3 0.0 copy-done.5
  7.3 1.0 %collective-permute-start.4 = (s32[1,256]{1,0:T(1,128)S(1)}, s32[1,256]{1,0:T(1,128)S(1)}, u32[]{:S(2)}, u32[]{:S(2)}) collective-permute-start(s32[1,256]{1,0:T(1,128)S(1)} %copy-done.5), channel_id=1, source_target_pairs={{0,4},{4,0},{8,12},{12,8},{16,20},{20,16},{24,28},{28,24},{1,5},{5... | collective-permute-start | bytes 3080 | tf_op jit(solution)/shard_map/ppermute | solution.py:446
  8.3 0.0 copy-start.7
  8.3 0.0 copy-start.3
  8.3 1.0 %fusion = (f32[512,64]{1,0:T(8,128)S(1)}, f32[512,64]{1,0:T(8,128)S(1)}, f32[512,64]{1,0:T(8,128)S(1)}) fusion(f32[64]{0:T(128)S(1)} %negate_power_fusion, f32[512]{0:T(512)S(1)} %add_convert_fusion), kind=kLoop, calls=%fused_computation.4 | loop fusion | flops 65536 | bytes 395520 | tf_op jit(solution)/shard_map/neg | solution.py:54
  9.3 0.0 copy-start.6
  9.3 0.0 copy-start.1
  9.4 0.0 copy-start.2
  9.4 0.0 copy-start.4
  9.4 0.1 pad_maximum_fusion.refs_7_
  9.5 0.1 pad_maximum_fusion.1.refs_8_
  9.7 2.5 %cut_weights.3 = bf16[256,512]{1,0:T(8,128)(2,1)} custom-call(s32[3]{0:T(128)} %pad_add_fusion.where, bf16[1024,512]{1,0:T(8,128)(2,1)} %refs_0_.1, bf16[1024,512]{1,0:T(8,128)(2,1)} %refs_1_.1), custom_call_target="tpu_custom_call" | custom-call | tf_op jit(solution)/shard_map/cut_weights/pallas_call | solution.py:83
  12.1 0.0 collective-permute-done.4.refs_10_
  12.2 0.0 collective-permute-done.1.refs_5_
  12.2 7.1 %collective-permute-done.refs_2_ = bf16[256,512]{1,0:T(8,128)(2,1)} collective-permute-done((bf16[256,512]{1,0:T(8,128)(2,1)}, bf16[256,512]{1,0:T(8,128)(2,1)}, u32[]{:S(2)}, u32[]{:S(2)}) %collective-permute-start) | collective-permute-done | bytes 262176 | tf_op jit(solution)/shard_map/ppermute | solution.py:454
  19.2 0.0 collective-permute-done.3.q_b
  19.2 0.0 collective-permute-done.2.other
  19.2 0.0 copy-done.6
  19.3 1.3 %collective-permute-start.5 = (bf16[256,512]{1,0:T(8,128)(2,1)S(1)}, bf16[256,512]{1,0:T(8,128)(2,1)S(1)}, u32[]{:S(2)}, u32[]{:S(2)}) collective-permute-start(bf16[256,512]{1,0:T(8,128)(2,1)S(1)} %copy-done.6), channel_id=1, source_target_pairs={{0,2},{1,3},{2,0},{3,1},{4,6},{5,7},{6,4},{7,5},{8,10},{9,11},{10,... | collective-permute-start | bytes 786440 | tf_op jit(solution)/shard_map/ppermute | solution.py:454
  20.5 0.2 collective-permute-start.7
  20.8 0.3 collective-permute-start.6
  21.0 1.2 %collective-permute-start.9 = (bf16[256,512]{1,0:T(8,128)(2,1)}, bf16[256,512]{1,0:T(8,128)(2,1)S(1)}, u32[]{:S(2)}, u32[]{:S(2)}) collective-permute-start(bf16[256,512]{1,0:T(8,128)(2,1)} %collective-permute-done.refs_2_), channel_id=1, source_target_pairs={{0,16},{4,20},{8,24},{12,28},{16,0},{20,4},{24,8},{28,12},{1,17},{... | collective-permute-start | bytes 786440 | tf_op jit(solution)/shard_map/ppermute | solution.py:451
  22.3 1.2 %collective-permute-start.8 = (bf16[256,512]{1,0:T(8,128)(2,1)}, bf16[256,512]{1,0:T(8,128)(2,1)S(1)}, u32[]{:S(2)}, u32[]{:S(2)}) collective-permute-start(bf16[256,512]{1,0:T(8,128)(2,1)} %collective-permute-done.refs_2_), channel_id=1, source_target_pairs={{0,8},{4,12},{8,0},{12,4},{16,24},{20,28},{24,16},{28,20},{1,9},{5... | collective-permute-start | bytes 786440 | tf_op jit(solution)/shard_map/ppermute | solution.py:451
  23.5 9.1 %collective-permute-done.5.refs_0_ = bf16[256,512]{1,0:T(8,128)(2,1)S(1)} collective-permute-done((bf16[256,512]{1,0:T(8,128)(2,1)S(1)}, bf16[256,512]{1,0:T(8,128)(2,1)S(1)}, u32[]{:S(2)}, u32[]{:S(2)}) %collective-permute-start.5) | collective-permute-done | bytes 262176 | tf_op jit(solution)/shard_map/ppermute | solution.py:454
  32.6 0.0 collective-permute-done.7.refs_7_
  32.6 0.0 collective-permute-done.6.refs_6_
  32.6 0.0 collective-permute-done.9.refs_4_
  32.6 0.0 collective-permute-done.8.refs_3_
  32.6 1.5 %collective-permute-start.14 = (bf16[256,512]{1,0:T(8,128)(2,1)}, bf16[256,512]{1,0:T(8,128)(2,1)S(1)}, u32[]{:S(2)}, u32[]{:S(2)}) collective-permute-start(bf16[256,512]{1,0:T(8,128)(2,1)} %cut_weights.3), channel_id=1, source_target_pairs={{0,3},{1,2},{2,1},{3,0},{4,7},{5,6},{6,5},{7,4},{8,11},{9,10},{10,... | collective-permute-start | bytes 786440 | tf_op jit(solution)/shard_map/ppermute | solution.py:454
  34.1 0.0 collective-permute-start.13
  34.1 1.0 %collective-permute-start.12 = (bf16[256,512]{1,0:T(8,128)(2,1)S(1)}, bf16[256,512]{1,0:T(8,128)(2,1)S(1)}, u32[]{:S(2)}, u32[]{:S(2)}) collective-permute-start(bf16[256,512]{1,0:T(8,128)(2,1)S(1)} %collective-permute-done.5.refs_0_), channel_id=1, source_target_pairs={{0,16},{4,20},{8,24},{12,28},{16,0},{20,4},{24,8},{28,12},{1,17},{... | collective-permute-start | bytes 786440 | tf_op jit(solution)/shard_map/ppermute | solution.py:451
  35.2 0.3 collective-permute-start.11
  35.4 1.3 %collective-permute-start.10 = (bf16[256,512]{1,0:T(8,128)(2,1)S(1)}, bf16[256,512]{1,0:T(8,128)(2,1)S(1)}, u32[]{:S(2)}, u32[]{:S(2)}) collective-permute-start(bf16[256,512]{1,0:T(8,128)(2,1)S(1)} %collective-permute-done.5.refs_0_), channel_id=1, source_target_pairs={{0,24},{4,28},{8,16},{12,20},{16,8},{20,12},{24,0},{28,4},{1,25},{... | collective-permute-start | bytes 786440 | tf_op jit(solution)/shard_map/ppermute | solution.py:451
  36.8 3.6 %project_partial.1.refs_6_ = f32[528,512]{1,0:T(8,128)S(1)} custom-call(s32[3]{0:T(128)S(1)} %copy-done.4, bf16[256,4096]{1,0:T(8,128)(2,1)S(1)} %bitcast.12, bf16[256,4096]{1,0:T(8,128)(2,1)S(1)} %collective-permute-done.2.other, bf16[16,4096]{1,0:T(8,128)(2,1)S(1)} %broadcast_in_dim.4.masks, bf16[1024,512]{1,0:T(8,128)(2,1)S(1)} %copy-done.1, ...), custom_call_target="tpu_custom_call" | custom-call | flops 1384120320 | tf_op jit(solution)/shard_map/project_partial/pallas_call | solution.py:191
  40.4 0.0 copy-start
  40.4 0.0 collective-permute-done.14.refs_5_
  40.4 7.3 %collective-permute-done.13.refs_4_ = bf16[256,512]{1,0:T(8,128)(2,1)S(1)} collective-permute-done((bf16[256,512]{1,0:T(8,128)(2,1)}, bf16[256,512]{1,0:T(8,128)(2,1)S(1)}, u32[]{:S(2)}, u32[]{:S(2)}) %collective-permute-start.13) | collective-permute-done | bytes 262176 | tf_op jit(solution)/shard_map/ppermute | solution.py:454
  47.7 0.0 collective-permute-done.12.refs_3_
  47.7 0.0 collective-permute-done.11.refs_2_
  47.7 0.0 collective-permute-done.10.refs_1_
  47.7 2.8 %project_finish.1 = (bf16[512,512]{1,0:T(8,128)(2,1)S(1)}, bf16[512,512]{1,0:T(8,128)(2,1)S(1)}) custom-call(s32[3]{0:T(128)S(1)} %copy-done.4, bf16[256,4096]{1,0:T(8,128)(2,1)S(1)} %bitcast.13, bf16[256,4096]{1,0:T(8,128)(2,1)S(1)} %collective-permute-done.2.other, bf16[16,4096]{1,0:T(8,128)(2,1)S(1)} %broadcast_in_dim.4.masks, ...), custom_call_target="tpu_custom_call" | custom-call | flops 830472192 | tf_op jit(solution)/shard_map/project_finish/pallas_call | solution.py:201
  50.5 1.3 %collective-permute-start.16 = (bf16[512,512]{1,0:T(8,128)(2,1)S(1)}, bf16[512,512]{1,0:T(8,128)(2,1)S(1)}, u32[]{:S(2)}, u32[]{:S(2)}) collective-permute-start(bf16[512,512]{1,0:T(8,128)(2,1)S(1)} %get-tuple-element.60.clean_in), channel_id=1, source_target_pairs={{0,16},{4,20},{8,24},{12,28},{1,17},{5,21},{9,25},{13,29},{2,18},{... | collective-permute-start | bytes 1572872 | tf_op jit(solution)/shard_map/ppermute | solution.py:451
  51.8 1.3 %collective-permute-start.15 = (bf16[512,512]{1,0:T(8,128)(2,1)S(1)}, bf16[512,512]{1,0:T(8,128)(2,1)S(1)}, u32[]{:S(2)}, u32[]{:S(2)}) collective-permute-start(bf16[512,512]{1,0:T(8,128)(2,1)S(1)} %get-tuple-element.60.clean_in), channel_id=1, source_target_pairs={{0,8},{4,12},{8,0},{12,4},{16,24},{20,28},{1,9},{5,13},{9,1},{13,5... | collective-permute-start | bytes 1572872 | tf_op jit(solution)/shard_map/ppermute | solution.py:451
  53.1 3.5 %attend_own.1 = (f32[8,512,128]{2,1,0:T(8,128)S(1)}, f32[8,512,128]{2,1,0:T(8,128)S(1)}, f32[8,512,128]{2,1,0:T(8,128)S(1)}) custom-call(s32[3]{0:T(128)S(1)} %copy-done.4, bf16[256,2048]{1,0:T(8,128)(2,1)S(1)} %bitcast.7, bf16[256,2048]{1,0:T(8,128)(2,1)S(1)} %collective-permute-done.3.q_b, bf16[512,512]{1,0:T(8,128)(2,1)S(1)} %get-tuple-element.60.clean_in, ...), custom_call_target="tpu_custom_call" | custom-call | flops 1073741824 | tf_op jit(solution)/shard_map/attend_own/pallas_call | solution.py:296
  56.6 7.2 %collective-permute-done.16.refs_1_ = bf16[512,512]{1,0:T(8,128)(2,1)S(1)} collective-permute-done((bf16[512,512]{1,0:T(8,128)(2,1)S(1)}, bf16[512,512]{1,0:T(8,128)(2,1)S(1)}, u32[]{:S(2)}, u32[]{:S(2)}) %collective-permute-start.16) | collective-permute-done | bytes 524320 | tf_op jit(solution)/shard_map/ppermute | solution.py:451
  63.8 1.3 %collective-permute-done.15.refs_0_ = bf16[512,512]{1,0:T(8,128)(2,1)S(1)} collective-permute-done((bf16[512,512]{1,0:T(8,128)(2,1)S(1)}, bf16[512,512]{1,0:T(8,128)(2,1)S(1)}, u32[]{:S(2)}, u32[]{:S(2)}) %collective-permute-start.15) | collective-permute-done | bytes 524320 | tf_op jit(solution)/shard_map/ppermute | solution.py:451
  65.1 1.3 %collective-permute-start.17 = (bf16[256,512]{1,0:T(8,128)(2,1)S(1)}, bf16[256,512]{1,0:T(8,128)(2,1)S(1)}, u32[]{:S(2)}, u32[]{:S(2)}) collective-permute-start(bf16[256,512]{1,0:T(8,128)(2,1)S(1)} %slice.6), channel_id=1, source_target_pairs={{0,16},{4,20},{8,24},{12,28},{1,17},{5,21},{9,25},{13,29},{2,18},{... | collective-permute-start | bytes 786440 | tf_op jit(solution)/shard_map/ppermute | solution.py:451
  66.4 1.9 %collective-permute-start.18 = (bf16[256,512]{1,0:T(8,128)(2,1)S(1)}, bf16[256,512]{1,0:T(8,128)(2,1)S(1)}, u32[]{:S(2)}, u32[]{:S(2)}) collective-permute-start(bf16[256,512]{1,0:T(8,128)(2,1)S(1)} %slice.7), channel_id=1, source_target_pairs={{16,24},{20,28},{24,16},{28,20},{17,25},{21,29},{25,17},{29,21},{1... | collective-permute-start | bytes 786440 | tf_op jit(solution)/shard_map/ppermute | solution.py:451
  68.4 6.9 %attend_later.1 = (f32[8,512,128]{2,1,0:T(8,128)S(1)}, f32[8,512,128]{2,1,0:T(8,128)S(1)}, f32[8,512,128]{2,1,0:T(8,128)S(1)}) custom-call(s32[3]{0:T(128)S(1)} %copy-done.4, bf16[256,2048]{1,0:T(8,128)(2,1)S(1)} %bitcast.8, bf16[256,2048]{1,0:T(8,128)(2,1)S(1)} %collective-permute-done.3.q_b, ...), custom_call_target="tpu_custom_call", output_to_operand_aliasing={{0}: (5, {}), {1}: (6, {}), {2}: (7, {})} | custom-call | flops 2147483648 | tf_op jit(solution)/shard_map/attend_later/pallas_call | solution.py:352
  75.3 0.0 collective-permute-done.17.refs_0_
  75.3 0.0 collective-permute-done.18.refs_1_
  75.3 2.5 %attend_last.3 = (bf16[256,512]{1,0:T(8,128)(2,1)S(1)}, bf16[256,512]{1,0:T(8,128)(2,1)S(1)}) custom-call(s32[3]{0:T(128)S(1)} %copy-done.4, bf16[256,2048]{1,0:T(8,128)(2,1)S(1)} %bitcast.9, bf16[256,2048]{1,0:T(8,128)(2,1)S(1)} %collective-permute-done.3.q_b, bf16[256,512]{1,0:T(8,128)(2,1)S(1)} %collective-permute-done.17.refs_0_, ...), custom_call_target="tpu_custom_call" | custom-call | flops 536870912 | tf_op jit(solution)/shard_map/attend_last/pallas_call | solution.py:390
  77.8 3.0 %collective-permute-start.20 = (bf16[256,512]{1,0:T(8,128)(2,1)S(1)}, bf16[256,512]{1,0:T(8,128)(2,1)S(1)}, u32[]{:S(2)}, u32[]{:S(2)}) collective-permute-start(bf16[256,512]{1,0:T(8,128)(2,1)S(1)} %get-tuple-element.76), channel_id=1, source_target_pairs={{0,4},{4,0},{8,12},{12,8},{16,20},{20,16},{24,28},{28,24},{1,5},{5... | collective-permute-start | bytes 786440 | tf_op jit(solution)/shard_map/ppermute | solution.py:446
  80.8 2.5 %attend_last.2 = (bf16[256,512]{1,0:T(8,128)(2,1)S(1)}, bf16[256,512]{1,0:T(8,128)(2,1)S(1)}) custom-call(s32[3]{0:T(128)S(1)} %copy-done.4, bf16[256,2048]{1,0:T(8,128)(2,1)S(1)} %bitcast.10, bf16[256,2048]{1,0:T(8,128)(2,1)S(1)} %collective-permute-done.3.q_b, bf16[256,512]{1,0:T(8,128)(2,1)S(1)} %collective-permute-done.17.refs_0_, ...), custom_call_target="tpu_custom_call" | custom-call | flops 536870912 | tf_op jit(solution)/shard_map/attend_last/pallas_call | solution.py:390
  83.2 0.1 collective-permute-start.19
  83.3 0.0 collective-permute-done.20.refs_3_
  83.3 1.5 %collective-permute-done.19.refs_2_ = bf16[256,512]{1,0:T(8,128)(2,1)S(1)} collective-permute-done((bf16[256,512]{1,0:T(8,128)(2,1)S(1)}, bf16[256,512]{1,0:T(8,128)(2,1)S(1)}, u32[]{:S(2)}, u32[]{:S(2)}) %collective-permute-start.19) | collective-permute-done | bytes 262176 | tf_op jit(solution)/shard_map/ppermute | solution.py:446
  84.8 1.5 %place_heads.1 = bf16[256,2048]{1,0:T(8,128)(2,1)} custom-call(s32[3]{0:T(128)S(1)} %copy-done.4, bf16[256,512]{1,0:T(8,128)(2,1)S(1)} %get-tuple-element.73.refs_0_, bf16[256,512]{1,0:T(8,128)(2,1)S(1)} %get-tuple-element.74.refs_1_, bf16[256,512]{1,0:T(8,128)(2,1)S(1)} %collective-permute-done.19.refs_2_, bf16[256,512]{1,0:T(8,128)(2,1)S(1)} %collective-permute-done.20.refs_3_), custom_call_target="tpu_custom_call" | custom-call | tf_op jit(solution)/shard_map/place_heads/pallas_call | solution.py:419
  (13 shorter events, 0.1 us)
Async XLA Ops:
  0.0 7.3 %copy-start.5 = (s32[1,256]{1,0:T(1,128)S(1)}, s32[1,256]{1,0:T(1,128)}, u32[]{:S(2)}) copy-start(s32[1,256]{1,0:T(1,128)} %refs_9_) | copy-start | bytes 3076
  0.0 19.2 %collective-permute-start.2 = (bf16[256,4096]{1,0:T(8,128)(2,1)}, bf16[256,4096]{1,0:T(8,128)(2,1)S(1)}, u32[]{:S(2)}, u32[]{:S(2)}) collective-permute-start(bf16[256,4096]{1,0:T(8,128)(2,1)} %bitcast.11), channel_id=1, source_target_pairs={{0,4},{4,0},{8,12},{12,8},{16,20},{20,16},{24,28},{28,24},{1,5},{5... | collective-permute-start | bytes 6291464 | tf_op jit(solution)/shard_map/ppermute | solution.py:446
  0.7 18.5 %collective-permute-start.3 = (bf16[256,2048]{1,0:T(8,128)(2,1)}, bf16[256,2048]{1,0:T(8,128)(2,1)S(1)}, u32[]{:S(2)}, u32[]{:S(2)}) collective-permute-start(bf16[256,2048]{1,0:T(8,128)(2,1)} %bitcast.6), channel_id=1, source_target_pairs={{0,4},{4,0},{8,12},{12,8},{16,20},{20,16},{24,28},{28,24},{1,5},{5... | collective-permute-start | bytes 3145736 | tf_op jit(solution)/shard_map/ppermute | solution.py:446
  3.7 8.4 %collective-permute-start.1 = (bf16[256,512]{1,0:T(8,128)(2,1)}, bf16[256,512]{1,0:T(8,128)(2,1)}, u32[]{:S(2)}, u32[]{:S(2)}) collective-permute-start(bf16[256,512]{1,0:T(8,128)(2,1)} %cut_weights.2), channel_id=1, source_target_pairs={{0,1},{1,0},{2,3},{3,2},{4,5},{5,4},{6,7},{7,6},{8,9},{9,8},{10,11... | collective-permute-start | bytes 786440 | tf_op jit(solution)/shard_map/ppermute | solution.py:454
  5.1 14.1 %collective-permute-start = (bf16[256,512]{1,0:T(8,128)(2,1)}, bf16[256,512]{1,0:T(8,128)(2,1)}, u32[]{:S(2)}, u32[]{:S(2)}) collective-permute-start(bf16[256,512]{1,0:T(8,128)(2,1)} %cut_weights.2), channel_id=1, source_target_pairs={{0,3},{1,2},{2,1},{3,0},{4,7},{5,6},{6,5},{7,4},{8,11},{9,10},{10,... | collective-permute-start | bytes 786440 | tf_op jit(solution)/shard_map/ppermute | solution.py:454
  7.3 4.9 %collective-permute-start.4 = (s32[1,256]{1,0:T(1,128)S(1)}, s32[1,256]{1,0:T(1,128)S(1)}, u32[]{:S(2)}, u32[]{:S(2)}) collective-permute-start(s32[1,256]{1,0:T(1,128)S(1)} %copy-done.5), channel_id=1, source_target_pairs={{0,4},{4,0},{8,12},{12,8},{16,20},{20,16},{24,28},{28,24},{1,5},{5... | collective-permute-start | bytes 3080 | tf_op jit(solution)/shard_map/ppermute | solution.py:446
  8.3 10.9 %copy-start.7 = (bf16[4096]{0:T(1024)(128)(2,1)S(1)}, bf16[4096]{0:T(1024)(128)(2,1)}, u32[]{:S(2)}) copy-start(bf16[4096]{0:T(1024)(128)(2,1)} %param.8) | copy-start | bytes 24580
  8.3 28.4 %copy-start.3 = (bf16[1,256,4096]{2,1,0:T(8,128)(2,1)S(1)}, bf16[1,256,4096]{2,1,0:T(8,128)(2,1)}, u32[]{:S(2)}) copy-start(bf16[1,256,4096]{2,1,0:T(8,128)(2,1)} %param.6) | copy-start | bytes 6291460
  9.3 9.9 %copy-start.6 = (bf16[256,512]{1,0:T(8,128)(2,1)S(1)}, bf16[256,512]{1,0:T(8,128)(2,1)}, u32[]{:S(2)}) copy-start(bf16[256,512]{1,0:T(8,128)(2,1)} %cut_weights.2) | copy-start | bytes 786436
  9.3 27.4 %copy-start.1 = (bf16[1024,512]{1,0:T(8,128)(2,1)S(1)}, bf16[1024,512]{1,0:T(8,128)(2,1)}, u32[]{:S(2)}) copy-start(bf16[1024,512]{1,0:T(8,128)(2,1)} %refs_0_.1) | copy-start | bytes 3145732
  9.4 27.4 %copy-start.2 = (bf16[1024,512]{1,0:T(8,128)(2,1)S(1)}, bf16[1024,512]{1,0:T(8,128)(2,1)}, u32[]{:S(2)}) copy-start(bf16[1024,512]{1,0:T(8,128)(2,1)} %refs_1_.1) | copy-start | bytes 3145732
  9.4 27.4 %copy-start.4 = (s32[3]{0:T(128)S(1)}, s32[3]{0:T(128)}, u32[]{:S(2)}) copy-start(s32[3]{0:T(128)} %pad_add_fusion.where) | copy-start | bytes 40
  19.3 13.3 %collective-permute-start.5 = (bf16[256,512]{1,0:T(8,128)(2,1)S(1)}, bf16[256,512]{1,0:T(8,128)(2,1)S(1)}, u32[]{:S(2)}, u32[]{:S(2)}) collective-permute-start(bf16[256,512]{1,0:T(8,128)(2,1)S(1)} %copy-done.6), channel_id=1, source_target_pairs={{0,2},{1,3},{2,0},{3,1},{4,6},{5,7},{6,4},{7,5},{8,10},{9,11},{10,... | collective-permute-start | bytes 786440 | tf_op jit(solution)/shard_map/ppermute | solution.py:454
  20.5 12.0 %collective-permute-start.7 = (bf16[256,512]{1,0:T(8,128)(2,1)}, bf16[256,512]{1,0:T(8,128)(2,1)S(1)}, u32[]{:S(2)}, u32[]{:S(2)}) collective-permute-start(bf16[256,512]{1,0:T(8,128)(2,1)} %collective-permute-done.1.refs_5_), channel_id=1, source_target_pairs={{0,16},{4,20},{8,24},{12,28},{16,0},{20,4},{24,8},{28,12},{1,17},{... | collective-permute-start | bytes 786440 | tf_op jit(solution)/shard_map/ppermute | solution.py:451
  20.8 11.8 %collective-permute-start.6 = (bf16[256,512]{1,0:T(8,128)(2,1)}, bf16[256,512]{1,0:T(8,128)(2,1)S(1)}, u32[]{:S(2)}, u32[]{:S(2)}) collective-permute-start(bf16[256,512]{1,0:T(8,128)(2,1)} %collective-permute-done.1.refs_5_), channel_id=1, source_target_pairs={{0,8},{4,12},{8,0},{12,4},{16,24},{20,28},{24,16},{28,20},{1,9},{5... | collective-permute-start | bytes 786440 | tf_op jit(solution)/shard_map/ppermute | solution.py:451
  21.0 11.6 %collective-permute-start.9 = (bf16[256,512]{1,0:T(8,128)(2,1)}, bf16[256,512]{1,0:T(8,128)(2,1)S(1)}, u32[]{:S(2)}, u32[]{:S(2)}) collective-permute-start(bf16[256,512]{1,0:T(8,128)(2,1)} %collective-permute-done.refs_2_), channel_id=1, source_target_pairs={{0,16},{4,20},{8,24},{12,28},{16,0},{20,4},{24,8},{28,12},{1,17},{... | collective-permute-start | bytes 786440 | tf_op jit(solution)/shard_map/ppermute | solution.py:451
  22.3 10.3 %collective-permute-start.8 = (bf16[256,512]{1,0:T(8,128)(2,1)}, bf16[256,512]{1,0:T(8,128)(2,1)S(1)}, u32[]{:S(2)}, u32[]{:S(2)}) collective-permute-start(bf16[256,512]{1,0:T(8,128)(2,1)} %collective-permute-done.refs_2_), channel_id=1, source_target_pairs={{0,8},{4,12},{8,0},{12,4},{16,24},{20,28},{24,16},{28,20},{1,9},{5... | collective-permute-start | bytes 786440 | tf_op jit(solution)/shard_map/ppermute | solution.py:451
  32.6 7.8 %collective-permute-start.14 = (bf16[256,512]{1,0:T(8,128)(2,1)}, bf16[256,512]{1,0:T(8,128)(2,1)S(1)}, u32[]{:S(2)}, u32[]{:S(2)}) collective-permute-start(bf16[256,512]{1,0:T(8,128)(2,1)} %cut_weights.3), channel_id=1, source_target_pairs={{0,3},{1,2},{2,1},{3,0},{4,7},{5,6},{6,5},{7,4},{8,11},{9,10},{10,... | collective-permute-start | bytes 786440 | tf_op jit(solution)/shard_map/ppermute | solution.py:454
  34.1 13.6 %collective-permute-start.13 = (bf16[256,512]{1,0:T(8,128)(2,1)}, bf16[256,512]{1,0:T(8,128)(2,1)S(1)}, u32[]{:S(2)}, u32[]{:S(2)}) collective-permute-start(bf16[256,512]{1,0:T(8,128)(2,1)} %cut_weights.3), channel_id=1, source_target_pairs={{0,1},{1,0},{2,3},{3,2},{4,5},{5,4},{6,7},{7,6},{8,9},{9,8},{10,11... | collective-permute-start | bytes 786440 | tf_op jit(solution)/shard_map/ppermute | solution.py:454
  34.1 13.6 %collective-permute-start.12 = (bf16[256,512]{1,0:T(8,128)(2,1)S(1)}, bf16[256,512]{1,0:T(8,128)(2,1)S(1)}, u32[]{:S(2)}, u32[]{:S(2)}) collective-permute-start(bf16[256,512]{1,0:T(8,128)(2,1)S(1)} %collective-permute-done.5.refs_0_), channel_id=1, source_target_pairs={{0,16},{4,20},{8,24},{12,28},{16,0},{20,4},{24,8},{28,12},{1,17},{... | collective-permute-start | bytes 786440 | tf_op jit(solution)/shard_map/ppermute | solution.py:451
  35.2 12.5 %collective-permute-start.11 = (bf16[256,512]{1,0:T(8,128)(2,1)S(1)}, bf16[256,512]{1,0:T(8,128)(2,1)S(1)}, u32[]{:S(2)}, u32[]{:S(2)}) collective-permute-start(bf16[256,512]{1,0:T(8,128)(2,1)S(1)} %collective-permute-done.5.refs_0_), channel_id=1, source_target_pairs={{0,8},{4,12},{8,0},{12,4},{16,24},{20,28},{24,16},{28,20},{1,9},{5... | collective-permute-start | bytes 786440 | tf_op jit(solution)/shard_map/ppermute | solution.py:451
  35.4 12.3 %collective-permute-start.10 = (bf16[256,512]{1,0:T(8,128)(2,1)S(1)}, bf16[256,512]{1,0:T(8,128)(2,1)S(1)}, u32[]{:S(2)}, u32[]{:S(2)}) collective-permute-start(bf16[256,512]{1,0:T(8,128)(2,1)S(1)} %collective-permute-done.5.refs_0_), channel_id=1, source_target_pairs={{0,24},{4,28},{8,16},{12,20},{16,8},{20,12},{24,0},{28,4},{1,25},{... | collective-permute-start | bytes 786440 | tf_op jit(solution)/shard_map/ppermute | solution.py:451
  40.4 12.7 %copy-start = (bf16[1,256,2048]{2,1,0:T(8,128)(2,1)S(1)}, bf16[1,256,2048]{2,1,0:T(8,128)(2,1)}, u32[]{:S(2)}) copy-start(bf16[1,256,2048]{2,1,0:T(8,128)(2,1)} %param.9) | copy-start | bytes 3145732
  50.5 13.3 %collective-permute-start.16 = (bf16[512,512]{1,0:T(8,128)(2,1)S(1)}, bf16[512,512]{1,0:T(8,128)(2,1)S(1)}, u32[]{:S(2)}, u32[]{:S(2)}) collective-permute-start(bf16[512,512]{1,0:T(8,128)(2,1)S(1)} %get-tuple-element.60.clean_in), channel_id=1, source_target_pairs={{0,16},{4,20},{8,24},{12,28},{1,17},{5,21},{9,25},{13,29},{2,18},{... | collective-permute-start | bytes 1572872 | tf_op jit(solution)/shard_map/ppermute | solution.py:451
  51.8 13.3 %collective-permute-start.15 = (bf16[512,512]{1,0:T(8,128)(2,1)S(1)}, bf16[512,512]{1,0:T(8,128)(2,1)S(1)}, u32[]{:S(2)}, u32[]{:S(2)}) collective-permute-start(bf16[512,512]{1,0:T(8,128)(2,1)S(1)} %get-tuple-element.60.clean_in), channel_id=1, source_target_pairs={{0,8},{4,12},{8,0},{12,4},{16,24},{20,28},{1,9},{5,13},{9,1},{13,5... | collective-permute-start | bytes 1572872 | tf_op jit(solution)/shard_map/ppermute | solution.py:451
  65.1 10.2 %collective-permute-start.17 = (bf16[256,512]{1,0:T(8,128)(2,1)S(1)}, bf16[256,512]{1,0:T(8,128)(2,1)S(1)}, u32[]{:S(2)}, u32[]{:S(2)}) collective-permute-start(bf16[256,512]{1,0:T(8,128)(2,1)S(1)} %slice.6), channel_id=1, source_target_pairs={{0,16},{4,20},{8,24},{12,28},{1,17},{5,21},{9,25},{13,29},{2,18},{... | collective-permute-start | bytes 786440 | tf_op jit(solution)/shard_map/ppermute | solution.py:451
  66.4 8.9 %collective-permute-start.18 = (bf16[256,512]{1,0:T(8,128)(2,1)S(1)}, bf16[256,512]{1,0:T(8,128)(2,1)S(1)}, u32[]{:S(2)}, u32[]{:S(2)}) collective-permute-start(bf16[256,512]{1,0:T(8,128)(2,1)S(1)} %slice.7), channel_id=1, source_target_pairs={{16,24},{20,28},{24,16},{28,20},{17,25},{21,29},{25,17},{29,21},{1... | collective-permute-start | bytes 786440 | tf_op jit(solution)/shard_map/ppermute | solution.py:451
  77.8 5.5 %collective-permute-start.20 = (bf16[256,512]{1,0:T(8,128)(2,1)S(1)}, bf16[256,512]{1,0:T(8,128)(2,1)S(1)}, u32[]{:S(2)}, u32[]{:S(2)}) collective-permute-start(bf16[256,512]{1,0:T(8,128)(2,1)S(1)} %get-tuple-element.76), channel_id=1, source_target_pairs={{0,4},{4,0},{8,12},{12,8},{16,20},{20,16},{24,28},{28,24},{1,5},{5... | collective-permute-start | bytes 786440 | tf_op jit(solution)/shard_map/ppermute | solution.py:446
  83.2 1.6 %collective-permute-start.19 = (bf16[256,512]{1,0:T(8,128)(2,1)S(1)}, bf16[256,512]{1,0:T(8,128)(2,1)S(1)}, u32[]{:S(2)}, u32[]{:S(2)}) collective-permute-start(bf16[256,512]{1,0:T(8,128)(2,1)S(1)} %get-tuple-element.75), channel_id=1, source_target_pairs={{0,4},{4,0},{8,12},{12,8},{16,20},{20,16},{24,28},{28,24},{1,5},{5... | collective-permute-start | bytes 786440 | tf_op jit(solution)/shard_map/ppermute | solution.py:446

commit v5 on v4

--- a/solution.py
+++ b/solution.py
@@ -15,7 +15,7 @@
 MASK_ROWS = 16
 CHIPS = 4
 SCORE_SCALE = HEAD_DIM**-0.5 * math.log2(math.e)
-VMEM_LIMIT = 12 * 1024 * 1024
+VMEM_LIMIT = 16 * 1024 * 1024
 WIDE_LIMIT = 56 * 1024 * 1024
 
 IN_VMEM = pl.BlockSpec(memory_space=pltpu.VMEM)
@@ -108,7 +108,9 @@
             for part in rows:
                 copies.append((part.at[:, columns], rows_held.at[low : low + part.shape[0], into]))
                 low += part.shape[0]
-            if as_given:
+            if held is None:
+                pass
+            elif as_given:
                 for side in range(2):
                     weight = refs.pop(0)
                     half = weight.shape[1] // 2
@@ -134,79 +136,108 @@
     return total
 
 
-def partial_kernel(segments, count, where, states, other, masks, *refs):
-    total_ref, rows_held, held, sem = refs[count:]
-    waits = fetch(segments, where, (states, other, masks), refs[:count], rows_held, held, sem)
+def partial_kernel(segments, final, count, where, states, other, masks, *refs):
+    total_ref, final_rows, rows_held, held, sem, final_sem = refs[count:]
+    rows = (states, other, masks)
+    waits = fetch(segments, where, rows, refs[:count], rows_held, held, sem)
+    final_waits = fetch(final, where, rows, (), final_rows, None, final_sem)
     total_ref[...] = products(waits, rows_held, held, None)
-
-
-def finish_kernel(segments, count, has_total, where, states, other, masks, *refs):
-    pieces, refs = refs[:count], refs[count:]
-    total_ref = refs[0] if has_total else None
-    cos_ref, sin_ref, marks_a, marks_b, *outs = refs[int(has_total) :]
-    *outs, rows_held, held, kept, sem, out_sem = outs
-    waits = fetch(segments, where, (states, other, masks), pieces, rows_held, held, sem)
-    tokens = other.shape[0]
-    masked = [jnp.broadcast_to(m[...].astype(jnp.float32), (HEAD_DIM, tokens)).T > 0.5 for m in (marks_a, marks_b)]
-    sums = products(waits, rows_held, held, None if total_ref is None else total_ref[...])
+    for copies, _ in final_waits:
+        for copy in copies:
+            copy.wait()
+
+
+def rotated(key, cosine, sine):
+    return key * cosine + pltpu.roll(key, HEAD_DIM // 2, 1) * sine
+
+
+def finish_kernel(segments, count, staged, tokens, where, *refs):
+    if staged:
+        total_ref, rows_held = refs[:2]
+        rows, total, refs = (), total_ref[...], refs[2:]
+    else:
+        rows, total, refs = refs[:3], None, refs[3:]
+    pieces, (cos_ref, sin_ref, *refs) = refs[:count], refs[count:]
+    clean_out, mask_out, refs = refs[0], refs[1], refs[2:]
+    if not staged:
+        rows_held, *refs = refs
+    held, kept, sem, out_sem = refs
+    waits = fetch(segments, where, rows, pieces, rows_held, held, sem)
+    sums = products(waits, rows_held, held, total)
     kv_heads = sums.shape[1] // 2 // HEAD_DIM
-    mask_sums = sums[2 * tokens : 2 * tokens + 1]
-    for head in range(kv_heads):
-        for side in range(2):
-            mine = slice(side * tokens, (side + 1) * tokens)
+    writes = []
+    for side in range(2):
+        mine = slice(side * tokens, (side + 1) * tokens)
+        for head in range(kv_heads):
             for is_value in range(2):
                 first = (is_value * kv_heads + head) * HEAD_DIM
-                clean = sums[mine, first : first + HEAD_DIM]
-                noisy = jnp.where(masked[side], mask_sums[:, first : first + HEAD_DIM], clean)
-                for copy, part in enumerate((clean, noisy)):
-                    if not is_value:
-                        part = part * cos_ref[mine, :] + pltpu.roll(part, HEAD_DIM // 2, 1) * sin_ref[mine, :]
-                    place = 2 * head + is_value
-                    kept[copy, mine, place * HEAD_DIM : (place + 1) * HEAD_DIM] = part.astype(jnp.bfloat16)
-    run_copies([pltpu.make_async_copy(kept.at[copy], outs[copy], out_sem.at[copy]) for copy in range(2)])
-
-
-def project(rows, segments, where, total=None, ending=None):
-    kinds, pieces = [], []
-    copies = 0
+                part = sums[mine, first : first + HEAD_DIM]
+                if not is_value:
+                    part = rotated(part, cos_ref[mine, :], sin_ref[mine, :])
+                place = (2 * head + is_value) * HEAD_DIM
+                kept[side, :, place : place + HEAD_DIM] = part.astype(jnp.bfloat16)
+        writes.append(pltpu.make_async_copy(kept.at[side], clean_out.at[mine, :], out_sem.at[side]))
+        writes[-1].start()
+    mask_out[...] = sums[2 * tokens : 2 * tokens + 8]
+    for write in writes:
+        write.wait()
+
+
+def describe(segments):
+    kinds, arrays, copies = [], [], 0
     for segment in segments:
         kinds.append([])
         for piece, shard_flip, chip_flip, depth in segment:
             as_given = isinstance(piece, tuple)
-            pieces.extend(piece if as_given else (piece,))
-            kinds[-1].append((shard_flip, chip_flip, depth, pieces[-1].shape[0], as_given))
+            arrays.extend(piece if as_given else (piece,))
+            kinds[-1].append((shard_flip, chip_flip, depth, arrays[-1].shape[0], as_given))
             copies += 5 if as_given else 4
-    width = pieces[0].shape[1]
+    return kinds, arrays, sum(kind[3] for segment in kinds for kind in segment), copies
+
+
+def project_partial(rows, segments, final, where):
+    kinds, arrays, inner, copies = describe(segments)
+    final_kinds, _, final_inner, final_copies = describe(final)
+    width = arrays[0].shape[1]
     height = sum(r.shape[0] for r in rows)
+    return kernel_call(
+        functools.partial(partial_kernel, kinds, final_kinds, len(arrays)),
+        "project_partial",
+        [f32(height, width), bf16(height, final_inner)],
+        [IN_SMEM] + [IN_PLACE] * (3 + len(arrays)),
+        [IN_VMEM] * 2,
+        [
+            pltpu.VMEM((height, inner), jnp.bfloat16),
+            pltpu.VMEM((inner, width), jnp.bfloat16),
+            pltpu.SemaphoreType.DMA((copies,)),
+            pltpu.SemaphoreType.DMA((final_copies,)),
+        ],
+        flops=2 * width * inner * height,
+    )(where, *rows, *arrays)
+
+
+def project_finish(rows, staged, segments, where, ending):
+    kinds, arrays, inner, copies = describe(segments)
+    width = arrays[0].shape[1]
     tokens = rows[0].shape[0]
-    inner = sum(kind[3] for segment in kinds for kind in segment)
-    held = [
-        pltpu.VMEM((height, inner), jnp.bfloat16),
-        pltpu.VMEM((inner, width), jnp.bfloat16),
-    ]
-    sems = pltpu.SemaphoreType.DMA((copies,))
-    flops = 2 * width * inner * height
-    specs = [IN_SMEM] + [IN_PLACE] * (3 + len(pieces))
-    if ending is None:
-        return kernel_call(
-            functools.partial(partial_kernel, kinds, len(pieces)),
-            "project_partial",
-            f32(height, width),
-            specs,
-            IN_VMEM,
-            [*held, sems],
-            flops=flops,
-        )(where, *rows, *pieces)
-    extra = [*(() if total is None else (total,)), *ending]
-    return kernel_call(
-        functools.partial(finish_kernel, kinds, len(pieces), total is not None),
+    height = sum(r.shape[0] for r in rows)
+    scratch = [] if staged else [pltpu.VMEM((height, inner), jnp.bfloat16)]
+    begin = staged or rows
+    return kernel_call(
+        functools.partial(finish_kernel, kinds, len(arrays), bool(staged), tokens),
         "project_finish",
-        [bf16(2 * tokens, width)] * 2,
-        specs + [IN_VMEM] * len(extra),
-        [IN_PLACE] * 2,
-        [*held, pltpu.VMEM((2, 2 * tokens, width), jnp.bfloat16), sems, pltpu.SemaphoreType.DMA((2,))],
-        flops=flops,
-    )(where, *rows, *pieces, *extra)
+        [bf16(2 * tokens, width), f32(8, width)],
+        [IN_SMEM] + [IN_VMEM if staged else IN_PLACE] * len(begin) + [IN_PLACE] * len(arrays) + [IN_VMEM] * len(ending),
+        [IN_PLACE, IN_VMEM],
+        [
+            *scratch,
+            pltpu.VMEM((inner, width), jnp.bfloat16),
+            pltpu.VMEM((2, tokens, width), jnp.bfloat16),
+            pltpu.SemaphoreType.DMA((copies,)),
+            pltpu.SemaphoreType.DMA((2,)),
+        ],
+        flops=2 * width * inner * height,
+    )(where, *begin, *arrays, *ending)
 
 
 def scores_of(query, key):
@@ -223,15 +254,13 @@
     top = jnp.broadcast_to(jnp.max(peak, -1, keepdims=True), peak.shape) * SCORE_SCALE
     if before is not None:
         top = jnp.maximum(top, before[0])
-    total = mixture = None
+    both = None
     for part, value in zip(tiles, values):
-        weights = [jnp.exp2(t * SCORE_SCALE - top) for t in part]
-        for weight in weights:
-            total = weight if total is None else total + weight
-        mixed = jnp.dot(
-            jnp.concatenate([w.astype(jnp.bfloat16) for w in weights], 1), value, preferred_element_type=jnp.float32
-        )
-        mixture = mixed if mixture is None else mixture + mixed
+        weights = jnp.concatenate([jnp.exp2(t * SCORE_SCALE - top).astype(jnp.bfloat16) for t in part], 1)
+        wide = jnp.concatenate([value, jnp.ones_like(value)], 1)
+        term = jnp.dot(weights, wide, preferred_element_type=jnp.float32)
+        both = term if both is None else both + term
+    mixture, total = both[:, :HEAD_DIM], both[:, HEAD_DIM:]
     if before is not None:
         rescale = jnp.exp2(before[0] - top)
         total = before[1] * rescale + total
@@ -259,31 +288,42 @@
     return slice(first, first + HEAD_DIM)
 
 
-def own_kernel(groups, where, q_a, q_b, clean_in, noisy_in, *refs):
-    *state, clean_ref, noisy_ref, sem = refs
+def own_kernel(groups, where, q_a, q_b, cos_ref, sin_ref, marks_a, marks_b, mask_ref, *refs):
+    clean_in, state, (clean_ref, noisy_ref, sem) = refs[0], refs[1:4], refs[4:]
     core = where[0]
     tokens = q_a.shape[0]
     heads = state[0].shape[0]
     run_copies(
         [
-            pltpu.make_async_copy(noisy_in, noisy_ref, sem.at[0]),
-            pltpu.make_async_copy(clean_in, clean_ref, sem.at[1]),
+            pltpu.make_async_copy(clean_in.at[i * tokens : (i + 1) * tokens, :], clean_ref.at[i], sem.at[i])
+            for i in range(2)
         ]
     )
-
-    def rows_of(side, ref, head, is_value):
-        return ref[side * tokens : (side + 1) * tokens, kv_lanes(groups, head, is_value)]
+    for side, marks in enumerate((marks_a, marks_b)):
+        mine = slice(side * tokens, (side + 1) * tokens)
+        masked = jnp.broadcast_to(marks[...].astype(jnp.float32), (HEAD_DIM, tokens)).T > 0.5
+        for head in range(heads // groups):
+            for is_value in range(2):
+                first = (is_value * (heads // groups) + head) * HEAD_DIM
+                token = jnp.broadcast_to(mask_ref[:1, first : first + HEAD_DIM], (tokens, HEAD_DIM))
+                if not is_value:
+                    token = rotated(token, cos_ref[mine, :], sin_ref[mine, :])
+                lanes = kv_lanes(groups, head * groups, is_value)
+                clean = clean_ref[side, :, lanes].astype(jnp.float32)
+                noisy_ref[side, :, lanes] = jnp.where(masked, token, clean).astype(jnp.bfloat16)
 
     def score(task):
         head, side = task
         query = query_of((q_a, q_b)[side], core, head)
-        near = scores_of(query, rows_of(side, noisy_ref, head, 0))
-        far = scores_of(query, rows_of(1 - side, clean_ref, head, 0))
+        lanes = kv_lanes(groups, head, 0)
+        near = scores_of(query, noisy_ref[side, :, lanes])
+        far = scores_of(query, clean_ref[1 - side, :, lanes])
         return [near, jnp.where(core == 1 - side, far, -1e30)]
 
     def use(task, scores):
         head, side = task
-        values = [rows_of(side, noisy_ref, head, 1), rows_of(1 - side, clean_ref, head, 1)]
+        lanes = kv_lanes(groups, head, 1)
+        values = [noisy_ref[side, :, lanes], clean_ref[1 - side, :, lanes]]
         mine = pl.ds(side * tokens, tokens)
         for ref, value in zip(state, absorb(scores, values, None)):
             ref[head, mine, :] = value
@@ -291,33 +331,28 @@
     pipelined([(head, side) for head in range(heads) for side in range(2)], score, use)
 
 
-def attend_own(where, queries, clean, noisy, heads, groups):
+def attend_own(where, queries, tables, marks, mask_sums, clean, heads, groups):
     tokens = queries[0].shape[0]
     return kernel_call(
         functools.partial(own_kernel, groups),
         "attend_own",
         [f32(heads, 2 * tokens, HEAD_DIM)] * 3,
-        [IN_SMEM] + [IN_VMEM] * 2 + [IN_PLACE] * 2,
+        [IN_SMEM] + [IN_VMEM] * 7 + [IN_PLACE],
         [IN_VMEM] * 3,
-        [pltpu.VMEM(clean.shape, jnp.bfloat16)] * 2 + [pltpu.SemaphoreType.DMA((2,))],
+        [pltpu.VMEM((2, tokens, clean.shape[1]), jnp.bfloat16)] * 2 + [pltpu.SemaphoreType.DMA((2,))],
         flops=16 * heads * tokens * tokens * HEAD_DIM,
-    )(where, *queries, clean, noisy)
+    )(where, *queries, *tables, *marks, mask_sums, clean)
 
 
 def later_tasks(core, heads, groups, q_a, q_b, parts, state, store):
-    tokens = q_a.shape[0]
-
-    def score(task):
-        head, side = task
-        query = query_of((q_a, q_b)[side], core, head)
+    def score(head):
+        query = jnp.concatenate([query_of(q, core, head) for q in (q_a, q_b)], 0)
         return [scores_of(query, part[:, kv_lanes(groups, head, 0)]) for part in parts]
 
-    def use(task, scores):
-        head, side = task
-        before = state(head, pl.ds(side * tokens, tokens))
-        store(head, side, absorb(scores, [part[:, kv_lanes(groups, head, 1)] for part in parts], before))
-
-    pipelined([(head, side) for head in heads for side in range(2)], score, use)
+    def use(head, scores):
+        store(head, absorb(scores, [part[:, kv_lanes(groups, head, 1)] for part in parts], state(head)))
+
+    pipelined(heads, score, use)
 
 
 def is_earlier(where, flip):
@@ -327,21 +362,21 @@
 def later_kernel(groups, flips, where, q_a, q_b, *refs):
     count = len(flips)
     parts, outs = refs[:count], refs[count + 3 :]
-    tokens = q_a.shape[0]
-
-    def state(head, mine):
-        return tuple(out[head, mine, :] for out in outs)
-
-    def store(head, side, values):
+
+    def state(head):
+        return tuple(out[head] for out in outs)
+
+    def store(head, values):
         for out, value in zip(outs, values):
-            out[head, pl.ds(side * tokens, tokens), :] = value
-
-    for chosen in range(1, 1 << count):
-        wanted = [bool(chosen >> number & 1) for number in range(count)]
-        hits = [is_earlier(where, flip) if want else ~is_earlier(where, flip) for flip, want in zip(flips, wanted)]
+            out[head] = value
+
+    chips = sorted(set(flips))
+    for chosen in range(1, 1 << len(chips)):
+        wanted = [flip for number, flip in enumerate(chips) if chosen >> number & 1]
+        hits = [is_earlier(where, flip) if flip in wanted else ~is_earlier(where, flip) for flip in chips]
 
         @pl.when(functools.reduce(jnp.logical_and, hits))
-        def _(used=[part for part, want in zip(parts, wanted) if want]):
+        def _(used=[part for part, flip in zip(parts, flips) if flip in wanted]):
             later_tasks(where[0], range(outs[0].shape[0]), groups, q_a, q_b, used, state, store)
 
 
@@ -364,14 +399,15 @@
     parts, state_refs, outs = refs[:count], refs[count : count + 3], refs[count + 3 :]
     tokens = q_a.shape[0]
 
-    def state(head, mine):
-        return tuple(ref[head, mine, :] for ref in state_refs)
-
-    def store(head, side, values):
+    def state(head):
+        return tuple(ref[head] for ref in state_refs)
+
+    def store(head, values):
         _, total, mixture = values
-        total = jnp.sum(total, -1, keepdims=True)
+        result = (mixture / total).astype(jnp.bfloat16)
         place = (head - heads[0]) * HEAD_DIM
-        outs[side][:, place : place + HEAD_DIM] = (mixture / total).astype(jnp.bfloat16)
+        for side, out in enumerate(outs):
+            out[:, place : place + HEAD_DIM] = result[side * tokens : (side + 1) * tokens]
 
     @pl.when(is_earlier(where, flip))
     def _():
@@ -380,8 +416,7 @@
     @pl.when(~is_earlier(where, flip))
     def _():
         for head in heads:
-            for side in range(2):
-                store(head, side, state(head, pl.ds(side * tokens, tokens)))
+            store(head, state(head))
 
 
 def attend_last(where, queries, parts, flip, running, heads, groups):
@@ -459,7 +494,10 @@
     query_own = queries[0]
     if square:
         quarter = depth // chips
-        (mine,) = cut_weights(where, (0,), quarter, w_key, w_value)
+        half = kv_width // 2
+        mine = jnp.concatenate(
+            [lax.dynamic_slice(w, (chip * quarter, core * half), (quarter, half)) for w in (w_key, w_value)], 1
+        )
         far, near = to_shard(mine, 3), to_shard(mine, 1)
 
     mask_rows = jnp.broadcast_to(mask_embed[None, :], (MASK_ROWS, mask_embed.shape[0]))
@@ -478,8 +516,8 @@
         near_x, far_x = to_chip(near, 1), to_chip(far, 1)
         near_y, far_y = to_chip(near, 2), to_chip(far, 2)
         middle, corner, near_x, near_y, far_x, far_y = barrier((middle, corner, near_x, near_y, far_x, far_y))
+        far_corner, near_corner = to_shard(corner, 3), to_shard(corner, 1)
         last = [to_chip(middle, flip) for flip in (3, 1, 2)]
-        far_corner, near_corner = to_shard(corner, 3), to_shard(corner, 1)
         segments = [
             [((w_key, w_value), 0, None, depth)],
             [
@@ -499,29 +537,29 @@
                 (far_corner, 3, 3, depth),
             ]
         ]
-        total = project(rows, segments, where)
+        staged = project_partial(rows, segments, final, where)
     else:
         (half_weights,) = cut_weights(where, (None,), depth, w_key, w_value)
         gathered = lax.all_gather(half_weights, "fsdp", axis=0, tiled=True)
-        final, total = [[(gathered, None, None, depth)]], None
-    clean, noisy = project(rows, final, where, total, (cosine, sine, *both_marks))
+        final, staged = [[(gathered, None, None, depth)]], ()
+    tables = (cosine, sine)
+    clean, mask_sums = project_finish(rows, staged, final, where, tables)
 
     heads = query_own.shape[1] // 2 // HEAD_DIM
     groups = heads // kv_heads
     if square:
-        along_x = to_chip(clean, 1, (0, 1, 2))
-        along_y = to_chip(clean, 2, (0, 1))
-        running = attend_own(where, query_rows, clean, noisy, heads, groups)
+        along_x, along_y = to_chip(clean, 1, (0, 1, 2)), to_chip(clean, 2, (0, 1))
+        running = attend_own(where, query_rows, tables, both_marks, mask_sums, clean, heads, groups)
         along_x, along_y, running = barrier((along_x, along_y, running))
         last_parts = [to_chip(along_x[:tokens], 2, (0, 1)), to_chip(along_y[tokens:], 1, (2, 3))]
         running = attend_later(where, query_rows, [along_x, along_y], (1, 2), running, groups)
     else:
-        running = attend_own(where, query_rows, clean, noisy, heads, groups)
+        running = attend_own(where, query_rows, tables, both_marks, mask_sums, clean, heads, groups)
         for flip in range(1, chips):
-            part = to_chip(clean, flip, [s for s in range(chips) if s < s ^ flip])
+            parts = [to_chip(clean, flip, [s for s in range(chips) if s < s ^ flip])]
             if flip < chips - 1:
-                running = attend_later(where, query_rows, [part], (flip,), running, groups)
-        last_parts = [part]
+                running = attend_later(where, query_rows, parts, (flip,), running, groups)
+        last_parts = parts
     kept, received = [], []
     for first in range(0, heads, groups):
         own, other = attend_last(

time: 86.8 us -> 85.4 us (0.984)
  waiting for transfers between devices: 33.5 us -> 28.9 us
  local copies, waits for them, and re-layouts: 0.1 us -> 3.5 us
  Pallas kernels: 28.1 us -> 25.3 us
  other arithmetic: 1.9 us -> 4.58 us
    ppermute x5, waiting for transfers between devices: 23.4 us -> 19.1 us  [to_shard(): lax.ppermute(array, 'fsdp', [(s, s ^ flip) for s in range(fsdp_size)])]
    pallas_call x2 -> x1, Pallas kernels: 4.83 us -> 2.47 us  [cut_weights(): kernel_call(functools.partial(cut_kernel, flips), 'cut_weights', [bf16(si...]
    dynamic_slice x0 -> x2, local copies, waits for them, and re-layouts: none -> 1.84 us  [shards(): lax.dynamic_slice(w, (chip * quarter, core * half), (quarter, half))]
    unnamed x16 -> x14, local copies, waits for them, and re-layouts: 0.05 us -> 1.62 us
    concatenate x1, other arithmetic: 0.14 us -> 1.29 us  [rotation(): jnp.concatenate([-sine, sine], -1)]
  transfers between devices with their start and end apart: 21 -> 21, of which waited for: 6 -> 6; matrix products, arithmetic and copies ran while one was open for 2% -> 8% of each run, Pallas kernels for 25% -> 23%
where the time goes in v5:
time: 85.4 us; the launch traced here: 85.1 us
  waiting for transfers between devices  28.9 us (34%)
  Pallas kernels  25.3 us (30%)
  starting transfers between devices  22.4 us (26%)
  other arithmetic  4.58 us (5%)
  local copies, waits for them, and re-layouts  3.5 us (4%)
    ppermute x5, waiting for transfers between devices, to_shard(): lax.ppermute(array, 'fsdp', [(s, s ^ flip) for s in range(fsdp_size)])  19.1 us
    ppermute x11, starting transfers between devices, to_chip(): return lax.ppermute(array, 'seq', pairs)  11.4 us
    ppermute x11, waiting for transfers between devices, to_chip(): return lax.ppermute(array, 'seq', pairs)  8.32 us
    pallas_call x1, Pallas kernels, attend_later(): kernel_call(functools.partial(later_kernel, groups, flips), 'attend_later...  6.57 us
    ppermute x5, starting transfers between devices, to_shard(): lax.ppermute(array, 'fsdp', [(s, s ^ flip) for s in range(fsdp_size)])  6.42 us
    pallas_call x2, Pallas kernels, attend_last(): kernel_call(functools.partial(last_kernel, heads, groups, count, flip), '...  4.68 us
    ppermute x5, starting transfers between devices, swap_cores(): return lax.ppermute(array, 'seq', [(s, s ^ 1) for s in range(seq_size)])  4.63 us
    pallas_call x1, Pallas kernels, project_partial(): kernel_call(functools.partial(partial_kernel, kinds, final_kinds, len(arr...  3.98 us
  transfers between devices with their start and end apart: 21, of which 6 were waited for; matrix products, arithmetic and copies ran while one was open for 8% of the time, Pallas kernels for 23%

profile of v5, /device:TPU:7, one launch (start us, length us, event | category | flops | bytes accessed | tf_op | source)
XLA Modules:
  0.0 85.1 jit_solution(12598796401655250477)
XLA Ops:
  0.0 0.7 collective-permute-start.2
  0.7 0.0 collective-permute-start.3
  0.7 0.9 %dynamic_slice.6 = bf16[256,256]{1,0:T(8,128)(2,1)S(1)} dynamic-slice(bf16[1024,512]{1,0:T(8,128)(2,1)} %refs_0_.1, s32[]{:T(128)S(6)} %select_n.14, s32[]{:T(128)S(6)} %select_n.15), dynamic_slice_sizes={256,256} | dynamic-slice | bytes 262148 | tf_op jit(solution)/shard_map/dynamic_slice | solution.py:499
  1.6 0.9 %dynamic_slice.7 = bf16[256,256]{1,0:T(8,128)(2,1)S(1)} dynamic-slice(bf16[1024,512]{1,0:T(8,128)(2,1)} %refs_1_.1, s32[]{:T(128)S(6)} %select_n.14, s32[]{:T(128)S(6)} %select_n.15), dynamic_slice_sizes={256,256} | dynamic-slice | bytes 262148 | tf_op jit(solution)/shard_map/dynamic_slice | solution.py:499
  2.5 0.7 pad_maximum_fusion
  3.2 1.3 %collective-permute-start.1 = (bf16[256,512]{1,0:T(8,128)(2,1)}, bf16[256,512]{1,0:T(8,128)(2,1)}, u32[]{:S(2)}, u32[]{:S(2)}) collective-permute-start(bf16[256,512]{1,0:T(8,128)(2,1)} %pad_maximum_fusion), channel_id=1, source_target_pairs={{0,1},{1,0},{2,3},{3,2},{4,5},{5,4},{6,7},{7,6},{8,9},{9,8},{10,11... | collective-permute-start | bytes 786440 | tf_op jit(solution)/shard_map/ppermute | solution.py:489
  4.5 2.2 %collective-permute-start = (bf16[256,512]{1,0:T(8,128)(2,1)}, bf16[256,512]{1,0:T(8,128)(2,1)}, u32[]{:S(2)}, u32[]{:S(2)}) collective-permute-start(bf16[256,512]{1,0:T(8,128)(2,1)} %pad_maximum_fusion), channel_id=1, source_target_pairs={{0,3},{1,2},{2,1},{3,0},{4,7},{5,6},{6,5},{7,4},{8,11},{9,10},{10,... | collective-permute-start | bytes 786440 | tf_op jit(solution)/shard_map/ppermute | solution.py:489
  6.7 1.1 %collective-permute-start.4 = (s32[1,256]{1,0:T(1,128)}, s32[1,256]{1,0:T(1,128)S(1)}, u32[]{:S(2)}, u32[]{:S(2)}) collective-permute-start(s32[1,256]{1,0:T(1,128)} %marks_a), channel_id=1, source_target_pairs={{0,4},{4,0},{8,12},{12,8},{16,20},{20,16},{24,28},{28,24},{1,5},{5... | collective-permute-start | bytes 3080 | tf_op jit(solution)/shard_map/ppermute | solution.py:481
  7.8 0.0 copy-start.6
  7.8 1.8 %fusion = (f32[512,64]{1,0:T(8,128)}, f32[512,64]{1,0:T(8,128)}, f32[512,64]{1,0:T(8,128)S(1)}) fusion(f32[64]{0:T(128)S(1)} %negate_power_fusion, f32[512]{0:T(512)S(1)} %add_convert_fusion), kind=kLoop, calls=%fused_computation.5 | loop fusion | flops 65536 | bytes 395520 | tf_op jit(solution)/shard_map/neg | solution.py:54
  9.7 0.1 pad_maximum_fusion.1.refs_8_.cos_ref
  9.8 1.3 %pad_maximum_fusion.2.refs_9_.sin_ref = f32[512,128]{1,0:T(8,128)S(1)} fusion(f32[512,64]{1,0:T(8,128)} %get-tuple-element.82, f32[512,64]{1,0:T(8,128)} %get-tuple-element.81), kind=kLoop, calls=%fused_computation.4 | loop fusion | flops 65536 | bytes 524288 | tf_op jit(solution)/shard_map/concatenate | solution.py:54
  11.1 0.6 pad_add_fusion.where
  11.7 2.5 %cut_weights.1 = bf16[256,512]{1,0:T(8,128)(2,1)} custom-call(s32[3]{0:T(128)} %pad_add_fusion.where, bf16[1024,512]{1,0:T(8,128)(2,1)} %refs_0_.1, bf16[1024,512]{1,0:T(8,128)(2,1)} %refs_1_.1), custom_call_target="tpu_custom_call" | custom-call | tf_op jit(solution)/shard_map/cut_weights/pallas_call | solution.py:83
  14.2 0.0 collective-permute-done.4.marks_b
  14.2 0.0 collective-permute-done.1.refs_5_
  14.2 4.4 %collective-permute-done.refs_2_ = bf16[256,512]{1,0:T(8,128)(2,1)} collective-permute-done((bf16[256,512]{1,0:T(8,128)(2,1)}, bf16[256,512]{1,0:T(8,128)(2,1)}, u32[]{:S(2)}, u32[]{:S(2)}) %collective-permute-start) | collective-permute-done | bytes 262176 | tf_op jit(solution)/shard_map/ppermute | solution.py:489
  18.6 0.0 collective-permute-done.3.q_b
  18.6 0.0 collective-permute-done.2.other
  18.6 0.0 copy-done.6
  18.6 1.3 %collective-permute-start.5 = (bf16[256,512]{1,0:T(8,128)(2,1)}, bf16[256,512]{1,0:T(8,128)(2,1)S(1)}, u32[]{:S(2)}, u32[]{:S(2)}) collective-permute-start(bf16[256,512]{1,0:T(8,128)(2,1)} %pad_maximum_fusion), channel_id=1, source_target_pairs={{0,2},{1,3},{2,0},{3,1},{4,6},{5,7},{6,4},{7,5},{8,10},{9,11},{10,... | collective-permute-start | bytes 786440 | tf_op jit(solution)/shard_map/ppermute | solution.py:489
  19.9 0.2 collective-permute-start.9
  20.2 0.3 collective-permute-start.8
  20.4 1.2 %collective-permute-start.7 = (bf16[256,512]{1,0:T(8,128)(2,1)}, bf16[256,512]{1,0:T(8,128)(2,1)S(1)}, u32[]{:S(2)}, u32[]{:S(2)}) collective-permute-start(bf16[256,512]{1,0:T(8,128)(2,1)} %collective-permute-done.1.refs_5_), channel_id=1, source_target_pairs={{0,16},{4,20},{8,24},{12,28},{16,0},{20,4},{24,8},{28,12},{1,17},{... | collective-permute-start | bytes 786440 | tf_op jit(solution)/shard_map/ppermute | solution.py:486
  21.6 1.2 %collective-permute-start.6 = (bf16[256,512]{1,0:T(8,128)(2,1)}, bf16[256,512]{1,0:T(8,128)(2,1)S(1)}, u32[]{:S(2)}, u32[]{:S(2)}) collective-permute-start(bf16[256,512]{1,0:T(8,128)(2,1)} %collective-permute-done.1.refs_5_), channel_id=1, source_target_pairs={{0,8},{4,12},{8,0},{12,4},{16,24},{20,28},{24,16},{28,20},{1,9},{5... | collective-permute-start | bytes 786440 | tf_op jit(solution)/shard_map/ppermute | solution.py:486
  22.9 9.2 %collective-permute-done.5.refs_2_ = bf16[256,512]{1,0:T(8,128)(2,1)S(1)} collective-permute-done((bf16[256,512]{1,0:T(8,128)(2,1)}, bf16[256,512]{1,0:T(8,128)(2,1)S(1)}, u32[]{:S(2)}, u32[]{:S(2)}) %collective-permute-start.5) | collective-permute-done | bytes 262176 | tf_op jit(solution)/shard_map/ppermute | solution.py:489
  32.0 0.0 collective-permute-done.9.refs_4_
  32.0 0.0 collective-permute-done.8.refs_3_
  32.0 0.0 collective-permute-done.7.refs_7_
  32.0 0.0 collective-permute-done.6.refs_6_
  32.1 1.6 %collective-permute-start.14 = (bf16[256,512]{1,0:T(8,128)(2,1)}, bf16[256,512]{1,0:T(8,128)(2,1)S(1)}, u32[]{:S(2)}, u32[]{:S(2)}) collective-permute-start(bf16[256,512]{1,0:T(8,128)(2,1)} %cut_weights.1), channel_id=1, source_target_pairs={{0,3},{1,2},{2,1},{3,0},{4,7},{5,6},{6,5},{7,4},{8,11},{9,10},{10,... | collective-permute-start | bytes 786440 | tf_op jit(solution)/shard_map/ppermute | solution.py:489
  33.7 0.0 collective-permute-start.13
  33.7 0.8 collective-permute-start.12
  34.5 0.3 collective-permute-start.11
  34.7 1.6 %collective-permute-start.10 = (bf16[256,512]{1,0:T(8,128)(2,1)S(1)}, bf16[256,512]{1,0:T(8,128)(2,1)S(1)}, u32[]{:S(2)}, u32[]{:S(2)}) collective-permute-start(bf16[256,512]{1,0:T(8,128)(2,1)S(1)} %collective-permute-done.5.refs_2_), channel_id=1, source_target_pairs={{0,24},{4,28},{8,16},{12,20},{16,8},{20,12},{24,0},{28,4},{1,25},{... | collective-permute-start | bytes 786440 | tf_op jit(solution)/shard_map/ppermute | solution.py:486
  36.4 0.0 copy-done.1
  36.4 0.0 copy-done.2
  36.4 1.6 %copy-done.3 = bf16[1,256,4096]{2,1,0:T(8,128)(2,1)S(1)} copy-done((bf16[1,256,4096]{2,1,0:T(8,128)(2,1)S(1)}, bf16[1,256,4096]{2,1,0:T(8,128)(2,1)}, u32[]{:S(2)}) %copy-start.3) | copy-done | bytes 2097176
  38.0 4.0 %project_partial.1 = (f32[528,512]{1,0:T(8,128)S(1)}, bf16[528,1536]{1,0:T(8,128)(2,1)S(1)}) custom-call(s32[3]{0:T(128)S(1)} %copy-done.4, bf16[256,4096]{1,0:T(8,128)(2,1)S(1)} %bitcast.12, bf16[256,4096]{1,0:T(8,128)(2,1)} %collective-permute-done.2.other, bf16[16,4096]{1,0:T(8,128)(2,1)S(1)} %broadcast_in_dim.4.masks, bf16[1024,512]{1,0:T(8,128)(2,1)S(1)} %copy-done.1, ...), custom_call_target="tpu_custom_call" | custom-call | flops 1384120320 | tf_op jit(solution)/shard_map/project_partial/pallas_call | solution.py:203
  41.9 0.0 collective-permute-done.14.refs_7_
  42.0 5.5 %collective-permute-done.13.refs_6_ = bf16[256,512]{1,0:T(8,128)(2,1)S(1)} collective-permute-done((bf16[256,512]{1,0:T(8,128)(2,1)}, bf16[256,512]{1,0:T(8,128)(2,1)S(1)}, u32[]{:S(2)}, u32[]{:S(2)}) %collective-permute-start.13) | collective-permute-done | bytes 262176 | tf_op jit(solution)/shard_map/ppermute | solution.py:489
  47.4 0.0 collective-permute-done.12.refs_5_
  47.4 0.0 collective-permute-done.11.refs_4_
  47.4 0.0 collective-permute-done.10.refs_3_
  47.4 0.0 copy-start
  47.4 0.0 copy-start.5
  47.5 2.2 %project_finish.1 = (bf16[512,512]{1,0:T(8,128)(2,1)S(1)}, f32[8,512]{1,0:T(8,128)S(1)}) custom-call(s32[3]{0:T(128)S(1)} %copy-done.4, f32[528,512]{1,0:T(8,128)S(1)} %get-tuple-element.56.refs_0_, bf16[528,1536]{1,0:T(8,128)(2,1)S(1)} %get-tuple-element.57.refs_1_, bf16[256,512]{1,0:T(8,128)(2,1)S(1)} %collective-permute-done.5.refs_2_, ...), custom_call_target="tpu_custom_call" | custom-call | flops 830472192 | tf_op jit(solution)/shard_map/project_finish/pallas_call | solution.py:226
  49.6 1.3 %collective-permute-start.16 = (bf16[512,512]{1,0:T(8,128)(2,1)S(1)}, bf16[512,512]{1,0:T(8,128)(2,1)S(1)}, u32[]{:S(2)}, u32[]{:S(2)}) collective-permute-start(bf16[512,512]{1,0:T(8,128)(2,1)S(1)} %get-tuple-element.62.refs_0_), channel_id=1, source_target_pairs={{0,16},{4,20},{8,24},{12,28},{1,17},{5,21},{9,25},{13,29},{2,18},{... | collective-permute-start | bytes 1572872 | tf_op jit(solution)/shard_map/ppermute | solution.py:486
  50.9 1.3 %collective-permute-start.15 = (bf16[512,512]{1,0:T(8,128)(2,1)S(1)}, bf16[512,512]{1,0:T(8,128)(2,1)S(1)}, u32[]{:S(2)}, u32[]{:S(2)}) collective-permute-start(bf16[512,512]{1,0:T(8,128)(2,1)S(1)} %get-tuple-element.62.refs_0_), channel_id=1, source_target_pairs={{0,8},{4,12},{8,0},{12,4},{16,24},{20,28},{1,9},{5,13},{9,1},{13,5... | collective-permute-start | bytes 1572872 | tf_op jit(solution)/shard_map/ppermute | solution.py:486
  52.2 3.9 %attend_own.1 = (f32[8,512,128]{2,1,0:T(8,128)S(1)}, f32[8,512,128]{2,1,0:T(8,128)S(1)}, f32[8,512,128]{2,1,0:T(8,128)S(1)}) custom-call(s32[3]{0:T(128)S(1)} %copy-done.4, bf16[256,2048]{1,0:T(8,128)(2,1)S(1)} %bitcast.7, bf16[256,2048]{1,0:T(8,128)(2,1)S(1)} %collective-permute-done.3.q_b, f32[512,128]{1,0:T(8,128)S(1)} %pad_maximum_fusion.1.refs_8_.cos_ref, ...), custom_call_target="tpu_custom_call" | custom-call | flops 1073741824 | tf_op jit(solution)/shard_map/attend_own/pallas_call | solution.py:336
  56.1 7.0 %collective-permute-done.16.refs_1_ = bf16[512,512]{1,0:T(8,128)(2,1)S(1)} collective-permute-done((bf16[512,512]{1,0:T(8,128)(2,1)S(1)}, bf16[512,512]{1,0:T(8,128)(2,1)S(1)}, u32[]{:S(2)}, u32[]{:S(2)}) %collective-permute-start.16) | collective-permute-done | bytes 524320 | tf_op jit(solution)/shard_map/ppermute | solution.py:486
  63.1 1.3 %collective-permute-done.15.refs_0_ = bf16[512,512]{1,0:T(8,128)(2,1)S(1)} collective-permute-done((bf16[512,512]{1,0:T(8,128)(2,1)S(1)}, bf16[512,512]{1,0:T(8,128)(2,1)S(1)}, u32[]{:S(2)}, u32[]{:S(2)}) %collective-permute-start.15) | collective-permute-done | bytes 524320 | tf_op jit(solution)/shard_map/ppermute | solution.py:486
  64.5 1.3 %collective-permute-start.17 = (bf16[256,512]{1,0:T(8,128)(2,1)S(1)}, bf16[256,512]{1,0:T(8,128)(2,1)S(1)}, u32[]{:S(2)}, u32[]{:S(2)}) collective-permute-start(bf16[256,512]{1,0:T(8,128)(2,1)S(1)} %slice.6), channel_id=1, source_target_pairs={{0,16},{4,20},{8,24},{12,28},{1,17},{5,21},{9,25},{13,29},{2,18},{... | collective-permute-start | bytes 786440 | tf_op jit(solution)/shard_map/ppermute | solution.py:486
  65.8 1.9 %collective-permute-start.18 = (bf16[256,512]{1,0:T(8,128)(2,1)S(1)}, bf16[256,512]{1,0:T(8,128)(2,1)S(1)}, u32[]{:S(2)}, u32[]{:S(2)}) collective-permute-start(bf16[256,512]{1,0:T(8,128)(2,1)S(1)} %slice.7), channel_id=1, source_target_pairs={{16,24},{20,28},{24,16},{28,20},{17,25},{21,29},{25,17},{29,21},{1... | collective-permute-start | bytes 786440 | tf_op jit(solution)/shard_map/ppermute | solution.py:486
  67.7 6.6 %attend_later.1 = (f32[8,512,128]{2,1,0:T(8,128)S(1)}, f32[8,512,128]{2,1,0:T(8,128)S(1)}, f32[8,512,128]{2,1,0:T(8,128)S(1)}) custom-call(s32[3]{0:T(128)S(1)} %copy-done.4, bf16[256,2048]{1,0:T(8,128)(2,1)S(1)} %bitcast.8, bf16[256,2048]{1,0:T(8,128)(2,1)S(1)} %collective-permute-done.3.q_b, ...), custom_call_target="tpu_custom_call", output_to_operand_aliasing={{0}: (5, {}), {1}: (6, {}), {2}: (7, {})} | custom-call | flops 2147483648 | tf_op jit(solution)/shard_map/attend_later/pallas_call | solution.py:387
  74.3 0.0 collective-permute-done.17.refs_0_
  74.3 0.0 collective-permute-done.18.refs_1_
  74.3 2.3 %attend_last.3 = (bf16[256,512]{1,0:T(8,128)(2,1)S(1)}, bf16[256,512]{1,0:T(8,128)(2,1)S(1)}) custom-call(s32[3]{0:T(128)S(1)} %copy-done.4, bf16[256,2048]{1,0:T(8,128)(2,1)S(1)} %bitcast.9, bf16[256,2048]{1,0:T(8,128)(2,1)S(1)} %collective-permute-done.3.q_b, bf16[256,512]{1,0:T(8,128)(2,1)S(1)} %collective-permute-done.17.refs_0_, ...), custom_call_target="tpu_custom_call" | custom-call | flops 536870912 | tf_op jit(solution)/shard_map/attend_last/pallas_call | solution.py:425
  76.6 2.8 %collective-permute-start.20 = (bf16[256,512]{1,0:T(8,128)(2,1)S(1)}, bf16[256,512]{1,0:T(8,128)(2,1)S(1)}, u32[]{:S(2)}, u32[]{:S(2)}) collective-permute-start(bf16[256,512]{1,0:T(8,128)(2,1)S(1)} %get-tuple-element.80), channel_id=1, source_target_pairs={{0,4},{4,0},{8,12},{12,8},{16,20},{20,16},{24,28},{28,24},{1,5},{5... | collective-permute-start | bytes 786440 | tf_op jit(solution)/shard_map/ppermute | solution.py:481
  79.4 2.3 %attend_last.2 = (bf16[256,512]{1,0:T(8,128)(2,1)S(1)}, bf16[256,512]{1,0:T(8,128)(2,1)S(1)}) custom-call(s32[3]{0:T(128)S(1)} %copy-done.4, bf16[256,2048]{1,0:T(8,128)(2,1)S(1)} %bitcast.10, bf16[256,2048]{1,0:T(8,128)(2,1)S(1)} %collective-permute-done.3.q_b, bf16[256,512]{1,0:T(8,128)(2,1)S(1)} %collective-permute-done.17.refs_0_, ...), custom_call_target="tpu_custom_call" | custom-call | flops 536870912 | tf_op jit(solution)/shard_map/attend_last/pallas_call | solution.py:425
  81.8 0.1 collective-permute-start.19
  81.9 0.0 collective-permute-done.20.refs_3_
  81.9 1.5 %collective-permute-done.19.refs_2_ = bf16[256,512]{1,0:T(8,128)(2,1)S(1)} collective-permute-done((bf16[256,512]{1,0:T(8,128)(2,1)S(1)}, bf16[256,512]{1,0:T(8,128)(2,1)S(1)}, u32[]{:S(2)}, u32[]{:S(2)}) %collective-permute-start.19) | collective-permute-done | bytes 262176 | tf_op jit(solution)/shard_map/ppermute | solution.py:481
  83.4 1.5 %place_heads.1 = bf16[256,2048]{1,0:T(8,128)(2,1)} custom-call(s32[3]{0:T(128)S(1)} %copy-done.4, bf16[256,512]{1,0:T(8,128)(2,1)S(1)} %get-tuple-element.77.refs_0_, bf16[256,512]{1,0:T(8,128)(2,1)S(1)} %get-tuple-element.78.refs_1_, bf16[256,512]{1,0:T(8,128)(2,1)S(1)} %collective-permute-done.19.refs_2_, bf16[256,512]{1,0:T(8,128)(2,1)S(1)} %collective-permute-done.20.refs_3_), custom_call_target="tpu_custom_call" | custom-call | tf_op jit(solution)/shard_map/place_heads/pallas_call | solution.py:454
  (13 shorter events, 0.1 us)
Async XLA Ops:
  0.0 18.6 %collective-permute-start.2 = (bf16[256,4096]{1,0:T(8,128)(2,1)}, bf16[256,4096]{1,0:T(8,128)(2,1)}, u32[]{:S(2)}, u32[]{:S(2)}) collective-permute-start(bf16[256,4096]{1,0:T(8,128)(2,1)} %bitcast.11), channel_id=1, source_target_pairs={{0,4},{4,0},{8,12},{12,8},{16,20},{20,16},{24,28},{28,24},{1,5},{5... | collective-permute-start | bytes 6291464 | tf_op jit(solution)/shard_map/ppermute | solution.py:481
  0.7 17.9 %collective-permute-start.3 = (bf16[256,2048]{1,0:T(8,128)(2,1)}, bf16[256,2048]{1,0:T(8,128)(2,1)S(1)}, u32[]{:S(2)}, u32[]{:S(2)}) collective-permute-start(bf16[256,2048]{1,0:T(8,128)(2,1)} %bitcast.6), channel_id=1, source_target_pairs={{0,4},{4,0},{8,12},{12,8},{16,20},{20,16},{24,28},{28,24},{1,5},{5... | collective-permute-start | bytes 3145736 | tf_op jit(solution)/shard_map/ppermute | solution.py:481
  3.2 10.9 %collective-permute-start.1 = (bf16[256,512]{1,0:T(8,128)(2,1)}, bf16[256,512]{1,0:T(8,128)(2,1)}, u32[]{:S(2)}, u32[]{:S(2)}) collective-permute-start(bf16[256,512]{1,0:T(8,128)(2,1)} %pad_maximum_fusion), channel_id=1, source_target_pairs={{0,1},{1,0},{2,3},{3,2},{4,5},{5,4},{6,7},{7,6},{8,9},{9,8},{10,11... | collective-permute-start | bytes 786440 | tf_op jit(solution)/shard_map/ppermute | solution.py:489
  4.5 14.1 %collective-permute-start = (bf16[256,512]{1,0:T(8,128)(2,1)}, bf16[256,512]{1,0:T(8,128)(2,1)}, u32[]{:S(2)}, u32[]{:S(2)}) collective-permute-start(bf16[256,512]{1,0:T(8,128)(2,1)} %pad_maximum_fusion), channel_id=1, source_target_pairs={{0,3},{1,2},{2,1},{3,0},{4,7},{5,6},{6,5},{7,4},{8,11},{9,10},{10,... | collective-permute-start | bytes 786440 | tf_op jit(solution)/shard_map/ppermute | solution.py:489
  6.7 7.4 %collective-permute-start.4 = (s32[1,256]{1,0:T(1,128)}, s32[1,256]{1,0:T(1,128)S(1)}, u32[]{:S(2)}, u32[]{:S(2)}) collective-permute-start(s32[1,256]{1,0:T(1,128)} %marks_a), channel_id=1, source_target_pairs={{0,4},{4,0},{8,12},{12,8},{16,20},{20,16},{24,28},{28,24},{1,5},{5... | collective-permute-start | bytes 3080 | tf_op jit(solution)/shard_map/ppermute | solution.py:481
  7.8 10.8 %copy-start.6 = (bf16[4096]{0:T(1024)(128)(2,1)S(1)}, bf16[4096]{0:T(1024)(128)(2,1)}, u32[]{:S(2)}) copy-start(bf16[4096]{0:T(1024)(128)(2,1)} %param.8) | copy-start | bytes 24580
  9.7 26.7 %copy-start.1 = (bf16[1024,512]{1,0:T(8,128)(2,1)S(1)}, bf16[1024,512]{1,0:T(8,128)(2,1)}, u32[]{:S(2)}) copy-start(bf16[1024,512]{1,0:T(8,128)(2,1)} %refs_0_.1) | copy-start | bytes 3145732
  9.7 26.7 %copy-start.2 = (bf16[1024,512]{1,0:T(8,128)(2,1)S(1)}, bf16[1024,512]{1,0:T(8,128)(2,1)}, u32[]{:S(2)}) copy-start(bf16[1024,512]{1,0:T(8,128)(2,1)} %refs_1_.1) | copy-start | bytes 3145732
  11.7 24.7 %copy-start.4 = (s32[3]{0:T(128)S(1)}, s32[3]{0:T(128)}, u32[]{:S(2)}) copy-start(s32[3]{0:T(128)} %pad_add_fusion.where) | copy-start | bytes 40
  18.6 13.4 %collective-permute-start.5 = (bf16[256,512]{1,0:T(8,128)(2,1)}, bf16[256,512]{1,0:T(8,128)(2,1)S(1)}, u32[]{:S(2)}, u32[]{:S(2)}) collective-permute-start(bf16[256,512]{1,0:T(8,128)(2,1)} %pad_maximum_fusion), channel_id=1, source_target_pairs={{0,2},{1,3},{2,0},{3,1},{4,6},{5,7},{6,4},{7,5},{8,10},{9,11},{10,... | collective-permute-start | bytes 786440 | tf_op jit(solution)/shard_map/ppermute | solution.py:489
  19.9 12.1 %collective-permute-start.9 = (bf16[256,512]{1,0:T(8,128)(2,1)}, bf16[256,512]{1,0:T(8,128)(2,1)S(1)}, u32[]{:S(2)}, u32[]{:S(2)}) collective-permute-start(bf16[256,512]{1,0:T(8,128)(2,1)} %collective-permute-done.refs_2_), channel_id=1, source_target_pairs={{0,16},{4,20},{8,24},{12,28},{16,0},{20,4},{24,8},{28,12},{1,17},{... | collective-permute-start | bytes 786440 | tf_op jit(solution)/shard_map/ppermute | solution.py:486
  20.2 11.9 %collective-permute-start.8 = (bf16[256,512]{1,0:T(8,128)(2,1)}, bf16[256,512]{1,0:T(8,128)(2,1)S(1)}, u32[]{:S(2)}, u32[]{:S(2)}) collective-permute-start(bf16[256,512]{1,0:T(8,128)(2,1)} %collective-permute-done.refs_2_), channel_id=1, source_target_pairs={{0,8},{4,12},{8,0},{12,4},{16,24},{20,28},{24,16},{28,20},{1,9},{5... | collective-permute-start | bytes 786440 | tf_op jit(solution)/shard_map/ppermute | solution.py:486
  20.4 11.6 %collective-permute-start.7 = (bf16[256,512]{1,0:T(8,128)(2,1)}, bf16[256,512]{1,0:T(8,128)(2,1)S(1)}, u32[]{:S(2)}, u32[]{:S(2)}) collective-permute-start(bf16[256,512]{1,0:T(8,128)(2,1)} %collective-permute-done.1.refs_5_), channel_id=1, source_target_pairs={{0,16},{4,20},{8,24},{12,28},{16,0},{20,4},{24,8},{28,12},{1,17},{... | collective-permute-start | bytes 786440 | tf_op jit(solution)/shard_map/ppermute | solution.py:486
  21.6 10.4 %collective-permute-start.6 = (bf16[256,512]{1,0:T(8,128)(2,1)}, bf16[256,512]{1,0:T(8,128)(2,1)S(1)}, u32[]{:S(2)}, u32[]{:S(2)}) collective-permute-start(bf16[256,512]{1,0:T(8,128)(2,1)} %collective-permute-done.1.refs_5_), channel_id=1, source_target_pairs={{0,8},{4,12},{8,0},{12,4},{16,24},{20,28},{24,16},{28,20},{1,9},{5... | collective-permute-start | bytes 786440 | tf_op jit(solution)/shard_map/ppermute | solution.py:486
  32.1 9.9 %collective-permute-start.14 = (bf16[256,512]{1,0:T(8,128)(2,1)}, bf16[256,512]{1,0:T(8,128)(2,1)S(1)}, u32[]{:S(2)}, u32[]{:S(2)}) collective-permute-start(bf16[256,512]{1,0:T(8,128)(2,1)} %cut_weights.1), channel_id=1, source_target_pairs={{0,3},{1,2},{2,1},{3,0},{4,7},{5,6},{6,5},{7,4},{8,11},{9,10},{10,... | collective-permute-start | bytes 786440 | tf_op jit(solution)/shard_map/ppermute | solution.py:489
  33.7 13.7 %collective-permute-start.13 = (bf16[256,512]{1,0:T(8,128)(2,1)}, bf16[256,512]{1,0:T(8,128)(2,1)S(1)}, u32[]{:S(2)}, u32[]{:S(2)}) collective-permute-start(bf16[256,512]{1,0:T(8,128)(2,1)} %cut_weights.1), channel_id=1, source_target_pairs={{0,1},{1,0},{2,3},{3,2},{4,5},{5,4},{6,7},{7,6},{8,9},{9,8},{10,11... | collective-permute-start | bytes 786440 | tf_op jit(solution)/shard_map/ppermute | solution.py:489
  33.7 13.7 %collective-permute-start.12 = (bf16[256,512]{1,0:T(8,128)(2,1)S(1)}, bf16[256,512]{1,0:T(8,128)(2,1)S(1)}, u32[]{:S(2)}, u32[]{:S(2)}) collective-permute-start(bf16[256,512]{1,0:T(8,128)(2,1)S(1)} %collective-permute-done.5.refs_2_), channel_id=1, source_target_pairs={{0,16},{4,20},{8,24},{12,28},{16,0},{20,4},{24,8},{28,12},{1,17},{... | collective-permute-start | bytes 786440 | tf_op jit(solution)/shard_map/ppermute | solution.py:486
  34.5 12.9 %collective-permute-start.11 = (bf16[256,512]{1,0:T(8,128)(2,1)S(1)}, bf16[256,512]{1,0:T(8,128)(2,1)S(1)}, u32[]{:S(2)}, u32[]{:S(2)}) collective-permute-start(bf16[256,512]{1,0:T(8,128)(2,1)S(1)} %collective-permute-done.5.refs_2_), channel_id=1, source_target_pairs={{0,8},{4,12},{8,0},{12,4},{16,24},{20,28},{24,16},{28,20},{1,9},{5... | collective-permute-start | bytes 786440 | tf_op jit(solution)/shard_map/ppermute | solution.py:486
  34.7 12.7 %collective-permute-start.10 = (bf16[256,512]{1,0:T(8,128)(2,1)S(1)}, bf16[256,512]{1,0:T(8,128)(2,1)S(1)}, u32[]{:S(2)}, u32[]{:S(2)}) collective-permute-start(bf16[256,512]{1,0:T(8,128)(2,1)S(1)} %collective-permute-done.5.refs_2_), channel_id=1, source_target_pairs={{0,24},{4,28},{8,16},{12,20},{16,8},{20,12},{24,0},{28,4},{1,25},{... | collective-permute-start | bytes 786440 | tf_op jit(solution)/shard_map/ppermute | solution.py:486
  36.4 1.6 %copy-start.3 = (bf16[1,256,4096]{2,1,0:T(8,128)(2,1)S(1)}, bf16[1,256,4096]{2,1,0:T(8,128)(2,1)}, u32[]{:S(2)}) copy-start(bf16[1,256,4096]{2,1,0:T(8,128)(2,1)} %param.6) | copy-start | bytes 6291460
  47.4 4.8 %copy-start = (bf16[1,256,2048]{2,1,0:T(8,128)(2,1)S(1)}, bf16[1,256,2048]{2,1,0:T(8,128)(2,1)}, u32[]{:S(2)}) copy-start(bf16[1,256,2048]{2,1,0:T(8,128)(2,1)} %param.9) | copy-start | bytes 3145732
  47.4 4.8 %copy-start.5 = (s32[1,256]{1,0:T(1,128)S(1)}, s32[1,256]{1,0:T(1,128)}, u32[]{:S(2)}) copy-start(s32[1,256]{1,0:T(1,128)} %marks_a) | copy-start | bytes 3076
  49.6 13.5 %collective-permute-start.16 = (bf16[512,512]{1,0:T(8,128)(2,1)S(1)}, bf16[512,512]{1,0:T(8,128)(2,1)S(1)}, u32[]{:S(2)}, u32[]{:S(2)}) collective-permute-start(bf16[512,512]{1,0:T(8,128)(2,1)S(1)} %get-tuple-element.62.refs_0_), channel_id=1, source_target_pairs={{0,16},{4,20},{8,24},{12,28},{1,17},{5,21},{9,25},{13,29},{2,18},{... | collective-permute-start | bytes 1572872 | tf_op jit(solution)/shard_map/ppermute | solution.py:486
  50.9 13.5 %collective-permute-start.15 = (bf16[512,512]{1,0:T(8,128)(2,1)S(1)}, bf16[512,512]{1,0:T(8,128)(2,1)S(1)}, u32[]{:S(2)}, u32[]{:S(2)}) collective-permute-start(bf16[512,512]{1,0:T(8,128)(2,1)S(1)} %get-tuple-element.62.refs_0_), channel_id=1, source_target_pairs={{0,8},{4,12},{8,0},{12,4},{16,24},{20,28},{1,9},{5,13},{9,1},{13,5... | collective-permute-start | bytes 1572872 | tf_op jit(solution)/shard_map/ppermute | solution.py:486
  64.5 9.8 %collective-permute-start.17 = (bf16[256,512]{1,0:T(8,128)(2,1)S(1)}, bf16[256,512]{1,0:T(8,128)(2,1)S(1)}, u32[]{:S(2)}, u32[]{:S(2)}) collective-permute-start(bf16[256,512]{1,0:T(8,128)(2,1)S(1)} %slice.6), channel_id=1, source_target_pairs={{0,16},{4,20},{8,24},{12,28},{1,17},{5,21},{9,25},{13,29},{2,18},{... | collective-permute-start | bytes 786440 | tf_op jit(solution)/shard_map/ppermute | solution.py:486
  65.8 8.5 %collective-permute-start.18 = (bf16[256,512]{1,0:T(8,128)(2,1)S(1)}, bf16[256,512]{1,0:T(8,128)(2,1)S(1)}, u32[]{:S(2)}, u32[]{:S(2)}) collective-permute-start(bf16[256,512]{1,0:T(8,128)(2,1)S(1)} %slice.7), channel_id=1, source_target_pairs={{16,24},{20,28},{24,16},{28,20},{17,25},{21,29},{25,17},{29,21},{1... | collective-permute-start | bytes 786440 | tf_op jit(solution)/shard_map/ppermute | solution.py:486
  76.6 5.2 %collective-permute-start.20 = (bf16[256,512]{1,0:T(8,128)(2,1)S(1)}, bf16[256,512]{1,0:T(8,128)(2,1)S(1)}, u32[]{:S(2)}, u32[]{:S(2)}) collective-permute-start(bf16[256,512]{1,0:T(8,128)(2,1)S(1)} %get-tuple-element.80), channel_id=1, source_target_pairs={{0,4},{4,0},{8,12},{12,8},{16,20},{20,16},{24,28},{28,24},{1,5},{5... | collective-permute-start | bytes 786440 | tf_op jit(solution)/shard_map/ppermute | solution.py:481
  81.8 1.6 %collective-permute-start.19 = (bf16[256,512]{1,0:T(8,128)(2,1)S(1)}, bf16[256,512]{1,0:T(8,128)(2,1)S(1)}, u32[]{:S(2)}, u32[]{:S(2)}) collective-permute-start(bf16[256,512]{1,0:T(8,128)(2,1)S(1)} %get-tuple-element.79), channel_id=1, source_target_pairs={{0,4},{4,0},{8,12},{12,8},{16,20},{20,16},{24,28},{28,24},{1,5},{5... | collective-permute-start | bytes 786440 | tf_op jit(solution)/shard_map/ppermute | solution.py:481

commit v6 on v5

--- a/solution.py
+++ b/solution.py
@@ -158,7 +158,7 @@
     else:
         rows, total, refs = refs[:3], None, refs[3:]
     pieces, (cos_ref, sin_ref, *refs) = refs[:count], refs[count:]
-    clean_out, mask_out, refs = refs[0], refs[1], refs[2:]
+    clean_outs, mask_out, refs = refs[:2], refs[2], refs[3:]
     if not staged:
         rows_held, *refs = refs
     held, kept, sem, out_sem = refs
@@ -166,17 +166,15 @@
     sums = products(waits, rows_held, held, total)
     kv_heads = sums.shape[1] // 2 // HEAD_DIM
     writes = []
-    for side in range(2):
-        mine = slice(side * tokens, (side + 1) * tokens)
+    for is_value, out in enumerate(clean_outs):
         for head in range(kv_heads):
-            for is_value in range(2):
-                first = (is_value * kv_heads + head) * HEAD_DIM
-                part = sums[mine, first : first + HEAD_DIM]
-                if not is_value:
-                    part = rotated(part, cos_ref[mine, :], sin_ref[mine, :])
-                place = (2 * head + is_value) * HEAD_DIM
-                kept[side, :, place : place + HEAD_DIM] = part.astype(jnp.bfloat16)
-        writes.append(pltpu.make_async_copy(kept.at[side], clean_out.at[mine, :], out_sem.at[side]))
+            lanes = slice(head * HEAD_DIM, (head + 1) * HEAD_DIM)
+            first = (is_value * kv_heads + head) * HEAD_DIM
+            part = sums[: 2 * tokens, first : first + HEAD_DIM]
+            if not is_value:
+                part = rotated(part, cos_ref[...], sin_ref[...])
+            kept[is_value, :, lanes] = part.astype(jnp.bfloat16)
+        writes.append(pltpu.make_async_copy(kept.at[is_value], out, out_sem.at[is_value]))
         writes[-1].start()
     mask_out[...] = sums[2 * tokens : 2 * tokens + 8]
     for write in writes:
@@ -226,13 +224,13 @@
     return kernel_call(
         functools.partial(finish_kernel, kinds, len(arrays), bool(staged), tokens),
         "project_finish",
-        [bf16(2 * tokens, width), f32(8, width)],
+        [bf16(2 * tokens, width // 2)] * 2 + [f32(8, width)],
         [IN_SMEM] + [IN_VMEM if staged else IN_PLACE] * len(begin) + [IN_PLACE] * len(arrays) + [IN_VMEM] * len(ending),
-        [IN_PLACE, IN_VMEM],
+        [IN_PLACE] * 2 + [IN_VMEM],
         [
             *scratch,
             pltpu.VMEM((inner, width), jnp.bfloat16),
-            pltpu.VMEM((2, tokens, width), jnp.bfloat16),
+            pltpu.VMEM((2, 2 * tokens, width // 2), jnp.bfloat16),
             pltpu.SemaphoreType.DMA((copies,)),
             pltpu.SemaphoreType.DMA((2,)),
         ],
@@ -283,22 +281,17 @@
     return query_ref[:, pl.ds(pl.multiple_of(first, HEAD_DIM), HEAD_DIM)]
 
 
-def kv_lanes(groups, head, is_value):
-    first = (2 * (head // groups) + is_value) * HEAD_DIM
+def kv_lanes(groups, head):
+    first = head // groups * HEAD_DIM
     return slice(first, first + HEAD_DIM)
 
 
 def own_kernel(groups, where, q_a, q_b, cos_ref, sin_ref, marks_a, marks_b, mask_ref, *refs):
-    clean_in, state, (clean_ref, noisy_ref, sem) = refs[0], refs[1:4], refs[4:]
+    clean_ins, state, (clean_ref, noisy_ref, sem) = refs[:2], refs[2:5], refs[5:]
     core = where[0]
     tokens = q_a.shape[0]
     heads = state[0].shape[0]
-    run_copies(
-        [
-            pltpu.make_async_copy(clean_in.at[i * tokens : (i + 1) * tokens, :], clean_ref.at[i], sem.at[i])
-            for i in range(2)
-        ]
-    )
+    run_copies([pltpu.make_async_copy(ref, clean_ref.at[i], sem.at[i]) for i, ref in enumerate(clean_ins)])
     for side, marks in enumerate((marks_a, marks_b)):
         mine = slice(side * tokens, (side + 1) * tokens)
         masked = jnp.broadcast_to(marks[...].astype(jnp.float32), (HEAD_DIM, tokens)).T > 0.5
@@ -308,22 +301,23 @@
                 token = jnp.broadcast_to(mask_ref[:1, first : first + HEAD_DIM], (tokens, HEAD_DIM))
                 if not is_value:
                     token = rotated(token, cos_ref[mine, :], sin_ref[mine, :])
-                lanes = kv_lanes(groups, head * groups, is_value)
-                clean = clean_ref[side, :, lanes].astype(jnp.float32)
-                noisy_ref[side, :, lanes] = jnp.where(masked, token, clean).astype(jnp.bfloat16)
+                lanes = kv_lanes(groups, head * groups)
+                clean = clean_ref[is_value, mine, lanes].astype(jnp.float32)
+                noisy_ref[is_value, mine, lanes] = jnp.where(masked, token, clean).astype(jnp.bfloat16)
+
+    def rows_of(ref, is_value, head, side):
+        return ref[is_value, side * tokens : (side + 1) * tokens, kv_lanes(groups, head)]
 
     def score(task):
         head, side = task
         query = query_of((q_a, q_b)[side], core, head)
-        lanes = kv_lanes(groups, head, 0)
-        near = scores_of(query, noisy_ref[side, :, lanes])
-        far = scores_of(query, clean_ref[1 - side, :, lanes])
+        near = scores_of(query, rows_of(noisy_ref, 0, head, side))
+        far = scores_of(query, rows_of(clean_ref, 0, head, 1 - side))
         return [near, jnp.where(core == 1 - side, far, -1e30)]
 
     def use(task, scores):
         head, side = task
-        lanes = kv_lanes(groups, head, 1)
-        values = [noisy_ref[side, :, lanes], clean_ref[1 - side, :, lanes]]
+        values = [rows_of(noisy_ref, 1, head, side), rows_of(clean_ref, 1, head, 1 - side)]
         mine = pl.ds(side * tokens, tokens)
         for ref, value in zip(state, absorb(scores, values, None)):
             ref[head, mine, :] = value
@@ -337,22 +331,26 @@
         functools.partial(own_kernel, groups),
         "attend_own",
         [f32(heads, 2 * tokens, HEAD_DIM)] * 3,
-        [IN_SMEM] + [IN_VMEM] * 7 + [IN_PLACE],
+        [IN_SMEM] + [IN_VMEM] * 7 + [IN_PLACE] * 2,
         [IN_VMEM] * 3,
-        [pltpu.VMEM((2, tokens, clean.shape[1]), jnp.bfloat16)] * 2 + [pltpu.SemaphoreType.DMA((2,))],
+        [pltpu.VMEM((2, *clean[0].shape), jnp.bfloat16)] * 2 + [pltpu.SemaphoreType.DMA((2,))],
         flops=16 * heads * tokens * tokens * HEAD_DIM,
-    )(where, *queries, *tables, *marks, mask_sums, clean)
+    )(where, *queries, *tables, *marks, mask_sums, *clean)
 
 
 def later_tasks(core, heads, groups, q_a, q_b, parts, state, store):
     def score(head):
         query = jnp.concatenate([query_of(q, core, head) for q in (q_a, q_b)], 0)
-        return [scores_of(query, part[:, kv_lanes(groups, head, 0)]) for part in parts]
+        return [scores_of(query, keys[:, kv_lanes(groups, head)]) for keys, _ in parts]
 
     def use(head, scores):
-        store(head, absorb(scores, [part[:, kv_lanes(groups, head, 1)] for part in parts], state(head)))
+        store(head, absorb(scores, [values[:, kv_lanes(groups, head)] for _, values in parts], state(head)))
 
     pipelined(heads, score, use)
+
+
+def pairs(refs):
+    return list(zip(refs[::2], refs[1::2]))
 
 
 def is_earlier(where, flip):
@@ -361,7 +359,7 @@
 
 def later_kernel(groups, flips, where, q_a, q_b, *refs):
     count = len(flips)
-    parts, outs = refs[:count], refs[count + 3 :]
+    parts, outs = pairs(refs[: 2 * count]), refs[2 * count + 3 :]
 
     def state(head):
         return tuple(out[head] for out in outs)
@@ -388,15 +386,16 @@
         functools.partial(later_kernel, groups, flips),
         "attend_later",
         [f32(heads, 2 * tokens, HEAD_DIM)] * 3,
-        [IN_SMEM] + [IN_VMEM] * (5 + count),
+        [IN_SMEM] + [IN_VMEM] * (5 + 2 * count),
         [IN_VMEM] * 3,
-        aliases={3 + count + i: i for i in range(3)},
-        flops=8 * heads * tokens * sum(p.shape[0] for p in parts) * HEAD_DIM,
-    )(where, *queries, *parts, *running)
+        aliases={3 + 2 * count + i: i for i in range(3)},
+        flops=8 * heads * tokens * sum(p[0].shape[0] for p in parts) * HEAD_DIM,
+    )(where, *queries, *(ref for part in parts for ref in part), *running)
 
 
 def last_kernel(heads, groups, count, flip, where, q_a, q_b, *refs):
-    parts, state_refs, outs = refs[:count], refs[count : count + 3], refs[count + 3 :]
+    parts, refs = pairs(refs[: 2 * count]), refs[2 * count :]
+    state_refs, outs = refs[:3], refs[3:]
     tokens = q_a.shape[0]
 
     def state(head):
@@ -426,39 +425,35 @@
         functools.partial(last_kernel, heads, groups, count, flip),
         "attend_last",
         [bf16(tokens, len(heads) * HEAD_DIM)] * 2,
-        [IN_SMEM] + [IN_VMEM] * (5 + count),
+        [IN_SMEM] + [IN_VMEM] * (5 + 2 * count),
         [IN_VMEM] * 2,
-        flops=8 * len(heads) * tokens * sum(p.shape[0] for p in parts) * HEAD_DIM,
-    )(where, *queries, *parts, *running)
-
-
-def place_kernel(count, where, *refs):
-    parts, out, sem = refs[: 2 * count], refs[2 * count], refs[2 * count + 1]
-    core = where[0]
+        flops=8 * len(heads) * tokens * sum(p[0].shape[0] for p in parts) * HEAD_DIM,
+    )(where, *queries, *(ref for part in parts for ref in part), *running)
+
+
+def place_kernel(places, where, *refs):
+    out, sem = refs[-2:]
     half = out.shape[1] // 2
-    width = half // count
     copies = []
-    for number, part in enumerate(parts):
-        side = core if number < count else 1 - core
-        first = pl.multiple_of(side * half + (number % count) * width, HEAD_DIM)
-        copies.append(pltpu.make_async_copy(part, out.at[:, pl.ds(first, width)], sem.at[number]))
-    for copy in copies:
-        copy.start()
-    for copy in copies:
-        copy.wait()
-
-
-def place_heads(where, mine, received):
-    count = len(mine)
-    tokens, width = mine[0].shape
-    return kernel_call(
-        functools.partial(place_kernel, count),
+    for part, (received, number) in zip(refs, places):
+        side = 1 - where[0] if received else where[0]
+        width = part.shape[1]
+        columns = pl.ds(pl.multiple_of(side * half + number * width, HEAD_DIM), width)
+        copies.append(pltpu.make_async_copy(part, out.at[:, columns], sem.at[len(copies)]))
+    run_copies(copies)
+
+
+def place_heads(where, parts, places, shape, base=None):
+    begun = [] if base is None else [base]
+    return kernel_call(
+        functools.partial(place_kernel, places),
         "place_heads",
-        bf16(tokens, 2 * count * width),
-        [IN_SMEM] + [IN_VMEM] * (2 * count),
+        bf16(*shape),
+        [IN_SMEM] + [IN_VMEM] * len(parts) + [IN_PLACE] * len(begun),
         IN_PLACE,
-        [pltpu.SemaphoreType.DMA((2 * count,))],
-    )(where, *mine, *received)
+        [pltpu.SemaphoreType.DMA((len(parts),))],
+        aliases={1 + len(parts): 0} if begun else {},
+    )(where, *parts, *begun)
 
 
 def as_scalars(values):
@@ -529,12 +524,12 @@
         ]
         final = [
             [
+                (far_corner, 3, 3, depth),
+                (near_corner, 1, 3, depth),
                 (middle, 2, 0, depth),
                 (last[0], 2, 3, depth),
                 (last[1], 2, 1, depth),
                 (last[2], 2, 2, depth),
-                (near_corner, 1, 3, depth),
-                (far_corner, 3, 3, depth),
             ]
         ]
         staged = project_partial(rows, segments, final, where)
@@ -543,20 +538,23 @@
         gathered = lax.all_gather(half_weights, "fsdp", axis=0, tiled=True)
         final, staged = [[(gathered, None, None, depth)]], ()
     tables = (cosine, sine)
-    clean, mask_sums = project_finish(rows, staged, final, where, tables)
+    *clean, mask_sums = project_finish(rows, staged, final, where, tables)
 
     heads = query_own.shape[1] // 2 // HEAD_DIM
     groups = heads // kv_heads
     if square:
-        along_x, along_y = to_chip(clean, 1, (0, 1, 2)), to_chip(clean, 2, (0, 1))
+        keys, values = clean
+        keys_x, keys_y = to_chip(keys, 1, (0, 1, 2)), to_chip(keys, 2, (0, 1))
+        values_x, values_y = to_chip(values, 1, (0, 2)), to_chip(values, 2, (0, 1))
         running = attend_own(where, query_rows, tables, both_marks, mask_sums, clean, heads, groups)
-        along_x, along_y, running = barrier((along_x, along_y, running))
-        last_parts = [to_chip(along_x[:tokens], 2, (0, 1)), to_chip(along_y[tokens:], 1, (2, 3))]
-        running = attend_later(where, query_rows, [along_x, along_y], (1, 2), running, groups)
+        keys_x, running = barrier((keys_x, running))
+        last_parts = [(to_chip(keys_x, 2, (0, 1)), to_chip(values_y, 1, (2, 3)))]
+        along = [(keys_x, values_x), (keys_y, values_y)]
+        running = attend_later(where, query_rows, along, (1, 2), running, groups)
     else:
         running = attend_own(where, query_rows, tables, both_marks, mask_sums, clean, heads, groups)
         for flip in range(1, chips):
-            parts = [to_chip(clean, flip, [s for s in range(chips) if s < s ^ flip])]
+            parts = [tuple(to_chip(part, flip, [s for s in range(chips) if s < s ^ flip]) for part in clean)]
             if flip < chips - 1:
                 running = attend_later(where, query_rows, parts, (flip,), running, groups)
         last_parts = parts
@@ -567,7 +565,11 @@
         )
         kept.append(own)
         received.append(swap_cores(other))
-    return place_heads(where, kept, received)[None]
+    parts = kept + received[:-1]
+    places = [(False, i) for i in range(len(kept))] + [(True, i) for i in range(len(received) - 1)]
+    output = place_heads(where, parts, places, query_own.shape)
+    output = place_heads(where, received[-1:], [(True, len(received) - 1)], query_own.shape, output)
+    return output[None]
 
 
 def solution(mesh):

time: 85.4 us -> 85.5 us (level)
  waiting for transfers between devices: 28.9 us -> 24.2 us
  starting transfers between devices: 22.4 us -> 25.7 us
  Pallas kernels: 25.3 us -> 26.2 us
    ppermute x11 -> x13, starting transfers between devices: 11.4 us -> 16.1 us  [to_chip(): return lax.ppermute(array, 'seq', pairs)]
    ppermute x11 -> x13, waiting for transfers between devices: 8.32 us -> 3.59 us  [to_chip(): return lax.ppermute(array, 'seq', pairs)]
    ppermute x5, starting transfers between devices: 6.42 us -> 4.2 us  [to_shard(): lax.ppermute(array, 'fsdp', [(s, s ^ flip) for s in range(fsdp_size)])]
    ppermute x5, waiting for transfers between devices: 19.1 us -> 20.5 us  [to_shard(): lax.ppermute(array, 'fsdp', [(s, s ^ flip) for s in range(fsdp_size)])]
    ppermute x5, waiting for transfers between devices: 1.52 us -> 0.07 us  [swap_cores(): return lax.ppermute(array, 'seq', [(s, s ^ 1) for s in range(seq_size)])]
    pallas_call x1 -> x2, Pallas kernels: 1.54 us -> 2.7 us  [place_heads(): kernel_call(functools.partial(place_kernel, places), 'place_heads', bf16(...]
  transfers between devices with their start and end apart: 21 -> 23, of which waited for: 6 -> 7; matrix products, arithmetic and copies ran while one was open for 8% -> 8% of each run, Pallas kernels for 23% -> 24%
where the time goes in v6:
time: 85.5 us; the launch traced here: 84.7 us
  Pallas kernels  26.2 us (31%)
  starting transfers between devices  25.7 us (30%)
  waiting for transfers between devices  24.2 us (28%)
  other arithmetic  4.65 us (5%)
  local copies, waits for them, and re-layouts  3.46 us (4%)
    ppermute x5, waiting for transfers between devices, to_shard(): lax.ppermute(array, 'fsdp', [(s, s ^ flip) for s in range(fsdp_size)])  20.5 us
    ppermute x13, starting transfers between devices, to_chip(): return lax.ppermute(array, 'seq', pairs)  16.1 us
    pallas_call x1, Pallas kernels, attend_later(): kernel_call(functools.partial(later_kernel, groups, flips), 'attend_later...  6.47 us
    ppermute x5, starting transfers between devices, swap_cores(): return lax.ppermute(array, 'seq', [(s, s ^ 1) for s in range(seq_size)])  5.39 us
    pallas_call x2, Pallas kernels, attend_last(): kernel_call(functools.partial(last_kernel, heads, groups, count, flip), '...  4.65 us
    ppermute x5, starting transfers between devices, to_shard(): lax.ppermute(array, 'fsdp', [(s, s ^ flip) for s in range(fsdp_size)])  4.2 us
    pallas_call x1, Pallas kernels, project_partial(): kernel_call(functools.partial(partial_kernel, kinds, final_kinds, len(arr...  3.98 us
    pallas_call x1, Pallas kernels, attend_own(): kernel_call(functools.partial(own_kernel, groups), 'attend_own', [f32(hea...  3.83 us
  transfers between devices with their start and end apart: 23, of which 7 were waited for; matrix products, arithmetic and copies ran while one was open for 8% of the time, Pallas kernels for 24%

profile of v6, /device:TPU:7, one launch (start us, length us, event | category | flops | bytes accessed | tf_op | source)
XLA Modules:
  0.0 84.7 jit_solution(10170260335704962752)
XLA Ops:
  0.0 0.7 collective-permute-start.2
  0.7 0.0 collective-permute-start.3
  0.7 0.9 %dynamic_slice.6 = bf16[256,256]{1,0:T(8,128)(2,1)S(1)} dynamic-slice(bf16[1024,512]{1,0:T(8,128)(2,1)} %refs_0_.1, s32[]{:T(128)S(6)} %select_n.14, s32[]{:T(128)S(6)} %select_n.15), dynamic_slice_sizes={256,256} | dynamic-slice | bytes 262148 | tf_op jit(solution)/shard_map/dynamic_slice | solution.py:494
  1.6 0.9 %dynamic_slice.7 = bf16[256,256]{1,0:T(8,128)(2,1)S(1)} dynamic-slice(bf16[1024,512]{1,0:T(8,128)(2,1)} %refs_1_.1, s32[]{:T(128)S(6)} %select_n.14, s32[]{:T(128)S(6)} %select_n.15), dynamic_slice_sizes={256,256} | dynamic-slice | bytes 262148 | tf_op jit(solution)/shard_map/dynamic_slice | solution.py:494
  2.5 0.7 pad_maximum_fusion
  3.2 3.3 %collective-permute-start = (bf16[256,512]{1,0:T(8,128)(2,1)}, bf16[256,512]{1,0:T(8,128)(2,1)}, u32[]{:S(2)}, u32[]{:S(2)}) collective-permute-start(bf16[256,512]{1,0:T(8,128)(2,1)} %pad_maximum_fusion), channel_id=1, source_target_pairs={{0,3},{1,2},{2,1},{3,0},{4,7},{5,6},{6,5},{7,4},{8,11},{9,10},{10,... | collective-permute-start | bytes 786440 | tf_op jit(solution)/shard_map/ppermute | solution.py:484
  6.6 0.0 collective-permute-start.1
  6.6 0.8 collective-permute-start.4
  7.4 0.0 copy-start.6
  7.4 1.8 %fusion = (f32[512,64]{1,0:T(8,128)}, f32[512,64]{1,0:T(8,128)}, f32[512,64]{1,0:T(8,128)S(1)}) fusion(f32[64]{0:T(128)S(1)} %negate_power_fusion, f32[512]{0:T(512)S(1)} %add_convert_fusion), kind=kLoop, calls=%fused_computation.5 | loop fusion | flops 65536 | bytes 395520 | tf_op jit(solution)/shard_map/neg | solution.py:54
  9.2 0.1 pad_maximum_fusion.1.refs_8_.cos_ref
  9.4 1.3 %pad_maximum_fusion.2.refs_9_.sin_ref = f32[512,128]{1,0:T(8,128)S(1)} fusion(f32[512,64]{1,0:T(8,128)} %get-tuple-element.82, f32[512,64]{1,0:T(8,128)} %get-tuple-element.81), kind=kLoop, calls=%fused_computation.4 | loop fusion | flops 65536 | bytes 524288 | tf_op jit(solution)/shard_map/concatenate | solution.py:54
  10.7 0.7 pad_add_fusion.where
  11.3 2.5 %cut_weights.1 = bf16[256,512]{1,0:T(8,128)(2,1)} custom-call(s32[3]{0:T(128)} %pad_add_fusion.where, bf16[1024,512]{1,0:T(8,128)(2,1)} %refs_0_.1, bf16[1024,512]{1,0:T(8,128)(2,1)} %refs_1_.1), custom_call_target="tpu_custom_call" | custom-call | tf_op jit(solution)/shard_map/cut_weights/pallas_call | solution.py:83
  13.8 0.0 collective-permute-done.4.marks_b
  13.8 0.0 collective-permute-done.refs_2_
  13.8 5.5 %collective-permute-done.1.refs_5_ = bf16[256,512]{1,0:T(8,128)(2,1)} collective-permute-done((bf16[256,512]{1,0:T(8,128)(2,1)}, bf16[256,512]{1,0:T(8,128)(2,1)}, u32[]{:S(2)}, u32[]{:S(2)}) %collective-permute-start.1) | collective-permute-done | bytes 262176 | tf_op jit(solution)/shard_map/ppermute | solution.py:484
  19.4 0.0 collective-permute-done.3.q_b
  19.4 0.0 collective-permute-done.2.other
  19.4 0.1 collective-permute-start.5
  19.5 0.3 collective-permute-start.6
  19.8 0.2 collective-permute-start.7
  20.0 1.2 %collective-permute-start.8 = (bf16[256,512]{1,0:T(8,128)(2,1)}, bf16[256,512]{1,0:T(8,128)(2,1)S(1)}, u32[]{:S(2)}, u32[]{:S(2)}) collective-permute-start(bf16[256,512]{1,0:T(8,128)(2,1)} %collective-permute-done.refs_2_), channel_id=1, source_target_pairs={{0,8},{4,12},{8,0},{12,4},{16,24},{20,28},{24,16},{28,20},{1,9},{5... | collective-permute-start | bytes 786440 | tf_op jit(solution)/shard_map/ppermute | solution.py:481
  21.2 1.2 %collective-permute-start.9 = (bf16[256,512]{1,0:T(8,128)(2,1)}, bf16[256,512]{1,0:T(8,128)(2,1)S(1)}, u32[]{:S(2)}, u32[]{:S(2)}) collective-permute-start(bf16[256,512]{1,0:T(8,128)(2,1)} %collective-permute-done.refs_2_), channel_id=1, source_target_pairs={{0,16},{4,20},{8,24},{12,28},{16,0},{20,4},{24,8},{28,12},{1,17},{... | collective-permute-start | bytes 786440 | tf_op jit(solution)/shard_map/ppermute | solution.py:481
  22.5 11.7 %collective-permute-done.5.refs_4_ = bf16[256,512]{1,0:T(8,128)(2,1)S(1)} collective-permute-done((bf16[256,512]{1,0:T(8,128)(2,1)}, bf16[256,512]{1,0:T(8,128)(2,1)S(1)}, u32[]{:S(2)}, u32[]{:S(2)}) %collective-permute-start.5) | collective-permute-done | bytes 262176 | tf_op jit(solution)/shard_map/ppermute | solution.py:484
  34.2 0.0 collective-permute-done.6.refs_6_
  34.2 0.0 collective-permute-done.7.refs_7_
  34.2 0.0 collective-permute-done.8.refs_3_
  34.2 0.0 collective-permute-done.9.refs_4_
  34.2 0.1 collective-permute-start.10
  34.3 0.7 collective-permute-start.11
  35.0 1.1 %collective-permute-start.12 = (bf16[256,512]{1,0:T(8,128)(2,1)S(1)}, bf16[256,512]{1,0:T(8,128)(2,1)S(1)}, u32[]{:S(2)}, u32[]{:S(2)}) collective-permute-start(bf16[256,512]{1,0:T(8,128)(2,1)S(1)} %collective-permute-done.5.refs_4_), channel_id=1, source_target_pairs={{0,24},{4,28},{8,16},{12,20},{16,8},{20,12},{24,0},{28,4},{1,25},{... | collective-permute-start | bytes 786440 | tf_op jit(solution)/shard_map/ppermute | solution.py:481
  36.1 0.3 collective-permute-start.13
  36.4 1.2 %collective-permute-start.14 = (bf16[256,512]{1,0:T(8,128)(2,1)S(1)}, bf16[256,512]{1,0:T(8,128)(2,1)S(1)}, u32[]{:S(2)}, u32[]{:S(2)}) collective-permute-start(bf16[256,512]{1,0:T(8,128)(2,1)S(1)} %collective-permute-done.5.refs_4_), channel_id=1, source_target_pairs={{0,16},{4,20},{8,24},{12,28},{16,0},{20,4},{24,8},{28,12},{1,17},{... | collective-permute-start | bytes 786440 | tf_op jit(solution)/shard_map/ppermute | solution.py:481
  37.7 1.6 %copy-done.3 = bf16[1,256,4096]{2,1,0:T(8,128)(2,1)S(1)} copy-done((bf16[1,256,4096]{2,1,0:T(8,128)(2,1)S(1)}, bf16[1,256,4096]{2,1,0:T(8,128)(2,1)}, u32[]{:S(2)}) %copy-start.3) | copy-done | bytes 2097176
  39.3 4.0 %project_partial.1 = (f32[528,512]{1,0:T(8,128)S(1)}, bf16[528,1536]{1,0:T(8,128)(2,1)S(1)}) custom-call(s32[3]{0:T(128)S(1)} %copy-done.4, bf16[256,4096]{1,0:T(8,128)(2,1)S(1)} %bitcast.12, bf16[256,4096]{1,0:T(8,128)(2,1)} %collective-permute-done.2.other, bf16[16,4096]{1,0:T(8,128)(2,1)S(1)} %broadcast_in_dim.4.masks, bf16[1024,512]{1,0:T(8,128)(2,1)S(1)} %copy-done.1, ...), custom_call_target="tpu_custom_call" | custom-call | flops 1384120320 | tf_op jit(solution)/shard_map/project_partial/pallas_call | solution.py:201
  43.2 0.2 collective-permute-done.10.refs_2_
  43.4 3.1 %collective-permute-done.11.refs_3_ = bf16[256,512]{1,0:T(8,128)(2,1)S(1)} collective-permute-done((bf16[256,512]{1,0:T(8,128)(2,1)}, bf16[256,512]{1,0:T(8,128)(2,1)S(1)}, u32[]{:S(2)}, u32[]{:S(2)}) %collective-permute-start.11) | collective-permute-done | bytes 262176 | tf_op jit(solution)/shard_map/ppermute | solution.py:484
  46.6 0.0 collective-permute-done.12.refs_5_
  46.6 0.0 collective-permute-done.13.refs_6_
  46.6 2.5 %collective-permute-done.14.refs_7_ = bf16[256,512]{1,0:T(8,128)(2,1)S(1)} collective-permute-done((bf16[256,512]{1,0:T(8,128)(2,1)S(1)}, bf16[256,512]{1,0:T(8,128)(2,1)S(1)}, u32[]{:S(2)}, u32[]{:S(2)}) %collective-permute-start.14) | collective-permute-done | bytes 262176 | tf_op jit(solution)/shard_map/ppermute | solution.py:481
  49.1 2.1 %project_finish.1 = (bf16[512,256]{1,0:T(8,128)(2,1)S(1)}, bf16[512,256]{1,0:T(8,128)(2,1)S(1)}, f32[8,512]{1,0:T(8,128)S(1)}) custom-call(s32[3]{0:T(128)S(1)} %copy-done.4, f32[528,512]{1,0:T(8,128)S(1)} %get-tuple-element.56.refs_0_, bf16[528,1536]{1,0:T(8,128)(2,1)S(1)} %get-tuple-element.57.refs_1_, ...), custom_call_target="tpu_custom_call" | custom-call | flops 830472192 | tf_op jit(solution)/shard_map/project_finish/pallas_call | solution.py:224
  51.2 1.3 %collective-permute-start.15 = (bf16[512,256]{1,0:T(8,128)(2,1)S(1)}, bf16[512,256]{1,0:T(8,128)(2,1)S(1)}, u32[]{:S(2)}, u32[]{:S(2)}) collective-permute-start(bf16[512,256]{1,0:T(8,128)(2,1)S(1)} %get-tuple-element.62.refs_0_), channel_id=1, source_target_pairs={{0,8},{4,12},{8,0},{12,4},{16,24},{20,28},{1,9},{5,13},{9,1},{13,5... | collective-permute-start | bytes 786440 | tf_op jit(solution)/shard_map/ppermute | solution.py:481
  52.5 1.3 %collective-permute-start.17 = (bf16[512,256]{1,0:T(8,128)(2,1)S(1)}, bf16[512,256]{1,0:T(8,128)(2,1)S(1)}, u32[]{:S(2)}, u32[]{:S(2)}) collective-permute-start(bf16[512,256]{1,0:T(8,128)(2,1)S(1)} %get-tuple-element.66.refs_1_), channel_id=1, source_target_pairs={{0,16},{4,20},{8,24},{12,28},{1,17},{5,21},{9,25},{13,29},{2,18},{... | collective-permute-start | bytes 786440 | tf_op jit(solution)/shard_map/ppermute | solution.py:481
  53.8 1.3 %collective-permute-start.19 = (bf16[512,256]{1,0:T(8,128)(2,1)S(1)}, bf16[512,256]{1,0:T(8,128)(2,1)S(1)}, u32[]{:S(2)}, u32[]{:S(2)}) collective-permute-start(bf16[512,256]{1,0:T(8,128)(2,1)S(1)} %get-tuple-element.66.refs_1_), channel_id=1, source_target_pairs={{0,8},{4,12},{16,24},{20,28},{1,9},{5,13},{17,25},{21,29},{2,10},{... | collective-permute-start | bytes 786440 | tf_op jit(solution)/shard_map/ppermute | solution.py:481
  55.1 1.3 %collective-permute-start.20 = (bf16[512,256]{1,0:T(8,128)(2,1)S(1)}, bf16[512,256]{1,0:T(8,128)(2,1)S(1)}, u32[]{:S(2)}, u32[]{:S(2)}) collective-permute-start(bf16[512,256]{1,0:T(8,128)(2,1)S(1)} %get-tuple-element.62.refs_0_), channel_id=1, source_target_pairs={{0,16},{4,20},{8,24},{12,28},{1,17},{5,21},{9,25},{13,29},{2,18},{... | collective-permute-start | bytes 786440 | tf_op jit(solution)/shard_map/ppermute | solution.py:481
  56.4 3.8 %attend_own.1 = (f32[8,512,128]{2,1,0:T(8,128)S(1)}, f32[8,512,128]{2,1,0:T(8,128)S(1)}, f32[8,512,128]{2,1,0:T(8,128)S(1)}) custom-call(s32[3]{0:T(128)S(1)} %copy-done.4, bf16[256,2048]{1,0:T(8,128)(2,1)S(1)} %bitcast.7, bf16[256,2048]{1,0:T(8,128)(2,1)S(1)} %collective-permute-done.3.q_b, f32[512,128]{1,0:T(8,128)S(1)} %pad_maximum_fusion.1.refs_8_.cos_ref, ...), custom_call_target="tpu_custom_call" | custom-call | flops 1073741824 | tf_op jit(solution)/shard_map/attend_own/pallas_call | solution.py:330
  60.3 0.0 collective-permute-done.15.refs_0_
  60.3 1.3 %collective-permute-start.16 = (bf16[512,256]{1,0:T(8,128)(2,1)S(1)}, bf16[512,256]{1,0:T(8,128)(2,1)S(1)}, u32[]{:S(2)}, u32[]{:S(2)}) collective-permute-start(bf16[512,256]{1,0:T(8,128)(2,1)S(1)} %collective-permute-done.15.refs_0_), channel_id=1, source_target_pairs={{0,16},{4,20},{8,24},{12,28},{1,17},{5,21},{9,25},{13,29},{2,18},{... | collective-permute-start | bytes 786440 | tf_op jit(solution)/shard_map/ppermute | solution.py:481
  61.6 0.0 collective-permute-done.17.refs_3_
  61.6 4.0 %collective-permute-start.18 = (bf16[512,256]{1,0:T(8,128)(2,1)S(1)}, bf16[512,256]{1,0:T(8,128)(2,1)S(1)}, u32[]{:S(2)}, u32[]{:S(2)}) collective-permute-start(bf16[512,256]{1,0:T(8,128)(2,1)S(1)} %collective-permute-done.17.refs_3_), channel_id=1, source_target_pairs={{16,24},{20,28},{24,16},{28,20},{17,25},{21,29},{25,17},{29,21},{1... | collective-permute-start | bytes 786440 | tf_op jit(solution)/shard_map/ppermute | solution.py:481
  65.6 0.0 collective-permute-done.19.refs_1_
  65.6 1.0 %collective-permute-done.20.refs_2_ = bf16[512,256]{1,0:T(8,128)(2,1)S(1)} collective-permute-done((bf16[512,256]{1,0:T(8,128)(2,1)S(1)}, bf16[512,256]{1,0:T(8,128)(2,1)S(1)}, u32[]{:S(2)}, u32[]{:S(2)}) %collective-permute-start.20) | collective-permute-done | bytes 262176 | tf_op jit(solution)/shard_map/ppermute | solution.py:481
  66.7 6.5 %attend_later.1 = (f32[8,512,128]{2,1,0:T(8,128)S(1)}, f32[8,512,128]{2,1,0:T(8,128)S(1)}, f32[8,512,128]{2,1,0:T(8,128)S(1)}) custom-call(s32[3]{0:T(128)S(1)} %copy-done.4, bf16[256,2048]{1,0:T(8,128)(2,1)S(1)} %bitcast.8, bf16[256,2048]{1,0:T(8,128)(2,1)S(1)} %collective-permute-done.3.q_b, ...), custom_call_target="tpu_custom_call", output_to_operand_aliasing={{0}: (7, {}), {1}: (8, {}), {2}: (9, {})} | custom-call | flops 2147483648 | tf_op jit(solution)/shard_map/attend_later/pallas_call | solution.py:385
  73.1 0.0 collective-permute-done.16.refs_0_
  73.2 0.0 collective-permute-done.18.refs_1_
  73.2 2.3 %attend_last.3 = (bf16[256,512]{1,0:T(8,128)(2,1)S(1)}, bf16[256,512]{1,0:T(8,128)(2,1)S(1)}) custom-call(s32[3]{0:T(128)S(1)} %copy-done.4, bf16[256,2048]{1,0:T(8,128)(2,1)S(1)} %bitcast.9, bf16[256,2048]{1,0:T(8,128)(2,1)S(1)} %collective-permute-done.3.q_b, bf16[512,256]{1,0:T(8,128)(2,1)S(1)} %collective-permute-done.16.refs_0_, ...), custom_call_target="tpu_custom_call" | custom-call | flops 536870912 | tf_op jit(solution)/shard_map/attend_last/pallas_call | solution.py:424
  75.5 3.8 %collective-permute-start.22 = (bf16[256,512]{1,0:T(8,128)(2,1)S(1)}, bf16[256,512]{1,0:T(8,128)(2,1)S(1)}, u32[]{:S(2)}, u32[]{:S(2)}) collective-permute-start(bf16[256,512]{1,0:T(8,128)(2,1)S(1)} %get-tuple-element.80), channel_id=1, source_target_pairs={{0,4},{4,0},{8,12},{12,8},{16,20},{20,16},{24,28},{28,24},{1,5},{5... | collective-permute-start | bytes 786440 | tf_op jit(solution)/shard_map/ppermute | solution.py:476
  79.4 2.3 %attend_last.2 = (bf16[256,512]{1,0:T(8,128)(2,1)S(1)}, bf16[256,512]{1,0:T(8,128)(2,1)S(1)}) custom-call(s32[3]{0:T(128)S(1)} %copy-done.4, bf16[256,2048]{1,0:T(8,128)(2,1)S(1)} %bitcast.10, bf16[256,2048]{1,0:T(8,128)(2,1)S(1)} %collective-permute-done.3.q_b, bf16[512,256]{1,0:T(8,128)(2,1)S(1)} %collective-permute-done.16.refs_0_, ...), custom_call_target="tpu_custom_call" | custom-call | flops 536870912 | tf_op jit(solution)/shard_map/attend_last/pallas_call | solution.py:424
  81.7 0.1 collective-permute-start.21
  81.8 0.0 collective-permute-done.22.refs_2_
  81.8 1.4 %place_heads.2.refs_1_ = bf16[256,2048]{1,0:T(8,128)(2,1)} custom-call(s32[3]{0:T(128)S(1)} %copy-done.4, bf16[256,512]{1,0:T(8,128)(2,1)S(1)} %get-tuple-element.78.refs_0_, bf16[256,512]{1,0:T(8,128)(2,1)S(1)} %get-tuple-element.79.refs_1_, bf16[256,512]{1,0:T(8,128)(2,1)S(1)} %collective-permute-done.22.refs_2_), custom_call_target="tpu_custom_call" | custom-call | tf_op jit(solution)/shard_map/place_heads/pallas_call | solution.py:448
  83.2 0.1 collective-permute-done.21.refs_0_
  83.3 1.3 %place_heads.3 = bf16[256,2048]{1,0:T(8,128)(2,1)} custom-call(s32[3]{0:T(128)S(1)} %copy-done.4, bf16[256,512]{1,0:T(8,128)(2,1)S(1)} %collective-permute-done.21.refs_0_, bf16[256,2048]{1,0:T(8,128)(2,1)} %place_heads.2.refs_1_), custom_call_target="tpu_custom_call", output_to_operand_aliasing={{}: (2, {})} | custom-call | tf_op jit(solution)/shard_map/place_heads/pallas_call | solution.py:448
  (16 shorter events, 0.1 us)
Async XLA Ops:
  0.0 19.4 %collective-permute-start.2 = (bf16[256,4096]{1,0:T(8,128)(2,1)}, bf16[256,4096]{1,0:T(8,128)(2,1)}, u32[]{:S(2)}, u32[]{:S(2)}) collective-permute-start(bf16[256,4096]{1,0:T(8,128)(2,1)} %bitcast.11), channel_id=1, source_target_pairs={{0,4},{4,0},{8,12},{12,8},{16,20},{20,16},{24,28},{28,24},{1,5},{5... | collective-permute-start | bytes 6291464 | tf_op jit(solution)/shard_map/ppermute | solution.py:476
  0.7 18.7 %collective-permute-start.3 = (bf16[256,2048]{1,0:T(8,128)(2,1)}, bf16[256,2048]{1,0:T(8,128)(2,1)S(1)}, u32[]{:S(2)}, u32[]{:S(2)}) collective-permute-start(bf16[256,2048]{1,0:T(8,128)(2,1)} %bitcast.6), channel_id=1, source_target_pairs={{0,4},{4,0},{8,12},{12,8},{16,20},{20,16},{24,28},{28,24},{1,5},{5... | collective-permute-start | bytes 3145736 | tf_op jit(solution)/shard_map/ppermute | solution.py:476
  3.2 10.6 %collective-permute-start = (bf16[256,512]{1,0:T(8,128)(2,1)}, bf16[256,512]{1,0:T(8,128)(2,1)}, u32[]{:S(2)}, u32[]{:S(2)}) collective-permute-start(bf16[256,512]{1,0:T(8,128)(2,1)} %pad_maximum_fusion), channel_id=1, source_target_pairs={{0,3},{1,2},{2,1},{3,0},{4,7},{5,6},{6,5},{7,4},{8,11},{9,10},{10,... | collective-permute-start | bytes 786440 | tf_op jit(solution)/shard_map/ppermute | solution.py:484
  6.6 12.8 %collective-permute-start.1 = (bf16[256,512]{1,0:T(8,128)(2,1)}, bf16[256,512]{1,0:T(8,128)(2,1)}, u32[]{:S(2)}, u32[]{:S(2)}) collective-permute-start(bf16[256,512]{1,0:T(8,128)(2,1)} %pad_maximum_fusion), channel_id=1, source_target_pairs={{0,1},{1,0},{2,3},{3,2},{4,5},{5,4},{6,7},{7,6},{8,9},{9,8},{10,11... | collective-permute-start | bytes 786440 | tf_op jit(solution)/shard_map/ppermute | solution.py:484
  6.6 7.2 %collective-permute-start.4 = (s32[1,256]{1,0:T(1,128)}, s32[1,256]{1,0:T(1,128)S(1)}, u32[]{:S(2)}, u32[]{:S(2)}) collective-permute-start(s32[1,256]{1,0:T(1,128)} %marks_a), channel_id=1, source_target_pairs={{0,4},{4,0},{8,12},{12,8},{16,20},{20,16},{24,28},{28,24},{1,5},{5... | collective-permute-start | bytes 3080 | tf_op jit(solution)/shard_map/ppermute | solution.py:476
  7.4 12.0 %copy-start.6 = (bf16[4096]{0:T(1024)(128)(2,1)S(1)}, bf16[4096]{0:T(1024)(128)(2,1)}, u32[]{:S(2)}) copy-start(bf16[4096]{0:T(1024)(128)(2,1)} %param.8) | copy-start | bytes 24580
  9.2 28.4 %copy-start.1 = (bf16[1024,512]{1,0:T(8,128)(2,1)S(1)}, bf16[1024,512]{1,0:T(8,128)(2,1)}, u32[]{:S(2)}) copy-start(bf16[1024,512]{1,0:T(8,128)(2,1)} %refs_0_.1) | copy-start | bytes 3145732
  9.2 28.4 %copy-start.2 = (bf16[1024,512]{1,0:T(8,128)(2,1)S(1)}, bf16[1024,512]{1,0:T(8,128)(2,1)}, u32[]{:S(2)}) copy-start(bf16[1024,512]{1,0:T(8,128)(2,1)} %refs_1_.1) | copy-start | bytes 3145732
  11.3 26.4 %copy-start.4 = (s32[3]{0:T(128)S(1)}, s32[3]{0:T(128)}, u32[]{:S(2)}) copy-start(s32[3]{0:T(128)} %pad_add_fusion.where) | copy-start | bytes 40
  19.4 14.8 %collective-permute-start.5 = (bf16[256,512]{1,0:T(8,128)(2,1)}, bf16[256,512]{1,0:T(8,128)(2,1)S(1)}, u32[]{:S(2)}, u32[]{:S(2)}) collective-permute-start(bf16[256,512]{1,0:T(8,128)(2,1)} %pad_maximum_fusion), channel_id=1, source_target_pairs={{0,2},{1,3},{2,0},{3,1},{4,6},{5,7},{6,4},{7,5},{8,10},{9,11},{10,... | collective-permute-start | bytes 786440 | tf_op jit(solution)/shard_map/ppermute | solution.py:484
  19.5 14.7 %collective-permute-start.6 = (bf16[256,512]{1,0:T(8,128)(2,1)}, bf16[256,512]{1,0:T(8,128)(2,1)S(1)}, u32[]{:S(2)}, u32[]{:S(2)}) collective-permute-start(bf16[256,512]{1,0:T(8,128)(2,1)} %collective-permute-done.1.refs_5_), channel_id=1, source_target_pairs={{0,8},{4,12},{8,0},{12,4},{16,24},{20,28},{24,16},{28,20},{1,9},{5... | collective-permute-start | bytes 786440 | tf_op jit(solution)/shard_map/ppermute | solution.py:481
  19.8 14.4 %collective-permute-start.7 = (bf16[256,512]{1,0:T(8,128)(2,1)}, bf16[256,512]{1,0:T(8,128)(2,1)S(1)}, u32[]{:S(2)}, u32[]{:S(2)}) collective-permute-start(bf16[256,512]{1,0:T(8,128)(2,1)} %collective-permute-done.1.refs_5_), channel_id=1, source_target_pairs={{0,16},{4,20},{8,24},{12,28},{16,0},{20,4},{24,8},{28,12},{1,17},{... | collective-permute-start | bytes 786440 | tf_op jit(solution)/shard_map/ppermute | solution.py:481
  20.0 14.2 %collective-permute-start.8 = (bf16[256,512]{1,0:T(8,128)(2,1)}, bf16[256,512]{1,0:T(8,128)(2,1)S(1)}, u32[]{:S(2)}, u32[]{:S(2)}) collective-permute-start(bf16[256,512]{1,0:T(8,128)(2,1)} %collective-permute-done.refs_2_), channel_id=1, source_target_pairs={{0,8},{4,12},{8,0},{12,4},{16,24},{20,28},{24,16},{28,20},{1,9},{5... | collective-permute-start | bytes 786440 | tf_op jit(solution)/shard_map/ppermute | solution.py:481
  21.2 12.9 %collective-permute-start.9 = (bf16[256,512]{1,0:T(8,128)(2,1)}, bf16[256,512]{1,0:T(8,128)(2,1)S(1)}, u32[]{:S(2)}, u32[]{:S(2)}) collective-permute-start(bf16[256,512]{1,0:T(8,128)(2,1)} %collective-permute-done.refs_2_), channel_id=1, source_target_pairs={{0,16},{4,20},{8,24},{12,28},{16,0},{20,4},{24,8},{28,12},{1,17},{... | collective-permute-start | bytes 786440 | tf_op jit(solution)/shard_map/ppermute | solution.py:481
  34.2 9.3 %collective-permute-start.10 = (bf16[256,512]{1,0:T(8,128)(2,1)}, bf16[256,512]{1,0:T(8,128)(2,1)S(1)}, u32[]{:S(2)}, u32[]{:S(2)}) collective-permute-start(bf16[256,512]{1,0:T(8,128)(2,1)} %cut_weights.1), channel_id=1, source_target_pairs={{0,3},{1,2},{2,1},{3,0},{4,7},{5,6},{6,5},{7,4},{8,11},{9,10},{10,... | collective-permute-start | bytes 786440 | tf_op jit(solution)/shard_map/ppermute | solution.py:484
  34.3 12.3 %collective-permute-start.11 = (bf16[256,512]{1,0:T(8,128)(2,1)}, bf16[256,512]{1,0:T(8,128)(2,1)S(1)}, u32[]{:S(2)}, u32[]{:S(2)}) collective-permute-start(bf16[256,512]{1,0:T(8,128)(2,1)} %cut_weights.1), channel_id=1, source_target_pairs={{0,1},{1,0},{2,3},{3,2},{4,5},{5,4},{6,7},{7,6},{8,9},{9,8},{10,11... | collective-permute-start | bytes 786440 | tf_op jit(solution)/shard_map/ppermute | solution.py:484
  35.0 11.5 %collective-permute-start.12 = (bf16[256,512]{1,0:T(8,128)(2,1)S(1)}, bf16[256,512]{1,0:T(8,128)(2,1)S(1)}, u32[]{:S(2)}, u32[]{:S(2)}) collective-permute-start(bf16[256,512]{1,0:T(8,128)(2,1)S(1)} %collective-permute-done.5.refs_4_), channel_id=1, source_target_pairs={{0,24},{4,28},{8,16},{12,20},{16,8},{20,12},{24,0},{28,4},{1,25},{... | collective-permute-start | bytes 786440 | tf_op jit(solution)/shard_map/ppermute | solution.py:481
  36.1 10.5 %collective-permute-start.13 = (bf16[256,512]{1,0:T(8,128)(2,1)S(1)}, bf16[256,512]{1,0:T(8,128)(2,1)S(1)}, u32[]{:S(2)}, u32[]{:S(2)}) collective-permute-start(bf16[256,512]{1,0:T(8,128)(2,1)S(1)} %collective-permute-done.5.refs_4_), channel_id=1, source_target_pairs={{0,8},{4,12},{8,0},{12,4},{16,24},{20,28},{24,16},{28,20},{1,9},{5... | collective-permute-start | bytes 786440 | tf_op jit(solution)/shard_map/ppermute | solution.py:481
  36.4 12.7 %collective-permute-start.14 = (bf16[256,512]{1,0:T(8,128)(2,1)S(1)}, bf16[256,512]{1,0:T(8,128)(2,1)S(1)}, u32[]{:S(2)}, u32[]{:S(2)}) collective-permute-start(bf16[256,512]{1,0:T(8,128)(2,1)S(1)} %collective-permute-done.5.refs_4_), channel_id=1, source_target_pairs={{0,16},{4,20},{8,24},{12,28},{16,0},{20,4},{24,8},{28,12},{1,17},{... | collective-permute-start | bytes 786440 | tf_op jit(solution)/shard_map/ppermute | solution.py:481
  37.7 1.6 %copy-start.3 = (bf16[1,256,4096]{2,1,0:T(8,128)(2,1)S(1)}, bf16[1,256,4096]{2,1,0:T(8,128)(2,1)}, u32[]{:S(2)}) copy-start(bf16[1,256,4096]{2,1,0:T(8,128)(2,1)} %param.6) | copy-start | bytes 6291460
  49.1 7.3 %copy-start = (bf16[1,256,2048]{2,1,0:T(8,128)(2,1)S(1)}, bf16[1,256,2048]{2,1,0:T(8,128)(2,1)}, u32[]{:S(2)}) copy-start(bf16[1,256,2048]{2,1,0:T(8,128)(2,1)} %param.9) | copy-start | bytes 3145732
  49.1 7.3 %copy-start.5 = (s32[1,256]{1,0:T(1,128)S(1)}, s32[1,256]{1,0:T(1,128)}, u32[]{:S(2)}) copy-start(s32[1,256]{1,0:T(1,128)} %marks_a) | copy-start | bytes 3076
  51.2 9.1 %collective-permute-start.15 = (bf16[512,256]{1,0:T(8,128)(2,1)S(1)}, bf16[512,256]{1,0:T(8,128)(2,1)S(1)}, u32[]{:S(2)}, u32[]{:S(2)}) collective-permute-start(bf16[512,256]{1,0:T(8,128)(2,1)S(1)} %get-tuple-element.62.refs_0_), channel_id=1, source_target_pairs={{0,8},{4,12},{8,0},{12,4},{16,24},{20,28},{1,9},{5,13},{9,1},{13,5... | collective-permute-start | bytes 786440 | tf_op jit(solution)/shard_map/ppermute | solution.py:481
  52.5 9.1 %collective-permute-start.17 = (bf16[512,256]{1,0:T(8,128)(2,1)S(1)}, bf16[512,256]{1,0:T(8,128)(2,1)S(1)}, u32[]{:S(2)}, u32[]{:S(2)}) collective-permute-start(bf16[512,256]{1,0:T(8,128)(2,1)S(1)} %get-tuple-element.66.refs_1_), channel_id=1, source_target_pairs={{0,16},{4,20},{8,24},{12,28},{1,17},{5,21},{9,25},{13,29},{2,18},{... | collective-permute-start | bytes 786440 | tf_op jit(solution)/shard_map/ppermute | solution.py:481
  53.8 11.8 %collective-permute-start.19 = (bf16[512,256]{1,0:T(8,128)(2,1)S(1)}, bf16[512,256]{1,0:T(8,128)(2,1)S(1)}, u32[]{:S(2)}, u32[]{:S(2)}) collective-permute-start(bf16[512,256]{1,0:T(8,128)(2,1)S(1)} %get-tuple-element.66.refs_1_), channel_id=1, source_target_pairs={{0,8},{4,12},{16,24},{20,28},{1,9},{5,13},{17,25},{21,29},{2,10},{... | collective-permute-start | bytes 786440 | tf_op jit(solution)/shard_map/ppermute | solution.py:481
  55.1 11.5 %collective-permute-start.20 = (bf16[512,256]{1,0:T(8,128)(2,1)S(1)}, bf16[512,256]{1,0:T(8,128)(2,1)S(1)}, u32[]{:S(2)}, u32[]{:S(2)}) collective-permute-start(bf16[512,256]{1,0:T(8,128)(2,1)S(1)} %get-tuple-element.62.refs_0_), channel_id=1, source_target_pairs={{0,16},{4,20},{8,24},{12,28},{1,17},{5,21},{9,25},{13,29},{2,18},{... | collective-permute-start | bytes 786440 | tf_op jit(solution)/shard_map/ppermute | solution.py:481
  60.3 12.9 %collective-permute-start.16 = (bf16[512,256]{1,0:T(8,128)(2,1)S(1)}, bf16[512,256]{1,0:T(8,128)(2,1)S(1)}, u32[]{:S(2)}, u32[]{:S(2)}) collective-permute-start(bf16[512,256]{1,0:T(8,128)(2,1)S(1)} %collective-permute-done.15.refs_0_), channel_id=1, source_target_pairs={{0,16},{4,20},{8,24},{12,28},{1,17},{5,21},{9,25},{13,29},{2,18},{... | collective-permute-start | bytes 786440 | tf_op jit(solution)/shard_map/ppermute | solution.py:481
  61.6 11.6 %collective-permute-start.18 = (bf16[512,256]{1,0:T(8,128)(2,1)S(1)}, bf16[512,256]{1,0:T(8,128)(2,1)S(1)}, u32[]{:S(2)}, u32[]{:S(2)}) collective-permute-start(bf16[512,256]{1,0:T(8,128)(2,1)S(1)} %collective-permute-done.17.refs_3_), channel_id=1, source_target_pairs={{16,24},{20,28},{24,16},{28,20},{17,25},{21,29},{25,17},{29,21},{1... | collective-permute-start | bytes 786440 | tf_op jit(solution)/shard_map/ppermute | solution.py:481
  75.5 6.3 %collective-permute-start.22 = (bf16[256,512]{1,0:T(8,128)(2,1)S(1)}, bf16[256,512]{1,0:T(8,128)(2,1)S(1)}, u32[]{:S(2)}, u32[]{:S(2)}) collective-permute-start(bf16[256,512]{1,0:T(8,128)(2,1)S(1)} %get-tuple-element.80), channel_id=1, source_target_pairs={{0,4},{4,0},{8,12},{12,8},{16,20},{20,16},{24,28},{28,24},{1,5},{5... | collective-permute-start | bytes 786440 | tf_op jit(solution)/shard_map/ppermute | solution.py:476
  81.7 1.6 %collective-permute-start.21 = (bf16[256,512]{1,0:T(8,128)(2,1)S(1)}, bf16[256,512]{1,0:T(8,128)(2,1)S(1)}, u32[]{:S(2)}, u32[]{:S(2)}) collective-permute-start(bf16[256,512]{1,0:T(8,128)(2,1)S(1)} %get-tuple-element.77), channel_id=1, source_target_pairs={{0,4},{4,0},{8,12},{12,8},{16,20},{20,16},{24,28},{28,24},{1,5},{5... | collective-permute-start | bytes 786440 | tf_op jit(solution)/shard_map/ppermute | solution.py:476

commit v7 on v5

--- a/solution.py
+++ b/solution.py
@@ -432,33 +432,29 @@
     )(where, *queries, *parts, *running)
 
 
-def place_kernel(count, where, *refs):
-    parts, out, sem = refs[: 2 * count], refs[2 * count], refs[2 * count + 1]
-    core = where[0]
+def place_kernel(places, where, *refs):
+    out, sem = refs[-2:]
     half = out.shape[1] // 2
-    width = half // count
     copies = []
-    for number, part in enumerate(parts):
-        side = core if number < count else 1 - core
-        first = pl.multiple_of(side * half + (number % count) * width, HEAD_DIM)
-        copies.append(pltpu.make_async_copy(part, out.at[:, pl.ds(first, width)], sem.at[number]))
-    for copy in copies:
-        copy.start()
-    for copy in copies:
-        copy.wait()
-
-
-def place_heads(where, mine, received):
-    count = len(mine)
-    tokens, width = mine[0].shape
-    return kernel_call(
-        functools.partial(place_kernel, count),
+    for part, (received, number) in zip(refs, places):
+        side = 1 - where[0] if received else where[0]
+        width = part.shape[1]
+        columns = pl.ds(pl.multiple_of(side * half + number * width, HEAD_DIM), width)
+        copies.append(pltpu.make_async_copy(part, out.at[:, columns], sem.at[len(copies)]))
+    run_copies(copies)
+
+
+def place_heads(where, parts, places, shape, base=None):
+    begun = [] if base is None else [base]
+    return kernel_call(
+        functools.partial(place_kernel, places),
         "place_heads",
-        bf16(tokens, 2 * count * width),
-        [IN_SMEM] + [IN_VMEM] * (2 * count),
+        bf16(*shape),
+        [IN_SMEM] + [IN_VMEM] * len(parts) + [IN_PLACE] * len(begun),
         IN_PLACE,
-        [pltpu.SemaphoreType.DMA((2 * count,))],
-    )(where, *mine, *received)
+        [pltpu.SemaphoreType.DMA((len(parts),))],
+        aliases={1 + len(parts): 0} if begun else {},
+    )(where, *parts, *begun)
 
 
 def as_scalars(values):
@@ -567,7 +563,11 @@
         )
         kept.append(own)
         received.append(swap_cores(other))
-    return place_heads(where, kept, received)[None]
+    parts = kept + received[:-1]
+    places = [(False, i) for i in range(len(kept))] + [(True, i) for i in range(len(received) - 1)]
+    output = place_heads(where, parts, places, query_own.shape)
+    output = place_heads(where, received[-1:], [(True, len(received) - 1)], query_own.shape, output)
+    return output[None]
 
 
 def solution(mesh):

time: 85.4 us -> 85.1 us (level)
  waiting for transfers between devices: 28.9 us -> 27.4 us
  Pallas kernels: 25.3 us -> 26.4 us
    ppermute x5, waiting for transfers between devices: 1.52 us -> 0.07 us  [swap_cores(): return lax.ppermute(array, 'seq', [(s, s ^ 1) for s in range(seq_size)])]
    pallas_call x1 -> x2, Pallas kernels: 1.54 us -> 2.7 us  [place_heads(): kernel_call(functools.partial(place_kernel, places), 'place_heads', bf16(...]
  transfers between devices with their start and end apart: 21 -> 21, of which waited for: 6 -> 6; matrix products, arithmetic and copies ran while one was open for 8% -> 8% of each run, Pallas kernels for 23% -> 24%
where the time goes in v7:
time: 85.1 us; the launch traced here: 84.8 us
  waiting for transfers between devices  27.4 us (32%)
  Pallas kernels  26.4 us (31%)
  starting transfers between devices  22.4 us (26%)
  other arithmetic  4.58 us (5%)
  local copies, waits for them, and re-layouts  3.5 us (4%)
    ppermute x5, waiting for transfers between devices, to_shard(): lax.ppermute(array, 'fsdp', [(s, s ^ flip) for s in range(fsdp_size)])  19.1 us
    ppermute x11, starting transfers between devices, to_chip(): return lax.ppermute(array, 'seq', pairs)  11.4 us
    ppermute x11, waiting for transfers between devices, to_chip(): return lax.ppermute(array, 'seq', pairs)  8.32 us
    pallas_call x1, Pallas kernels, attend_later(): kernel_call(functools.partial(later_kernel, groups, flips), 'attend_later...  6.57 us
    ppermute x5, starting transfers between devices, to_shard(): lax.ppermute(array, 'fsdp', [(s, s ^ flip) for s in range(fsdp_size)])  6.42 us
    pallas_call x2, Pallas kernels, attend_last(): kernel_call(functools.partial(last_kernel, heads, groups, count, flip), '...  4.68 us
    ppermute x5, starting transfers between devices, swap_cores(): return lax.ppermute(array, 'seq', [(s, s ^ 1) for s in range(seq_size)])  4.64 us
    pallas_call x1, Pallas kernels, project_partial(): kernel_call(functools.partial(partial_kernel, kinds, final_kinds, len(arr...  3.98 us
  transfers between devices with their start and end apart: 21, of which 6 were waited for; matrix products, arithmetic and copies ran while one was open for 8% of the time, Pallas kernels for 24%

profile of v7, /device:TPU:7, one launch (start us, length us, event | category | flops | bytes accessed | tf_op | source)
XLA Modules:
  0.0 84.8 jit_solution(1236011985293648625)
XLA Ops:
  0.0 0.7 collective-permute-start.2
  0.7 0.0 collective-permute-start.3
  0.7 0.9 %dynamic_slice.6 = bf16[256,256]{1,0:T(8,128)(2,1)S(1)} dynamic-slice(bf16[1024,512]{1,0:T(8,128)(2,1)} %refs_0_.1, s32[]{:T(128)S(6)} %select_n.14, s32[]{:T(128)S(6)} %select_n.15), dynamic_slice_sizes={256,256} | dynamic-slice | bytes 262148 | tf_op jit(solution)/shard_map/dynamic_slice | solution.py:495
  1.6 0.9 %dynamic_slice.7 = bf16[256,256]{1,0:T(8,128)(2,1)S(1)} dynamic-slice(bf16[1024,512]{1,0:T(8,128)(2,1)} %refs_1_.1, s32[]{:T(128)S(6)} %select_n.14, s32[]{:T(128)S(6)} %select_n.15), dynamic_slice_sizes={256,256} | dynamic-slice | bytes 262148 | tf_op jit(solution)/shard_map/dynamic_slice | solution.py:495
  2.5 0.7 pad_maximum_fusion
  3.2 1.3 %collective-permute-start.1 = (bf16[256,512]{1,0:T(8,128)(2,1)}, bf16[256,512]{1,0:T(8,128)(2,1)}, u32[]{:S(2)}, u32[]{:S(2)}) collective-permute-start(bf16[256,512]{1,0:T(8,128)(2,1)} %pad_maximum_fusion), channel_id=1, source_target_pairs={{0,1},{1,0},{2,3},{3,2},{4,5},{5,4},{6,7},{7,6},{8,9},{9,8},{10,11... | collective-permute-start | bytes 786440 | tf_op jit(solution)/shard_map/ppermute | solution.py:485
  4.5 2.2 %collective-permute-start = (bf16[256,512]{1,0:T(8,128)(2,1)}, bf16[256,512]{1,0:T(8,128)(2,1)}, u32[]{:S(2)}, u32[]{:S(2)}) collective-permute-start(bf16[256,512]{1,0:T(8,128)(2,1)} %pad_maximum_fusion), channel_id=1, source_target_pairs={{0,3},{1,2},{2,1},{3,0},{4,7},{5,6},{6,5},{7,4},{8,11},{9,10},{10,... | collective-permute-start | bytes 786440 | tf_op jit(solution)/shard_map/ppermute | solution.py:485
  6.7 1.1 %collective-permute-start.4 = (s32[1,256]{1,0:T(1,128)}, s32[1,256]{1,0:T(1,128)S(1)}, u32[]{:S(2)}, u32[]{:S(2)}) collective-permute-start(s32[1,256]{1,0:T(1,128)} %marks_a), channel_id=1, source_target_pairs={{0,4},{4,0},{8,12},{12,8},{16,20},{20,16},{24,28},{28,24},{1,5},{5... | collective-permute-start | bytes 3080 | tf_op jit(solution)/shard_map/ppermute | solution.py:477
  7.8 0.0 copy-start.6
  7.8 1.8 %fusion = (f32[512,64]{1,0:T(8,128)}, f32[512,64]{1,0:T(8,128)}, f32[512,64]{1,0:T(8,128)S(1)}) fusion(f32[64]{0:T(128)S(1)} %negate_power_fusion, f32[512]{0:T(512)S(1)} %add_convert_fusion), kind=kLoop, calls=%fused_computation.5 | loop fusion | flops 65536 | bytes 395520 | tf_op jit(solution)/shard_map/neg | solution.py:54
  9.7 0.1 pad_maximum_fusion.1.refs_8_.cos_ref
  9.8 1.3 %pad_maximum_fusion.2.refs_9_.sin_ref = f32[512,128]{1,0:T(8,128)S(1)} fusion(f32[512,64]{1,0:T(8,128)} %get-tuple-element.82, f32[512,64]{1,0:T(8,128)} %get-tuple-element.81), kind=kLoop, calls=%fused_computation.4 | loop fusion | flops 65536 | bytes 524288 | tf_op jit(solution)/shard_map/concatenate | solution.py:54
  11.1 0.6 pad_add_fusion.where
  11.7 2.5 %cut_weights.1 = bf16[256,512]{1,0:T(8,128)(2,1)} custom-call(s32[3]{0:T(128)} %pad_add_fusion.where, bf16[1024,512]{1,0:T(8,128)(2,1)} %refs_0_.1, bf16[1024,512]{1,0:T(8,128)(2,1)} %refs_1_.1), custom_call_target="tpu_custom_call" | custom-call | tf_op jit(solution)/shard_map/cut_weights/pallas_call | solution.py:83
  14.2 0.0 collective-permute-done.4.marks_b
  14.2 0.0 collective-permute-done.1.refs_5_
  14.2 4.4 %collective-permute-done.refs_2_ = bf16[256,512]{1,0:T(8,128)(2,1)} collective-permute-done((bf16[256,512]{1,0:T(8,128)(2,1)}, bf16[256,512]{1,0:T(8,128)(2,1)}, u32[]{:S(2)}, u32[]{:S(2)}) %collective-permute-start) | collective-permute-done | bytes 262176 | tf_op jit(solution)/shard_map/ppermute | solution.py:485
  18.6 0.0 collective-permute-done.3.q_b
  18.6 0.0 collective-permute-done.2.other
  18.6 1.3 %collective-permute-start.5 = (bf16[256,512]{1,0:T(8,128)(2,1)}, bf16[256,512]{1,0:T(8,128)(2,1)S(1)}, u32[]{:S(2)}, u32[]{:S(2)}) collective-permute-start(bf16[256,512]{1,0:T(8,128)(2,1)} %pad_maximum_fusion), channel_id=1, source_target_pairs={{0,2},{1,3},{2,0},{3,1},{4,6},{5,7},{6,4},{7,5},{8,10},{9,11},{10,... | collective-permute-start | bytes 786440 | tf_op jit(solution)/shard_map/ppermute | solution.py:485
  19.9 0.2 collective-permute-start.9
  20.2 0.3 collective-permute-start.8
  20.4 1.2 %collective-permute-start.7 = (bf16[256,512]{1,0:T(8,128)(2,1)}, bf16[256,512]{1,0:T(8,128)(2,1)S(1)}, u32[]{:S(2)}, u32[]{:S(2)}) collective-permute-start(bf16[256,512]{1,0:T(8,128)(2,1)} %collective-permute-done.1.refs_5_), channel_id=1, source_target_pairs={{0,16},{4,20},{8,24},{12,28},{16,0},{20,4},{24,8},{28,12},{1,17},{... | collective-permute-start | bytes 786440 | tf_op jit(solution)/shard_map/ppermute | solution.py:482
  21.6 1.2 %collective-permute-start.6 = (bf16[256,512]{1,0:T(8,128)(2,1)}, bf16[256,512]{1,0:T(8,128)(2,1)S(1)}, u32[]{:S(2)}, u32[]{:S(2)}) collective-permute-start(bf16[256,512]{1,0:T(8,128)(2,1)} %collective-permute-done.1.refs_5_), channel_id=1, source_target_pairs={{0,8},{4,12},{8,0},{12,4},{16,24},{20,28},{24,16},{28,20},{1,9},{5... | collective-permute-start | bytes 786440 | tf_op jit(solution)/shard_map/ppermute | solution.py:482
  22.9 9.2 %collective-permute-done.5.refs_2_ = bf16[256,512]{1,0:T(8,128)(2,1)S(1)} collective-permute-done((bf16[256,512]{1,0:T(8,128)(2,1)}, bf16[256,512]{1,0:T(8,128)(2,1)S(1)}, u32[]{:S(2)}, u32[]{:S(2)}) %collective-permute-start.5) | collective-permute-done | bytes 262176 | tf_op jit(solution)/shard_map/ppermute | solution.py:485
  32.0 0.0 collective-permute-done.9.refs_4_
  32.0 0.0 collective-permute-done.8.refs_3_
  32.0 0.0 collective-permute-done.7.refs_7_
  32.0 0.0 collective-permute-done.6.refs_6_
  32.1 1.6 %collective-permute-start.14 = (bf16[256,512]{1,0:T(8,128)(2,1)}, bf16[256,512]{1,0:T(8,128)(2,1)S(1)}, u32[]{:S(2)}, u32[]{:S(2)}) collective-permute-start(bf16[256,512]{1,0:T(8,128)(2,1)} %cut_weights.1), channel_id=1, source_target_pairs={{0,3},{1,2},{2,1},{3,0},{4,7},{5,6},{6,5},{7,4},{8,11},{9,10},{10,... | collective-permute-start | bytes 786440 | tf_op jit(solution)/shard_map/ppermute | solution.py:485
  33.7 0.0 collective-permute-start.13
  33.7 0.8 collective-permute-start.12
  34.5 0.3 collective-permute-start.11
  34.7 1.6 %collective-permute-start.10 = (bf16[256,512]{1,0:T(8,128)(2,1)S(1)}, bf16[256,512]{1,0:T(8,128)(2,1)S(1)}, u32[]{:S(2)}, u32[]{:S(2)}) collective-permute-start(bf16[256,512]{1,0:T(8,128)(2,1)S(1)} %collective-permute-done.5.refs_2_), channel_id=1, source_target_pairs={{0,24},{4,28},{8,16},{12,20},{16,8},{20,12},{24,0},{28,4},{1,25},{... | collective-permute-start | bytes 786440 | tf_op jit(solution)/shard_map/ppermute | solution.py:482
  36.4 1.6 %copy-done.3 = bf16[1,256,4096]{2,1,0:T(8,128)(2,1)S(1)} copy-done((bf16[1,256,4096]{2,1,0:T(8,128)(2,1)S(1)}, bf16[1,256,4096]{2,1,0:T(8,128)(2,1)}, u32[]{:S(2)}) %copy-start.3) | copy-done | bytes 2097176
  38.0 4.0 %project_partial.1 = (f32[528,512]{1,0:T(8,128)S(1)}, bf16[528,1536]{1,0:T(8,128)(2,1)S(1)}) custom-call(s32[3]{0:T(128)S(1)} %copy-done.4, bf16[256,4096]{1,0:T(8,128)(2,1)S(1)} %bitcast.12, bf16[256,4096]{1,0:T(8,128)(2,1)} %collective-permute-done.2.other, bf16[16,4096]{1,0:T(8,128)(2,1)S(1)} %broadcast_in_dim.4.masks, bf16[1024,512]{1,0:T(8,128)(2,1)S(1)} %copy-done.1, ...), custom_call_target="tpu_custom_call" | custom-call | flops 1384120320 | tf_op jit(solution)/shard_map/project_partial/pallas_call | solution.py:203
  41.9 0.0 collective-permute-done.14.refs_7_
  42.0 5.5 %collective-permute-done.13.refs_6_ = bf16[256,512]{1,0:T(8,128)(2,1)S(1)} collective-permute-done((bf16[256,512]{1,0:T(8,128)(2,1)}, bf16[256,512]{1,0:T(8,128)(2,1)S(1)}, u32[]{:S(2)}, u32[]{:S(2)}) %collective-permute-start.13) | collective-permute-done | bytes 262176 | tf_op jit(solution)/shard_map/ppermute | solution.py:485
  47.4 0.0 collective-permute-done.12.refs_5_
  47.4 0.0 collective-permute-done.11.refs_4_
  47.4 0.0 collective-permute-done.10.refs_3_
  47.4 0.0 copy-start
  47.4 0.0 copy-start.5
  47.5 2.2 %project_finish.1 = (bf16[512,512]{1,0:T(8,128)(2,1)S(1)}, f32[8,512]{1,0:T(8,128)S(1)}) custom-call(s32[3]{0:T(128)S(1)} %copy-done.4, f32[528,512]{1,0:T(8,128)S(1)} %get-tuple-element.56.refs_0_, bf16[528,1536]{1,0:T(8,128)(2,1)S(1)} %get-tuple-element.57.refs_1_, bf16[256,512]{1,0:T(8,128)(2,1)S(1)} %collective-permute-done.5.refs_2_, ...), custom_call_target="tpu_custom_call" | custom-call | flops 830472192 | tf_op jit(solution)/shard_map/project_finish/pallas_call | solution.py:226
  49.6 1.3 %collective-permute-start.16 = (bf16[512,512]{1,0:T(8,128)(2,1)S(1)}, bf16[512,512]{1,0:T(8,128)(2,1)S(1)}, u32[]{:S(2)}, u32[]{:S(2)}) collective-permute-start(bf16[512,512]{1,0:T(8,128)(2,1)S(1)} %get-tuple-element.62.refs_0_), channel_id=1, source_target_pairs={{0,16},{4,20},{8,24},{12,28},{1,17},{5,21},{9,25},{13,29},{2,18},{... | collective-permute-start | bytes 1572872 | tf_op jit(solution)/shard_map/ppermute | solution.py:482
  50.9 1.3 %collective-permute-start.15 = (bf16[512,512]{1,0:T(8,128)(2,1)S(1)}, bf16[512,512]{1,0:T(8,128)(2,1)S(1)}, u32[]{:S(2)}, u32[]{:S(2)}) collective-permute-start(bf16[512,512]{1,0:T(8,128)(2,1)S(1)} %get-tuple-element.62.refs_0_), channel_id=1, source_target_pairs={{0,8},{4,12},{8,0},{12,4},{16,24},{20,28},{1,9},{5,13},{9,1},{13,5... | collective-permute-start | bytes 1572872 | tf_op jit(solution)/shard_map/ppermute | solution.py:482
  52.2 0.0 copy-done
  52.2 0.0 copy-done.5
  52.2 3.9 %attend_own.1 = (f32[8,512,128]{2,1,0:T(8,128)S(1)}, f32[8,512,128]{2,1,0:T(8,128)S(1)}, f32[8,512,128]{2,1,0:T(8,128)S(1)}) custom-call(s32[3]{0:T(128)S(1)} %copy-done.4, bf16[256,2048]{1,0:T(8,128)(2,1)S(1)} %bitcast.7, bf16[256,2048]{1,0:T(8,128)(2,1)S(1)} %collective-permute-done.3.q_b, f32[512,128]{1,0:T(8,128)S(1)} %pad_maximum_fusion.1.refs_8_.cos_ref, ...), custom_call_target="tpu_custom_call" | custom-call | flops 1073741824 | tf_op jit(solution)/shard_map/attend_own/pallas_call | solution.py:336
  56.1 7.0 %collective-permute-done.16.refs_1_ = bf16[512,512]{1,0:T(8,128)(2,1)S(1)} collective-permute-done((bf16[512,512]{1,0:T(8,128)(2,1)S(1)}, bf16[512,512]{1,0:T(8,128)(2,1)S(1)}, u32[]{:S(2)}, u32[]{:S(2)}) %collective-permute-start.16) | collective-permute-done | bytes 524320 | tf_op jit(solution)/shard_map/ppermute | solution.py:482
  63.1 1.3 %collective-permute-done.15.refs_0_ = bf16[512,512]{1,0:T(8,128)(2,1)S(1)} collective-permute-done((bf16[512,512]{1,0:T(8,128)(2,1)S(1)}, bf16[512,512]{1,0:T(8,128)(2,1)S(1)}, u32[]{:S(2)}, u32[]{:S(2)}) %collective-permute-start.15) | collective-permute-done | bytes 524320 | tf_op jit(solution)/shard_map/ppermute | solution.py:482
  64.5 1.3 %collective-permute-start.17 = (bf16[256,512]{1,0:T(8,128)(2,1)S(1)}, bf16[256,512]{1,0:T(8,128)(2,1)S(1)}, u32[]{:S(2)}, u32[]{:S(2)}) collective-permute-start(bf16[256,512]{1,0:T(8,128)(2,1)S(1)} %slice.6), channel_id=1, source_target_pairs={{0,16},{4,20},{8,24},{12,28},{1,17},{5,21},{9,25},{13,29},{2,18},{... | collective-permute-start | bytes 786440 | tf_op jit(solution)/shard_map/ppermute | solution.py:482
  65.8 1.9 %collective-permute-start.18 = (bf16[256,512]{1,0:T(8,128)(2,1)S(1)}, bf16[256,512]{1,0:T(8,128)(2,1)S(1)}, u32[]{:S(2)}, u32[]{:S(2)}) collective-permute-start(bf16[256,512]{1,0:T(8,128)(2,1)S(1)} %slice.7), channel_id=1, source_target_pairs={{16,24},{20,28},{24,16},{28,20},{17,25},{21,29},{25,17},{29,21},{1... | collective-permute-start | bytes 786440 | tf_op jit(solution)/shard_map/ppermute | solution.py:482
  67.7 6.6 %attend_later.1 = (f32[8,512,128]{2,1,0:T(8,128)S(1)}, f32[8,512,128]{2,1,0:T(8,128)S(1)}, f32[8,512,128]{2,1,0:T(8,128)S(1)}) custom-call(s32[3]{0:T(128)S(1)} %copy-done.4, bf16[256,2048]{1,0:T(8,128)(2,1)S(1)} %bitcast.8, bf16[256,2048]{1,0:T(8,128)(2,1)S(1)} %collective-permute-done.3.q_b, ...), custom_call_target="tpu_custom_call", output_to_operand_aliasing={{0}: (5, {}), {1}: (6, {}), {2}: (7, {})} | custom-call | flops 2147483648 | tf_op jit(solution)/shard_map/attend_later/pallas_call | solution.py:387
  74.3 0.0 collective-permute-done.17.refs_0_
  74.3 0.0 collective-permute-done.18.refs_1_
  74.3 2.3 %attend_last.3 = (bf16[256,512]{1,0:T(8,128)(2,1)S(1)}, bf16[256,512]{1,0:T(8,128)(2,1)S(1)}) custom-call(s32[3]{0:T(128)S(1)} %copy-done.4, bf16[256,2048]{1,0:T(8,128)(2,1)S(1)} %bitcast.9, bf16[256,2048]{1,0:T(8,128)(2,1)S(1)} %collective-permute-done.3.q_b, bf16[256,512]{1,0:T(8,128)(2,1)S(1)} %collective-permute-done.17.refs_0_, ...), custom_call_target="tpu_custom_call" | custom-call | flops 536870912 | tf_op jit(solution)/shard_map/attend_last/pallas_call | solution.py:425
  76.6 2.8 %collective-permute-start.20 = (bf16[256,512]{1,0:T(8,128)(2,1)S(1)}, bf16[256,512]{1,0:T(8,128)(2,1)S(1)}, u32[]{:S(2)}, u32[]{:S(2)}) collective-permute-start(bf16[256,512]{1,0:T(8,128)(2,1)S(1)} %get-tuple-element.80), channel_id=1, source_target_pairs={{0,4},{4,0},{8,12},{12,8},{16,20},{20,16},{24,28},{28,24},{1,5},{5... | collective-permute-start | bytes 786440 | tf_op jit(solution)/shard_map/ppermute | solution.py:477
  79.4 2.3 %attend_last.2 = (bf16[256,512]{1,0:T(8,128)(2,1)S(1)}, bf16[256,512]{1,0:T(8,128)(2,1)S(1)}) custom-call(s32[3]{0:T(128)S(1)} %copy-done.4, bf16[256,2048]{1,0:T(8,128)(2,1)S(1)} %bitcast.10, bf16[256,2048]{1,0:T(8,128)(2,1)S(1)} %collective-permute-done.3.q_b, bf16[256,512]{1,0:T(8,128)(2,1)S(1)} %collective-permute-done.17.refs_0_, ...), custom_call_target="tpu_custom_call" | custom-call | flops 536870912 | tf_op jit(solution)/shard_map/attend_last/pallas_call | solution.py:425
  81.8 0.1 collective-permute-start.19
  81.9 0.0 collective-permute-done.20.refs_2_
  81.9 1.4 %place_heads.2.refs_1_ = bf16[256,2048]{1,0:T(8,128)(2,1)} custom-call(s32[3]{0:T(128)S(1)} %copy-done.4, bf16[256,512]{1,0:T(8,128)(2,1)S(1)} %get-tuple-element.78.refs_0_, bf16[256,512]{1,0:T(8,128)(2,1)S(1)} %get-tuple-element.79.refs_1_, bf16[256,512]{1,0:T(8,128)(2,1)S(1)} %collective-permute-done.20.refs_2_), custom_call_target="tpu_custom_call" | custom-call | tf_op jit(solution)/shard_map/place_heads/pallas_call | solution.py:449
  83.3 0.1 collective-permute-done.19.refs_0_
  83.4 1.3 %place_heads.3 = bf16[256,2048]{1,0:T(8,128)(2,1)} custom-call(s32[3]{0:T(128)S(1)} %copy-done.4, bf16[256,512]{1,0:T(8,128)(2,1)S(1)} %collective-permute-done.19.refs_0_, bf16[256,2048]{1,0:T(8,128)(2,1)} %place_heads.2.refs_1_), custom_call_target="tpu_custom_call", output_to_operand_aliasing={{}: (2, {})} | custom-call | tf_op jit(solution)/shard_map/place_heads/pallas_call | solution.py:449
  (14 shorter events, 0.1 us)
Async XLA Ops:
  0.0 18.6 %collective-permute-start.2 = (bf16[256,4096]{1,0:T(8,128)(2,1)}, bf16[256,4096]{1,0:T(8,128)(2,1)}, u32[]{:S(2)}, u32[]{:S(2)}) collective-permute-start(bf16[256,4096]{1,0:T(8,128)(2,1)} %bitcast.11), channel_id=1, source_target_pairs={{0,4},{4,0},{8,12},{12,8},{16,20},{20,16},{24,28},{28,24},{1,5},{5... | collective-permute-start | bytes 6291464 | tf_op jit(solution)/shard_map/ppermute | solution.py:477
  0.7 17.9 %collective-permute-start.3 = (bf16[256,2048]{1,0:T(8,128)(2,1)}, bf16[256,2048]{1,0:T(8,128)(2,1)S(1)}, u32[]{:S(2)}, u32[]{:S(2)}) collective-permute-start(bf16[256,2048]{1,0:T(8,128)(2,1)} %bitcast.6), channel_id=1, source_target_pairs={{0,4},{4,0},{8,12},{12,8},{16,20},{20,16},{24,28},{28,24},{1,5},{5... | collective-permute-start | bytes 3145736 | tf_op jit(solution)/shard_map/ppermute | solution.py:477
  3.2 10.9 %collective-permute-start.1 = (bf16[256,512]{1,0:T(8,128)(2,1)}, bf16[256,512]{1,0:T(8,128)(2,1)}, u32[]{:S(2)}, u32[]{:S(2)}) collective-permute-start(bf16[256,512]{1,0:T(8,128)(2,1)} %pad_maximum_fusion), channel_id=1, source_target_pairs={{0,1},{1,0},{2,3},{3,2},{4,5},{5,4},{6,7},{7,6},{8,9},{9,8},{10,11... | collective-permute-start | bytes 786440 | tf_op jit(solution)/shard_map/ppermute | solution.py:485
  4.5 14.1 %collective-permute-start = (bf16[256,512]{1,0:T(8,128)(2,1)}, bf16[256,512]{1,0:T(8,128)(2,1)}, u32[]{:S(2)}, u32[]{:S(2)}) collective-permute-start(bf16[256,512]{1,0:T(8,128)(2,1)} %pad_maximum_fusion), channel_id=1, source_target_pairs={{0,3},{1,2},{2,1},{3,0},{4,7},{5,6},{6,5},{7,4},{8,11},{9,10},{10,... | collective-permute-start | bytes 786440 | tf_op jit(solution)/shard_map/ppermute | solution.py:485
  6.7 7.4 %collective-permute-start.4 = (s32[1,256]{1,0:T(1,128)}, s32[1,256]{1,0:T(1,128)S(1)}, u32[]{:S(2)}, u32[]{:S(2)}) collective-permute-start(s32[1,256]{1,0:T(1,128)} %marks_a), channel_id=1, source_target_pairs={{0,4},{4,0},{8,12},{12,8},{16,20},{20,16},{24,28},{28,24},{1,5},{5... | collective-permute-start | bytes 3080 | tf_op jit(solution)/shard_map/ppermute | solution.py:477
  7.8 10.8 %copy-start.6 = (bf16[4096]{0:T(1024)(128)(2,1)S(1)}, bf16[4096]{0:T(1024)(128)(2,1)}, u32[]{:S(2)}) copy-start(bf16[4096]{0:T(1024)(128)(2,1)} %param.8) | copy-start | bytes 24580
  9.7 26.7 %copy-start.1 = (bf16[1024,512]{1,0:T(8,128)(2,1)S(1)}, bf16[1024,512]{1,0:T(8,128)(2,1)}, u32[]{:S(2)}) copy-start(bf16[1024,512]{1,0:T(8,128)(2,1)} %refs_0_.1) | copy-start | bytes 3145732
  9.7 26.7 %copy-start.2 = (bf16[1024,512]{1,0:T(8,128)(2,1)S(1)}, bf16[1024,512]{1,0:T(8,128)(2,1)}, u32[]{:S(2)}) copy-start(bf16[1024,512]{1,0:T(8,128)(2,1)} %refs_1_.1) | copy-start | bytes 3145732
  11.7 24.7 %copy-start.4 = (s32[3]{0:T(128)S(1)}, s32[3]{0:T(128)}, u32[]{:S(2)}) copy-start(s32[3]{0:T(128)} %pad_add_fusion.where) | copy-start | bytes 40
  18.6 13.4 %collective-permute-start.5 = (bf16[256,512]{1,0:T(8,128)(2,1)}, bf16[256,512]{1,0:T(8,128)(2,1)S(1)}, u32[]{:S(2)}, u32[]{:S(2)}) collective-permute-start(bf16[256,512]{1,0:T(8,128)(2,1)} %pad_maximum_fusion), channel_id=1, source_target_pairs={{0,2},{1,3},{2,0},{3,1},{4,6},{5,7},{6,4},{7,5},{8,10},{9,11},{10,... | collective-permute-start | bytes 786440 | tf_op jit(solution)/shard_map/ppermute | solution.py:485
  19.9 12.1 %collective-permute-start.9 = (bf16[256,512]{1,0:T(8,128)(2,1)}, bf16[256,512]{1,0:T(8,128)(2,1)S(1)}, u32[]{:S(2)}, u32[]{:S(2)}) collective-permute-start(bf16[256,512]{1,0:T(8,128)(2,1)} %collective-permute-done.refs_2_), channel_id=1, source_target_pairs={{0,16},{4,20},{8,24},{12,28},{16,0},{20,4},{24,8},{28,12},{1,17},{... | collective-permute-start | bytes 786440 | tf_op jit(solution)/shard_map/ppermute | solution.py:482
  20.2 11.9 %collective-permute-start.8 = (bf16[256,512]{1,0:T(8,128)(2,1)}, bf16[256,512]{1,0:T(8,128)(2,1)S(1)}, u32[]{:S(2)}, u32[]{:S(2)}) collective-permute-start(bf16[256,512]{1,0:T(8,128)(2,1)} %collective-permute-done.refs_2_), channel_id=1, source_target_pairs={{0,8},{4,12},{8,0},{12,4},{16,24},{20,28},{24,16},{28,20},{1,9},{5... | collective-permute-start | bytes 786440 | tf_op jit(solution)/shard_map/ppermute | solution.py:482
  20.4 11.6 %collective-permute-start.7 = (bf16[256,512]{1,0:T(8,128)(2,1)}, bf16[256,512]{1,0:T(8,128)(2,1)S(1)}, u32[]{:S(2)}, u32[]{:S(2)}) collective-permute-start(bf16[256,512]{1,0:T(8,128)(2,1)} %collective-permute-done.1.refs_5_), channel_id=1, source_target_pairs={{0,16},{4,20},{8,24},{12,28},{16,0},{20,4},{24,8},{28,12},{1,17},{... | collective-permute-start | bytes 786440 | tf_op jit(solution)/shard_map/ppermute | solution.py:482
  21.6 10.4 %collective-permute-start.6 = (bf16[256,512]{1,0:T(8,128)(2,1)}, bf16[256,512]{1,0:T(8,128)(2,1)S(1)}, u32[]{:S(2)}, u32[]{:S(2)}) collective-permute-start(bf16[256,512]{1,0:T(8,128)(2,1)} %collective-permute-done.1.refs_5_), channel_id=1, source_target_pairs={{0,8},{4,12},{8,0},{12,4},{16,24},{20,28},{24,16},{28,20},{1,9},{5... | collective-permute-start | bytes 786440 | tf_op jit(solution)/shard_map/ppermute | solution.py:482
  32.1 9.9 %collective-permute-start.14 = (bf16[256,512]{1,0:T(8,128)(2,1)}, bf16[256,512]{1,0:T(8,128)(2,1)S(1)}, u32[]{:S(2)}, u32[]{:S(2)}) collective-permute-start(bf16[256,512]{1,0:T(8,128)(2,1)} %cut_weights.1), channel_id=1, source_target_pairs={{0,3},{1,2},{2,1},{3,0},{4,7},{5,6},{6,5},{7,4},{8,11},{9,10},{10,... | collective-permute-start | bytes 786440 | tf_op jit(solution)/shard_map/ppermute | solution.py:485
  33.7 13.7 %collective-permute-start.13 = (bf16[256,512]{1,0:T(8,128)(2,1)}, bf16[256,512]{1,0:T(8,128)(2,1)S(1)}, u32[]{:S(2)}, u32[]{:S(2)}) collective-permute-start(bf16[256,512]{1,0:T(8,128)(2,1)} %cut_weights.1), channel_id=1, source_target_pairs={{0,1},{1,0},{2,3},{3,2},{4,5},{5,4},{6,7},{7,6},{8,9},{9,8},{10,11... | collective-permute-start | bytes 786440 | tf_op jit(solution)/shard_map/ppermute | solution.py:485
  33.7 13.7 %collective-permute-start.12 = (bf16[256,512]{1,0:T(8,128)(2,1)S(1)}, bf16[256,512]{1,0:T(8,128)(2,1)S(1)}, u32[]{:S(2)}, u32[]{:S(2)}) collective-permute-start(bf16[256,512]{1,0:T(8,128)(2,1)S(1)} %collective-permute-done.5.refs_2_), channel_id=1, source_target_pairs={{0,16},{4,20},{8,24},{12,28},{16,0},{20,4},{24,8},{28,12},{1,17},{... | collective-permute-start | bytes 786440 | tf_op jit(solution)/shard_map/ppermute | solution.py:482
  34.5 12.9 %collective-permute-start.11 = (bf16[256,512]{1,0:T(8,128)(2,1)S(1)}, bf16[256,512]{1,0:T(8,128)(2,1)S(1)}, u32[]{:S(2)}, u32[]{:S(2)}) collective-permute-start(bf16[256,512]{1,0:T(8,128)(2,1)S(1)} %collective-permute-done.5.refs_2_), channel_id=1, source_target_pairs={{0,8},{4,12},{8,0},{12,4},{16,24},{20,28},{24,16},{28,20},{1,9},{5... | collective-permute-start | bytes 786440 | tf_op jit(solution)/shard_map/ppermute | solution.py:482
  34.7 12.7 %collective-permute-start.10 = (bf16[256,512]{1,0:T(8,128)(2,1)S(1)}, bf16[256,512]{1,0:T(8,128)(2,1)S(1)}, u32[]{:S(2)}, u32[]{:S(2)}) collective-permute-start(bf16[256,512]{1,0:T(8,128)(2,1)S(1)} %collective-permute-done.5.refs_2_), channel_id=1, source_target_pairs={{0,24},{4,28},{8,16},{12,20},{16,8},{20,12},{24,0},{28,4},{1,25},{... | collective-permute-start | bytes 786440 | tf_op jit(solution)/shard_map/ppermute | solution.py:482
  36.4 1.6 %copy-start.3 = (bf16[1,256,4096]{2,1,0:T(8,128)(2,1)S(1)}, bf16[1,256,4096]{2,1,0:T(8,128)(2,1)}, u32[]{:S(2)}) copy-start(bf16[1,256,4096]{2,1,0:T(8,128)(2,1)} %param.6) | copy-start | bytes 6291460
  47.4 4.8 %copy-start = (bf16[1,256,2048]{2,1,0:T(8,128)(2,1)S(1)}, bf16[1,256,2048]{2,1,0:T(8,128)(2,1)}, u32[]{:S(2)}) copy-start(bf16[1,256,2048]{2,1,0:T(8,128)(2,1)} %param.9) | copy-start | bytes 3145732
  47.4 4.8 %copy-start.5 = (s32[1,256]{1,0:T(1,128)S(1)}, s32[1,256]{1,0:T(1,128)}, u32[]{:S(2)}) copy-start(s32[1,256]{1,0:T(1,128)} %marks_a) | copy-start | bytes 3076
  49.6 13.5 %collective-permute-start.16 = (bf16[512,512]{1,0:T(8,128)(2,1)S(1)}, bf16[512,512]{1,0:T(8,128)(2,1)S(1)}, u32[]{:S(2)}, u32[]{:S(2)}) collective-permute-start(bf16[512,512]{1,0:T(8,128)(2,1)S(1)} %get-tuple-element.62.refs_0_), channel_id=1, source_target_pairs={{0,16},{4,20},{8,24},{12,28},{1,17},{5,21},{9,25},{13,29},{2,18},{... | collective-permute-start | bytes 1572872 | tf_op jit(solution)/shard_map/ppermute | solution.py:482
  50.9 13.5 %collective-permute-start.15 = (bf16[512,512]{1,0:T(8,128)(2,1)S(1)}, bf16[512,512]{1,0:T(8,128)(2,1)S(1)}, u32[]{:S(2)}, u32[]{:S(2)}) collective-permute-start(bf16[512,512]{1,0:T(8,128)(2,1)S(1)} %get-tuple-element.62.refs_0_), channel_id=1, source_target_pairs={{0,8},{4,12},{8,0},{12,4},{16,24},{20,28},{1,9},{5,13},{9,1},{13,5... | collective-permute-start | bytes 1572872 | tf_op jit(solution)/shard_map/ppermute | solution.py:482
  64.5 9.8 %collective-permute-start.17 = (bf16[256,512]{1,0:T(8,128)(2,1)S(1)}, bf16[256,512]{1,0:T(8,128)(2,1)S(1)}, u32[]{:S(2)}, u32[]{:S(2)}) collective-permute-start(bf16[256,512]{1,0:T(8,128)(2,1)S(1)} %slice.6), channel_id=1, source_target_pairs={{0,16},{4,20},{8,24},{12,28},{1,17},{5,21},{9,25},{13,29},{2,18},{... | collective-permute-start | bytes 786440 | tf_op jit(solution)/shard_map/ppermute | solution.py:482
  65.8 8.5 %collective-permute-start.18 = (bf16[256,512]{1,0:T(8,128)(2,1)S(1)}, bf16[256,512]{1,0:T(8,128)(2,1)S(1)}, u32[]{:S(2)}, u32[]{:S(2)}) collective-permute-start(bf16[256,512]{1,0:T(8,128)(2,1)S(1)} %slice.7), channel_id=1, source_target_pairs={{16,24},{20,28},{24,16},{28,20},{17,25},{21,29},{25,17},{29,21},{1... | collective-permute-start | bytes 786440 | tf_op jit(solution)/shard_map/ppermute | solution.py:482
  76.6 5.2 %collective-permute-start.20 = (bf16[256,512]{1,0:T(8,128)(2,1)S(1)}, bf16[256,512]{1,0:T(8,128)(2,1)S(1)}, u32[]{:S(2)}, u32[]{:S(2)}) collective-permute-start(bf16[256,512]{1,0:T(8,128)(2,1)S(1)} %get-tuple-element.80), channel_id=1, source_target_pairs={{0,4},{4,0},{8,12},{12,8},{16,20},{20,16},{24,28},{28,24},{1,5},{5... | collective-permute-start | bytes 786440 | tf_op jit(solution)/shard_map/ppermute | solution.py:477
  81.8 1.6 %collective-permute-start.19 = (bf16[256,512]{1,0:T(8,128)(2,1)S(1)}, bf16[256,512]{1,0:T(8,128)(2,1)S(1)}, u32[]{:S(2)}, u32[]{:S(2)}) collective-permute-start(bf16[256,512]{1,0:T(8,128)(2,1)S(1)} %get-tuple-element.77), channel_id=1, source_target_pairs={{0,4},{4,0},{8,12},{12,8},{16,20},{20,16},{24,28},{28,24},{1,5},{5... | collective-permute-start | bytes 786440 | tf_op jit(solution)/shard_map/ppermute | solution.py:477

commit v8 on v7

--- a/solution.py
+++ b/solution.py
@@ -436,10 +436,10 @@
     out, sem = refs[-2:]
     half = out.shape[1] // 2
     copies = []
-    for part, (received, number) in zip(refs, places):
+    for part, (received, begin) in zip(refs, places):
         side = 1 - where[0] if received else where[0]
         width = part.shape[1]
-        columns = pl.ds(pl.multiple_of(side * half + number * width, HEAD_DIM), width)
+        columns = pl.ds(pl.multiple_of(side * half + begin, HEAD_DIM), width)
         copies.append(pltpu.make_async_copy(part, out.at[:, columns], sem.at[len(copies)]))
     run_copies(copies)
 
@@ -557,16 +557,18 @@
                 running = attend_later(where, query_rows, parts, (flip,), running, groups)
         last_parts = parts
     kept, received = [], []
-    for first in range(0, heads, groups):
+    middle_head = 3 * heads // 4
+    for first, end in ((0, middle_head), (middle_head, heads)):
         own, other = attend_last(
-            where, query_rows, last_parts, chips - 1, running, range(first, first + groups), groups
+            where, query_rows, last_parts, chips - 1, running, range(first, end), groups
         )
         kept.append(own)
         received.append(swap_cores(other))
     parts = kept + received[:-1]
-    places = [(False, i) for i in range(len(kept))] + [(True, i) for i in range(len(received) - 1)]
+    begin = middle_head * HEAD_DIM
+    places = [(False, 0), (False, begin), (True, 0)]
     output = place_heads(where, parts, places, query_own.shape)
-    output = place_heads(where, received[-1:], [(True, len(received) - 1)], query_own.shape, output)
+    output = place_heads(where, received[-1:], [(True, begin)], query_own.shape, output)
     return output[None]
 
 

time: 85.1 us -> 85 us (level)
  transfers between devices with their start and end apart: 21 -> 21, of which waited for: 6 -> 5; matrix products, arithmetic and copies ran while one was open for 8% -> 8% of each run, Pallas kernels for 24% -> 24%
where the time goes in v8:
time: 85 us; the launch traced here: 84.7 us
  waiting for transfers between devices  27.4 us (32%)
  Pallas kernels  26.3 us (31%)
  starting transfers between devices  22.4 us (26%)
  other arithmetic  4.58 us (5%)
  local copies, waits for them, and re-layouts  3.5 us (4%)
    ppermute x5, waiting for transfers between devices, to_shard(): lax.ppermute(array, 'fsdp', [(s, s ^ flip) for s in range(fsdp_size)])  19.1 us
    ppermute x11, starting transfers between devices, to_chip(): return lax.ppermute(array, 'seq', pairs)  11.4 us
    ppermute x11, waiting for transfers between devices, to_chip(): return lax.ppermute(array, 'seq', pairs)  8.32 us
    pallas_call x1, Pallas kernels, attend_later(): kernel_call(functools.partial(later_kernel, groups, flips), 'attend_later...  6.57 us
    ppermute x5, starting transfers between devices, to_shard(): lax.ppermute(array, 'fsdp', [(s, s ^ flip) for s in range(fsdp_size)])  6.42 us
    ppermute x5, starting transfers between devices, swap_cores(): return lax.ppermute(array, 'seq', [(s, s ^ 1) for s in range(seq_size)])  4.63 us
    pallas_call x2, Pallas kernels, attend_last(): kernel_call(functools.partial(last_kernel, heads, groups, count, flip), '...  4.57 us
    pallas_call x1, Pallas kernels, project_partial(): kernel_call(functools.partial(partial_kernel, kinds, final_kinds, len(arr...  3.98 us
  transfers between devices with their start and end apart: 21, of which 5 were waited for; matrix products, arithmetic and copies ran while one was open for 8% of the time, Pallas kernels for 24%

profile of v8, /device:TPU:7, one launch (start us, length us, event | category | flops | bytes accessed | tf_op | source)
XLA Modules:
  0.0 84.7 jit_solution(15577717468140682412)
XLA Ops:
  0.0 0.7 collective-permute-start.2
  0.7 0.0 collective-permute-start.3
  0.7 0.9 %dynamic_slice.6 = bf16[256,256]{1,0:T(8,128)(2,1)S(1)} dynamic-slice(bf16[1024,512]{1,0:T(8,128)(2,1)} %refs_0_.1, s32[]{:T(128)S(6)} %select_n.14, s32[]{:T(128)S(6)} %select_n.15), dynamic_slice_sizes={256,256} | dynamic-slice | bytes 262148 | tf_op jit(solution)/shard_map/dynamic_slice | solution.py:495
  1.6 0.9 %dynamic_slice.7 = bf16[256,256]{1,0:T(8,128)(2,1)S(1)} dynamic-slice(bf16[1024,512]{1,0:T(8,128)(2,1)} %refs_1_.1, s32[]{:T(128)S(6)} %select_n.14, s32[]{:T(128)S(6)} %select_n.15), dynamic_slice_sizes={256,256} | dynamic-slice | bytes 262148 | tf_op jit(solution)/shard_map/dynamic_slice | solution.py:495
  2.5 0.7 pad_maximum_fusion
  3.2 1.3 %collective-permute-start.1 = (bf16[256,512]{1,0:T(8,128)(2,1)}, bf16[256,512]{1,0:T(8,128)(2,1)}, u32[]{:S(2)}, u32[]{:S(2)}) collective-permute-start(bf16[256,512]{1,0:T(8,128)(2,1)} %pad_maximum_fusion), channel_id=1, source_target_pairs={{0,1},{1,0},{2,3},{3,2},{4,5},{5,4},{6,7},{7,6},{8,9},{9,8},{10,11... | collective-permute-start | bytes 786440 | tf_op jit(solution)/shard_map/ppermute | solution.py:485
  4.5 2.2 %collective-permute-start = (bf16[256,512]{1,0:T(8,128)(2,1)}, bf16[256,512]{1,0:T(8,128)(2,1)}, u32[]{:S(2)}, u32[]{:S(2)}) collective-permute-start(bf16[256,512]{1,0:T(8,128)(2,1)} %pad_maximum_fusion), channel_id=1, source_target_pairs={{0,3},{1,2},{2,1},{3,0},{4,7},{5,6},{6,5},{7,4},{8,11},{9,10},{10,... | collective-permute-start | bytes 786440 | tf_op jit(solution)/shard_map/ppermute | solution.py:485
  6.7 1.1 %collective-permute-start.4 = (s32[1,256]{1,0:T(1,128)}, s32[1,256]{1,0:T(1,128)S(1)}, u32[]{:S(2)}, u32[]{:S(2)}) collective-permute-start(s32[1,256]{1,0:T(1,128)} %marks_a), channel_id=1, source_target_pairs={{0,4},{4,0},{8,12},{12,8},{16,20},{20,16},{24,28},{28,24},{1,5},{5... | collective-permute-start | bytes 3080 | tf_op jit(solution)/shard_map/ppermute | solution.py:477
  7.8 0.0 copy-start.6
  7.8 1.8 %fusion = (f32[512,64]{1,0:T(8,128)}, f32[512,64]{1,0:T(8,128)}, f32[512,64]{1,0:T(8,128)S(1)}) fusion(f32[64]{0:T(128)S(1)} %negate_power_fusion, f32[512]{0:T(512)S(1)} %add_convert_fusion), kind=kLoop, calls=%fused_computation.5 | loop fusion | flops 65536 | bytes 395520 | tf_op jit(solution)/shard_map/neg | solution.py:54
  9.7 0.1 pad_maximum_fusion.1.refs_8_.cos_ref
  9.8 1.3 %pad_maximum_fusion.2.refs_9_.sin_ref = f32[512,128]{1,0:T(8,128)S(1)} fusion(f32[512,64]{1,0:T(8,128)} %get-tuple-element.82, f32[512,64]{1,0:T(8,128)} %get-tuple-element.81), kind=kLoop, calls=%fused_computation.4 | loop fusion | flops 65536 | bytes 524288 | tf_op jit(solution)/shard_map/concatenate | solution.py:54
  11.1 0.6 pad_add_fusion.where
  11.7 2.5 %cut_weights.1 = bf16[256,512]{1,0:T(8,128)(2,1)} custom-call(s32[3]{0:T(128)} %pad_add_fusion.where, bf16[1024,512]{1,0:T(8,128)(2,1)} %refs_0_.1, bf16[1024,512]{1,0:T(8,128)(2,1)} %refs_1_.1), custom_call_target="tpu_custom_call" | custom-call | tf_op jit(solution)/shard_map/cut_weights/pallas_call | solution.py:83
  14.2 0.0 collective-permute-done.4.marks_b
  14.2 0.0 collective-permute-done.1.refs_5_
  14.2 4.4 %collective-permute-done.refs_2_ = bf16[256,512]{1,0:T(8,128)(2,1)} collective-permute-done((bf16[256,512]{1,0:T(8,128)(2,1)}, bf16[256,512]{1,0:T(8,128)(2,1)}, u32[]{:S(2)}, u32[]{:S(2)}) %collective-permute-start) | collective-permute-done | bytes 262176 | tf_op jit(solution)/shard_map/ppermute | solution.py:485
  18.6 0.0 collective-permute-done.3.q_b
  18.6 0.0 collective-permute-done.2.other
  18.6 0.0 copy-done.6
  18.6 1.3 %collective-permute-start.5 = (bf16[256,512]{1,0:T(8,128)(2,1)}, bf16[256,512]{1,0:T(8,128)(2,1)S(1)}, u32[]{:S(2)}, u32[]{:S(2)}) collective-permute-start(bf16[256,512]{1,0:T(8,128)(2,1)} %pad_maximum_fusion), channel_id=1, source_target_pairs={{0,2},{1,3},{2,0},{3,1},{4,6},{5,7},{6,4},{7,5},{8,10},{9,11},{10,... | collective-permute-start | bytes 786440 | tf_op jit(solution)/shard_map/ppermute | solution.py:485
  19.9 0.2 collective-permute-start.9
  20.2 0.3 collective-permute-start.8
  20.4 1.2 %collective-permute-start.7 = (bf16[256,512]{1,0:T(8,128)(2,1)}, bf16[256,512]{1,0:T(8,128)(2,1)S(1)}, u32[]{:S(2)}, u32[]{:S(2)}) collective-permute-start(bf16[256,512]{1,0:T(8,128)(2,1)} %collective-permute-done.1.refs_5_), channel_id=1, source_target_pairs={{0,16},{4,20},{8,24},{12,28},{16,0},{20,4},{24,8},{28,12},{1,17},{... | collective-permute-start | bytes 786440 | tf_op jit(solution)/shard_map/ppermute | solution.py:482
  21.6 1.2 %collective-permute-start.6 = (bf16[256,512]{1,0:T(8,128)(2,1)}, bf16[256,512]{1,0:T(8,128)(2,1)S(1)}, u32[]{:S(2)}, u32[]{:S(2)}) collective-permute-start(bf16[256,512]{1,0:T(8,128)(2,1)} %collective-permute-done.1.refs_5_), channel_id=1, source_target_pairs={{0,8},{4,12},{8,0},{12,4},{16,24},{20,28},{24,16},{28,20},{1,9},{5... | collective-permute-start | bytes 786440 | tf_op jit(solution)/shard_map/ppermute | solution.py:482
  22.9 9.2 %collective-permute-done.5.refs_2_ = bf16[256,512]{1,0:T(8,128)(2,1)S(1)} collective-permute-done((bf16[256,512]{1,0:T(8,128)(2,1)}, bf16[256,512]{1,0:T(8,128)(2,1)S(1)}, u32[]{:S(2)}, u32[]{:S(2)}) %collective-permute-start.5) | collective-permute-done | bytes 262176 | tf_op jit(solution)/shard_map/ppermute | solution.py:485
  32.0 0.0 collective-permute-done.9.refs_4_
  32.0 0.0 collective-permute-done.8.refs_3_
  32.0 0.0 collective-permute-done.7.refs_7_
  32.0 0.0 collective-permute-done.6.refs_6_
  32.1 1.6 %collective-permute-start.14 = (bf16[256,512]{1,0:T(8,128)(2,1)}, bf16[256,512]{1,0:T(8,128)(2,1)S(1)}, u32[]{:S(2)}, u32[]{:S(2)}) collective-permute-start(bf16[256,512]{1,0:T(8,128)(2,1)} %cut_weights.1), channel_id=1, source_target_pairs={{0,3},{1,2},{2,1},{3,0},{4,7},{5,6},{6,5},{7,4},{8,11},{9,10},{10,... | collective-permute-start | bytes 786440 | tf_op jit(solution)/shard_map/ppermute | solution.py:485
  33.7 0.0 collective-permute-start.13
  33.7 0.8 collective-permute-start.12
  34.5 0.3 collective-permute-start.11
  34.7 1.6 %collective-permute-start.10 = (bf16[256,512]{1,0:T(8,128)(2,1)S(1)}, bf16[256,512]{1,0:T(8,128)(2,1)S(1)}, u32[]{:S(2)}, u32[]{:S(2)}) collective-permute-start(bf16[256,512]{1,0:T(8,128)(2,1)S(1)} %collective-permute-done.5.refs_2_), channel_id=1, source_target_pairs={{0,24},{4,28},{8,16},{12,20},{16,8},{20,12},{24,0},{28,4},{1,25},{... | collective-permute-start | bytes 786440 | tf_op jit(solution)/shard_map/ppermute | solution.py:482
  36.4 0.0 copy-done.4
  36.4 1.6 %copy-done.3 = bf16[1,256,4096]{2,1,0:T(8,128)(2,1)S(1)} copy-done((bf16[1,256,4096]{2,1,0:T(8,128)(2,1)S(1)}, bf16[1,256,4096]{2,1,0:T(8,128)(2,1)}, u32[]{:S(2)}) %copy-start.3) | copy-done | bytes 2097176
  38.0 4.0 %project_partial.1 = (f32[528,512]{1,0:T(8,128)S(1)}, bf16[528,1536]{1,0:T(8,128)(2,1)S(1)}) custom-call(s32[3]{0:T(128)S(1)} %copy-done.4, bf16[256,4096]{1,0:T(8,128)(2,1)S(1)} %bitcast.12, bf16[256,4096]{1,0:T(8,128)(2,1)} %collective-permute-done.2.other, bf16[16,4096]{1,0:T(8,128)(2,1)S(1)} %broadcast_in_dim.4.masks, bf16[1024,512]{1,0:T(8,128)(2,1)S(1)} %copy-done.1, ...), custom_call_target="tpu_custom_call" | custom-call | flops 1384120320 | tf_op jit(solution)/shard_map/project_partial/pallas_call | solution.py:203
  41.9 0.0 collective-permute-done.14.refs_7_
  42.0 5.5 %collective-permute-done.13.refs_6_ = bf16[256,512]{1,0:T(8,128)(2,1)S(1)} collective-permute-done((bf16[256,512]{1,0:T(8,128)(2,1)}, bf16[256,512]{1,0:T(8,128)(2,1)S(1)}, u32[]{:S(2)}, u32[]{:S(2)}) %collective-permute-start.13) | collective-permute-done | bytes 262176 | tf_op jit(solution)/shard_map/ppermute | solution.py:485
  47.4 0.0 collective-permute-done.12.refs_5_
  47.4 0.0 collective-permute-done.11.refs_4_
  47.4 0.0 collective-permute-done.10.refs_3_
  47.4 0.0 copy-start
  47.4 0.0 copy-start.5
  47.5 2.2 %project_finish.1 = (bf16[512,512]{1,0:T(8,128)(2,1)S(1)}, f32[8,512]{1,0:T(8,128)S(1)}) custom-call(s32[3]{0:T(128)S(1)} %copy-done.4, f32[528,512]{1,0:T(8,128)S(1)} %get-tuple-element.56.refs_0_, bf16[528,1536]{1,0:T(8,128)(2,1)S(1)} %get-tuple-element.57.refs_1_, bf16[256,512]{1,0:T(8,128)(2,1)S(1)} %collective-permute-done.5.refs_2_, ...), custom_call_target="tpu_custom_call" | custom-call | flops 830472192 | tf_op jit(solution)/shard_map/project_finish/pallas_call | solution.py:226
  49.6 1.3 %collective-permute-start.16 = (bf16[512,512]{1,0:T(8,128)(2,1)S(1)}, bf16[512,512]{1,0:T(8,128)(2,1)S(1)}, u32[]{:S(2)}, u32[]{:S(2)}) collective-permute-start(bf16[512,512]{1,0:T(8,128)(2,1)S(1)} %get-tuple-element.62.refs_0_), channel_id=1, source_target_pairs={{0,16},{4,20},{8,24},{12,28},{1,17},{5,21},{9,25},{13,29},{2,18},{... | collective-permute-start | bytes 1572872 | tf_op jit(solution)/shard_map/ppermute | solution.py:482
  50.9 1.3 %collective-permute-start.15 = (bf16[512,512]{1,0:T(8,128)(2,1)S(1)}, bf16[512,512]{1,0:T(8,128)(2,1)S(1)}, u32[]{:S(2)}, u32[]{:S(2)}) collective-permute-start(bf16[512,512]{1,0:T(8,128)(2,1)S(1)} %get-tuple-element.62.refs_0_), channel_id=1, source_target_pairs={{0,8},{4,12},{8,0},{12,4},{16,24},{20,28},{1,9},{5,13},{9,1},{13,5... | collective-permute-start | bytes 1572872 | tf_op jit(solution)/shard_map/ppermute | solution.py:482
  52.2 3.9 %attend_own.1 = (f32[8,512,128]{2,1,0:T(8,128)S(1)}, f32[8,512,128]{2,1,0:T(8,128)S(1)}, f32[8,512,128]{2,1,0:T(8,128)S(1)}) custom-call(s32[3]{0:T(128)S(1)} %copy-done.4, bf16[256,2048]{1,0:T(8,128)(2,1)S(1)} %bitcast.7, bf16[256,2048]{1,0:T(8,128)(2,1)S(1)} %collective-permute-done.3.q_b, f32[512,128]{1,0:T(8,128)S(1)} %pad_maximum_fusion.1.refs_8_.cos_ref, ...), custom_call_target="tpu_custom_call" | custom-call | flops 1073741824 | tf_op jit(solution)/shard_map/attend_own/pallas_call | solution.py:336
  56.1 7.0 %collective-permute-done.16.refs_1_ = bf16[512,512]{1,0:T(8,128)(2,1)S(1)} collective-permute-done((bf16[512,512]{1,0:T(8,128)(2,1)S(1)}, bf16[512,512]{1,0:T(8,128)(2,1)S(1)}, u32[]{:S(2)}, u32[]{:S(2)}) %collective-permute-start.16) | collective-permute-done | bytes 524320 | tf_op jit(solution)/shard_map/ppermute | solution.py:482
  63.1 1.3 %collective-permute-done.15.refs_0_ = bf16[512,512]{1,0:T(8,128)(2,1)S(1)} collective-permute-done((bf16[512,512]{1,0:T(8,128)(2,1)S(1)}, bf16[512,512]{1,0:T(8,128)(2,1)S(1)}, u32[]{:S(2)}, u32[]{:S(2)}) %collective-permute-start.15) | collective-permute-done | bytes 524320 | tf_op jit(solution)/shard_map/ppermute | solution.py:482
  64.5 1.3 %collective-permute-start.17 = (bf16[256,512]{1,0:T(8,128)(2,1)S(1)}, bf16[256,512]{1,0:T(8,128)(2,1)S(1)}, u32[]{:S(2)}, u32[]{:S(2)}) collective-permute-start(bf16[256,512]{1,0:T(8,128)(2,1)S(1)} %slice.6), channel_id=1, source_target_pairs={{0,16},{4,20},{8,24},{12,28},{1,17},{5,21},{9,25},{13,29},{2,18},{... | collective-permute-start | bytes 786440 | tf_op jit(solution)/shard_map/ppermute | solution.py:482
  65.8 1.9 %collective-permute-start.18 = (bf16[256,512]{1,0:T(8,128)(2,1)S(1)}, bf16[256,512]{1,0:T(8,128)(2,1)S(1)}, u32[]{:S(2)}, u32[]{:S(2)}) collective-permute-start(bf16[256,512]{1,0:T(8,128)(2,1)S(1)} %slice.7), channel_id=1, source_target_pairs={{16,24},{20,28},{24,16},{28,20},{17,25},{21,29},{25,17},{29,21},{1... | collective-permute-start | bytes 786440 | tf_op jit(solution)/shard_map/ppermute | solution.py:482
  67.7 6.6 %attend_later.1 = (f32[8,512,128]{2,1,0:T(8,128)S(1)}, f32[8,512,128]{2,1,0:T(8,128)S(1)}, f32[8,512,128]{2,1,0:T(8,128)S(1)}) custom-call(s32[3]{0:T(128)S(1)} %copy-done.4, bf16[256,2048]{1,0:T(8,128)(2,1)S(1)} %bitcast.8, bf16[256,2048]{1,0:T(8,128)(2,1)S(1)} %collective-permute-done.3.q_b, ...), custom_call_target="tpu_custom_call", output_to_operand_aliasing={{0}: (5, {}), {1}: (6, {}), {2}: (7, {})} | custom-call | flops 2147483648 | tf_op jit(solution)/shard_map/attend_later/pallas_call | solution.py:387
  74.3 0.0 collective-permute-done.17.refs_0_
  74.3 0.0 collective-permute-done.18.refs_1_
  74.3 3.0 %attend_last.3 = (bf16[256,768]{1,0:T(8,128)(2,1)S(1)}, bf16[256,768]{1,0:T(8,128)(2,1)S(1)}) custom-call(s32[3]{0:T(128)S(1)} %copy-done.4, bf16[256,2048]{1,0:T(8,128)(2,1)S(1)} %bitcast.9, bf16[256,2048]{1,0:T(8,128)(2,1)S(1)} %collective-permute-done.3.q_b, bf16[256,512]{1,0:T(8,128)(2,1)S(1)} %collective-permute-done.17.refs_0_, ...), custom_call_target="tpu_custom_call" | custom-call | flops 805306368 | tf_op jit(solution)/shard_map/attend_last/pallas_call | solution.py:425
  77.3 2.8 %collective-permute-start.20 = (bf16[256,768]{1,0:T(8,128)(2,1)S(1)}, bf16[256,768]{1,0:T(8,128)(2,1)S(1)}, u32[]{:S(2)}, u32[]{:S(2)}) collective-permute-start(bf16[256,768]{1,0:T(8,128)(2,1)S(1)} %get-tuple-element.80), channel_id=1, source_target_pairs={{0,4},{4,0},{8,12},{12,8},{16,20},{20,16},{24,28},{28,24},{1,5},{5... | collective-permute-start | bytes 1179656 | tf_op jit(solution)/shard_map/ppermute | solution.py:477
  80.1 1.6 %attend_last.2 = (bf16[256,256]{1,0:T(8,128)(2,1)S(1)}, bf16[256,256]{1,0:T(8,128)(2,1)S(1)}) custom-call(s32[3]{0:T(128)S(1)} %copy-done.4, bf16[256,2048]{1,0:T(8,128)(2,1)S(1)} %bitcast.10, bf16[256,2048]{1,0:T(8,128)(2,1)S(1)} %collective-permute-done.3.q_b, bf16[256,512]{1,0:T(8,128)(2,1)S(1)} %collective-permute-done.17.refs_0_, ...), custom_call_target="tpu_custom_call" | custom-call | flops 268435456 | tf_op jit(solution)/shard_map/attend_last/pallas_call | solution.py:425
  81.7 0.1 collective-permute-start.19
  81.8 0.0 collective-permute-done.20.refs_2_
  81.8 1.5 %place_heads.2.refs_1_ = bf16[256,2048]{1,0:T(8,128)(2,1)} custom-call(s32[3]{0:T(128)S(1)} %copy-done.4, bf16[256,768]{1,0:T(8,128)(2,1)S(1)} %get-tuple-element.78.refs_0_, bf16[256,256]{1,0:T(8,128)(2,1)S(1)} %get-tuple-element.79.refs_1_, bf16[256,768]{1,0:T(8,128)(2,1)S(1)} %collective-permute-done.20.refs_2_), custom_call_target="tpu_custom_call" | custom-call | tf_op jit(solution)/shard_map/place_heads/pallas_call | solution.py:449
  83.3 0.0 collective-permute-done.19.refs_0_
  83.3 1.2 %place_heads.3 = bf16[256,2048]{1,0:T(8,128)(2,1)} custom-call(s32[3]{0:T(128)S(1)} %copy-done.4, bf16[256,256]{1,0:T(8,128)(2,1)S(1)} %collective-permute-done.19.refs_0_, bf16[256,2048]{1,0:T(8,128)(2,1)} %place_heads.2.refs_1_), custom_call_target="tpu_custom_call", output_to_operand_aliasing={{}: (2, {})} | custom-call | tf_op jit(solution)/shard_map/place_heads/pallas_call | solution.py:449
  (14 shorter events, 0.1 us)
Async XLA Ops:
  0.0 18.6 %collective-permute-start.2 = (bf16[256,4096]{1,0:T(8,128)(2,1)}, bf16[256,4096]{1,0:T(8,128)(2,1)}, u32[]{:S(2)}, u32[]{:S(2)}) collective-permute-start(bf16[256,4096]{1,0:T(8,128)(2,1)} %bitcast.11), channel_id=1, source_target_pairs={{0,4},{4,0},{8,12},{12,8},{16,20},{20,16},{24,28},{28,24},{1,5},{5... | collective-permute-start | bytes 6291464 | tf_op jit(solution)/shard_map/ppermute | solution.py:477
  0.7 17.9 %collective-permute-start.3 = (bf16[256,2048]{1,0:T(8,128)(2,1)}, bf16[256,2048]{1,0:T(8,128)(2,1)S(1)}, u32[]{:S(2)}, u32[]{:S(2)}) collective-permute-start(bf16[256,2048]{1,0:T(8,128)(2,1)} %bitcast.6), channel_id=1, source_target_pairs={{0,4},{4,0},{8,12},{12,8},{16,20},{20,16},{24,28},{28,24},{1,5},{5... | collective-permute-start | bytes 3145736 | tf_op jit(solution)/shard_map/ppermute | solution.py:477
  3.2 10.9 %collective-permute-start.1 = (bf16[256,512]{1,0:T(8,128)(2,1)}, bf16[256,512]{1,0:T(8,128)(2,1)}, u32[]{:S(2)}, u32[]{:S(2)}) collective-permute-start(bf16[256,512]{1,0:T(8,128)(2,1)} %pad_maximum_fusion), channel_id=1, source_target_pairs={{0,1},{1,0},{2,3},{3,2},{4,5},{5,4},{6,7},{7,6},{8,9},{9,8},{10,11... | collective-permute-start | bytes 786440 | tf_op jit(solution)/shard_map/ppermute | solution.py:485
  4.5 14.1 %collective-permute-start = (bf16[256,512]{1,0:T(8,128)(2,1)}, bf16[256,512]{1,0:T(8,128)(2,1)}, u32[]{:S(2)}, u32[]{:S(2)}) collective-permute-start(bf16[256,512]{1,0:T(8,128)(2,1)} %pad_maximum_fusion), channel_id=1, source_target_pairs={{0,3},{1,2},{2,1},{3,0},{4,7},{5,6},{6,5},{7,4},{8,11},{9,10},{10,... | collective-permute-start | bytes 786440 | tf_op jit(solution)/shard_map/ppermute | solution.py:485
  6.7 7.4 %collective-permute-start.4 = (s32[1,256]{1,0:T(1,128)}, s32[1,256]{1,0:T(1,128)S(1)}, u32[]{:S(2)}, u32[]{:S(2)}) collective-permute-start(s32[1,256]{1,0:T(1,128)} %marks_a), channel_id=1, source_target_pairs={{0,4},{4,0},{8,12},{12,8},{16,20},{20,16},{24,28},{28,24},{1,5},{5... | collective-permute-start | bytes 3080 | tf_op jit(solution)/shard_map/ppermute | solution.py:477
  7.8 10.8 %copy-start.6 = (bf16[4096]{0:T(1024)(128)(2,1)S(1)}, bf16[4096]{0:T(1024)(128)(2,1)}, u32[]{:S(2)}) copy-start(bf16[4096]{0:T(1024)(128)(2,1)} %param.8) | copy-start | bytes 24580
  9.7 26.7 %copy-start.1 = (bf16[1024,512]{1,0:T(8,128)(2,1)S(1)}, bf16[1024,512]{1,0:T(8,128)(2,1)}, u32[]{:S(2)}) copy-start(bf16[1024,512]{1,0:T(8,128)(2,1)} %refs_0_.1) | copy-start | bytes 3145732
  9.7 26.7 %copy-start.2 = (bf16[1024,512]{1,0:T(8,128)(2,1)S(1)}, bf16[1024,512]{1,0:T(8,128)(2,1)}, u32[]{:S(2)}) copy-start(bf16[1024,512]{1,0:T(8,128)(2,1)} %refs_1_.1) | copy-start | bytes 3145732
  11.7 24.7 %copy-start.4 = (s32[3]{0:T(128)S(1)}, s32[3]{0:T(128)}, u32[]{:S(2)}) copy-start(s32[3]{0:T(128)} %pad_add_fusion.where) | copy-start | bytes 40
  18.6 13.4 %collective-permute-start.5 = (bf16[256,512]{1,0:T(8,128)(2,1)}, bf16[256,512]{1,0:T(8,128)(2,1)S(1)}, u32[]{:S(2)}, u32[]{:S(2)}) collective-permute-start(bf16[256,512]{1,0:T(8,128)(2,1)} %pad_maximum_fusion), channel_id=1, source_target_pairs={{0,2},{1,3},{2,0},{3,1},{4,6},{5,7},{6,4},{7,5},{8,10},{9,11},{10,... | collective-permute-start | bytes 786440 | tf_op jit(solution)/shard_map/ppermute | solution.py:485
  19.9 12.1 %collective-permute-start.9 = (bf16[256,512]{1,0:T(8,128)(2,1)}, bf16[256,512]{1,0:T(8,128)(2,1)S(1)}, u32[]{:S(2)}, u32[]{:S(2)}) collective-permute-start(bf16[256,512]{1,0:T(8,128)(2,1)} %collective-permute-done.refs_2_), channel_id=1, source_target_pairs={{0,16},{4,20},{8,24},{12,28},{16,0},{20,4},{24,8},{28,12},{1,17},{... | collective-permute-start | bytes 786440 | tf_op jit(solution)/shard_map/ppermute | solution.py:482
  20.2 11.9 %collective-permute-start.8 = (bf16[256,512]{1,0:T(8,128)(2,1)}, bf16[256,512]{1,0:T(8,128)(2,1)S(1)}, u32[]{:S(2)}, u32[]{:S(2)}) collective-permute-start(bf16[256,512]{1,0:T(8,128)(2,1)} %collective-permute-done.refs_2_), channel_id=1, source_target_pairs={{0,8},{4,12},{8,0},{12,4},{16,24},{20,28},{24,16},{28,20},{1,9},{5... | collective-permute-start | bytes 786440 | tf_op jit(solution)/shard_map/ppermute | solution.py:482
  20.4 11.6 %collective-permute-start.7 = (bf16[256,512]{1,0:T(8,128)(2,1)}, bf16[256,512]{1,0:T(8,128)(2,1)S(1)}, u32[]{:S(2)}, u32[]{:S(2)}) collective-permute-start(bf16[256,512]{1,0:T(8,128)(2,1)} %collective-permute-done.1.refs_5_), channel_id=1, source_target_pairs={{0,16},{4,20},{8,24},{12,28},{16,0},{20,4},{24,8},{28,12},{1,17},{... | collective-permute-start | bytes 786440 | tf_op jit(solution)/shard_map/ppermute | solution.py:482
  21.6 10.4 %collective-permute-start.6 = (bf16[256,512]{1,0:T(8,128)(2,1)}, bf16[256,512]{1,0:T(8,128)(2,1)S(1)}, u32[]{:S(2)}, u32[]{:S(2)}) collective-permute-start(bf16[256,512]{1,0:T(8,128)(2,1)} %collective-permute-done.1.refs_5_), channel_id=1, source_target_pairs={{0,8},{4,12},{8,0},{12,4},{16,24},{20,28},{24,16},{28,20},{1,9},{5... | collective-permute-start | bytes 786440 | tf_op jit(solution)/shard_map/ppermute | solution.py:482
  32.1 9.9 %collective-permute-start.14 = (bf16[256,512]{1,0:T(8,128)(2,1)}, bf16[256,512]{1,0:T(8,128)(2,1)S(1)}, u32[]{:S(2)}, u32[]{:S(2)}) collective-permute-start(bf16[256,512]{1,0:T(8,128)(2,1)} %cut_weights.1), channel_id=1, source_target_pairs={{0,3},{1,2},{2,1},{3,0},{4,7},{5,6},{6,5},{7,4},{8,11},{9,10},{10,... | collective-permute-start | bytes 786440 | tf_op jit(solution)/shard_map/ppermute | solution.py:485
  33.7 13.7 %collective-permute-start.13 = (bf16[256,512]{1,0:T(8,128)(2,1)}, bf16[256,512]{1,0:T(8,128)(2,1)S(1)}, u32[]{:S(2)}, u32[]{:S(2)}) collective-permute-start(bf16[256,512]{1,0:T(8,128)(2,1)} %cut_weights.1), channel_id=1, source_target_pairs={{0,1},{1,0},{2,3},{3,2},{4,5},{5,4},{6,7},{7,6},{8,9},{9,8},{10,11... | collective-permute-start | bytes 786440 | tf_op jit(solution)/shard_map/ppermute | solution.py:485
  33.7 13.7 %collective-permute-start.12 = (bf16[256,512]{1,0:T(8,128)(2,1)S(1)}, bf16[256,512]{1,0:T(8,128)(2,1)S(1)}, u32[]{:S(2)}, u32[]{:S(2)}) collective-permute-start(bf16[256,512]{1,0:T(8,128)(2,1)S(1)} %collective-permute-done.5.refs_2_), channel_id=1, source_target_pairs={{0,16},{4,20},{8,24},{12,28},{16,0},{20,4},{24,8},{28,12},{1,17},{... | collective-permute-start | bytes 786440 | tf_op jit(solution)/shard_map/ppermute | solution.py:482
  34.5 12.9 %collective-permute-start.11 = (bf16[256,512]{1,0:T(8,128)(2,1)S(1)}, bf16[256,512]{1,0:T(8,128)(2,1)S(1)}, u32[]{:S(2)}, u32[]{:S(2)}) collective-permute-start(bf16[256,512]{1,0:T(8,128)(2,1)S(1)} %collective-permute-done.5.refs_2_), channel_id=1, source_target_pairs={{0,8},{4,12},{8,0},{12,4},{16,24},{20,28},{24,16},{28,20},{1,9},{5... | collective-permute-start | bytes 786440 | tf_op jit(solution)/shard_map/ppermute | solution.py:482
  34.7 12.7 %collective-permute-start.10 = (bf16[256,512]{1,0:T(8,128)(2,1)S(1)}, bf16[256,512]{1,0:T(8,128)(2,1)S(1)}, u32[]{:S(2)}, u32[]{:S(2)}) collective-permute-start(bf16[256,512]{1,0:T(8,128)(2,1)S(1)} %collective-permute-done.5.refs_2_), channel_id=1, source_target_pairs={{0,24},{4,28},{8,16},{12,20},{16,8},{20,12},{24,0},{28,4},{1,25},{... | collective-permute-start | bytes 786440 | tf_op jit(solution)/shard_map/ppermute | solution.py:482
  36.4 1.6 %copy-start.3 = (bf16[1,256,4096]{2,1,0:T(8,128)(2,1)S(1)}, bf16[1,256,4096]{2,1,0:T(8,128)(2,1)}, u32[]{:S(2)}) copy-start(bf16[1,256,4096]{2,1,0:T(8,128)(2,1)} %param.6) | copy-start | bytes 6291460
  47.4 4.8 %copy-start = (bf16[1,256,2048]{2,1,0:T(8,128)(2,1)S(1)}, bf16[1,256,2048]{2,1,0:T(8,128)(2,1)}, u32[]{:S(2)}) copy-start(bf16[1,256,2048]{2,1,0:T(8,128)(2,1)} %param.9) | copy-start | bytes 3145732
  47.4 4.8 %copy-start.5 = (s32[1,256]{1,0:T(1,128)S(1)}, s32[1,256]{1,0:T(1,128)}, u32[]{:S(2)}) copy-start(s32[1,256]{1,0:T(1,128)} %marks_a) | copy-start | bytes 3076
  49.6 13.5 %collective-permute-start.16 = (bf16[512,512]{1,0:T(8,128)(2,1)S(1)}, bf16[512,512]{1,0:T(8,128)(2,1)S(1)}, u32[]{:S(2)}, u32[]{:S(2)}) collective-permute-start(bf16[512,512]{1,0:T(8,128)(2,1)S(1)} %get-tuple-element.62.refs_0_), channel_id=1, source_target_pairs={{0,16},{4,20},{8,24},{12,28},{1,17},{5,21},{9,25},{13,29},{2,18},{... | collective-permute-start | bytes 1572872 | tf_op jit(solution)/shard_map/ppermute | solution.py:482
  50.9 13.5 %collective-permute-start.15 = (bf16[512,512]{1,0:T(8,128)(2,1)S(1)}, bf16[512,512]{1,0:T(8,128)(2,1)S(1)}, u32[]{:S(2)}, u32[]{:S(2)}) collective-permute-start(bf16[512,512]{1,0:T(8,128)(2,1)S(1)} %get-tuple-element.62.refs_0_), channel_id=1, source_target_pairs={{0,8},{4,12},{8,0},{12,4},{16,24},{20,28},{1,9},{5,13},{9,1},{13,5... | collective-permute-start | bytes 1572872 | tf_op jit(solution)/shard_map/ppermute | solution.py:482
  64.5 9.8 %collective-permute-start.17 = (bf16[256,512]{1,0:T(8,128)(2,1)S(1)}, bf16[256,512]{1,0:T(8,128)(2,1)S(1)}, u32[]{:S(2)}, u32[]{:S(2)}) collective-permute-start(bf16[256,512]{1,0:T(8,128)(2,1)S(1)} %slice.6), channel_id=1, source_target_pairs={{0,16},{4,20},{8,24},{12,28},{1,17},{5,21},{9,25},{13,29},{2,18},{... | collective-permute-start | bytes 786440 | tf_op jit(solution)/shard_map/ppermute | solution.py:482
  65.8 8.5 %collective-permute-start.18 = (bf16[256,512]{1,0:T(8,128)(2,1)S(1)}, bf16[256,512]{1,0:T(8,128)(2,1)S(1)}, u32[]{:S(2)}, u32[]{:S(2)}) collective-permute-start(bf16[256,512]{1,0:T(8,128)(2,1)S(1)} %slice.7), channel_id=1, source_target_pairs={{16,24},{20,28},{24,16},{28,20},{17,25},{21,29},{25,17},{29,21},{1... | collective-permute-start | bytes 786440 | tf_op jit(solution)/shard_map/ppermute | solution.py:482
  77.3 4.5 %collective-permute-start.20 = (bf16[256,768]{1,0:T(8,128)(2,1)S(1)}, bf16[256,768]{1,0:T(8,128)(2,1)S(1)}, u32[]{:S(2)}, u32[]{:S(2)}) collective-permute-start(bf16[256,768]{1,0:T(8,128)(2,1)S(1)} %get-tuple-element.80), channel_id=1, source_target_pairs={{0,4},{4,0},{8,12},{12,8},{16,20},{20,16},{24,28},{28,24},{1,5},{5... | collective-permute-start | bytes 1179656 | tf_op jit(solution)/shard_map/ppermute | solution.py:477
  81.7 1.6 %collective-permute-start.19 = (bf16[256,256]{1,0:T(8,128)(2,1)S(1)}, bf16[256,256]{1,0:T(8,128)(2,1)S(1)}, u32[]{:S(2)}, u32[]{:S(2)}) collective-permute-start(bf16[256,256]{1,0:T(8,128)(2,1)S(1)} %get-tuple-element.77), channel_id=1, source_target_pairs={{0,4},{4,0},{8,12},{12,8},{16,20},{20,16},{24,28},{28,24},{1,5},{5... | collective-permute-start | bytes 393224 | tf_op jit(solution)/shard_map/ppermute | solution.py:477
